TPU v7x, 512 devices: a whole 4x8x8 slice. The times are simulated.
512 devices in a mesh: ctx: 16 (over z_lo, y), exp: 32 (over x, z_hi, core).
Axes of the slice: x: 4, y: 8, z: 8 (z_hi: 4, z_lo: 2; z = z_hi * 2 + z_lo), core: 2. Of those that a mesh axis runs over, the one named last changes fastest.
Arguments:
- queries: bfloat16 [2048, 8192], P('ctx', 'exp'), may hold values from -6 to 6
- keys: bfloat16 [2048, 512], P('ctx'), may hold values from -6 to 6
- values: bfloat16 [2048, 512], P('ctx'), may hold values from -5 to 5
- residual: bfloat16 [2048, 4096], P(('ctx', 'exp')), may hold values from -6 to 6
- out_weight: bfloat16 [8192, 4096], P('exp'), may hold values from -0.125 to 0.125
- norm_gain: float32 [4096], replicated, may hold values from 0.25 to 1.75
- expert_ids: int32 [2048, 8], P(('ctx', 'exp')), may hold values from 0 to 31, all different within a row; in each aligned block of 4 rows (0 to 3, 4 to 7, ...) at most 2 rows name the same one
- expert_gates: float32 [2048, 8], P(('ctx', 'exp')), may hold values from 0.05 to 0.35
- w_gate: bfloat16 [32, 4096, 1536], P('exp', None, 'ctx'), may hold values from -0.09375 to 0.09375
- w_up: bfloat16 [32, 4096, 1536], P('exp', None, 'ctx'), may hold values from -0.09375 to 0.09375
- w_down: bfloat16 [32, 1536, 4096], P('exp', None, 'ctx'), may hold values from -0.3125 to 0.3125
Outputs:
- mixed: bfloat16 [2048, 4096], P(('ctx', 'exp'))
- experts_out: bfloat16 [2048, 4096], P(('ctx', 'exp'))
Inputs may be any that keep to these rules, and one draw needn't show every extreme that they name: `expert_ids`: in each aligned block of 4 rows (the rows of one device) no expert is named by more than 2 rows, a bound that some block reaches.
All inputs are finite; a program needn't handle non-finite values.
Results may differ from a plain program's by a relative error of at most 0.034.
Values may be sent and summed in bfloat16 or wider, within the bound.
No kernel may reach another device: no remote copies, remote signals or barrier semaphores. Data moves between devices by JAX's collectives and lax.ppermute only.
A program may use at most 64 MiB of HBM per device.

v0:
```python
import jax
import jax.numpy as jnp
from jax import lax
from jax.sharding import PartitionSpec as P

QUERY_HEAD_COUNT = 64
KEY_VALUE_HEADS = 4
HEAD_WIDTH = 128


neg_large = -1e30
eps_norm = 1e-06


def shifted(value, axis, by):
    size = lax.axis_size(axis)
    pairs = [(i, i + by) for i in range(size) if 0 <= i + by < size]
    return lax.ppermute(value, axis, pairs)


def slot_numbers(expert_ids):
    tok_rows, top_count = expert_ids.shape
    flat_ids = expert_ids.reshape(-1)
    owner_row = jnp.arange(tok_rows * top_count, dtype=jnp.int32) // top_count
    earlier = (flat_ids[:, None] == flat_ids[None, :]) & (owner_row[None, :] < owner_row[:, None])
    return jnp.sum(earlier.astype(jnp.int32), axis=1).reshape(tok_rows, top_count)


def route_hits(expert_ids, slot_ids, expert_count, capacity):
    expert_hit = (
        expert_ids[None, None, :, :]
        == jnp.arange(expert_count, dtype=jnp.int32)[:, None, None, None]
    )
    slot_hit = (
        slot_ids[None, None, :, :] == jnp.arange(capacity, dtype=jnp.int32)[None, :, None, None]
    )
    return expert_hit & slot_hit


def expert_hidden(rows_block, gate_local, up_local):
    gate = jnp.dot(rows_block, gate_local, preferred_element_type=jnp.float32)
    upper = jnp.dot(rows_block, up_local, preferred_element_type=jnp.float32)
    return (jax.nn.silu(gate) * upper).astype(jnp.bfloat16)


def on_device(
    queries,
    keys,
    values,
    residual,
    out_weight,
    norm_gain,
    expert_ids,
    expert_gates,
    w_gate,
    w_up,
    w_down,
):
    tok_query = queries.shape[0]
    device_share = queries.shape[1] // HEAD_WIDTH
    ctx_pos = lax.axis_index("ctx")
    key_value_head = lax.axis_index("exp") * device_share // (QUERY_HEAD_COUNT // KEY_VALUE_HEADS)
    own_keys = lax.dynamic_slice_in_dim(keys, key_value_head * HEAD_WIDTH, HEAD_WIDTH, 1)
    own_values = lax.dynamic_slice_in_dim(values, key_value_head * HEAD_WIDTH, HEAD_WIDTH, 1)
    own_block = jnp.stack([own_keys, own_values])
    query_heads = queries.reshape(tok_query, device_share, HEAD_WIDTH)
    query_start = ctx_pos * tok_query
    query_pos = query_start + jnp.arange(tok_query, dtype=jnp.int32)
    scale = 1.0 / HEAD_WIDTH**0.5
    start_state = (
        jnp.full((device_share, tok_query), neg_large, jnp.float32),
        jnp.zeros((device_share, tok_query), jnp.float32),
        jnp.zeros((device_share, tok_query, HEAD_WIDTH), jnp.float32),
    )

    def attend(state_now, kv_piece, key_start):

        def compute(current):
            running_max, running_sum, weighted = current
            key_pos = key_start + jnp.arange(kv_piece.shape[1], dtype=jnp.int32)
            allowed = key_pos[None, :] <= query_pos[:, None]
            scores = (
                jnp.einsum(
                    "qhd,kd->hqk", query_heads, kv_piece[0], preferred_element_type=jnp.float32
                )
                * scale
            )
            scores = jnp.where(allowed[None], scores, neg_large)
            new_max = jnp.maximum(running_max, jnp.max(scores, axis=2))
            weights_blk = jnp.where(allowed[None], jnp.exp(scores - new_max[:, :, None]), 0.0)
            shrink = jnp.exp(running_max - new_max)
            new_sum = running_sum * shrink + jnp.sum(weights_blk, axis=2)
            added = jnp.einsum(
                "hqk,kd->hqd",
                weights_blk.astype(jnp.bfloat16),
                kv_piece[1],
                preferred_element_type=jnp.float32,
            )
            return (new_max, new_sum, weighted * shrink[:, :, None] + added)

        def unchanged(current):
            return current

        useful = (key_start >= 0) & (key_start <= query_start + tok_query - 1)
        return lax.cond(useful, compute, unchanged, state_now)

    ctx_count = lax.axis_size("ctx")
    state_now = attend(start_state, own_block, query_start)

    def cycle_turn(cycle_step, carried):
        state_cur, moving = carried
        moving = shifted(moving, "ctx", 1)
        source = ctx_pos - cycle_step
        return (attend(state_cur, moving, source * tok_query), moving)

    state_now, _ = lax.fori_loop(1, ctx_count, cycle_turn, (state_now, own_block))
    running_max, running_sum, weighted = state_now
    heads_done = (weighted / running_sum[:, :, None]).astype(jnp.bfloat16)
    heads_done = jnp.transpose(heads_done, (1, 0, 2)).reshape(tok_query, device_share * HEAD_WIDTH)
    tok_rows, top_count = expert_ids.shape
    projected = lax.psum_scatter(
        jnp.dot(heads_done, out_weight, preferred_element_type=jnp.float32).astype(jnp.bfloat16),
        "exp",
        scatter_dimension=0,
        tiled=True,
    ).astype(jnp.float32)
    mixed = (residual.astype(jnp.float32) + projected).astype(jnp.bfloat16)
    stream = mixed.astype(jnp.float32)
    mean_sq = jnp.mean(stream * stream, axis=1, keepdims=True)
    normed = (stream * lax.rsqrt(mean_sq + eps_norm) * norm_gain[None, :]).astype(jnp.bfloat16)
    expert_count = lax.axis_size("exp")
    ctx_count = lax.axis_size("ctx")
    capacity = min(tok_rows, 2 * tok_rows * top_count // expert_count)
    slot_ids = slot_numbers(expert_ids)
    hits = route_hits(expert_ids, slot_ids, expert_count, capacity)
    send_table = jnp.any(hits, axis=3).astype(jnp.bfloat16)
    gate_local = w_gate[0]
    up_local = w_up[0]
    down_local = w_down[0]
    width = normed.shape[1]
    outgoing = jnp.einsum(
        "ecm,md->ecd", send_table, normed, preferred_element_type=jnp.float32
    ).astype(jnp.bfloat16)
    arrived = lax.all_to_all(outgoing, "exp", split_axis=0, concat_axis=0, tiled=True)
    local_rows = arrived.reshape(-1, width)
    hidden = expert_hidden(
        lax.all_gather(local_rows, "ctx", axis=0, tiled=True), gate_local, up_local
    )
    expert_result = jnp.dot(
        lax.all_gather(hidden, "ctx", axis=1, tiled=True),
        down_local,
        preferred_element_type=jnp.float32,
    ).astype(jnp.bfloat16)
    expert_result = expert_result.reshape(ctx_count, expert_count, capacity, down_local.shape[1])
    returned = lax.all_to_all(
        lax.all_to_all(expert_result, "ctx", split_axis=0, concat_axis=3, tiled=True),
        "exp",
        split_axis=1,
        concat_axis=0,
        tiled=True,
    )
    returned = returned.reshape(expert_count, capacity, width)
    mix_table = jnp.sum(jnp.where(hits, expert_gates[None, None, :, :], 0.0), axis=3)
    experts_out = jnp.einsum(
        "ecm,ecd->md", mix_table, returned.astype(jnp.float32), precision=lax.Precision.HIGHEST
    )
    return (mixed, experts_out.astype(jnp.bfloat16))


def solution(mesh):
    return jax.shard_map(
        on_device,
        mesh=mesh,
        in_specs=(
            P("ctx", "exp"),
            P("ctx", None),
            P("ctx", None),
            P(("ctx", "exp"), None),
            P("exp", None),
            P(),
            P(("ctx", "exp"), None),
            P(("ctx", "exp"), None),
            P("exp", None, "ctx"),
            P("exp", None, "ctx"),
            P("exp", None, "ctx"),
        ),
        out_specs=(P(("ctx", "exp"), None), P(("ctx", "exp"), None)),
        check_vma=False,
    )
```

profile of v0, /device:TPU:1, one launch (start us, length us, event | category | flops | bytes accessed | tf_op | source)
XLA Modules:
  0.0 722.0 jit_solution(5886836841934353712)
XLA Ops:
  12.4 103.2 %while.22 = (s32[]{:T(128)}, f32[2,128]{1,0:T(2,128)}, f32[2,128]{1,0:T(2,128)S(1)}, f32[2,128,128]{2,1,0:T(8,128)S(1)}, bf16[2,128,128]{2,1,0:T(8,128)(2,1)S(1)...) while((s32[]{:T(128)}, f32[2,128]{1,0:T(2,128)}, ...), condition=%wide.region_9.10_spmd.clone, body=%wide.region_4.9_spmd.clone.sunk | while | flops 17154824 | bytes 1264975 | solution.py:116
  12.4 4.0 collective-permute-start
  17.8 6.2 collective-permute-start
  25.4 3.7 collective-permute-start
  30.6 5.7 collective-permute-start
  37.9 4.7 collective-permute-start
  44.5 6.8 collective-permute-start
  52.7 4.9 collective-permute-start
  59.2 7.1 collective-permute-start
  67.6 5.2 collective-permute-start
  74.2 4.8 collective-permute-start
  80.3 4.9 collective-permute-start
  86.6 4.9 collective-permute-start
  92.8 5.0 collective-permute-start
  99.2 8.3 %collective-permute-start = (bf16[2,128,128]{2,1,0:T(8,128)(2,1)S(1)}, bf16[2,128,128]{2,1,0:T(8,128)(2,1)S(1)}, u32[]{:S(2)}, u32[]{:S(2)}) collective-permute-start(bf16[2,128,128]{2,1,0:T(8,128)(2,1)S(1)} %get-tuple-element.477), channel_id=1, source_target_pairs={{0,32},{32,64},{64,96},{96,128},{128,160},{160,192},{192,224},{224... | collective-permute-start | bytes 196616 | tf_op jit(solution)/shard_map/while/body/eval_jaxpr/ppermute | solution.py:18
  108.9 5.4 collective-permute-start
  119.9 333.2 %all-reduce.3.cloned.1.call-done = bf16[128,4096]{1,0:T(8,128)(2,1)} async-done(((bf16[128,4096]{1,0:T(8,128)(2,1)}), bf16[128,4096]{1,0:T(8,128)(2,1)}) %all-reduce.3.cloned.1.call-update) | async-done | bytes 1048592
  455.0 26.1 %all_to_all.32 = bf16[32,2,4096]{2,1,0:T(2,128)(2,1)S(1)} all-to-all(bf16[32,2,4096]{2,1,0:T(2,128)(2,1)S(1)} %copy.39), channel_id=1, replica_groups=mesh['ctx'=16,'exp'=32] {'exp'}, dimensions={0} | all-to-all | bytes 1048576 | tf_op jit(solution)/shard_map/all_to_all | solution.py:144
  482.2 99.0 %all-gather.3.cloned.1.call-done = bf16[1024,4096]{1,0:T(8,128)(2,1)} async-done(((bf16[64,4096]{1,0:T(8,128)(2,1)}), bf16[1024,4096]{1,0:T(8,128)(2,1)}) %all-gather.3.cloned.1.call-update) | async-done | bytes 8388624 | tf_op jit(solution)/shard_map/all_gather | solution.py:147
  581.2 6.2 fusion.31
  590.9 65.8 %all-gather.5.cloned.1.call-done = bf16[1024,1536]{0,1:T(8,128)(2,1)} async-done(((bf16[1024,96]{0,1:T(8,128)(2,1)}), bf16[1024,1536]{0,1:T(8,128)(2,1)}) %all-gather.5.cloned.1.call-update) | async-done | bytes 3145744 | tf_op jit(solution)/shard_map/all_gather | solution.py:150
  660.1 13.9 %all_to_all.33 = bf16[16,32,2,256]{3,2,1,0:T(2,128)(2,1)S(1)} all-to-all(bf16[16,32,2,256]{3,2,1,0:T(2,128)(2,1)S(1)} %reshape.150), channel_id=1, replica_groups=mesh['ctx'=16,'exp'=32] {'ctx'}, dimensions={0} | all-to-all | bytes 1048576 | tf_op jit(solution)/shard_map/all_to_all | solution.py:156
  675.4 20.8 %all-to-all-start.2 = ((bf16[1,32,2,4096]{3,2,0,1:T(2,128)(2,1)}), bf16[1,32,2,4096]{3,2,0,1:T(2,128)(2,1)S(1)}, u32[]{:S(2)}, u32[]{:S(2)}) async-start(bf16[1,32,2,4096]{3,2,0,1:T(2,128)(2,1)} %all_to_all.27), calls=%async_computation.2 | async-start | bytes 1048576 | tf_op jit(solution)/shard_map/all_to_all | solution.py:155
  696.3 18.0 %all-to-all-done.2 = bf16[1,32,2,4096]{3,2,0,1:T(2,128)(2,1)S(1)} async-done(((bf16[1,32,2,4096]{3,2,0,1:T(2,128)(2,1)}), bf16[1,32,2,4096]{3,2,0,1:T(2,128)(2,1)S(1)}, u32[]{:S(2)}, u32[]{:S(2)}) %all-to-all-start.2) | async-done | bytes 524320 | tf_op jit(solution)/shard_map/all_to_all | solution.py:155
  (120 shorter events, 45.1 us)
Async XLA Ops:
  7.2 108.7 %copy-start = (bf16[256,4096]{1,0:T(8,128)(2,1)S(1)}, bf16[256,4096]{1,0:T(8,128)(2,1)}, u32[]{:S(2)}) copy-start(bf16[256,4096]{1,0:T(8,128)(2,1)} %param.21) | copy-start | bytes 6291460
  7.2 445.9 %all-reduce.3.cloned.1.call-start = ((), (), s32[]{:S(2)}) async-start(), calls=%async_computation.5 | async-start | bytes 2097152
  12.4 5.3 collective-permute-start
  17.8 7.5 %collective-permute-start = (bf16[2,128,128]{2,1,0:T(8,128)(2,1)S(1)}, bf16[2,128,128]{2,1,0:T(8,128)(2,1)S(1)}, u32[]{:S(2)}, u32[]{:S(2)}) collective-permute-start(bf16[2,128,128]{2,1,0:T(8,128)(2,1)S(1)} %get-tuple-element.477), channel_id=1, source_target_pairs={{0,32},{32,64},{64,96},{96,128},{128,160},{160,192},{192,224},{224... | collective-permute-start | bytes 196616 | tf_op jit(solution)/shard_map/while/body/eval_jaxpr/ppermute | solution.py:18
  25.4 5.2 collective-permute-start
  30.6 7.2 collective-permute-start
  37.9 6.6 collective-permute-start
  44.5 8.1 %collective-permute-start = (bf16[2,128,128]{2,1,0:T(8,128)(2,1)S(1)}, bf16[2,128,128]{2,1,0:T(8,128)(2,1)S(1)}, u32[]{:S(2)}, u32[]{:S(2)}) collective-permute-start(bf16[2,128,128]{2,1,0:T(8,128)(2,1)S(1)} %get-tuple-element.477), channel_id=1, source_target_pairs={{0,32},{32,64},{64,96},{96,128},{128,160},{160,192},{192,224},{224... | collective-permute-start | bytes 196616 | tf_op jit(solution)/shard_map/while/body/eval_jaxpr/ppermute | solution.py:18
  52.7 6.6 collective-permute-start
  59.2 8.4 %collective-permute-start = (bf16[2,128,128]{2,1,0:T(8,128)(2,1)S(1)}, bf16[2,128,128]{2,1,0:T(8,128)(2,1)S(1)}, u32[]{:S(2)}, u32[]{:S(2)}) collective-permute-start(bf16[2,128,128]{2,1,0:T(8,128)(2,1)S(1)} %get-tuple-element.477), channel_id=1, source_target_pairs={{0,32},{32,64},{64,96},{96,128},{128,160},{160,192},{192,224},{224... | collective-permute-start | bytes 196616 | tf_op jit(solution)/shard_map/while/body/eval_jaxpr/ppermute | solution.py:18
  67.6 6.5 collective-permute-start
  74.2 6.1 collective-permute-start
  80.3 6.2 collective-permute-start
  86.6 6.2 collective-permute-start
  92.8 6.3 collective-permute-start
  99.2 9.7 %collective-permute-start = (bf16[2,128,128]{2,1,0:T(8,128)(2,1)S(1)}, bf16[2,128,128]{2,1,0:T(8,128)(2,1)S(1)}, u32[]{:S(2)}, u32[]{:S(2)}) collective-permute-start(bf16[2,128,128]{2,1,0:T(8,128)(2,1)S(1)} %get-tuple-element.477), channel_id=1, source_target_pairs={{0,32},{32,64},{64,96},{96,128},{128,160},{160,192},{192,224},{224... | collective-permute-start | bytes 196616 | tf_op jit(solution)/shard_map/while/body/eval_jaxpr/ppermute | solution.py:18
  108.9 6.8 collective-permute-start
  115.7 337.4 %copy-start.4 = (bf16[4,4096]{1,0:T(4,128)(2,1)S(1)}, bf16[4,4096]{1,0:T(4,128)(2,1)}, u32[]{:S(2)}) copy-start(bf16[4,4096]{1,0:T(4,128)(2,1)} %param.20) | copy-start | bytes 98308
  115.7 338.4 %copy-start.5 = (f32[4096]{0:T(1024)S(1)}, f32[4096]{0:T(1024)}, u32[]{:S(2)}) copy-start(f32[4096]{0:T(1024)} %param.22) | copy-start | bytes 49156
  117.4 463.9 %copy-start.2 = (bf16[1,4096,96]{1,2,0:T(8,128)(2,1)S(1)}, bf16[1,4096,96]{1,2,0:T(8,128)(2,1)}, u32[]{:S(2)}) copy-start(bf16[1,4096,96]{1,2,0:T(8,128)(2,1)} %param.25) | copy-start | bytes 2359300
  117.4 463.8 %all-gather.3.cloned.1.call-start = ((), (), s32[]{:S(2)}) async-start(), calls=%async_computation.3 | async-start | bytes 8912896 | tf_op jit(solution)/shard_map/all_gather | solution.py:147
  454.1 133.4 %copy-start.3 = (bf16[4,4096]{1,0:T(4,128)(2,1)}, bf16[4,4096]{1,0:T(4,128)(2,1)S(1)}, u32[]{:S(2)}) copy-start(bf16[4,4096]{1,0:T(4,128)(2,1)S(1)} %get-tuple-element.377) | copy-start | bytes 98308
  482.2 174.6 %all-gather.5.cloned.1.call-start = ((), (), s32[]{:S(2)}) async-start(), calls=%async_computation.4 | async-start | bytes 3342336 | tf_op jit(solution)/shard_map/all_gather | solution.py:150
  675.4 38.9 %all-to-all-start.2 = ((bf16[1,32,2,4096]{3,2,0,1:T(2,128)(2,1)}), bf16[1,32,2,4096]{3,2,0,1:T(2,128)(2,1)S(1)}, u32[]{:S(2)}, u32[]{:S(2)}) async-start(bf16[1,32,2,4096]{3,2,0,1:T(2,128)(2,1)} %all_to_all.27), calls=%async_computation.2 | async-start | bytes 1048576 | tf_op jit(solution)/shard_map/all_to_all | solution.py:155
  (4 other events, 50.6 us)
Sparse Core Ops, SparseCore 0:
  117.5 335.5 all-reduce.2
  482.3 98.8 all-gather.2
  591.0 65.6 all-gather.4
where the time goes:
time: 723 us; the launch traced here: 722 us
  waiting for transfers between devices  537 us (74%)
  starting transfers between devices  103 us (14%)
  blocking collectives  40 us (6%)
  matrix products  16.8 us (2%)
  between operations  14.6 us (2%)
    unnamed x4, waiting for transfers between devices  333 us
    all_gather x1, waiting for transfers between devices, on_device(): lax.all_gather(local_rows, 'ctx', axis=0, tiled=True)  99 us
    ppermute x15, starting transfers between devices, shifted(): return lax.ppermute(value, axis, pairs)  81.7 us
    all_gather x1, waiting for transfers between devices, on_device(): lax.all_gather(hidden, 'ctx', axis=1, tiled=True)  65.8 us
    all_to_all x1, blocking collectives, on_device(): lax.all_to_all(outgoing, 'exp', split_axis=0, concat_axis=0, tiled=True)  26.1 us
    all_to_all x1, starting transfers between devices, on_device(): lax.all_to_all(lax.all_to_all(expert_result, 'ctx', split_axis=0, concat_...  20.8 us
    ppermute x15, waiting for transfers between devices, shifted(): return lax.ppermute(value, axis, pairs)  20.8 us
    all_to_all x1, waiting for transfers between devices, on_device(): lax.all_to_all(lax.all_to_all(expert_result, 'ctx', split_axis=0, concat_...  18 us
  transfers between devices with their start and end apart: 19, of which 19 were waited for; matrix products, arithmetic and copies ran while one was open for 0% of the time, Pallas kernels for 0%

commit v1 on v0

v1 whole, which is shorter than its diff:
```python
import jax
import jax.numpy as jnp
import numpy as np
from jax import lax
from jax.sharding import Mesh, PartitionSpec as P

HEAD_WIDTH = 128
EXTRA = 128

CTX = ("zl", "y")
EXP = ("x", "zh", "co")
EPS_NORM = 1e-06
NEG_LARGE = -1e30


def exchange(pieces, axis):
    return lax.all_to_all(pieces, axis, 0, 0, tiled=True)


def spread(value, axis, count):
    return exchange(jnp.broadcast_to(value[None], (count,) + value.shape), axis)


def added(pieces):
    return jnp.sum(pieces.astype(jnp.float32), axis=0)


def rows_dot(left, right):
    return lax.dot_general(
        left, right, (((1,), (1,)), ((), ())), preferred_element_type=jnp.float32
    )


def route(expert_ids, expert_gates, expert_count, slots):
    flat_ids = expert_ids.reshape(-1)
    tok_rows, top_count = expert_ids.shape
    owner_row = jnp.arange(tok_rows * top_count, dtype=jnp.int32) // top_count
    earlier = (flat_ids[:, None] == flat_ids[None, :]) & (owner_row[None, :] < owner_row[:, None])
    slot_ids = jnp.sum(earlier.astype(jnp.int32), axis=1).reshape(tok_rows, top_count)
    expert_hit = (
        expert_ids[None, None] == jnp.arange(expert_count, dtype=jnp.int32)[:, None, None, None]
    )
    slot_hit = slot_ids[None, None] == jnp.arange(slots, dtype=jnp.int32)[None, :, None, None]
    hits = expert_hit & slot_hit
    table = jnp.any(hits, axis=3).astype(jnp.bfloat16)
    mix = jnp.sum(jnp.where(hits, expert_gates[None, None], 0.0), axis=3)
    return table.reshape(expert_count * slots, tok_rows), mix.reshape(
        expert_count * slots, tok_rows
    )


def on_device(
    queries,
    keys,
    values,
    residual,
    out_weight,
    norm_gain,
    expert_ids,
    expert_gates,
    w_gate,
    w_up,
    w_down,
):
    n_zl, n_y = lax.axis_size("zl"), lax.axis_size("y")
    n_x, n_zh, n_co = lax.axis_size("x"), lax.axis_size("zh"), lax.axis_size("co")
    zl, y_pos, x_pos, co = (lax.axis_index(a) for a in ("zl", "y", "x", "co"))
    ctx_count, expert_count = n_zl * n_y, n_x * n_zh * n_co
    width = residual.shape[1]
    tok_dev, top_count = expert_ids.shape
    slots = 2
    tok_block = queries.shape[0]
    heads = queries.shape[1] // HEAD_WIDTH
    swap = [(i, n_zl - 1 - i) for i in range(n_zl)]

    gate_up = jnp.stack([w_gate[0].T, w_up[0].T])
    gate_up_other = lax.ppermute(gate_up, "zl", swap)
    down_other = lax.ppermute(w_down[0], "zl", swap)

    mine = jnp.where(co == 0, keys, values)
    mine = lax.dynamic_slice_in_dim(mine, x_pos * HEAD_WIDTH, HEAD_WIDTH, 1)
    gathered = spread(mine, CTX, ctx_count).reshape(ctx_count * tok_block, HEAD_WIDTH)
    key_all, value_all = spread(gathered, "co", n_co)

    order = np.arange(tok_block).reshape(n_x, n_zh, n_co, tok_dev).transpose(2, 0, 1, 3)
    split = queries.reshape(n_x, n_zh, n_co, tok_dev, heads, HEAD_WIDTH)
    query_rows = jnp.transpose(split, (4, 2, 0, 1, 3, 5)).reshape(heads * tok_block, HEAD_WIDTH)
    query_pos = (zl * n_y + y_pos) * tok_block + jnp.asarray(
        np.tile(order.reshape(-1), heads), jnp.int32
    )
    key_pos = jnp.arange(key_all.shape[0], dtype=jnp.int32)
    allowed = key_pos[None, :] <= query_pos[:, None]
    scores = rows_dot(query_rows, key_all) * (1.0 / HEAD_WIDTH**0.5)
    scores = jnp.where(allowed, scores, NEG_LARGE)
    weights = jnp.exp(scores - jnp.max(scores, axis=1, keepdims=True))
    total = jnp.sum(weights, axis=1, keepdims=True)
    numer = jnp.dot(weights.astype(jnp.bfloat16), value_all, preferred_element_type=jnp.float32)
    done = (numer / total).astype(jnp.bfloat16).reshape(heads, tok_block, HEAD_WIDTH)
    heads_out = jnp.transpose(done, (1, 0, 2)).reshape(tok_block, heads * HEAD_WIDTH)

    partial = jnp.dot(heads_out, out_weight, preferred_element_type=jnp.float32)
    partial = partial.astype(jnp.bfloat16).reshape(n_co, tok_block // n_co, width)
    partial = added(exchange(partial, "co")).astype(jnp.bfloat16)
    projected = added(exchange(partial.reshape(n_x * n_zh, tok_dev, width), ("x", "zh")))
    mixed = (residual.astype(jnp.float32) + projected).astype(jnp.bfloat16)

    stream = mixed.astype(jnp.float32)
    mean_sq = jnp.mean(stream * stream, axis=1, keepdims=True)
    normed = (stream * lax.rsqrt(mean_sq + EPS_NORM) * norm_gain[None, :]).astype(jnp.bfloat16)

    table, mix = route(expert_ids, expert_gates, expert_count, slots)
    mix_high = mix.astype(jnp.bfloat16)
    mix_low = (mix - mix_high.astype(jnp.float32)).astype(jnp.bfloat16)
    extra = jnp.concatenate([mix_high, mix_low], axis=1)
    extra = jnp.pad(extra, ((0, 0), (0, EXTRA - extra.shape[1])))
    outgoing = jnp.dot(table, normed, preferred_element_type=jnp.float32).astype(jnp.bfloat16)
    outgoing = jnp.concatenate([outgoing, extra], axis=1)
    arrived = exchange(outgoing.reshape(expert_count, slots, width + EXTRA), EXP)
    rows = lax.all_gather(
        arrived.reshape(expert_count * slots, width + EXTRA), "y", axis=0, tiled=True
    )

    weight_in = jnp.stack([gate_up, gate_up_other], axis=1)
    weight_in = jnp.pad(weight_in, ((0, 0),) * 3 + ((0, EXTRA),)).reshape(-1, width + EXTRA)
    both = rows_dot(weight_in, rows)
    units = both.shape[0] // 2
    hidden = (jax.nn.silu(both[:units]) * both[units:]).astype(jnp.bfloat16)
    hidden = spread(hidden, "y", n_y).reshape(n_y * units, -1)

    down = jnp.concatenate([w_down[0], down_other], axis=1)
    down = down.reshape(n_zl, n_y, units // n_zl, down.shape[1])
    down = jnp.where(zl == 0, down, down[::-1])
    down = jnp.transpose(down, (1, 0, 2, 3)).reshape(n_y * units, -1)
    result = lax.dot_general(
        hidden, down, (((0,), (0,)), ((), ())), preferred_element_type=jnp.float32
    )
    gates = rows[:, width : width + 2 * tok_dev].astype(jnp.float32)
    gates = gates[:, :tok_dev] + gates[:, tok_dev:]
    result = (result * jnp.sum(gates, axis=1, keepdims=True)).astype(jnp.bfloat16)

    block_of = np.arange(n_y * expert_count).reshape(n_y, n_x, n_zh, n_co)
    block_of = block_of.transpose(3, 1, 2, 0).reshape(-1)
    token_of = (block_of[:, None] * tok_dev + np.arange(tok_dev)[None, :]).reshape(-1)
    place = jnp.sum(
        (gates != 0).astype(jnp.int32) * jnp.arange(1, tok_dev + 1, dtype=jnp.int32)[None, :],
        axis=1,
    )
    slot_block = jnp.arange(n_y * expert_count * slots, dtype=jnp.int32) // slots
    slot_token = jnp.where(place > 0, slot_block * tok_dev + place - 1, -1)
    onehot = (jnp.asarray(token_of, jnp.int32)[:, None] == slot_token[None, :]).astype(jnp.bfloat16)
    tokens = jnp.dot(onehot, result, preferred_element_type=jnp.float32).astype(jnp.bfloat16)

    cols = tokens.shape[1]
    tokens = added(exchange(tokens.reshape(n_co, -1, cols), "co")).astype(jnp.bfloat16)
    tokens = added(exchange(tokens.reshape(n_x, -1, cols), "x")).astype(jnp.bfloat16)
    tokens = exchange(tokens.reshape(n_zh * n_y, tok_dev, cols), ("zh", "y"))
    tokens = added(tokens.reshape(n_zh, n_y, tok_dev, cols))
    tokens = tokens.reshape(n_y, tok_dev, n_zl, cols // n_zl).transpose(1, 2, 0, 3)
    tokens = jnp.where(zl == 0, tokens, tokens[:, ::-1])
    return (mixed, tokens.reshape(tok_dev, width).astype(jnp.bfloat16))


def solution(mesh):
    fine = Mesh(mesh.devices.reshape(2, 8, 4, 4, 2), CTX + EXP)
    return jax.shard_map(
        on_device,
        mesh=fine,
        in_specs=(
            P(CTX, EXP),
            P(CTX, None),
            P(CTX, None),
            P(CTX + EXP, None),
            P(EXP, None),
            P(),
            P(CTX + EXP, None),
            P(CTX + EXP, None),
            P(EXP, None, CTX),
            P(EXP, None, CTX),
            P(EXP, None, CTX),
        ),
        out_specs=(P(CTX + EXP, None), P(CTX + EXP, None)),
        check_vma=False,
    )
```

time: 723 us -> 260 us (0.36)
  waiting for transfers between devices: 537 us -> 104 us
  starting transfers between devices: 103 us -> 30.8 us
  blocking collectives: 40 us -> 74.7 us
  other arithmetic: 3.56 us -> 11.8 us
    unnamed x4 -> x1, waiting for transfers between devices: 333 us -> 0.02 us
    all_gather x2 -> x1, waiting for transfers between devices: 165 us -> 11.3 us  [on_device(): lax.all_gather(arrived.reshape(expert_count * slots, width + EXTRA), 'y',...]
    ppermute x15 -> x2, starting transfers between devices: 81.7 us -> 5.19 us  [the longest x1 3.27 us: on_device(): down_other = lax.ppermute(w_down[0], 'zl', swap)]
    all_to_all x2 -> x6, blocking collectives: 40 us -> 74.7 us  [exchange(): return lax.all_to_all(pieces, axis, 0, 0, tiled=True)]
    ppermute x15 -> x2, waiting for transfers between devices: 20.8 us -> 51.8 us  [the longest x1 34.9 us: on_device(): gate_up_other = lax.ppermute(gate_up, 'zl', swap)]
    all_to_all x1 -> x3, waiting for transfers between devices: 18 us -> 41.3 us  [exchange(): return lax.all_to_all(pieces, axis, 0, 0, tiled=True)]
    dot_general x8 -> x6, matrix products: 16.8 us -> 11.5 us  [the longest x2 5.64 us: rows_dot(): lax.dot_general(left, right, (((1,), (1,)), ((), ())), preferred_element_...]
    all_to_all x1 -> x3, starting transfers between devices: 20.8 us -> 25.5 us  [exchange(): return lax.all_to_all(pieces, axis, 0, 0, tiled=True)]
  transfers between devices with their start and end apart: 19 -> 6, of which waited for: 19 -> 6; matrix products, arithmetic and copies ran while one was open for 0% -> 4% of each run, Pallas kernels for 0% -> 0%
where the time goes in v1:
time: 260 us; the launch traced here: 258 us
  waiting for transfers between devices  104 us (40%)
  blocking collectives  74.7 us (29%)
  starting transfers between devices  30.8 us (12%)
  between operations  14.4 us (6%)
  other arithmetic  11.8 us (5%)
  matrix products  11.5 us (4%)
  local copies, waits for them, and re-layouts  10.4 us (4%)
    all_to_all x6, blocking collectives, exchange(): return lax.all_to_all(pieces, axis, 0, 0, tiled=True)  74.7 us
    all_to_all x3, waiting for transfers between devices, exchange(): return lax.all_to_all(pieces, axis, 0, 0, tiled=True)  41.3 us
    ppermute x1, waiting for transfers between devices, on_device(): gate_up_other = lax.ppermute(gate_up, 'zl', swap)  34.9 us
    all_to_all x3, starting transfers between devices, exchange(): return lax.all_to_all(pieces, axis, 0, 0, tiled=True)  25.5 us
    ppermute x1, waiting for transfers between devices, on_device(): down_other = lax.ppermute(w_down[0], 'zl', swap)  16.9 us
    all_gather x1, waiting for transfers between devices, on_device(): lax.all_gather(arrived.reshape(expert_count * slots, width + EXTRA), 'y',...  11.3 us
    dot_general x2, matrix products, rows_dot(): lax.dot_general(left, right, (((1,), (1,)), ((), ())), preferred_element_...  5.64 us
  transfers between devices with their start and end apart: 6, of which 6 were waited for; matrix products, arithmetic and copies ran while one was open for 4% of the time, Pallas kernels for 0%

profile of v1, /device:TPU:1, one launch (start us, length us, event | category | flops | bytes accessed | tf_op | source)
XLA Modules:
  0.0 257.9 jit_solution(8927563244535573260)
XLA Ops:
  9.0 9.6 %all-to-all-start = ((bf16[16,128,128]{2,1,0:T(8,128)(2,1)}), bf16[16,128,128]{2,1,0:T(8,128)(2,1)S(1)}, u32[]{:S(2)}, u32[]{:S(2)}) async-start(bf16[16,128,128]{2,1,0:T(8,128)(2,1)} %broadcast_in_dim.21), calls=%async_computation | async-start | bytes 1048576 | tf_op jit(solution)/shard_map/all_to_all | solution.py:17
  21.2 11.1 %all-to-all-done = bf16[16,128,128]{2,1,0:T(8,128)(2,1)S(1)} async-done(((bf16[16,128,128]{2,1,0:T(8,128)(2,1)}), bf16[16,128,128]{2,1,0:T(8,128)(2,1)S(1)}, u32[]{:S(2)}, u32[]{:S(2)}) %all-to-all-start) | async-done | bytes 524320 | tf_op jit(solution)/shard_map/all_to_all | solution.py:17
  32.4 7.1 %all_to_all.45 = bf16[2,2048,128]{2,1,0:T(8,128)(2,1)S(1)} all-to-all(bf16[2,2048,128]{2,1,0:T(8,128)(2,1)S(1)} %broadcast_in_dim.23), channel_id=1, replica_groups=mesh['zl'=2,'y'=8,'x'=4,'zh'=4,'co'=2] {'co'}, dimensions={0} | all-to-all | bytes 2097152 | tf_op jit(solution)/shard_map/all_to_all | solution.py:17
  41.5 4.6 %all_to_all.46 = bf16[2,64,4096]{2,1,0:T(8,128)(2,1)S(1)} all-to-all(bf16[2,64,4096]{2,1,0:T(8,128)(2,1)S(1)} %bitcast.69), channel_id=1, replica_groups=mesh['zl'=2,'y'=8,'x'=4,'zh'=4,'co'=2] {'co'}, dimensions={0} | all-to-all | bytes 2097152 | tf_op jit(solution)/shard_map/all_to_all | solution.py:17
  47.2 2.0 reshape.155
  49.3 11.7 %all-to-all-start.3 = ((bf16[16,4,4096]{2,1,0:T(4,128)(2,1)}), bf16[16,4,4096]{2,1,0:T(4,128)(2,1)S(1)}, u32[]{:S(2)}, u32[]{:S(2)}) async-start(bf16[16,4,4096]{2,1,0:T(4,128)(2,1)} %reshape.155), calls=%async_computation.3 | async-start | bytes 1048576 | tf_op jit(solution)/shard_map/all_to_all | solution.py:17
  61.9 16.5 %all-to-all-done.3 = bf16[16,4,4096]{2,1,0:T(4,128)(2,1)S(1)} async-done(((bf16[16,4,4096]{2,1,0:T(4,128)(2,1)}), bf16[16,4,4096]{2,1,0:T(4,128)(2,1)S(1)}, u32[]{:S(2)}, u32[]{:S(2)}) %all-to-all-start.3) | async-done | bytes 524320 | tf_op jit(solution)/shard_map/all_to_all | solution.py:17
  79.6 23.5 %all_to_all.47 = bf16[32,2,4224]{2,1,0:T(2,128)(2,1)S(1)} all-to-all(bf16[32,2,4224]{2,1,0:T(2,128)(2,1)S(1)} %reshape.158), channel_id=1, replica_groups=mesh['zl'=2,'y'=8,'x'=4,'zh'=4,'co'=2] {'x','zh','co'}, dimensions={0} | all-to-all | bytes 1081344 | tf_op jit(solution)/shard_map/all_to_all | solution.py:17
  104.3 1.3 fusion.38
  105.6 1.9 collective-permute-start
  107.6 34.9 %collective-permute-done = bf16[2,96,4096]{2,1,0:T(8,128)(2,1)S(1)} collective-permute-done((bf16[2,96,4096]{2,1,0:T(8,128)(2,1)S(1)}, bf16[2,96,4096]{2,1,0:T(8,128)(2,1)S(1)}, u32[]{:S(2)}, u32[]{:S(2)}) %collective-permute-start) | collective-permute-done | bytes 1572896 | tf_op jit(solution)/shard_map/ppermute | solution.py:77
  142.4 2.0 fusion.2
  144.4 11.3 %all-gather.2.cloned.1.call-done = bf16[512,4224]{1,0:T(8,128)(2,1)} async-done(((bf16[64,4224]{1,0:T(8,128)(2,1)}), bf16[512,4224]{1,0:T(8,128)(2,1)}) %all-gather.2.cloned.1.call-update) | async-done | bytes 4325392 | tf_op jit(solution)/shard_map/all_gather | solution.py:119
  155.7 5.1 %fusion.40 = f32[384,512]{1,0:T(8,128)S(1)} fusion(bf16[384,4224]{1,0:T(8,128)(2,1)} %bitcast.70, bf16[512,4224]{1,0:T(8,128)(2,1)} %all-gather.2.cloned.1.call-done), kind=kOutput, calls=%fused_computation.80 | convolution fusion | flops 1660944384 | bytes 8355840 | tf_op jit(solution)/shard_map/dot_general | solution.py:29
  161.0 1.3 broadcast_in_dim.31
  162.3 4.3 %all-to-all-start.5 = ((bf16[8,192,512]{2,1,0:T(8,128)(2,1)}), bf16[8,192,512]{2,1,0:T(8,128)(2,1)}, u32[]{:S(2)}, u32[]{:S(2)}) async-start(bf16[8,192,512]{2,1,0:T(8,128)(2,1)} %broadcast_in_dim.31), calls=%async_computation.5 | async-start | bytes 3145728 | tf_op jit(solution)/shard_map/all_to_all | solution.py:17
  166.6 3.3 %collective-permute-start.1 = (bf16[1536,256]{1,0:T(8,128)(2,1)S(1)}, bf16[1536,256]{1,0:T(8,128)(2,1)}, u32[]{:S(2)}, u32[]{:S(2)}) collective-permute-start(bf16[1536,256]{1,0:T(8,128)(2,1)S(1)} %bitcast.78), channel_id=1, source_target_pairs={{0,256},{256,0},{1,257},{257,1},{2,258},{258,2},{3,259},{259,3},{4... | collective-permute-start | bytes 2359304 | tf_op jit(solution)/shard_map/ppermute | solution.py:78
  169.9 16.9 %collective-permute-done.1 = bf16[1536,256]{1,0:T(8,128)(2,1)} collective-permute-done((bf16[1536,256]{1,0:T(8,128)(2,1)S(1)}, bf16[1536,256]{1,0:T(8,128)(2,1)}, u32[]{:S(2)}, u32[]{:S(2)}) %collective-permute-start.1) | collective-permute-done | bytes 786464 | tf_op jit(solution)/shard_map/ppermute | solution.py:78
  188.4 1.4 copy.86
  191.2 13.6 %all-to-all-done.5 = bf16[8,192,512]{2,1,0:T(8,128)(2,1)} async-done(((bf16[8,192,512]{2,1,0:T(8,128)(2,1)}), bf16[8,192,512]{2,1,0:T(8,128)(2,1)}, u32[]{:S(2)}, u32[]{:S(2)}) %all-to-all-start.5) | async-done | bytes 1572896 | tf_op jit(solution)/shard_map/all_to_all | solution.py:17
  204.8 4.5 %fusion.10 = bf16[1024,512]{1,0:T(8,128)(2,1)} fusion(s32[512]{0:T(512)S(1)} %fusion.34, s32[1024]{0:T(1024)S(1)} %copy-done.8, bf16[1536,512]{1,0:T(8,128)(2,1)} %bitcast.21, bf16[1536,512]{1,0:T(8,128)(2,1)} %bitcast.73, f32[512]{0:T(512)S(1)} %fusion.23), kind=kOutput, calls=%fused_computation.19 | convolution fusion | flops 1343750144 | bytes 4202496 | tf_op jit(solution)/shard_map/dot_general | solution.py:151
  209.3 8.0 %all_to_all.48 = bf16[2,512,512]{2,1,0:T(8,128)(2,1)S(1)} all-to-all(bf16[2,512,512]{2,1,0:T(8,128)(2,1)} %bitcast.75), channel_id=1, replica_groups=mesh['zl'=2,'y'=8,'x'=4,'zh'=4,'co'=2] {'co'}, dimensions={0} | all-to-all | bytes 2097152 | tf_op jit(solution)/shard_map/all_to_all | solution.py:17
  218.4 12.6 %all_to_all.49 = bf16[4,128,512]{2,1,0:T(8,128)(2,1)S(1)} all-to-all(bf16[4,128,512]{2,1,0:T(8,128)(2,1)} %bitcast.72), channel_id=1, replica_groups=mesh['zl'=2,'y'=8,'x'=4,'zh'=4,'co'=2] {'x'}, dimensions={0} | all-to-all | bytes 1048576 | tf_op jit(solution)/shard_map/all_to_all | solution.py:17
  231.1 18.9 %all_to_all.50 = bf16[32,4,512]{2,1,0:T(4,128)(2,1)S(1)} all-to-all(bf16[32,4,512]{2,1,0:T(4,128)(2,1)S(1)} %reshape.165), channel_id=1, replica_groups=mesh['zl'=2,'y'=8,'x'=4,'zh'=4,'co'=2] {'zh','y'}, dimensions={0} | all-to-all | bytes 262144 | tf_op jit(solution)/shard_map/all_to_all | solution.py:17
  (71 shorter events, 16.1 us)
Async XLA Ops:
  7.2 33.9 %copy-start = (bf16[256,4096]{1,0:T(8,128)(2,1)S(1)}, bf16[256,4096]{1,0:T(8,128)(2,1)}, u32[]{:S(2)}) copy-start(bf16[256,4096]{1,0:T(8,128)(2,1)} %param.17) | copy-start | bytes 6291460
  9.0 23.3 %all-to-all-start = ((bf16[16,128,128]{2,1,0:T(8,128)(2,1)}), bf16[16,128,128]{2,1,0:T(8,128)(2,1)S(1)}, u32[]{:S(2)}, u32[]{:S(2)}) async-start(bf16[16,128,128]{2,1,0:T(8,128)(2,1)} %broadcast_in_dim.21), calls=%async_computation | async-start | bytes 1048576 | tf_op jit(solution)/shard_map/all_to_all | solution.py:17
  46.1 14.9 %copy-start.6 = (s32[4,8]{1,0:T(4,128)S(1)}, s32[4,8]{1,0:T(4,128)}, u32[]{:S(2)}) copy-start(s32[4,8]{1,0:T(4,128)} %param.19) | copy-start | bytes 388
  46.1 15.3 %copy-start.7 = (f32[4,8]{1,0:T(4,128)S(1)}, f32[4,8]{1,0:T(4,128)}, u32[]{:S(2)}) copy-start(f32[4,8]{1,0:T(4,128)} %param.20) | copy-start | bytes 388
  46.1 32.7 %copy-start.4 = (bf16[4,4096]{1,0:T(4,128)(2,1)S(1)}, bf16[4,4096]{1,0:T(4,128)(2,1)}, u32[]{:S(2)}) copy-start(bf16[4,4096]{1,0:T(4,128)(2,1)} %param.16) | copy-start | bytes 98308
  46.1 32.9 %copy-start.5 = (f32[4096]{0:T(1024)S(1)}, f32[4096]{0:T(1024)}, u32[]{:S(2)}) copy-start(f32[4096]{0:T(1024)} %param.18) | copy-start | bytes 49156
  49.3 29.1 %all-to-all-start.3 = ((bf16[16,4,4096]{2,1,0:T(4,128)(2,1)}), bf16[16,4,4096]{2,1,0:T(4,128)(2,1)S(1)}, u32[]{:S(2)}, u32[]{:S(2)}) async-start(bf16[16,4,4096]{2,1,0:T(4,128)(2,1)} %reshape.155), calls=%async_computation.3 | async-start | bytes 1048576 | tf_op jit(solution)/shard_map/all_to_all | solution.py:17
  61.0 94.7 %all-gather.2.cloned.1.call-start = ((), (), s32[]{:S(2)}) async-start(), calls=%async_computation.9 | async-start | bytes 4866048 | tf_op jit(solution)/shard_map/all_gather | solution.py:119
  79.0 25.1 %copy-start.3 = (bf16[4,4096]{1,0:T(4,128)(2,1)}, bf16[4,4096]{1,0:T(4,128)(2,1)S(1)}, u32[]{:S(2)}) copy-start(bf16[4,4096]{1,0:T(4,128)(2,1)S(1)} %get-tuple-element.3) | copy-start | bytes 98308
  103.1 1.2 copy-start.1
  105.6 36.8 %collective-permute-start = (bf16[2,96,4096]{2,1,0:T(8,128)(2,1)S(1)}, bf16[2,96,4096]{2,1,0:T(8,128)(2,1)S(1)}, u32[]{:S(2)}, u32[]{:S(2)}) collective-permute-start(bf16[2,96,4096]{2,1,0:T(8,128)(2,1)S(1)} %get-tuple-element.7), channel_id=1, source_target_pairs={{0,256},{256,0},{1,257},{257,1},{2,258},{258,2},{3,259},{259,3},{4... | collective-permute-start | bytes 4718600 | tf_op jit(solution)/shard_map/ppermute | solution.py:77
  161.0 5.6 %copy-start.2 = (bf16[1,1536,256]{2,1,0:T(8,128)(2,1)S(1)}, bf16[1,1536,256]{2,1,0:T(8,128)(2,1)}, u32[]{:S(2)}) copy-start(bf16[1,1536,256]{2,1,0:T(8,128)(2,1)} %param.23) | copy-start | bytes 2359300
  162.3 42.5 %all-to-all-start.5 = ((bf16[8,192,512]{2,1,0:T(8,128)(2,1)}), bf16[8,192,512]{2,1,0:T(8,128)(2,1)}, u32[]{:S(2)}, u32[]{:S(2)}) async-start(bf16[8,192,512]{2,1,0:T(8,128)(2,1)} %broadcast_in_dim.31), calls=%async_computation.5 | async-start | bytes 3145728 | tf_op jit(solution)/shard_map/all_to_all | solution.py:17
  166.6 20.2 %collective-permute-start.1 = (bf16[1536,256]{1,0:T(8,128)(2,1)S(1)}, bf16[1536,256]{1,0:T(8,128)(2,1)}, u32[]{:S(2)}, u32[]{:S(2)}) collective-permute-start(bf16[1536,256]{1,0:T(8,128)(2,1)S(1)} %bitcast.78), channel_id=1, source_target_pairs={{0,256},{256,0},{1,257},{257,1},{2,258},{258,2},{3,259},{259,3},{4... | collective-permute-start | bytes 2359304 | tf_op jit(solution)/shard_map/ppermute | solution.py:78
  188.4 16.4 %copy-start.8 = (s32[1024]{0:T(1024)S(1)}, s32[1024]{0:T(1024)}, u32[]{:S(2)}) copy-start(s32[1024]{0:T(1024)} %constant.94.clone) | copy-start | bytes 12292
Sparse Core Ops, SparseCore 0:
  104.3 51.3 all-gather.1

commit v2 on v1

--- a/solution.py
+++ b/solution.py
@@ -101,12 +101,17 @@
     partial = jnp.dot(heads_out, out_weight, preferred_element_type=jnp.float32)
     partial = partial.astype(jnp.bfloat16).reshape(n_co, tok_block // n_co, width)
     partial = added(exchange(partial, "co")).astype(jnp.bfloat16)
-    projected = added(exchange(partial.reshape(n_x * n_zh, tok_dev, width), ("x", "zh")))
+    partial = added(exchange(partial.reshape(n_x, -1, width), "x")).astype(jnp.bfloat16)
+    projected = added(exchange(partial.reshape(n_zh, tok_dev, width), "zh"))
     mixed = (residual.astype(jnp.float32) + projected).astype(jnp.bfloat16)
 
     stream = mixed.astype(jnp.float32)
     mean_sq = jnp.mean(stream * stream, axis=1, keepdims=True)
     normed = (stream * lax.rsqrt(mean_sq + EPS_NORM) * norm_gain[None, :]).astype(jnp.bfloat16)
+
+    normed, gate_up_other, down_other = lax.optimization_barrier(
+        (normed, gate_up_other, down_other)
+    )
 
     table, mix = route(expert_ids, expert_gates, expert_count, slots)
     mix_high = mix.astype(jnp.bfloat16)

time: 260 us -> 275 us (1.058)
  waiting for transfers between devices: 104 us -> 116 us
  other arithmetic: 11.8 us -> 14.9 us
  local copies, waits for them, and re-layouts: 10.4 us -> 7.39 us
    all_gather x1, waiting for transfers between devices: 11.3 us -> 50.4 us  [on_device(): lax.all_gather(arrived.reshape(expert_count * slots, width + EXTRA), 'y',...]
    ppermute x1, waiting for transfers between devices: 34.9 us -> 0.01 us  [on_device(): gate_up_other = lax.ppermute(gate_up, 'zl', swap)]
    all_to_all x3 -> x4, waiting for transfers between devices: 41.3 us -> 65.4 us  [exchange(): return lax.all_to_all(pieces, axis, 0, 0, tiled=True)]
    ppermute x1, waiting for transfers between devices: 16.9 us -> 0.01 us  [on_device(): down_other = lax.ppermute(w_down[0], 'zl', swap)]
    another operation x2, other arithmetic: 3.3 us -> 6.93 us  [on_device(): weight_in = jnp.stack([gate_up, gate_up_other], axis=1)]
    all_to_all x3 -> x4, starting transfers between devices: 25.5 us -> 27 us  [exchange(): return lax.all_to_all(pieces, axis, 0, 0, tiled=True)]
  transfers between devices with their start and end apart: 6 -> 7, of which waited for: 6 -> 5; matrix products, arithmetic and copies ran while one was open for 4% -> 6% of each run, Pallas kernels for 0% -> 0%
where the time goes in v2:
time: 275 us; the launch traced here: 273 us
  waiting for transfers between devices  116 us (42%)
  blocking collectives  76.4 us (28%)
  starting transfers between devices  32.3 us (12%)
  other arithmetic  14.9 us (5%)
  between operations  14.4 us (5%)
  matrix products  11.5 us (4%)
  local copies, waits for them, and re-layouts  7.39 us (3%)
    all_to_all x6, blocking collectives, exchange(): return lax.all_to_all(pieces, axis, 0, 0, tiled=True)  76.4 us
    all_to_all x4, waiting for transfers between devices, exchange(): return lax.all_to_all(pieces, axis, 0, 0, tiled=True)  65.4 us
    all_gather x1, waiting for transfers between devices, on_device(): lax.all_gather(arrived.reshape(expert_count * slots, width + EXTRA), 'y',...  50.4 us
    all_to_all x4, starting transfers between devices, exchange(): return lax.all_to_all(pieces, axis, 0, 0, tiled=True)  27 us
    another operation x2, other arithmetic, on_device(): weight_in = jnp.stack([gate_up, gate_up_other], axis=1)  6.93 us
    dot_general x2, matrix products, rows_dot(): lax.dot_general(left, right, (((1,), (1,)), ((), ())), preferred_element_...  5.65 us
  transfers between devices with their start and end apart: 7, of which 5 were waited for; matrix products, arithmetic and copies ran while one was open for 6% of the time, Pallas kernels for 0%

profile of v2, /device:TPU:1, one launch (start us, length us, event | category | flops | bytes accessed | tf_op | source)
XLA Modules:
  0.0 272.7 jit_solution(10830892669653134169)
XLA Ops:
  9.1 9.6 %all-to-all-start = ((bf16[16,128,128]{2,1,0:T(8,128)(2,1)}), bf16[16,128,128]{2,1,0:T(8,128)(2,1)S(1)}, u32[]{:S(2)}, u32[]{:S(2)}) async-start(bf16[16,128,128]{2,1,0:T(8,128)(2,1)} %broadcast_in_dim.21), calls=%async_computation | async-start | bytes 1048576 | tf_op jit(solution)/shard_map/all_to_all | solution.py:17
  18.7 3.1 %fusion.35 = (bf16[2,1,96,4096]{3,2,1,0:T(8,128)(2,1)}, bf16[2,96,4096]{2,1,0:T(8,128)(2,1)}) fusion(bf16[1,96,4096]{2,1,0:T(8,128)(2,1)S(1)} %bitcast.78, bf16[1,96,4096]{2,1,0:T(8,128)(2,1)} %bitcast.79), kind=kLoop, calls=%fused_computation.76 | loop fusion | flops 786432 | bytes 4718592 | tf_op jit(solution)/shard_map/stack | solution.py:128
  21.8 3.3 %collective-permute-start = (bf16[2,96,4096]{2,1,0:T(8,128)(2,1)}, bf16[2,96,4096]{2,1,0:T(8,128)(2,1)}, u32[]{:S(2)}, u32[]{:S(2)}) collective-permute-start(bf16[2,96,4096]{2,1,0:T(8,128)(2,1)} %get-tuple-element.13), channel_id=1, source_target_pairs={{0,256},{256,0},{1,257},{257,1},{2,258},{258,2},{3,259},{259,3},{4... | collective-permute-start | bytes 4718600 | tf_op jit(solution)/shard_map/ppermute | solution.py:77
  25.0 2.0 collective-permute-start.1
  27.6 4.8 %all-to-all-done = bf16[16,128,128]{2,1,0:T(8,128)(2,1)S(1)} async-done(((bf16[16,128,128]{2,1,0:T(8,128)(2,1)}), bf16[16,128,128]{2,1,0:T(8,128)(2,1)S(1)}, u32[]{:S(2)}, u32[]{:S(2)}) %all-to-all-start) | async-done | bytes 524320 | tf_op jit(solution)/shard_map/all_to_all | solution.py:17
  32.5 7.1 %all_to_all.50 = bf16[2,2048,128]{2,1,0:T(8,128)(2,1)S(1)} all-to-all(bf16[2,2048,128]{2,1,0:T(8,128)(2,1)S(1)} %broadcast_in_dim.23), channel_id=1, replica_groups=mesh['zl'=2,'y'=8,'x'=4,'zh'=4,'co'=2] {'co'}, dimensions={0} | all-to-all | bytes 2097152 | tf_op jit(solution)/shard_map/all_to_all | solution.py:17
  41.6 4.6 %all_to_all.51 = bf16[2,64,4096]{2,1,0:T(8,128)(2,1)S(1)} all-to-all(bf16[2,64,4096]{2,1,0:T(8,128)(2,1)S(1)} %bitcast.71), channel_id=1, replica_groups=mesh['zl'=2,'y'=8,'x'=4,'zh'=4,'co'=2] {'co'}, dimensions={0} | all-to-all | bytes 2097152 | tf_op jit(solution)/shard_map/all_to_all | solution.py:17
  47.3 4.0 %all-to-all-start.3 = ((bf16[4,16,4096]{2,1,0:T(8,128)(2,1)}), bf16[4,16,4096]{2,1,0:T(8,128)(2,1)S(1)}, u32[]{:S(2)}, u32[]{:S(2)}) async-start(bf16[4,16,4096]{2,1,0:T(8,128)(2,1)} %bitcast.74), calls=%async_computation.3 | async-start | bytes 1048576 | tf_op jit(solution)/shard_map/all_to_all | solution.py:17
  51.6 8.6 %all-to-all-done.3 = bf16[4,16,4096]{2,1,0:T(8,128)(2,1)S(1)} async-done(((bf16[4,16,4096]{2,1,0:T(8,128)(2,1)}), bf16[4,16,4096]{2,1,0:T(8,128)(2,1)S(1)}, u32[]{:S(2)}, u32[]{:S(2)}) %all-to-all-start.3) | async-done | bytes 524320 | tf_op jit(solution)/shard_map/all_to_all | solution.py:17
  61.0 9.1 %all-to-all-start.4 = ((bf16[4,4,4096]{2,1,0:T(4,128)(2,1)}), bf16[4,4,4096]{2,1,0:T(4,128)(2,1)S(1)}, u32[]{:S(2)}, u32[]{:S(2)}) async-start(bf16[4,4,4096]{2,1,0:T(4,128)(2,1)} %reshape.159), calls=%async_computation.4 | async-start | bytes 262144 | tf_op jit(solution)/shard_map/all_to_all | solution.py:17
  70.6 18.4 %all-to-all-done.4 = bf16[4,4,4096]{2,1,0:T(4,128)(2,1)S(1)} async-done(((bf16[4,4,4096]{2,1,0:T(4,128)(2,1)}), bf16[4,4,4096]{2,1,0:T(4,128)(2,1)S(1)}, u32[]{:S(2)}, u32[]{:S(2)}) %all-to-all-start.4) | async-done | bytes 131104 | tf_op jit(solution)/shard_map/all_to_all | solution.py:17
  89.9 25.2 %all_to_all.52 = bf16[32,2,4224]{2,1,0:T(2,128)(2,1)S(1)} all-to-all(bf16[32,2,4224]{2,1,0:T(2,128)(2,1)S(1)} %reshape.162), channel_id=1, replica_groups=mesh['zl'=2,'y'=8,'x'=4,'zh'=4,'co'=2] {'x','zh','co'}, dimensions={0} | all-to-all | bytes 1081344 | tf_op jit(solution)/shard_map/all_to_all | solution.py:17
  116.2 3.9 %fusion.2 = bf16[2,2,96,4224]{3,2,1,0:T(8,128)(2,1)} fusion(bf16[2,1,96,4096]{3,2,1,0:T(8,128)(2,1)} %bitcast.21, bf16[2,1,96,4096]{3,2,1,0:T(8,128)(2,1)} %get-tuple-element.12), kind=kLoop, calls=%fused_computation.5 | loop fusion | flops 11354112 | bytes 6389760 | tf_op jit(solution)/shard_map/stack | solution.py:128
  120.1 50.4 %all-gather.2.cloned.1.call-done = bf16[512,4224]{1,0:T(8,128)(2,1)} async-done(((bf16[64,4224]{1,0:T(8,128)(2,1)}), bf16[512,4224]{1,0:T(8,128)(2,1)}) %all-gather.2.cloned.1.call-update) | async-done | bytes 4325392 | tf_op jit(solution)/shard_map/all_gather | solution.py:124
  170.5 5.1 %fusion.37 = f32[384,512]{1,0:T(8,128)S(1)} fusion(bf16[384,4224]{1,0:T(8,128)(2,1)} %bitcast.72, bf16[512,4224]{1,0:T(8,128)(2,1)} %all-gather.2.cloned.1.call-done), kind=kOutput, calls=%fused_computation.78 | convolution fusion | flops 1660944384 | bytes 8355840 | tf_op jit(solution)/shard_map/dot_general | solution.py:29
  175.7 1.3 broadcast_in_dim.31
  177.0 4.3 %all-to-all-start.6 = ((bf16[8,192,512]{2,1,0:T(8,128)(2,1)}), bf16[8,192,512]{2,1,0:T(8,128)(2,1)}, u32[]{:S(2)}, u32[]{:S(2)}) async-start(bf16[8,192,512]{2,1,0:T(8,128)(2,1)} %broadcast_in_dim.31), calls=%async_computation.6 | async-start | bytes 3145728 | tf_op jit(solution)/shard_map/all_to_all | solution.py:17
  181.4 1.5 pad_maximum_fusion.1
  183.2 1.4 copy.70
  186.0 33.6 %all-to-all-done.6 = bf16[8,192,512]{2,1,0:T(8,128)(2,1)} async-done(((bf16[8,192,512]{2,1,0:T(8,128)(2,1)}), bf16[8,192,512]{2,1,0:T(8,128)(2,1)}, u32[]{:S(2)}, u32[]{:S(2)}) %all-to-all-start.6) | async-done | bytes 1572896 | tf_op jit(solution)/shard_map/all_to_all | solution.py:17
  219.6 4.5 %fusion.10 = bf16[1024,512]{1,0:T(8,128)(2,1)} fusion(s32[512]{0:T(512)S(1)} %fusion.31, s32[1024]{0:T(1024)S(1)} %copy-done.9, bf16[1536,512]{1,0:T(8,128)(2,1)} %bitcast.23, bf16[1536,512]{1,0:T(8,128)(2,1)} %bitcast.76, f32[512]{0:T(512)S(1)} %fusion.23), kind=kOutput, calls=%fused_computation.19 | convolution fusion | flops 1343750144 | bytes 4202496 | tf_op jit(solution)/shard_map/dot_general | solution.py:156
  224.1 8.0 %all_to_all.53 = bf16[2,512,512]{2,1,0:T(8,128)(2,1)S(1)} all-to-all(bf16[2,512,512]{2,1,0:T(8,128)(2,1)} %bitcast.77), channel_id=1, replica_groups=mesh['zl'=2,'y'=8,'x'=4,'zh'=4,'co'=2] {'co'}, dimensions={0} | all-to-all | bytes 2097152 | tf_op jit(solution)/shard_map/all_to_all | solution.py:17
  233.2 12.6 %all_to_all.54 = bf16[4,128,512]{2,1,0:T(8,128)(2,1)S(1)} all-to-all(bf16[4,128,512]{2,1,0:T(8,128)(2,1)} %bitcast.75), channel_id=1, replica_groups=mesh['zl'=2,'y'=8,'x'=4,'zh'=4,'co'=2] {'x'}, dimensions={0} | all-to-all | bytes 1048576 | tf_op jit(solution)/shard_map/all_to_all | solution.py:17
  245.9 18.9 %all_to_all.55 = bf16[32,4,512]{2,1,0:T(4,128)(2,1)S(1)} all-to-all(bf16[32,4,512]{2,1,0:T(4,128)(2,1)S(1)} %reshape.169), channel_id=1, replica_groups=mesh['zl'=2,'y'=8,'x'=4,'zh'=4,'co'=2] {'zh','y'}, dimensions={0} | all-to-all | bytes 262144 | tf_op jit(solution)/shard_map/all_to_all | solution.py:17
  (77 shorter events, 13.1 us)
Async XLA Ops:
  7.2 34.0 %copy-start = (bf16[256,4096]{1,0:T(8,128)(2,1)S(1)}, bf16[256,4096]{1,0:T(8,128)(2,1)}, u32[]{:S(2)}) copy-start(bf16[256,4096]{1,0:T(8,128)(2,1)} %param.17) | copy-start | bytes 6291460
  7.2 11.5 %copy-start.1 = (bf16[1,4096,96]{1,2,0:T(8,128)(2,1)S(1)}, bf16[1,4096,96]{1,2,0:T(8,128)(2,1)}, u32[]{:S(2)}) copy-start(bf16[1,4096,96]{1,2,0:T(8,128)(2,1)} %param.22) | copy-start | bytes 2359300
  9.1 23.3 %all-to-all-start = ((bf16[16,128,128]{2,1,0:T(8,128)(2,1)}), bf16[16,128,128]{2,1,0:T(8,128)(2,1)S(1)}, u32[]{:S(2)}, u32[]{:S(2)}) async-start(bf16[16,128,128]{2,1,0:T(8,128)(2,1)} %broadcast_in_dim.21), calls=%async_computation | async-start | bytes 1048576 | tf_op jit(solution)/shard_map/all_to_all | solution.py:17
  18.7 8.4 %copy-start.3 = (bf16[128,256]{1,0:T(8,128)(2,1)S(1)}, bf16[128,256]{1,0:T(8,128)(2,1)}, u32[]{:S(2)}) copy-start(bf16[128,256]{1,0:T(8,128)(2,1)} %param.13) | copy-start | bytes 196612
  18.7 8.5 %copy-start.6 = (s32[4,8]{1,0:T(4,128)S(1)}, s32[4,8]{1,0:T(4,128)}, u32[]{:S(2)}) copy-start(s32[4,8]{1,0:T(4,128)} %param.19) | copy-start | bytes 388
  18.7 8.8 %copy-start.8 = (s32[256]{0:T(256)S(1)}, s32[256]{0:T(256)}, u32[]{:S(2)}) copy-start(s32[256]{0:T(256)} %constant.94.clone) | copy-start | bytes 3076
  21.8 67.6 %collective-permute-start = (bf16[2,96,4096]{2,1,0:T(8,128)(2,1)}, bf16[2,96,4096]{2,1,0:T(8,128)(2,1)}, u32[]{:S(2)}, u32[]{:S(2)}) collective-permute-start(bf16[2,96,4096]{2,1,0:T(8,128)(2,1)} %get-tuple-element.13), channel_id=1, source_target_pairs={{0,256},{256,0},{1,257},{257,1},{2,258},{258,2},{3,259},{259,3},{4... | collective-permute-start | bytes 4718600 | tf_op jit(solution)/shard_map/ppermute | solution.py:77
  25.0 64.3 %collective-permute-start.1 = (bf16[1536,256]{1,0:T(8,128)(2,1)}, bf16[1536,256]{1,0:T(8,128)(2,1)}, u32[]{:S(2)}, u32[]{:S(2)}) collective-permute-start(bf16[1536,256]{1,0:T(8,128)(2,1)} %bitcast.17), channel_id=1, source_target_pairs={{0,256},{256,0},{1,257},{257,1},{2,258},{258,2},{3,259},{259,3},{4... | collective-permute-start | bytes 2359304 | tf_op jit(solution)/shard_map/ppermute | solution.py:78
  41.6 9.7 %copy-start.7 = (f32[4,8]{1,0:T(4,128)S(1)}, f32[4,8]{1,0:T(4,128)}, u32[]{:S(2)}) copy-start(f32[4,8]{1,0:T(4,128)} %param.20) | copy-start | bytes 388
  46.2 42.9 %copy-start.4 = (bf16[4,4096]{1,0:T(4,128)(2,1)S(1)}, bf16[4,4096]{1,0:T(4,128)(2,1)}, u32[]{:S(2)}) copy-start(bf16[4,4096]{1,0:T(4,128)(2,1)} %param.16) | copy-start | bytes 98308
  46.2 43.0 %copy-start.5 = (f32[4096]{0:T(1024)S(1)}, f32[4096]{0:T(1024)}, u32[]{:S(2)}) copy-start(f32[4096]{0:T(1024)} %param.18) | copy-start | bytes 49156
  47.3 12.9 %all-to-all-start.3 = ((bf16[4,16,4096]{2,1,0:T(8,128)(2,1)}), bf16[4,16,4096]{2,1,0:T(8,128)(2,1)S(1)}, u32[]{:S(2)}, u32[]{:S(2)}) async-start(bf16[4,16,4096]{2,1,0:T(8,128)(2,1)} %bitcast.74), calls=%async_computation.3 | async-start | bytes 1048576 | tf_op jit(solution)/shard_map/all_to_all | solution.py:17
  61.0 28.0 %all-to-all-start.4 = ((bf16[4,4,4096]{2,1,0:T(4,128)(2,1)}), bf16[4,4,4096]{2,1,0:T(4,128)(2,1)S(1)}, u32[]{:S(2)}, u32[]{:S(2)}) async-start(bf16[4,4,4096]{2,1,0:T(4,128)(2,1)} %reshape.159), calls=%async_computation.4 | async-start | bytes 262144 | tf_op jit(solution)/shard_map/all_to_all | solution.py:17
  70.1 100.3 %all-gather.2.cloned.1.call-start = ((), (), s32[]{:S(2)}) async-start(), calls=%async_computation.10 | async-start | bytes 4866048 | tf_op jit(solution)/shard_map/all_gather | solution.py:124
  89.2 27.0 %copy-start.2 = (bf16[4,4096]{1,0:T(4,128)(2,1)}, bf16[4,4096]{1,0:T(4,128)(2,1)S(1)}, u32[]{:S(2)}) copy-start(bf16[4,4096]{1,0:T(4,128)(2,1)S(1)} %get-tuple-element.9) | copy-start | bytes 98308
  177.0 42.5 %all-to-all-start.6 = ((bf16[8,192,512]{2,1,0:T(8,128)(2,1)}), bf16[8,192,512]{2,1,0:T(8,128)(2,1)}, u32[]{:S(2)}, u32[]{:S(2)}) async-start(bf16[8,192,512]{2,1,0:T(8,128)(2,1)} %broadcast_in_dim.31), calls=%async_computation.6 | async-start | bytes 3145728 | tf_op jit(solution)/shard_map/all_to_all | solution.py:17
  183.2 36.4 %copy-start.9 = (s32[1024]{0:T(1024)S(1)}, s32[1024]{0:T(1024)}, u32[]{:S(2)}) copy-start(s32[1024]{0:T(1024)} %constant.95.clone) | copy-start | bytes 12292
Sparse Core Ops, SparseCore 0:
  116.3 54.0 all-gather.1

commit v3 on v2

--- a/solution.py
+++ b/solution.py
@@ -73,13 +73,19 @@
     heads = queries.shape[1] // HEAD_WIDTH
     swap = [(i, n_zl - 1 - i) for i in range(n_zl)]
 
-    gate_up = jnp.stack([w_gate[0].T, w_up[0].T])
-    gate_up_other = lax.ppermute(gate_up, "zl", swap)
-    down_other = lax.ppermute(w_down[0], "zl", swap)
-
     mine = jnp.where(co == 0, keys, values)
     mine = lax.dynamic_slice_in_dim(mine, x_pos * HEAD_WIDTH, HEAD_WIDTH, 1)
     gathered = spread(mine, CTX, ctx_count).reshape(ctx_count * tok_block, HEAD_WIDTH)
+
+    table, mix = route(expert_ids, expert_gates, expert_count, slots)
+    places = n_y * tok_dev
+    own_place = jnp.arange(places, dtype=jnp.int32) // tok_dev == y_pos
+    mix = jnp.where(own_place[None, :], jnp.tile(mix, (1, n_y)), 0.0)
+    mix_high = mix.astype(jnp.bfloat16)
+    mix_low = (mix - mix_high.astype(jnp.float32)).astype(jnp.bfloat16)
+    extra = jnp.concatenate([mix_high, mix_low], axis=1)
+    extra = jnp.pad(extra, ((0, 0), (0, EXTRA - extra.shape[1])))
+    gathered, table, extra = lax.optimization_barrier((gathered, table, extra))
     key_all, value_all = spread(gathered, "co", n_co)
 
     order = np.arange(tok_block).reshape(n_x, n_zh, n_co, tok_dev).transpose(2, 0, 1, 3)
@@ -109,60 +115,48 @@
     mean_sq = jnp.mean(stream * stream, axis=1, keepdims=True)
     normed = (stream * lax.rsqrt(mean_sq + EPS_NORM) * norm_gain[None, :]).astype(jnp.bfloat16)
 
-    normed, gate_up_other, down_other = lax.optimization_barrier(
-        (normed, gate_up_other, down_other)
-    )
-
-    table, mix = route(expert_ids, expert_gates, expert_count, slots)
-    mix_high = mix.astype(jnp.bfloat16)
-    mix_low = (mix - mix_high.astype(jnp.float32)).astype(jnp.bfloat16)
-    extra = jnp.concatenate([mix_high, mix_low], axis=1)
-    extra = jnp.pad(extra, ((0, 0), (0, EXTRA - extra.shape[1])))
     outgoing = jnp.dot(table, normed, preferred_element_type=jnp.float32).astype(jnp.bfloat16)
     outgoing = jnp.concatenate([outgoing, extra], axis=1)
     arrived = exchange(outgoing.reshape(expert_count, slots, width + EXTRA), EXP)
-    rows = lax.all_gather(
-        arrived.reshape(expert_count * slots, width + EXTRA), "y", axis=0, tiled=True
-    )
+    arrived = arrived.reshape(expert_count * slots, width + EXTRA)
 
-    weight_in = jnp.stack([gate_up, gate_up_other], axis=1)
+    gate_up = jnp.stack([w_gate[0].T, w_up[0].T])
+    arrived, gate_up, down_own = lax.optimization_barrier((arrived, gate_up, w_down[0]))
+    rows = lax.all_gather(arrived, "y", axis=0, tiled=True)
+    weight_in = jnp.stack([gate_up, lax.ppermute(gate_up, "zl", swap)], axis=1)
     weight_in = jnp.pad(weight_in, ((0, 0),) * 3 + ((0, EXTRA),)).reshape(-1, width + EXTRA)
-    both = rows_dot(weight_in, rows)
-    units = both.shape[0] // 2
-    hidden = (jax.nn.silu(both[:units]) * both[units:]).astype(jnp.bfloat16)
-    hidden = spread(hidden, "y", n_y).reshape(n_y * units, -1)
-
-    down = jnp.concatenate([w_down[0], down_other], axis=1)
+    units = weight_in.shape[0] // 2
+    down = jnp.concatenate([down_own, lax.ppermute(down_own, "zl", swap)], axis=1)
     down = down.reshape(n_zl, n_y, units // n_zl, down.shape[1])
     down = jnp.where(zl == 0, down, down[::-1])
     down = jnp.transpose(down, (1, 0, 2, 3)).reshape(n_y * units, -1)
+    rows, weight_in, down = lax.optimization_barrier((rows, weight_in, down))
+
+    both = rows_dot(weight_in, rows)
+    hidden = (jax.nn.silu(both[:units]) * both[units:]).astype(jnp.bfloat16)
+    hidden, down, extra = lax.optimization_barrier((hidden, down, rows[:, width:]))
+    hidden = spread(hidden, "y", n_y).reshape(n_y * units, -1)
+
     result = lax.dot_general(
         hidden, down, (((0,), (0,)), ((), ())), preferred_element_type=jnp.float32
+    ).astype(jnp.bfloat16)
+    cols = result.shape[1]
+    result = jnp.concatenate([result, extra], axis=1)
+    result = result.reshape(n_y, expert_count, slots, cols + EXTRA).transpose(1, 0, 2, 3)
+    result = exchange(result.reshape(expert_count, n_y * slots, cols + EXTRA), EXP)
+    result = result.reshape(-1, cols + EXTRA)
+
+    tokens = lax.dot_general(
+        result[:, cols : cols + 2 * places],
+        result[:, :cols],
+        (((0,), (0,)), ((), ())),
+        preferred_element_type=jnp.float32,
     )
-    gates = rows[:, width : width + 2 * tok_dev].astype(jnp.float32)
-    gates = gates[:, :tok_dev] + gates[:, tok_dev:]
-    result = (result * jnp.sum(gates, axis=1, keepdims=True)).astype(jnp.bfloat16)
-
-    block_of = np.arange(n_y * expert_count).reshape(n_y, n_x, n_zh, n_co)
-    block_of = block_of.transpose(3, 1, 2, 0).reshape(-1)
-    token_of = (block_of[:, None] * tok_dev + np.arange(tok_dev)[None, :]).reshape(-1)
-    place = jnp.sum(
-        (gates != 0).astype(jnp.int32) * jnp.arange(1, tok_dev + 1, dtype=jnp.int32)[None, :],
-        axis=1,
-    )
-    slot_block = jnp.arange(n_y * expert_count * slots, dtype=jnp.int32) // slots
-    slot_token = jnp.where(place > 0, slot_block * tok_dev + place - 1, -1)
-    onehot = (jnp.asarray(token_of, jnp.int32)[:, None] == slot_token[None, :]).astype(jnp.bfloat16)
-    tokens = jnp.dot(onehot, result, preferred_element_type=jnp.float32).astype(jnp.bfloat16)
-
-    cols = tokens.shape[1]
-    tokens = added(exchange(tokens.reshape(n_co, -1, cols), "co")).astype(jnp.bfloat16)
-    tokens = added(exchange(tokens.reshape(n_x, -1, cols), "x")).astype(jnp.bfloat16)
-    tokens = exchange(tokens.reshape(n_zh * n_y, tok_dev, cols), ("zh", "y"))
-    tokens = added(tokens.reshape(n_zh, n_y, tok_dev, cols))
+    tokens = (tokens[:places] + tokens[places:]).astype(jnp.bfloat16)
+    tokens = exchange(tokens.reshape(n_y, tok_dev, cols), "y")
     tokens = tokens.reshape(n_y, tok_dev, n_zl, cols // n_zl).transpose(1, 2, 0, 3)
     tokens = jnp.where(zl == 0, tokens, tokens[:, ::-1])
-    return (mixed, tokens.reshape(tok_dev, width).astype(jnp.bfloat16))
+    return (mixed, tokens.reshape(tok_dev, width))
 
 
 def solution(mesh):

time: 275 us -> 268 us (0.975)
  blocking collectives: 76.4 us -> 120 us
  waiting for transfers between devices: 116 us -> 74.4 us
  starting transfers between devices: 32.3 us -> 21.7 us
  local copies, waits for them, and re-layouts: 7.39 us -> 15.4 us
  matrix products: 11.5 us -> 8.21 us
    all_gather x1, waiting for transfers between devices: 50.4 us -> 0.01 us  [on_device(): rows = lax.all_gather(arrived, 'y', axis=0, tiled=True)]
    ppermute x2, waiting for transfers between devices: 0.01 us -> 48.6 us  [the longest x1 48.6 us: on_device(): lax.ppermute(down_own, 'zl', swap)]
    all_to_all x6 -> x7, blocking collectives: 76.4 us -> 120 us  [exchange(): return lax.all_to_all(pieces, axis, 0, 0, tiled=True)]
    all_to_all x4 -> x2, waiting for transfers between devices: 65.4 us -> 25.8 us  [exchange(): return lax.all_to_all(pieces, axis, 0, 0, tiled=True)]
    all_to_all x4 -> x2, starting transfers between devices: 27 us -> 16.3 us  [exchange(): return lax.all_to_all(pieces, axis, 0, 0, tiled=True)]
    optimization_barrier x0 -> x1, local copies, waits for them, and re-layouts: none -> 6.55 us  [on_device(): rows, weight_in, down = lax.optimization_barrier((rows, weight_in, down))]
    dot_general x1 -> x2, matrix products: 4.51 us -> 1.24 us  [the longest x1 1.02 us: on_device(): lax.dot_general(hidden, down, (((0,), (0,)), ((), ())), preferred_element...]
  transfers between devices with their start and end apart: 7 -> 5, of which waited for: 5 -> 3; matrix products, arithmetic and copies ran while one was open for 6% -> 5% of each run, Pallas kernels for 0% -> 0%
where the time goes in v3:
time: 268 us; the launch traced here: 266 us
  blocking collectives  120 us (45%)
  waiting for transfers between devices  74.4 us (28%)
  starting transfers between devices  21.7 us (8%)
  local copies, waits for them, and re-layouts  15.4 us (6%)
  between operations  14.4 us (5%)
  other arithmetic  12.2 us (5%)
  matrix products  8.21 us (3%)
    all_to_all x7, blocking collectives, exchange(): return lax.all_to_all(pieces, axis, 0, 0, tiled=True)  120 us
    ppermute x1, waiting for transfers between devices, on_device(): lax.ppermute(down_own, 'zl', swap)  48.6 us
    all_to_all x2, waiting for transfers between devices, exchange(): return lax.all_to_all(pieces, axis, 0, 0, tiled=True)  25.8 us
    all_to_all x2, starting transfers between devices, exchange(): return lax.all_to_all(pieces, axis, 0, 0, tiled=True)  16.3 us
    optimization_barrier x1, local copies, waits for them, and re-layouts, on_device(): rows, weight_in, down = lax.optimization_barrier((rows, weight_in, down))  6.55 us
    dot_general x2, matrix products, rows_dot(): lax.dot_general(left, right, (((1,), (1,)), ((), ())), preferred_element_...  5.65 us
  transfers between devices with their start and end apart: 5, of which 3 were waited for; matrix products, arithmetic and copies ran while one was open for 5% of the time, Pallas kernels for 0%

profile of v3, /device:TPU:1, one launch (start us, length us, event | category | flops | bytes accessed | tf_op | source)
XLA Modules:
  0.0 266.4 jit_solution(1443334650530041101)
XLA Ops:
  9.0 9.6 %all-to-all-start = ((bf16[16,128,128]{2,1,0:T(8,128)(2,1)}), bf16[16,128,128]{2,1,0:T(8,128)(2,1)S(1)}, u32[]{:S(2)}, u32[]{:S(2)}) async-start(bf16[16,128,128]{2,1,0:T(8,128)(2,1)} %broadcast_in_dim.33), calls=%async_computation | async-start | bytes 1048576 | tf_op jit(solution)/shard_map/all_to_all | solution.py:17
  22.7 9.6 %all-to-all-done = bf16[16,128,128]{2,1,0:T(8,128)(2,1)S(1)} async-done(((bf16[16,128,128]{2,1,0:T(8,128)(2,1)}), bf16[16,128,128]{2,1,0:T(8,128)(2,1)S(1)}, u32[]{:S(2)}, u32[]{:S(2)}) %all-to-all-start) | async-done | bytes 524320 | tf_op jit(solution)/shard_map/all_to_all | solution.py:17
  32.4 7.1 %all_to_all.45 = bf16[2,2048,128]{2,1,0:T(8,128)(2,1)S(1)} all-to-all(bf16[2,2048,128]{2,1,0:T(8,128)(2,1)S(1)} %broadcast_in_dim.39), channel_id=1, replica_groups=mesh['zl'=2,'y'=8,'x'=4,'zh'=4,'co'=2] {'co'}, dimensions={0} | all-to-all | bytes 2097152 | tf_op jit(solution)/shard_map/all_to_all | solution.py:17
  41.6 4.6 %all_to_all.46 = bf16[2,64,4096]{2,1,0:T(8,128)(2,1)S(1)} all-to-all(bf16[2,64,4096]{2,1,0:T(8,128)(2,1)S(1)} %bitcast.66), channel_id=1, replica_groups=mesh['zl'=2,'y'=8,'x'=4,'zh'=4,'co'=2] {'co'}, dimensions={0} | all-to-all | bytes 2097152 | tf_op jit(solution)/shard_map/all_to_all | solution.py:17
  46.1 1.1 reduce_sum.72
  47.2 12.6 %all_to_all.47 = bf16[4,16,4096]{2,1,0:T(8,128)(2,1)S(1)} all-to-all(bf16[4,16,4096]{2,1,0:T(8,128)(2,1)} %bitcast.72), channel_id=1, replica_groups=mesh['zl'=2,'y'=8,'x'=4,'zh'=4,'co'=2] {'x'}, dimensions={0} | all-to-all | bytes 1048576 | tf_op jit(solution)/shard_map/all_to_all | solution.py:17
  60.0 16.2 %all_to_all.48 = bf16[4,4,4096]{2,1,0:T(4,128)(2,1)S(1)} all-to-all(bf16[4,4,4096]{2,1,0:T(4,128)(2,1)S(1)} %reshape.152), channel_id=1, replica_groups=mesh['zl'=2,'y'=8,'x'=4,'zh'=4,'co'=2] {'zh'}, dimensions={0} | all-to-all | bytes 262144 | tf_op jit(solution)/shard_map/all_to_all | solution.py:17
  76.8 1.0 reshape.153
  77.8 6.8 %all-to-all-start.5 = ((bf16[32,2,4224]{2,1,0:T(2,128)(2,1)}), bf16[32,2,4224]{2,1,0:T(2,128)(2,1)S(1)}, u32[]{:S(2)}, u32[]{:S(2)}) async-start(bf16[32,2,4224]{2,1,0:T(2,128)(2,1)} %reshape.153), calls=%async_computation.5 | async-start | bytes 1081344 | tf_op jit(solution)/shard_map/all_to_all | solution.py:17
  84.6 2.5 pad_maximum_fusion
  87.1 16.2 %all-to-all-done.5 = bf16[32,2,4224]{2,1,0:T(2,128)(2,1)S(1)} async-done(((bf16[32,2,4224]{2,1,0:T(2,128)(2,1)}), bf16[32,2,4224]{2,1,0:T(2,128)(2,1)S(1)}, u32[]{:S(2)}, u32[]{:S(2)}) %all-to-all-start.5) | async-done | bytes 540704 | tf_op jit(solution)/shard_map/all_to_all | solution.py:17
  103.2 1.0 reshape.154
  104.3 1.9 collective-permute-start
  106.2 3.4 %collective-permute-start.1 = (bf16[1536,256]{1,0:T(8,128)(2,1)}, bf16[1536,256]{1,0:T(8,128)(2,1)}, u32[]{:S(2)}, u32[]{:S(2)}) collective-permute-start(bf16[1536,256]{1,0:T(8,128)(2,1)} %bitcast.77), channel_id=1, source_target_pairs={{0,256},{256,0},{1,257},{257,1},{2,258},{258,2},{3,259},{259,3},{4... | collective-permute-start | bytes 2359304 | tf_op jit(solution)/shard_map/ppermute | solution.py:129
  109.6 48.6 %collective-permute-done.1 = bf16[1536,256]{1,0:T(8,128)(2,1)} collective-permute-done((bf16[1536,256]{1,0:T(8,128)(2,1)}, bf16[1536,256]{1,0:T(8,128)(2,1)}, u32[]{:S(2)}, u32[]{:S(2)}) %collective-permute-start.1) | collective-permute-done | bytes 786464 | tf_op jit(solution)/shard_map/ppermute | solution.py:129
  158.2 1.2 pad_maximum_fusion.1
  159.8 1.4 copy.65
  161.7 3.4 %fusion.2 = bf16[2,2,96,4224]{3,2,1,0:T(8,128)(2,1)} fusion(bf16[2,1,96,4096]{3,2,1,0:T(8,128)(2,1)} %bitcast.23, bf16[2,1,96,4096]{3,2,1,0:T(8,128)(2,1)S(1)} %bitcast.64), kind=kLoop, calls=%fused_computation.5 | loop fusion | flops 11354112 | bytes 6389760 | tf_op jit(solution)/shard_map/stack | solution.py:126
  165.1 6.5 %copy.66 = bf16[512,4224]{0,1:T(8,128)(2,1)} copy(bf16[512,4224]{1,0:T(8,128)(2,1)} %all-gather.2.cloned.1.call-done) | data formatting | bytes 8650752 | tf_op jit(solution)/shard_map/optimization_barrier | solution.py:133
  171.6 5.1 %fusion.29 = f32[384,512]{1,0:T(8,128)S(1)} fusion(bf16[384,4224]{1,0:T(8,128)(2,1)} %bitcast.67, bf16[512,4224]{1,0:T(8,128)(2,1)} %all-gather.2.cloned.1.call-done), kind=kOutput, calls=%fused_computation.68 | convolution fusion | flops 1660944384 | bytes 8355840 | tf_op jit(solution)/shard_map/dot_general | solution.py:29
  177.0 40.8 %all_to_all.49 = bf16[8,192,512]{2,1,0:T(8,128)(2,1)S(1)} all-to-all(bf16[8,192,512]{2,1,0:T(8,128)(2,1)S(1)} %broadcast_in_dim.41), channel_id=1, replica_groups=mesh['zl'=2,'y'=8,'x'=4,'zh'=4,'co'=2] {'y'}, dimensions={0} | all-to-all | bytes 3145728 | tf_op jit(solution)/shard_map/all_to_all | solution.py:17
  217.8 1.0 convolution_convert_fusion.2
  219.8 29.6 %all_to_all.50 = bf16[32,16,640]{2,1,0:T(8,128)(2,1)S(1)} all-to-all(bf16[32,16,640]{2,1,0:T(8,128)(2,1)S(1)} %copy.69), channel_id=1, replica_groups=mesh['zl'=2,'y'=8,'x'=4,'zh'=4,'co'=2] {'x','zh','co'}, dimensions={0} | all-to-all | bytes 1310720 | tf_op jit(solution)/shard_map/all_to_all | solution.py:17
  249.6 9.2 %all_to_all.51 = bf16[8,4,512]{2,1,0:T(4,128)(2,1)S(1)} all-to-all(bf16[8,4,512]{2,1,0:T(4,128)(2,1)S(1)} %reshape.162), channel_id=1, replica_groups=mesh['zl'=2,'y'=8,'x'=4,'zh'=4,'co'=2] {'y'}, dimensions={0} | all-to-all | bytes 65536 | tf_op jit(solution)/shard_map/all_to_all | solution.py:17
  (75 shorter events, 11.7 us)
Async XLA Ops:
  7.2 33.9 %copy-start = (bf16[256,4096]{1,0:T(8,128)(2,1)S(1)}, bf16[256,4096]{1,0:T(8,128)(2,1)}, u32[]{:S(2)}) copy-start(bf16[256,4096]{1,0:T(8,128)(2,1)} %param.16) | copy-start | bytes 6291460
  7.2 15.5 %copy-start.8 = (s32[256]{0:T(256)S(1)}, s32[256]{0:T(256)}, u32[]{:S(2)}) copy-start(s32[256]{0:T(256)} %constant.80.clone) | copy-start | bytes 3076
  9.0 23.3 %all-to-all-start = ((bf16[16,128,128]{2,1,0:T(8,128)(2,1)}), bf16[16,128,128]{2,1,0:T(8,128)(2,1)S(1)}, u32[]{:S(2)}, u32[]{:S(2)}) async-start(bf16[16,128,128]{2,1,0:T(8,128)(2,1)} %broadcast_in_dim.33), calls=%async_computation | async-start | bytes 1048576 | tf_op jit(solution)/shard_map/all_to_all | solution.py:17
  46.1 30.1 %copy-start.6 = (bf16[4,4096]{1,0:T(4,128)(2,1)S(1)}, bf16[4,4096]{1,0:T(4,128)(2,1)}, u32[]{:S(2)}) copy-start(bf16[4,4096]{1,0:T(4,128)(2,1)} %param.15) | copy-start | bytes 98308
  46.1 30.3 %copy-start.7 = (f32[4096]{0:T(1024)S(1)}, f32[4096]{0:T(1024)}, u32[]{:S(2)}) copy-start(f32[4096]{0:T(1024)} %param.17) | copy-start | bytes 49156
  76.2 8.5 %copy-start.3 = (bf16[1,4096,96]{1,2,0:T(8,128)(2,1)S(1)}, bf16[1,4096,96]{1,2,0:T(8,128)(2,1)}, u32[]{:S(2)}) copy-start(bf16[1,4096,96]{1,2,0:T(8,128)(2,1)} %param.21) | copy-start | bytes 2359300
  76.4 10.7 %copy-start.5 = (bf16[4,4096]{1,0:T(4,128)(2,1)}, bf16[4,4096]{1,0:T(4,128)(2,1)S(1)}, u32[]{:S(2)}) copy-start(bf16[4,4096]{1,0:T(4,128)(2,1)S(1)} %get-tuple-element.27) | copy-start | bytes 98308
  77.8 25.5 %all-to-all-start.5 = ((bf16[32,2,4224]{2,1,0:T(2,128)(2,1)}), bf16[32,2,4224]{2,1,0:T(2,128)(2,1)S(1)}, u32[]{:S(2)}, u32[]{:S(2)}) async-start(bf16[32,2,4224]{2,1,0:T(2,128)(2,1)} %reshape.153), calls=%async_computation.5 | async-start | bytes 1081344 | tf_op jit(solution)/shard_map/all_to_all | solution.py:17
  84.6 80.5 %all-gather.2.cloned.1.call-start = ((), (), s32[]{:S(2)}) async-start(), calls=%async_computation.9 | async-start | bytes 4866048 | tf_op jit(solution)/shard_map/all_gather | solution.py:125
  87.1 71.1 %copy-start.4 = (bf16[1,1536,256]{2,1,0:T(8,128)(2,1)S(1)}, bf16[1,1536,256]{2,1,0:T(8,128)(2,1)}, u32[]{:S(2)}) copy-start(bf16[1,1536,256]{2,1,0:T(8,128)(2,1)} %param.22) | copy-start | bytes 2359300
  104.3 56.8 %collective-permute-start = (bf16[2,96,4096]{2,1,0:T(8,128)(2,1)}, bf16[2,96,4096]{2,1,0:T(8,128)(2,1)}, u32[]{:S(2)}, u32[]{:S(2)}) collective-permute-start(bf16[2,96,4096]{2,1,0:T(8,128)(2,1)} %pad_maximum_fusion), channel_id=1, source_target_pairs={{0,256},{256,0},{1,257},{257,1},{2,258},{258,2},{3,259},{259,3},{4... | collective-permute-start | bytes 4718600 | tf_op jit(solution)/shard_map/ppermute | solution.py:126
  106.2 52.0 %collective-permute-start.1 = (bf16[1536,256]{1,0:T(8,128)(2,1)}, bf16[1536,256]{1,0:T(8,128)(2,1)}, u32[]{:S(2)}, u32[]{:S(2)}) collective-permute-start(bf16[1536,256]{1,0:T(8,128)(2,1)} %bitcast.77), channel_id=1, source_target_pairs={{0,256},{256,0},{1,257},{257,1},{2,258},{258,2},{3,259},{259,3},{4... | collective-permute-start | bytes 2359304 | tf_op jit(solution)/shard_map/ppermute | solution.py:129
  159.7 2.0 copy-start.1
  176.9 40.9 %copy-start.2 = (bf16[8,2,96,512]{3,2,1,0:T(8,128)(2,1)S(1)}, bf16[8,2,96,512]{3,2,1,0:T(8,128)(2,1)}, u32[]{:S(2)}) copy-start(bf16[8,2,96,512]{3,2,1,0:T(8,128)(2,1)} %copy.65) | copy-start | bytes 4718596
  217.8 1.0 slice-start
Sparse Core Ops, SparseCore 0:
  104.4 51.6 all-gather.1

commit v4 on v3

--- a/solution.py
+++ b/solution.py
@@ -2,6 +2,8 @@
 import jax.numpy as jnp
 import numpy as np
 from jax import lax
+from jax.experimental import pallas as pl
+from jax.experimental.pallas import tpu as pltpu
 from jax.sharding import Mesh, PartitionSpec as P
 
 HEAD_WIDTH = 128
@@ -47,6 +49,118 @@
     return table.reshape(expert_count * slots, tok_rows), mix.reshape(
         expert_count * slots, tok_rows
     )
+
+
+def whole(shape):
+    return pl.BlockSpec(shape, lambda *_: (0,) * len(shape))
+
+
+def hidden_kernel(zl_ref, rows_ref, gate_a, gate_b, up_a, up_b, out_ref, weight, total):
+    step = pl.program_id(0)
+    units = gate_a.shape[0]
+
+    for place, (own, other) in enumerate(((gate_a, gate_b), (up_a, up_b))):
+        low = pl.ds(2 * place * units, units)
+        high = pl.ds((2 * place + 1) * units, units)
+
+        @pl.when(zl_ref[0] == 0)
+        def _():
+            weight[low, :] = own[...]
+            weight[high, :] = other[...]
+
+        @pl.when(zl_ref[0] != 0)
+        def _():
+            weight[low, :] = other[...]
+            weight[high, :] = own[...]
+
+    @pl.when(step == 0)
+    def _():
+        total[...] = jnp.zeros_like(total)
+
+    total[...] += rows_dot(weight[...], rows_ref[...])
+
+    @pl.when(step == pl.num_programs(0) - 1)
+    def _():
+        gate, upper = total[: 2 * units, :], total[2 * units :, :]
+        hidden = (gate / (1.0 + jnp.exp(-gate)) * upper).astype(jnp.bfloat16)
+        half = hidden.shape[1] // 2
+        for peer in range(out_ref.shape[0]):
+            start = (peer % 2) * half
+            out_ref[peer] = hidden[:, start : start + half]
+
+
+def hidden_pieces(rows, zl, weights, width, peers):
+    units = weights[0].shape[0]
+    count, step = rows.shape[0], 1024 if width % 1024 == 0 else width
+    weight_spec = pl.BlockSpec((units, step), lambda k, *_: (0, k))
+    return pl.pallas_call(
+        hidden_kernel,
+        out_shape=jax.ShapeDtypeStruct((peers, 2 * units, count // 2), jnp.bfloat16),
+        grid_spec=pltpu.PrefetchScalarGridSpec(
+            num_scalar_prefetch=1,
+            grid=(width // step,),
+            in_specs=[pl.BlockSpec((count, step), lambda k, *_: (0, k))] + [weight_spec] * 4,
+            out_specs=whole((peers, 2 * units, count // 2)),
+            scratch_shapes=[
+                pltpu.VMEM((4 * units, step), jnp.bfloat16),
+                pltpu.VMEM((4 * units, count), jnp.float32),
+            ],
+        ),
+        compiler_params=pltpu.CompilerParams(vmem_limit_bytes=60 * 2**20),
+        cost_estimate=pl.CostEstimate(
+            flops=8 * units * count * width, bytes_accessed=2 * count * width, transcendentals=0
+        ),
+    )(zl.reshape(1), rows, *weights)
+
+
+def down_kernel(half_ref, hidden_ref, extra_ref, *refs):
+    weights, out_ref, stacked = refs[:4], refs[4], refs[5]
+    peers, units, count = hidden_ref.shape
+    for peer in range(peers):
+        for z in range(2):
+            rows = pl.ds((z * peers + peer) * (units // 2), units // 2)
+            stacked[rows, :] = hidden_ref[peer, z * (units // 2) : (z + 1) * (units // 2), :]
+    blocks = peers // 2
+    each = count // blocks
+    to = lax.broadcasted_iota(jnp.int32, (count, count), 0)
+    source = (to % (2 * blocks)) // 2 * each + to // (2 * blocks) * 2 + to % 2
+    move = (lax.broadcasted_iota(jnp.int32, (count, count), 1) == source).astype(jnp.bfloat16)
+    rows = stacked[...].T
+    cols = weights[0].shape[1]
+    for place, weight in enumerate(weights):
+        result = jnp.dot(rows, weight[...], preferred_element_type=jnp.float32)
+        result = jnp.dot(
+            move, result.astype(jnp.bfloat16), preferred_element_type=jnp.float32
+        )
+        out_ref[:, place * cols : (place + 1) * cols] = result.astype(jnp.bfloat16)
+    extra = jnp.where(half_ref[0] == 0, extra_ref[:count, :], extra_ref[count:, :])
+    extra = jnp.dot(move, extra, preferred_element_type=jnp.float32)
+    out_ref[:, 4 * cols :] = extra.astype(jnp.bfloat16)
+
+
+def down_slots(half, hidden, extra, weights):
+    peers, units, count = hidden.shape
+    deep, cols = weights[0].shape
+    out = (count, 4 * cols + EXTRA)
+    return pl.pallas_call(
+        down_kernel,
+        out_shape=jax.ShapeDtypeStruct(out, jnp.bfloat16),
+        grid_spec=pltpu.PrefetchScalarGridSpec(
+            num_scalar_prefetch=1,
+            grid=(1,),
+            in_specs=[
+                whole(hidden.shape),
+                whole(extra.shape),
+            ]
+            + [whole((deep, cols))] * 4,
+            out_specs=whole(out),
+            scratch_shapes=[pltpu.VMEM((deep, count), jnp.bfloat16)],
+        ),
+        compiler_params=pltpu.CompilerParams(vmem_limit_bytes=60 * 2**20),
+        cost_estimate=pl.CostEstimate(
+            flops=8 * deep * count * cols, bytes_accessed=8 * deep * cols, transcendentals=0
+        ),
+    )(half.reshape(1), hidden, extra, *weights)
 
 
 def on_device(
@@ -71,7 +185,11 @@
     slots = 2
     tok_block = queries.shape[0]
     heads = queries.shape[1] // HEAD_WIDTH
-    swap = [(i, n_zl - 1 - i) for i in range(n_zl)]
+    swap_z = [(i, i ^ 1) for i in range(n_zl)]
+    swap_y = [(i, i ^ 1) for i in range(n_y)]
+    gate_own, up_own, down_own = w_gate[0].T, w_up[0].T, w_down[0]
+
+    gate_z, up_z = lax.ppermute(gate_own, "zl", swap_z), lax.ppermute(up_own, "zl", swap_z)
 
     mine = jnp.where(co == 0, keys, values)
     mine = lax.dynamic_slice_in_dim(mine, x_pos * HEAD_WIDTH, HEAD_WIDTH, 1)
@@ -104,10 +222,14 @@
     done = (numer / total).astype(jnp.bfloat16).reshape(heads, tok_block, HEAD_WIDTH)
     heads_out = jnp.transpose(done, (1, 0, 2)).reshape(tok_block, heads * HEAD_WIDTH)
 
+    heads_out, down_own = lax.optimization_barrier((heads_out, down_own))
+    down_y = lax.ppermute(down_own, "y", swap_y)
+
     partial = jnp.dot(heads_out, out_weight, preferred_element_type=jnp.float32)
     partial = partial.astype(jnp.bfloat16).reshape(n_co, tok_block // n_co, width)
     partial = added(exchange(partial, "co")).astype(jnp.bfloat16)
     partial = added(exchange(partial.reshape(n_x, -1, width), "x")).astype(jnp.bfloat16)
+    partial, gate_z, up_z, down_y = lax.optimization_barrier((partial, gate_z, up_z, down_y))
     projected = added(exchange(partial.reshape(n_zh, tok_dev, width), "zh"))
     mixed = (residual.astype(jnp.float32) + projected).astype(jnp.bfloat16)
 
@@ -120,32 +242,19 @@
     arrived = exchange(outgoing.reshape(expert_count, slots, width + EXTRA), EXP)
     arrived = arrived.reshape(expert_count * slots, width + EXTRA)
 
-    gate_up = jnp.stack([w_gate[0].T, w_up[0].T])
-    arrived, gate_up, down_own = lax.optimization_barrier((arrived, gate_up, w_down[0]))
+    arrived, down_own, down_y = lax.optimization_barrier((arrived, down_own, down_y))
     rows = lax.all_gather(arrived, "y", axis=0, tiled=True)
-    weight_in = jnp.stack([gate_up, lax.ppermute(gate_up, "zl", swap)], axis=1)
-    weight_in = jnp.pad(weight_in, ((0, 0),) * 3 + ((0, EXTRA),)).reshape(-1, width + EXTRA)
-    units = weight_in.shape[0] // 2
-    down = jnp.concatenate([down_own, lax.ppermute(down_own, "zl", swap)], axis=1)
-    down = down.reshape(n_zl, n_y, units // n_zl, down.shape[1])
-    down = jnp.where(zl == 0, down, down[::-1])
-    down = jnp.transpose(down, (1, 0, 2, 3)).reshape(n_y * units, -1)
-    rows, weight_in, down = lax.optimization_barrier((rows, weight_in, down))
-
-    both = rows_dot(weight_in, rows)
-    hidden = (jax.nn.silu(both[:units]) * both[units:]).astype(jnp.bfloat16)
-    hidden, down, extra = lax.optimization_barrier((hidden, down, rows[:, width:]))
-    hidden = spread(hidden, "y", n_y).reshape(n_y * units, -1)
-
-    result = lax.dot_general(
-        hidden, down, (((0,), (0,)), ((), ())), preferred_element_type=jnp.float32
-    ).astype(jnp.bfloat16)
-    cols = result.shape[1]
-    result = jnp.concatenate([result, extra], axis=1)
-    result = result.reshape(n_y, expert_count, slots, cols + EXTRA).transpose(1, 0, 2, 3)
-    result = exchange(result.reshape(expert_count, n_y * slots, cols + EXTRA), EXP)
+    down_z, down_zy = lax.ppermute(down_own, "zl", swap_z), lax.ppermute(down_y, "zl", swap_z)
+    rows, down_z, down_zy = lax.optimization_barrier((rows, down_z, down_zy))
+
+    hidden = hidden_pieces(rows, zl, (gate_own, gate_z, up_own, up_z), width, n_y)
+    hidden, extra = lax.optimization_barrier((hidden, rows[:, width:]))
+    hidden = exchange(hidden, "y")
+
+    result = down_slots(y_pos % 2, hidden, extra, (down_own, down_y, down_z, down_zy))
+    cols = result.shape[1] - EXTRA
+    result = exchange(result.reshape(expert_count, -1, cols + EXTRA), EXP)
     result = result.reshape(-1, cols + EXTRA)
-
     tokens = lax.dot_general(
         result[:, cols : cols + 2 * places],
         result[:, :cols],
@@ -154,8 +263,11 @@
     )
     tokens = (tokens[:places] + tokens[places:]).astype(jnp.bfloat16)
     tokens = exchange(tokens.reshape(n_y, tok_dev, cols), "y")
-    tokens = tokens.reshape(n_y, tok_dev, n_zl, cols // n_zl).transpose(1, 2, 0, 3)
-    tokens = jnp.where(zl == 0, tokens, tokens[:, ::-1])
+    tokens = added(tokens.reshape(n_y // 2, 2, tok_dev, cols).transpose(1, 0, 2, 3))
+    tokens = tokens.astype(jnp.bfloat16).reshape(n_y // 2, tok_dev, n_zl, 2, cols // 4)
+    tokens = jnp.where(zl == 0, tokens, tokens[:, :, ::-1])
+    tokens = jnp.where(y_pos < n_y // 2, tokens, tokens[:, :, :, ::-1])
+    tokens = tokens.transpose(1, 2, 0, 3, 4)
     return (mixed, tokens.reshape(tok_dev, width))
 
 

time: 268 us -> 251 us (0.937)
  blocking collectives: 120 us -> 95.6 us
  Pallas kernels: 0 us -> 11.7 us
  starting transfers between devices: 21.7 us -> 30.6 us
  waiting for transfers between devices: 74.4 us -> 81.9 us
  other arithmetic: 12.2 us -> 4.82 us
  local copies, waits for them, and re-layouts: 15.4 us -> 8.55 us
  matrix products: 8.21 us -> 2.07 us
    all_to_all x7 -> x6, blocking collectives: 120 us -> 95.6 us  [exchange(): return lax.all_to_all(pieces, axis, 0, 0, tiled=True)]
    ppermute x2 -> x5, waiting for transfers between devices: 48.6 us -> 32.4 us  [the longest x1 16.9 us: on_device(): lax.ppermute(down_y, 'zl', swap_z)]
    all_gather x1, waiting for transfers between devices: 0.01 us -> 14.5 us  [on_device(): rows = lax.all_gather(arrived, 'y', axis=0, tiled=True)]
    pallas_call x0 -> x2, Pallas kernels: none -> 11.7 us  [the longest x1 6.2 us: hidden_pieces(): pl.pallas_call(hidden_kernel, out_shape=jax.ShapeDtypeStruct((peers, 2 *...]
    all_to_all x2 -> x3, waiting for transfers between devices: 25.8 us -> 35 us  [exchange(): return lax.all_to_all(pieces, axis, 0, 0, tiled=True)]
    ppermute x2 -> x5, starting transfers between devices: 5.29 us -> 13.4 us  [the longest x1 3.38 us: on_device(): lax.ppermute(down_own, 'zl', swap_z)]
    optimization_barrier x1 -> x0, local copies, waits for them, and re-layouts: 6.55 us -> none  [on_device(): rows, weight_in, down = lax.optimization_barrier((rows, weight_in, down))]
    another operation x2 -> x0, other arithmetic: 5.81 us -> none  [the longest x1 3.36 us: on_device(): weight_in = jnp.stack([gate_up, lax.ppermute(gate_up, 'zl', swap)], axis=1)]
  transfers between devices with their start and end apart: 5 -> 9, of which waited for: 3 -> 6; matrix products, arithmetic and copies ran while one was open for 5% -> 3% of each run, Pallas kernels for 0% -> 0%
where the time goes in v4:
time: 251 us; the launch traced here: 250 us
  blocking collectives  95.6 us (38%)
  waiting for transfers between devices  81.9 us (33%)
  starting transfers between devices  30.6 us (12%)
  between operations  14.4 us (6%)
  Pallas kernels  11.7 us (5%)
  local copies, waits for them, and re-layouts  8.55 us (3%)
  other arithmetic  4.82 us (2%)
    all_to_all x6, blocking collectives, exchange(): return lax.all_to_all(pieces, axis, 0, 0, tiled=True)  95.6 us
    all_to_all x3, waiting for transfers between devices, exchange(): return lax.all_to_all(pieces, axis, 0, 0, tiled=True)  35 us
    all_to_all x3, starting transfers between devices, exchange(): return lax.all_to_all(pieces, axis, 0, 0, tiled=True)  17.1 us
    ppermute x1, waiting for transfers between devices, on_device(): lax.ppermute(down_y, 'zl', swap_z)  16.9 us
    ppermute x1, waiting for transfers between devices, on_device(): lax.ppermute(down_own, 'zl', swap_z)  15.6 us
    all_gather x1, waiting for transfers between devices, on_device(): rows = lax.all_gather(arrived, 'y', axis=0, tiled=True)  14.5 us
    pallas_call x1, Pallas kernels, hidden_pieces(): pl.pallas_call(hidden_kernel, out_shape=jax.ShapeDtypeStruct((peers, 2 *...  6.2 us
    pallas_call x1, Pallas kernels, down_slots(): pl.pallas_call(down_kernel, out_shape=jax.ShapeDtypeStruct(out, jnp.bfloa...  5.54 us
  transfers between devices with their start and end apart: 9, of which 6 were waited for; matrix products, arithmetic and copies ran while one was open for 3% of the time, Pallas kernels for 0%

profile of v4, /device:TPU:1, one launch (start us, length us, event | category | flops | bytes accessed | tf_op | source)
XLA Modules:
  0.0 249.6 jit_solution(2502053311729067830)
XLA Ops:
  9.0 9.6 %all-to-all-start = ((bf16[16,128,128]{2,1,0:T(8,128)(2,1)}), bf16[16,128,128]{2,1,0:T(8,128)(2,1)S(1)}, u32[]{:S(2)}, u32[]{:S(2)}) async-start(bf16[16,128,128]{2,1,0:T(8,128)(2,1)} %broadcast_in_dim.31), calls=%async_computation | async-start | bytes 1048576 | tf_op jit(solution)/shard_map/all_to_all | solution.py:19
  18.6 3.3 %collective-permute-start = (bf16[96,4096]{1,0:T(8,128)(2,1)}, bf16[96,4096]{1,0:T(8,128)(2,1)}, u32[]{:S(2)}, u32[]{:S(2)}) collective-permute-start(bf16[96,4096]{1,0:T(8,128)(2,1)} %bitcast.49), channel_id=1, source_target_pairs={{0,256},{256,0},{1,257},{257,1},{2,258},{258,2},{3,259},{259,3},{4... | collective-permute-start | bytes 2359304 | tf_op jit(solution)/shard_map/ppermute | solution.py:192
  21.9 2.0 collective-permute-start.1
  28.1 4.3 %all-to-all-done = bf16[16,128,128]{2,1,0:T(8,128)(2,1)S(1)} async-done(((bf16[16,128,128]{2,1,0:T(8,128)(2,1)}), bf16[16,128,128]{2,1,0:T(8,128)(2,1)S(1)}, u32[]{:S(2)}, u32[]{:S(2)}) %all-to-all-start) | async-done | bytes 524320 | tf_op jit(solution)/shard_map/all_to_all | solution.py:19
  32.4 7.1 %all_to_all.45 = bf16[2,2048,128]{2,1,0:T(8,128)(2,1)S(1)} all-to-all(bf16[2,2048,128]{2,1,0:T(8,128)(2,1)S(1)} %broadcast_in_dim.37), channel_id=1, replica_groups=mesh['zl'=2,'y'=8,'x'=4,'zh'=4,'co'=2] {'co'}, dimensions={0} | all-to-all | bytes 2097152 | tf_op jit(solution)/shard_map/all_to_all | solution.py:19
  41.1 2.8 %collective-permute-start.2 = (bf16[1536,256]{1,0:T(8,128)(2,1)}, bf16[1536,256]{1,0:T(8,128)(2,1)}, u32[]{:S(2)}, u32[]{:S(2)}) collective-permute-start(bf16[1536,256]{1,0:T(8,128)(2,1)} %bitcast.12.refs_0_), channel_id=1, source_target_pairs={{0,32},{32,0},{64,96},{96,64},{128,160},{160,128},{192,224},{224,1... | collective-permute-start | bytes 2359304 | tf_op jit(solution)/shard_map/ppermute | solution.py:226
  44.4 4.9 %all_to_all.46 = bf16[2,64,4096]{2,1,0:T(8,128)(2,1)S(1)} all-to-all(bf16[2,64,4096]{2,1,0:T(8,128)(2,1)S(1)} %bitcast.44), channel_id=1, replica_groups=mesh['zl'=2,'y'=8,'x'=4,'zh'=4,'co'=2] {'co'}, dimensions={0} | all-to-all | bytes 2097152 | tf_op jit(solution)/shard_map/all_to_all | solution.py:19
  49.3 1.1 reduce_sum.84
  50.4 12.6 %all_to_all.47 = bf16[4,16,4096]{2,1,0:T(8,128)(2,1)S(1)} all-to-all(bf16[4,16,4096]{2,1,0:T(8,128)(2,1)} %bitcast.48), channel_id=1, replica_groups=mesh['zl'=2,'y'=8,'x'=4,'zh'=4,'co'=2] {'x'}, dimensions={0} | all-to-all | bytes 1048576 | tf_op jit(solution)/shard_map/all_to_all | solution.py:19
  63.2 16.6 %all_to_all.48 = bf16[4,4,4096]{2,1,0:T(4,128)(2,1)S(1)} all-to-all(bf16[4,4,4096]{2,1,0:T(4,128)(2,1)S(1)} %reshape.145), channel_id=1, replica_groups=mesh['zl'=2,'y'=8,'x'=4,'zh'=4,'co'=2] {'zh'}, dimensions={0} | all-to-all | bytes 262144 | tf_op jit(solution)/shard_map/all_to_all | solution.py:19
  80.6 24.5 %all_to_all.49 = bf16[32,2,4224]{2,1,0:T(2,128)(2,1)S(1)} all-to-all(bf16[32,2,4224]{2,1,0:T(2,128)(2,1)S(1)} %reshape.148), channel_id=1, replica_groups=mesh['zl'=2,'y'=8,'x'=4,'zh'=4,'co'=2] {'x','zh','co'}, dimensions={0} | all-to-all | bytes 1081344 | tf_op jit(solution)/shard_map/all_to_all | solution.py:19
  106.2 3.4 %collective-permute-start.3 = (bf16[1536,256]{1,0:T(8,128)(2,1)}, bf16[1536,256]{1,0:T(8,128)(2,1)}, u32[]{:S(2)}, u32[]{:S(2)}) collective-permute-start(bf16[1536,256]{1,0:T(8,128)(2,1)} %bitcast.12.refs_0_), channel_id=1, source_target_pairs={{0,256},{256,0},{1,257},{257,1},{2,258},{258,2},{3,259},{259,3},{4... | collective-permute-start | bytes 2359304 | tf_op jit(solution)/shard_map/ppermute | solution.py:247
  109.6 1.9 collective-permute-start.4
  111.5 15.6 %collective-permute-done.3.refs_2_ = bf16[1536,256]{1,0:T(8,128)(2,1)} collective-permute-done((bf16[1536,256]{1,0:T(8,128)(2,1)}, bf16[1536,256]{1,0:T(8,128)(2,1)}, u32[]{:S(2)}, u32[]{:S(2)}) %collective-permute-start.3) | collective-permute-done | bytes 786464 | tf_op jit(solution)/shard_map/ppermute | solution.py:247
  127.1 16.9 %collective-permute-done.4.refs_3_ = bf16[1536,256]{1,0:T(8,128)(2,1)} collective-permute-done((bf16[1536,256]{1,0:T(8,128)(2,1)}, bf16[1536,256]{1,0:T(8,128)(2,1)}, u32[]{:S(2)}, u32[]{:S(2)}) %collective-permute-start.4) | collective-permute-done | bytes 786464 | tf_op jit(solution)/shard_map/ppermute | solution.py:247
  143.9 14.5 %all-gather.2.cloned.1.call-done.rows_ref = bf16[512,4224]{1,0:T(8,128)(2,1)} async-done(((bf16[64,4224]{1,0:T(8,128)(2,1)}), bf16[512,4224]{1,0:T(8,128)(2,1)}) %all-gather.2.cloned.1.call-update) | async-done | bytes 4325392 | tf_op jit(solution)/shard_map/all_gather | solution.py:246
  158.5 1.6 slice.15.extra_ref
  160.0 6.2 %shard_map.131 = bf16[8,192,256]{2,1,0:T(8,128)(2,1)} custom-call(s32[1]{0:T(128)} %bitcast.20.zl_ref, bf16[512,4224]{1,0:T(8,128)(2,1)} %all-gather.2.cloned.1.call-done.rows_ref, bf16[96,4096]{1,0:T(8,128)(2,1)} %bitcast.50, bf16[96,4096]{1,0:T(8,128)(2,1)} %collective-permute-done.gate_b, bf16[96,4096]{1,0:T(8,128)(2,1)} %bitcast.52, ...), custom_call_target="tpu_custom_call" | custom-call | flops 1610612736 | bytes 4194304 | tf_op jit(solution)/shard_map/pallas_call | solution.py:96
  166.2 4.2 %all-to-all-start.6 = ((bf16[8,192,256]{2,1,0:T(8,128)(2,1)}), bf16[8,192,256]{2,1,0:T(8,128)(2,1)S(1)}, u32[]{:S(2)}, u32[]{:S(2)}) async-start(bf16[8,192,256]{2,1,0:T(8,128)(2,1)} %shard_map.131), calls=%async_computation.6 | async-start | bytes 1572864 | tf_op jit(solution)/shard_map/all_to_all | solution.py:19
  170.4 23.6 %all-to-all-done.6.hidden_ref = bf16[8,192,256]{2,1,0:T(8,128)(2,1)S(1)} async-done(((bf16[8,192,256]{2,1,0:T(8,128)(2,1)}), bf16[8,192,256]{2,1,0:T(8,128)(2,1)S(1)}, u32[]{:S(2)}, u32[]{:S(2)}) %all-to-all-start.6) | async-done | bytes 786464 | tf_op jit(solution)/shard_map/all_to_all | solution.py:19
  194.9 5.5 %shard_map.132 = bf16[256,1152]{1,0:T(8,128)(2,1)} custom-call(s32[1]{0:T(128)} %bitcast.19.half_ref, bf16[8,192,256]{2,1,0:T(8,128)(2,1)} %copy-done.1, bf16[512,128]{1,0:T(8,128)(2,1)} %slice.15.extra_ref, bf16[1536,256]{1,0:T(8,128)(2,1)} %bitcast.12.refs_0_, bf16[1536,256]{1,0:T(8,128)(2,1)} %collective-permute-done.2.refs_1_, ...), custom_call_target="tpu_custom_call" | custom-call | flops 805306368 | bytes 3145728 | tf_op jit(solution)/shard_map/pallas_call | solution.py:145
  200.4 29.9 %all_to_all.50 = bf16[32,8,1152]{2,1,0:T(8,128)(2,1)S(1)} all-to-all(bf16[32,8,1152]{2,1,0:T(8,128)(2,1)} %bitcast.45), channel_id=1, replica_groups=mesh['zl'=2,'y'=8,'x'=4,'zh'=4,'co'=2] {'x','zh','co'}, dimensions={0} | all-to-all | bytes 1179648 | tf_op jit(solution)/shard_map/all_to_all | solution.py:19
  231.2 3.3 %all-to-all-start.8 = ((bf16[8,4,1024]{2,1,0:T(4,128)(2,1)}), bf16[8,4,1024]{2,1,0:T(4,128)(2,1)S(1)}, u32[]{:S(2)}, u32[]{:S(2)}) async-start(bf16[8,4,1024]{2,1,0:T(4,128)(2,1)} %reshape.152), calls=%async_computation.8 | async-start | bytes 131072 | tf_op jit(solution)/shard_map/all_to_all | solution.py:19
  234.5 7.1 %all-to-all-done.8 = bf16[8,4,1024]{2,1,0:T(4,128)(2,1)S(1)} async-done(((bf16[8,4,1024]{2,1,0:T(4,128)(2,1)}), bf16[8,4,1024]{2,1,0:T(4,128)(2,1)S(1)}, u32[]{:S(2)}, u32[]{:S(2)}) %all-to-all-start.8) | async-done | bytes 65568 | tf_op jit(solution)/shard_map/all_to_all | solution.py:19
  (65 shorter events, 12.8 us)
Async XLA Ops:
  7.2 36.7 %copy-start = (bf16[256,4096]{1,0:T(8,128)(2,1)S(1)}, bf16[256,4096]{1,0:T(8,128)(2,1)}, u32[]{:S(2)}) copy-start(bf16[256,4096]{1,0:T(8,128)(2,1)} %param.16) | copy-start | bytes 6291460
  7.2 20.9 %copy-start.5 = (s32[256]{0:T(256)S(1)}, s32[256]{0:T(256)}, u32[]{:S(2)}) copy-start(s32[256]{0:T(256)} %constant.89.clone) | copy-start | bytes 3076
  9.0 23.3 %all-to-all-start = ((bf16[16,128,128]{2,1,0:T(8,128)(2,1)}), bf16[16,128,128]{2,1,0:T(8,128)(2,1)S(1)}, u32[]{:S(2)}, u32[]{:S(2)}) async-start(bf16[16,128,128]{2,1,0:T(8,128)(2,1)} %broadcast_in_dim.31), calls=%async_computation | async-start | bytes 1048576 | tf_op jit(solution)/shard_map/all_to_all | solution.py:19
  18.6 139.9 %all-gather.2.cloned.1.call-start = ((), (), s32[]{:S(2)}) async-start(), calls=%async_computation.9 | async-start | bytes 4866048 | tf_op jit(solution)/shard_map/all_gather | solution.py:246
  18.6 44.4 %collective-permute-start = (bf16[96,4096]{1,0:T(8,128)(2,1)}, bf16[96,4096]{1,0:T(8,128)(2,1)}, u32[]{:S(2)}, u32[]{:S(2)}) collective-permute-start(bf16[96,4096]{1,0:T(8,128)(2,1)} %bitcast.49), channel_id=1, source_target_pairs={{0,256},{256,0},{1,257},{257,1},{2,258},{258,2},{3,259},{259,3},{4... | collective-permute-start | bytes 2359304 | tf_op jit(solution)/shard_map/ppermute | solution.py:192
  21.9 41.2 %collective-permute-start.1 = (bf16[96,4096]{1,0:T(8,128)(2,1)}, bf16[96,4096]{1,0:T(8,128)(2,1)}, u32[]{:S(2)}, u32[]{:S(2)}) collective-permute-start(bf16[96,4096]{1,0:T(8,128)(2,1)} %bitcast.51), channel_id=1, source_target_pairs={{0,256},{256,0},{1,257},{257,1},{2,258},{258,2},{3,259},{259,3},{4... | collective-permute-start | bytes 2359304 | tf_op jit(solution)/shard_map/ppermute | solution.py:192
  41.1 22.0 %collective-permute-start.2 = (bf16[1536,256]{1,0:T(8,128)(2,1)}, bf16[1536,256]{1,0:T(8,128)(2,1)}, u32[]{:S(2)}, u32[]{:S(2)}) collective-permute-start(bf16[1536,256]{1,0:T(8,128)(2,1)} %bitcast.12.refs_0_), channel_id=1, source_target_pairs={{0,32},{32,0},{64,96},{96,64},{128,160},{160,128},{192,224},{224,1... | collective-permute-start | bytes 2359304 | tf_op jit(solution)/shard_map/ppermute | solution.py:226
  49.3 30.6 %copy-start.3 = (bf16[4,4096]{1,0:T(4,128)(2,1)S(1)}, bf16[4,4096]{1,0:T(4,128)(2,1)}, u32[]{:S(2)}) copy-start(bf16[4,4096]{1,0:T(4,128)(2,1)} %param.15) | copy-start | bytes 98308
  49.3 30.8 %copy-start.4 = (f32[4096]{0:T(1024)S(1)}, f32[4096]{0:T(1024)}, u32[]{:S(2)}) copy-start(f32[4096]{0:T(1024)} %param.17) | copy-start | bytes 49156
  80.0 26.2 %copy-start.2 = (bf16[4,4096]{1,0:T(4,128)(2,1)}, bf16[4,4096]{1,0:T(4,128)(2,1)S(1)}, u32[]{:S(2)}) copy-start(bf16[4,4096]{1,0:T(4,128)(2,1)S(1)} %get-tuple-element.37) | copy-start | bytes 98308
  106.2 20.9 %collective-permute-start.3 = (bf16[1536,256]{1,0:T(8,128)(2,1)}, bf16[1536,256]{1,0:T(8,128)(2,1)}, u32[]{:S(2)}, u32[]{:S(2)}) collective-permute-start(bf16[1536,256]{1,0:T(8,128)(2,1)} %bitcast.12.refs_0_), channel_id=1, source_target_pairs={{0,256},{256,0},{1,257},{257,1},{2,258},{258,2},{3,259},{259,3},{4... | collective-permute-start | bytes 2359304 | tf_op jit(solution)/shard_map/ppermute | solution.py:247
  109.6 34.3 %collective-permute-start.4 = (bf16[1536,256]{1,0:T(8,128)(2,1)}, bf16[1536,256]{1,0:T(8,128)(2,1)}, u32[]{:S(2)}, u32[]{:S(2)}) collective-permute-start(bf16[1536,256]{1,0:T(8,128)(2,1)} %collective-permute-done.2.refs_1_), channel_id=1, source_target_pairs={{0,256},{256,0},{1,257},{257,1},{2,258},{258,2},{3,259},{259,3},{4... | collective-permute-start | bytes 2359304 | tf_op jit(solution)/shard_map/ppermute | solution.py:247
  166.2 27.8 %all-to-all-start.6 = ((bf16[8,192,256]{2,1,0:T(8,128)(2,1)}), bf16[8,192,256]{2,1,0:T(8,128)(2,1)S(1)}, u32[]{:S(2)}, u32[]{:S(2)}) async-start(bf16[8,192,256]{2,1,0:T(8,128)(2,1)} %shard_map.131), calls=%async_computation.6 | async-start | bytes 1572864 | tf_op jit(solution)/shard_map/all_to_all | solution.py:19
  194.0 0.9 copy-start.1
  231.2 10.5 %all-to-all-start.8 = ((bf16[8,4,1024]{2,1,0:T(4,128)(2,1)}), bf16[8,4,1024]{2,1,0:T(4,128)(2,1)S(1)}, u32[]{:S(2)}, u32[]{:S(2)}) async-start(bf16[8,4,1024]{2,1,0:T(4,128)(2,1)} %reshape.152), calls=%async_computation.8 | async-start | bytes 131072 | tf_op jit(solution)/shard_map/all_to_all | solution.py:19
Sparse Core Ops, SparseCore 0:
  106.3 52.0 all-gather.1

commit v5 on v4

--- a/solution.py
+++ b/solution.py
@@ -55,11 +55,10 @@
     return pl.BlockSpec(shape, lambda *_: (0,) * len(shape))
 
 
-def hidden_kernel(zl_ref, rows_ref, gate_a, gate_b, up_a, up_b, out_ref, weight, total):
-    step = pl.program_id(0)
-    units = gate_a.shape[0]
-
-    for place, (own, other) in enumerate(((gate_a, gate_b), (up_a, up_b))):
+def weight_rows(zl_ref, refs, weight):
+    units = refs[0].shape[0]
+    for place in range(2):
+        own, other = refs[2 * place], refs[2 * place + 1]
         low = pl.ds(2 * place * units, units)
         high = pl.ds((2 * place + 1) * units, units)
 
@@ -73,48 +72,142 @@
             weight[low, :] = other[...]
             weight[high, :] = own[...]
 
-    @pl.when(step == 0)
+
+def gated(total, units):
+    gate, upper = total[: 2 * units, :], total[2 * units :, :]
+    return (gate / (1.0 + jnp.exp(-gate)) * upper).astype(jnp.bfloat16)
+
+
+def accumulate(weight, rows, block_refs, total):
+    start = 0
+    for block in block_refs:
+        rows[pl.ds(start, block.shape[0]), :] = block[...]
+        start += block.shape[0]
+
+    @pl.when(pl.program_id(0) == 0)
     def _():
         total[...] = jnp.zeros_like(total)
 
-    total[...] += rows_dot(weight[...], rows_ref[...])
-
-    @pl.when(step == pl.num_programs(0) - 1)
+    total[...] += rows_dot(weight[...], rows[...])
+
+
+def first_kernel(zl_ref, *refs):
+    blocks, weights, (out_ref, weight, rows, total) = refs[:-8], refs[-8:-4], refs[-4:]
+    weight_rows(zl_ref, weights, weight)
+    accumulate(weight, rows, blocks, total)
+
+    @pl.when(pl.program_id(0) == pl.num_programs(0) - 1)
     def _():
-        gate, upper = total[: 2 * units, :], total[2 * units :, :]
-        hidden = (gate / (1.0 + jnp.exp(-gate)) * upper).astype(jnp.bfloat16)
-        half = hidden.shape[1] // 2
-        for peer in range(out_ref.shape[0]):
-            start = (peer % 2) * half
-            out_ref[peer] = hidden[:, start : start + half]
-
-
-def hidden_pieces(rows, zl, weights, width, peers):
-    units = weights[0].shape[0]
-    count, step = rows.shape[0], 1024 if width % 1024 == 0 else width
-    weight_spec = pl.BlockSpec((units, step), lambda k, *_: (0, k))
+        out_ref[...] = gated(total, weights[0].shape[0])
+
+
+def last_kernel(count, place_ref, *refs):
+    blocks, weights, first = refs[:count], refs[count : count + 4], refs[count + 4]
+    extras, (out_ref, extra_ref, weight, rows, total, tags) = refs[count + 5 : -6], refs[-6:]
+    weight_rows(place_ref, weights, weight)
+    accumulate(weight, rows, blocks, total)
+
+    @pl.when(pl.program_id(0) == pl.num_programs(0) - 1)
+    def _():
+        hidden = jnp.concatenate([first[...], gated(total, weights[0].shape[0])], axis=1)
+        slots = hidden.shape[1]
+        peers = out_ref.shape[0]
+        each = slots // peers
+        start = 0
+        for extra in extras:
+            tags[pl.ds(start, extra.shape[0]), :] = extra[...]
+            start += extra.shape[0]
+        held = lax.broadcasted_iota(jnp.int32, (slots, slots), 0)
+        turn = held // each
+        away = jnp.where(turn % 2 == 1, peers - (turn + 1) // 2, turn // 2)
+        goal = (place_ref[1] + away) % peers * each + held % each
+        column = lax.broadcasted_iota(jnp.int32, (slots, slots), 1)
+        move = jnp.where(goal == column, 1.0, 0.0).astype(jnp.bfloat16)
+        hidden = jnp.dot(hidden, move, preferred_element_type=jnp.float32).astype(jnp.bfloat16)
+        half = slots // 2
+        for peer in range(peers):
+            out_ref[peer] = hidden[:, (peer % 2) * half : (peer % 2 + 1) * half]
+        extra_ref[...] = lax.dot_general(
+            move, tags[...], (((0,), (0,)), ((), ())), preferred_element_type=jnp.float32
+        ).astype(jnp.bfloat16)
+
+
+def row_specs(blocks, weights, step):
+    return [pl.BlockSpec((b.shape[0], step), lambda k, *_: (0, k)) for b in blocks] + [
+        pl.BlockSpec((w.shape[0], step), lambda k, *_: (0, k)) for w in weights
+    ]
+
+
+def held_scratch(units, count, step):
+    return [
+        pltpu.VMEM((4 * units, step), jnp.bfloat16),
+        pltpu.VMEM((count, step), jnp.bfloat16),
+        pltpu.VMEM((4 * units, count), jnp.float32),
+    ]
+
+
+def cost(units, count, width):
+    return pl.CostEstimate(
+        flops=8 * units * count * width,
+        bytes_accessed=2 * (count + 4 * units) * width,
+        transcendentals=0,
+    )
+
+
+def first_hidden(zl, blocks, weights, width):
+    units, step = weights[0].shape[0], 1024
+    count = sum(b.shape[0] for b in blocks)
     return pl.pallas_call(
-        hidden_kernel,
-        out_shape=jax.ShapeDtypeStruct((peers, 2 * units, count // 2), jnp.bfloat16),
+        first_kernel,
+        out_shape=jax.ShapeDtypeStruct((2 * units, count), jnp.bfloat16),
         grid_spec=pltpu.PrefetchScalarGridSpec(
             num_scalar_prefetch=1,
             grid=(width // step,),
-            in_specs=[pl.BlockSpec((count, step), lambda k, *_: (0, k))] + [weight_spec] * 4,
-            out_specs=whole((peers, 2 * units, count // 2)),
-            scratch_shapes=[
-                pltpu.VMEM((4 * units, step), jnp.bfloat16),
-                pltpu.VMEM((4 * units, count), jnp.float32),
+            in_specs=row_specs(blocks, weights, step),
+            out_specs=whole((2 * units, count)),
+            scratch_shapes=held_scratch(units, count, step),
+        ),
+        compiler_params=pltpu.CompilerParams(vmem_limit_bytes=60 * 2**20),
+        cost_estimate=cost(units, count, width),
+    )(zl.reshape(1), *blocks, *weights)
+
+
+def last_hidden(place, blocks, weights, first, every, width, peers):
+    units, step = weights[0].shape[0], 1024
+    count = sum(b.shape[0] for b in blocks)
+    slots = sum(b.shape[0] for b in every)
+    pieces = (peers, 2 * units, slots // 2)
+    return pl.pallas_call(
+        lambda *refs: last_kernel(len(blocks), *refs),
+        out_shape=(
+            jax.ShapeDtypeStruct(pieces, jnp.bfloat16),
+            jax.ShapeDtypeStruct((slots, EXTRA), jnp.bfloat16),
+        ),
+        grid_spec=pltpu.PrefetchScalarGridSpec(
+            num_scalar_prefetch=1,
+            grid=(width // step,),
+            in_specs=row_specs(blocks, weights, step)
+            + [whole(first.shape)]
+            + [
+                pl.BlockSpec((b.shape[0], EXTRA), lambda k, *_: (0, width // EXTRA))
+                for b in every
             ],
+            out_specs=(whole(pieces), whole((slots, EXTRA))),
+            scratch_shapes=held_scratch(units, count, step)
+            + [pltpu.VMEM((slots, EXTRA), jnp.bfloat16)],
         ),
         compiler_params=pltpu.CompilerParams(vmem_limit_bytes=60 * 2**20),
-        cost_estimate=pl.CostEstimate(
-            flops=8 * units * count * width, bytes_accessed=2 * count * width, transcendentals=0
-        ),
-    )(zl.reshape(1), rows, *weights)
+        cost_estimate=cost(units, count, width),
+    )(place, *blocks, *weights, first, *every)
 
 
 def down_kernel(half_ref, hidden_ref, extra_ref, *refs):
-    weights, out_ref, stacked = refs[:4], refs[4], refs[5]
+    weights, out_ref, stacked, held, arrived = refs[:4], refs[4], refs[5], refs[6], refs[7]
+    copies = [
+        pltpu.make_async_copy(weight, held.at[i], arrived.at[i]) for i, weight in enumerate(weights)
+    ]
+    for copy in copies:
+        copy.start()
     peers, units, count = hidden_ref.shape
     for peer in range(peers):
         for z in range(2):
@@ -124,18 +217,17 @@
     each = count // blocks
     to = lax.broadcasted_iota(jnp.int32, (count, count), 0)
     source = (to % (2 * blocks)) // 2 * each + to // (2 * blocks) * 2 + to % 2
-    move = (lax.broadcasted_iota(jnp.int32, (count, count), 1) == source).astype(jnp.bfloat16)
-    rows = stacked[...].T
-    cols = weights[0].shape[1]
-    for place, weight in enumerate(weights):
-        result = jnp.dot(rows, weight[...], preferred_element_type=jnp.float32)
-        result = jnp.dot(
-            move, result.astype(jnp.bfloat16), preferred_element_type=jnp.float32
-        )
-        out_ref[:, place * cols : (place + 1) * cols] = result.astype(jnp.bfloat16)
+    column = lax.broadcasted_iota(jnp.int32, (count, count), 1)
+    move = jnp.where(source == column, 1.0, 0.0).astype(jnp.bfloat16)
+    rows = rows_dot(move, stacked[...]).astype(jnp.bfloat16)
+    cols = held.shape[2]
     extra = jnp.where(half_ref[0] == 0, extra_ref[:count, :], extra_ref[count:, :])
     extra = jnp.dot(move, extra, preferred_element_type=jnp.float32)
     out_ref[:, 4 * cols :] = extra.astype(jnp.bfloat16)
+    for i, copy in enumerate(copies):
+        copy.wait()
+        result = jnp.dot(rows, held[i], preferred_element_type=jnp.float32)
+        out_ref[:, i * cols : (i + 1) * cols] = result.astype(jnp.bfloat16)
 
 
 def down_slots(half, hidden, extra, weights):
@@ -148,13 +240,14 @@
         grid_spec=pltpu.PrefetchScalarGridSpec(
             num_scalar_prefetch=1,
             grid=(1,),
-            in_specs=[
-                whole(hidden.shape),
-                whole(extra.shape),
-            ]
-            + [whole((deep, cols))] * 4,
+            in_specs=[whole(hidden.shape), whole(extra.shape)]
+            + [pl.BlockSpec(memory_space=pl.ANY)] * 4,
             out_specs=whole(out),
-            scratch_shapes=[pltpu.VMEM((deep, count), jnp.bfloat16)],
+            scratch_shapes=[
+                pltpu.VMEM((deep, count), jnp.bfloat16),
+                pltpu.VMEM((4, deep, cols), jnp.bfloat16),
+                pltpu.SemaphoreType.DMA((4,)),
+            ],
         ),
         compiler_params=pltpu.CompilerParams(vmem_limit_bytes=60 * 2**20),
         cost_estimate=pl.CostEstimate(
@@ -243,12 +336,23 @@
     arrived = arrived.reshape(expert_count * slots, width + EXTRA)
 
     arrived, down_own, down_y = lax.optimization_barrier((arrived, down_own, down_y))
-    rows = lax.all_gather(arrived, "y", axis=0, tiled=True)
+    after = [(i, (i + 1) % n_y) for i in range(n_y)]
+    before = [(b, a) for a, b in after]
+    blocks, left, right = [arrived], arrived, arrived
+    for _ in range(n_y // 2 - 1):
+        left, right = lax.ppermute(left, "y", after), lax.ppermute(right, "y", before)
+        blocks += [left, right]
+    part = arrived.shape[0] // 2
+    blocks.append(lax.ppermute(left[:part], "y", after))
+    blocks.append(lax.ppermute(right[part:], "y", before))
     down_z, down_zy = lax.ppermute(down_own, "zl", swap_z), lax.ppermute(down_y, "zl", swap_z)
-    rows, down_z, down_zy = lax.optimization_barrier((rows, down_z, down_zy))
-
-    hidden = hidden_pieces(rows, zl, (gate_own, gate_z, up_own, up_z), width, n_y)
-    hidden, extra = lax.optimization_barrier((hidden, rows[:, width:]))
+    weights = (gate_own, gate_z, up_own, up_z)
+    first = first_hidden(zl, blocks[:5], weights, width)
+    last, first, down_z, down_zy = lax.optimization_barrier((blocks[5:], first, down_z, down_zy))
+
+    hidden, extra = last_hidden(
+        jnp.stack([zl, y_pos]), last, weights, first, blocks[:5] + last, width, n_y
+    )
     hidden = exchange(hidden, "y")
 
     result = down_slots(y_pos % 2, hidden, extra, (down_own, down_y, down_z, down_zy))

time: 251 us -> 255 us (1.016)
  starting transfers between devices: 30.6 us -> 59.3 us
  waiting for transfers between devices: 81.9 us -> 63.7 us
  between operations: 14.4 us -> 1.18 us
  Pallas kernels: 11.7 us -> 18 us
    ppermute x0 -> x8, starting transfers between devices: none -> 26.1 us  [the longest x3 13.9 us: on_device(): lax.ppermute(right, 'y', before)]
    ppermute x0 -> x8, waiting for transfers between devices: none -> 15.8 us  [the longest x3 15.8 us: on_device(): lax.ppermute(right, 'y', before)]
    ppermute x1, waiting for transfers between devices: 15.6 us -> 0.01 us  [on_device(): lax.ppermute(down_own, 'zl', swap_z)]
    all_gather x1 -> x0, waiting for transfers between devices: 14.5 us -> none  [on_device(): rows = lax.all_gather(arrived, 'y', axis=0, tiled=True)]
    pallas_call x1 -> x2, Pallas kernels: 6.2 us -> 12.6 us  [the longest x1 6.74 us: last_hidden(): pl.pallas_call(lambda *refs: last_kernel(len(blocks), *refs), out_shape=(...]
    all_to_all x3, waiting for transfers between devices: 35 us -> 31.7 us  [exchange(): return lax.all_to_all(pieces, axis, 0, 0, tiled=True)]
    ppermute x1, starting transfers between devices: 3.38 us -> 6.41 us  [on_device(): lax.ppermute(down_own, 'zl', swap_z)]
  transfers between devices with their start and end apart: 9 -> 16, of which waited for: 6 -> 6; matrix products, arithmetic and copies ran while one was open for 3% -> 4% of each run, Pallas kernels for 0% -> 2%
where the time goes in v5:
time: 255 us; the launch traced here: 253 us
  blocking collectives  93.4 us (37%)
  waiting for transfers between devices  63.7 us (25%)
  starting transfers between devices  59.3 us (23%)
  Pallas kernels  18 us (7%)
  local copies, waits for them, and re-layouts  9.48 us (4%)
  other arithmetic  5.49 us (2%)
    all_to_all x6, blocking collectives, exchange(): return lax.all_to_all(pieces, axis, 0, 0, tiled=True)  93.4 us
    all_to_all x3, waiting for transfers between devices, exchange(): return lax.all_to_all(pieces, axis, 0, 0, tiled=True)  31.7 us
    all_to_all x3, starting transfers between devices, exchange(): return lax.all_to_all(pieces, axis, 0, 0, tiled=True)  16.7 us
    ppermute x1, waiting for transfers between devices, on_device(): lax.ppermute(down_y, 'zl', swap_z)  16.2 us
    ppermute x3, waiting for transfers between devices, on_device(): lax.ppermute(right, 'y', before)  15.8 us
    ppermute x3, starting transfers between devices, on_device(): lax.ppermute(right, 'y', before)  13.9 us
    pallas_call x1, Pallas kernels, last_hidden(): pl.pallas_call(lambda *refs: last_kernel(len(blocks), *refs), out_shape=(...  6.74 us
    ppermute x1, starting transfers between devices, on_device(): lax.ppermute(down_own, 'zl', swap_z)  6.41 us
  transfers between devices with their start and end apart: 16, of which 6 were waited for; matrix products, arithmetic and copies ran while one was open for 4% of the time, Pallas kernels for 2%

profile of v5, /device:TPU:1, one launch (start us, length us, event | category | flops | bytes accessed | tf_op | source)
XLA Modules:
  0.0 252.6 jit_solution(5753787826493710230)
XLA Ops:
  2.5 9.6 %all-to-all-start = ((bf16[16,128,128]{2,1,0:T(8,128)(2,1)}), bf16[16,128,128]{2,1,0:T(8,128)(2,1)S(1)}, u32[]{:S(2)}, u32[]{:S(2)}) async-start(bf16[16,128,128]{2,1,0:T(8,128)(2,1)} %broadcast_in_dim.31), calls=%async_computation | async-start | bytes 1048576 | tf_op jit(solution)/shard_map/all_to_all | solution.py:19
  12.1 3.3 %collective-permute-start = (bf16[96,4096]{1,0:T(8,128)(2,1)}, bf16[96,4096]{1,0:T(8,128)(2,1)}, u32[]{:S(2)}, u32[]{:S(2)}) collective-permute-start(bf16[96,4096]{1,0:T(8,128)(2,1)} %bitcast.46), channel_id=1, source_target_pairs={{0,256},{256,0},{1,257},{257,1},{2,258},{258,2},{3,259},{259,3},{4... | collective-permute-start | bytes 2359304 | tf_op jit(solution)/shard_map/ppermute | solution.py:285
  21.5 4.3 %all-to-all-done = bf16[16,128,128]{2,1,0:T(8,128)(2,1)S(1)} async-done(((bf16[16,128,128]{2,1,0:T(8,128)(2,1)}), bf16[16,128,128]{2,1,0:T(8,128)(2,1)S(1)}, u32[]{:S(2)}, u32[]{:S(2)}) %all-to-all-start) | async-done | bytes 524320 | tf_op jit(solution)/shard_map/all_to_all | solution.py:19
  25.9 7.1 %all_to_all.45 = bf16[2,2048,128]{2,1,0:T(8,128)(2,1)S(1)} all-to-all(bf16[2,2048,128]{2,1,0:T(8,128)(2,1)S(1)} %broadcast_in_dim.37), channel_id=1, replica_groups=mesh['zl'=2,'y'=8,'x'=4,'zh'=4,'co'=2] {'co'}, dimensions={0} | all-to-all | bytes 2097152 | tf_op jit(solution)/shard_map/all_to_all | solution.py:19
  37.9 4.8 %all_to_all.46 = bf16[2,64,4096]{2,1,0:T(8,128)(2,1)S(1)} all-to-all(bf16[2,64,4096]{2,1,0:T(8,128)(2,1)S(1)} %bitcast.45), channel_id=1, replica_groups=mesh['zl'=2,'y'=8,'x'=4,'zh'=4,'co'=2] {'co'}, dimensions={0} | all-to-all | bytes 2097152 | tf_op jit(solution)/shard_map/all_to_all | solution.py:19
  43.8 12.6 %all_to_all.47 = bf16[4,16,4096]{2,1,0:T(8,128)(2,1)S(1)} all-to-all(bf16[4,16,4096]{2,1,0:T(8,128)(2,1)} %bitcast.55), channel_id=1, replica_groups=mesh['zl'=2,'y'=8,'x'=4,'zh'=4,'co'=2] {'x'}, dimensions={0} | all-to-all | bytes 1048576 | tf_op jit(solution)/shard_map/all_to_all | solution.py:19
  56.6 16.6 %all_to_all.48 = bf16[4,4,4096]{2,1,0:T(4,128)(2,1)S(1)} all-to-all(bf16[4,4,4096]{2,1,0:T(4,128)(2,1)S(1)} %reshape.143), channel_id=1, replica_groups=mesh['zl'=2,'y'=8,'x'=4,'zh'=4,'co'=2] {'zh'}, dimensions={0} | all-to-all | bytes 262144 | tf_op jit(solution)/shard_map/all_to_all | solution.py:19
  74.1 25.0 %all_to_all.49 = bf16[32,2,4224]{2,1,0:T(2,128)(2,1)} all-to-all(bf16[32,2,4224]{2,1,0:T(2,128)(2,1)S(1)} %reshape.145), channel_id=1, replica_groups=mesh['zl'=2,'y'=8,'x'=4,'zh'=4,'co'=2] {'x','zh','co'}, dimensions={0} | all-to-all | bytes 1081344 | tf_op jit(solution)/shard_map/all_to_all | solution.py:19
  100.4 3.7 %collective-permute-start.6 = (bf16[64,4224]{1,0:T(8,128)(2,1)S(1)}, bf16[64,4224]{1,0:T(8,128)(2,1)S(1)}, u32[]{:S(2)}, u32[]{:S(2)}) collective-permute-start(bf16[64,4224]{1,0:T(8,128)(2,1)S(1)} %reshape.146.refs_0_.refs_10_), channel_id=1, source_target_pairs={{32,0},{64,32},{96,64},{128,96},{160,128},{192,160},{224,192},{0,2... | collective-permute-start | bytes 1622024 | tf_op jit(solution)/shard_map/ppermute | solution.py:343
  106.0 8.6 %collective-permute-done.6.refs_2_.refs_12_ = bf16[64,4224]{1,0:T(8,128)(2,1)S(1)} collective-permute-done((bf16[64,4224]{1,0:T(8,128)(2,1)S(1)}, bf16[64,4224]{1,0:T(8,128)(2,1)S(1)}, u32[]{:S(2)}, u32[]{:S(2)}) %collective-permute-start.6) | collective-permute-done | bytes 540704 | tf_op jit(solution)/shard_map/ppermute | solution.py:343
  114.6 4.9 %collective-permute-start.7 = (bf16[64,4224]{1,0:T(8,128)(2,1)S(1)}, bf16[64,4224]{1,0:T(8,128)(2,1)S(1)}, u32[]{:S(2)}, u32[]{:S(2)}) collective-permute-start(bf16[64,4224]{1,0:T(8,128)(2,1)S(1)} %collective-permute-done.6.refs_2_.refs_12_), channel_id=1, source_target_pairs={{32,0},{64,32},{96,64},{128,96},{160,128},{192,160},{224,192},{0,2... | collective-permute-start | bytes 1622024 | tf_op jit(solution)/shard_map/ppermute | solution.py:343
  121.4 7.2 %collective-permute-done.7.refs_4_.refs_14_ = bf16[64,4224]{1,0:T(8,128)(2,1)S(1)} collective-permute-done((bf16[64,4224]{1,0:T(8,128)(2,1)S(1)}, bf16[64,4224]{1,0:T(8,128)(2,1)S(1)}, u32[]{:S(2)}, u32[]{:S(2)}) %collective-permute-start.7) | collective-permute-done | bytes 540704 | tf_op jit(solution)/shard_map/ppermute | solution.py:343
  128.6 5.3 %collective-permute-start.8 = (bf16[64,4224]{1,0:T(8,128)(2,1)S(1)}, bf16[64,4224]{1,0:T(8,128)(2,1)S(1)}, u32[]{:S(2)}, u32[]{:S(2)}) collective-permute-start(bf16[64,4224]{1,0:T(8,128)(2,1)S(1)} %collective-permute-done.7.refs_4_.refs_14_), channel_id=1, source_target_pairs={{32,0},{64,32},{96,64},{128,96},{160,128},{192,160},{224,192},{0,2... | collective-permute-start | bytes 1622024 | tf_op jit(solution)/shard_map/ppermute | solution.py:343
  135.9 6.4 %collective-permute-start.11 = (bf16[1536,256]{1,0:T(8,128)(2,1)}, bf16[1536,256]{1,0:T(8,128)(2,1)}, u32[]{:S(2)}, u32[]{:S(2)}) collective-permute-start(bf16[1536,256]{1,0:T(8,128)(2,1)} %bitcast.12.refs_0_), channel_id=1, source_target_pairs={{0,256},{256,0},{1,257},{257,1},{2,258},{258,2},{3,259},{259,3},{4... | collective-permute-start | bytes 2359304 | tf_op jit(solution)/shard_map/ppermute | solution.py:348
  145.1 4.6 %collective-permute-start.10 = (bf16[32,4224]{1,0:T(8,128)(2,1)}, bf16[32,4224]{1,0:T(8,128)(2,1)S(1)}, u32[]{:S(2)}, u32[]{:S(2)}) collective-permute-start(bf16[32,4224]{1,0:T(8,128)(2,1)} %slice.25), channel_id=1, source_target_pairs={{32,0},{64,32},{96,64},{128,96},{160,128},{192,160},{224,192},{0,2... | collective-permute-start | bytes 811016 | tf_op jit(solution)/shard_map/ppermute | solution.py:347
  153.0 5.9 %shard_map.131.refs_9_ = bf16[192,320]{1,0:T(8,128)(2,1)} custom-call(s32[1]{0:T(128)} %bitcast.20.zl_ref, bf16[64,4224]{1,0:T(8,128)(2,1)} %copy-done.1, bf16[64,4224]{1,0:T(8,128)(2,1)} %copy-done.6, bf16[64,4224]{1,0:T(8,128)(2,1)} %copy-done.5, bf16[64,4224]{1,0:T(8,128)(2,1)} %copy-done.8, bf16[64,4224]{1,0:T(8,128)(2,1)} %copy-done.7, ...), custom_call_target="tpu_custom_call" | custom-call | flops 1006632960 | bytes 5767168 | tf_op jit(solution)/shard_map/pallas_call | solution.py:160
  158.9 16.2 %collective-permute-done.12.refs_3_ = bf16[1536,256]{1,0:T(8,128)(2,1)} collective-permute-done((bf16[1536,256]{1,0:T(8,128)(2,1)}, bf16[1536,256]{1,0:T(8,128)(2,1)}, u32[]{:S(2)}, u32[]{:S(2)}) %collective-permute-start.12) | collective-permute-done | bytes 786464 | tf_op jit(solution)/shard_map/ppermute | solution.py:348
  175.8 6.7 %shard_map.132 = (bf16[8,192,256]{2,1,0:T(8,128)(2,1)}, bf16[512,128]{1,0:T(8,128)(2,1)}) custom-call(s32[2]{0:T(128)} %pad_add_fusion.refs_0_, bf16[64,4224]{1,0:T(8,128)(2,1)} %copy-done.3, bf16[64,4224]{1,0:T(8,128)(2,1)} %copy-done.2, bf16[32,4224]{1,0:T(8,128)(2,1)} %collective-permute-done.9.refs_3_.refs_17_, bf16[32,4224]{1,0:T(8,128)(2,1)} %copy-done.9, ...), custom_call_target="tpu_custom_call" | custom-call | flops 603979776 | bytes 4718592 | tf_op jit(solution)/shard_map/pallas_call | solution.py:180
  182.6 3.8 %all-to-all-start.6 = ((bf16[8,192,256]{2,1,0:T(8,128)(2,1)}), bf16[8,192,256]{2,1,0:T(8,128)(2,1)S(1)}, u32[]{:S(2)}, u32[]{:S(2)}) async-start(bf16[8,192,256]{2,1,0:T(8,128)(2,1)} %get-tuple-element.40), calls=%async_computation.6 | async-start | bytes 1572864 | tf_op jit(solution)/shard_map/all_to_all | solution.py:19
  186.4 20.3 %all-to-all-done.6.hidden_ref = bf16[8,192,256]{2,1,0:T(8,128)(2,1)S(1)} async-done(((bf16[8,192,256]{2,1,0:T(8,128)(2,1)}), bf16[8,192,256]{2,1,0:T(8,128)(2,1)S(1)}, u32[]{:S(2)}, u32[]{:S(2)}) %all-to-all-start.6) | async-done | bytes 786464 | tf_op jit(solution)/shard_map/all_to_all | solution.py:19
  207.6 5.4 %shard_map.133 = bf16[256,1152]{1,0:T(8,128)(2,1)} custom-call(s32[1]{0:T(128)} %bitcast.19.half_ref, bf16[8,192,256]{2,1,0:T(8,128)(2,1)} %copy-done.4, bf16[512,128]{1,0:T(8,128)(2,1)} %get-tuple-element.41.extra_ref, bf16[1536,256]{1,0:T(8,128)(2,1)} %bitcast.12.refs_0_, bf16[1536,256]{1,0:T(8,128)(2,1)} %collective-permute-done.2.refs_1_, ...), custom_call_target="tpu_custom_call" | custom-call | flops 805306368 | bytes 3145728 | tf_op jit(solution)/shard_map/pallas_call | solution.py:237
  213.0 27.2 %all_to_all.50 = bf16[32,8,1152]{2,1,0:T(8,128)(2,1)S(1)} all-to-all(bf16[32,8,1152]{2,1,0:T(8,128)(2,1)} %bitcast.52), channel_id=1, replica_groups=mesh['zl'=2,'y'=8,'x'=4,'zh'=4,'co'=2] {'x','zh','co'}, dimensions={0} | all-to-all | bytes 1179648 | tf_op jit(solution)/shard_map/all_to_all | solution.py:19
  241.1 3.3 %all-to-all-start.8 = ((bf16[8,4,1024]{2,1,0:T(4,128)(2,1)}), bf16[8,4,1024]{2,1,0:T(4,128)(2,1)S(1)}, u32[]{:S(2)}, u32[]{:S(2)}) async-start(bf16[8,4,1024]{2,1,0:T(4,128)(2,1)} %reshape.149), calls=%async_computation.8 | async-start | bytes 131072 | tf_op jit(solution)/shard_map/all_to_all | solution.py:19
  244.5 7.1 %all-to-all-done.8 = bf16[8,4,1024]{2,1,0:T(4,128)(2,1)S(1)} async-done(((bf16[8,4,1024]{2,1,0:T(4,128)(2,1)}), bf16[8,4,1024]{2,1,0:T(4,128)(2,1)S(1)}, u32[]{:S(2)}, u32[]{:S(2)}) %all-to-all-start.8) | async-done | bytes 65568 | tf_op jit(solution)/shard_map/all_to_all | solution.py:19
  (97 shorter events, 31.5 us)
Async XLA Ops:
  0.6 36.8 %copy-start = (bf16[256,4096]{1,0:T(8,128)(2,1)S(1)}, bf16[256,4096]{1,0:T(8,128)(2,1)}, u32[]{:S(2)}) copy-start(bf16[256,4096]{1,0:T(8,128)(2,1)} %param.16) | copy-start | bytes 6291460
  0.6 20.9 %copy-start.13 = (s32[256]{0:T(256)S(1)}, s32[256]{0:T(256)}, u32[]{:S(2)}) copy-start(s32[256]{0:T(256)} %constant.89.clone) | copy-start | bytes 3076
  2.5 23.3 %all-to-all-start = ((bf16[16,128,128]{2,1,0:T(8,128)(2,1)}), bf16[16,128,128]{2,1,0:T(8,128)(2,1)S(1)}, u32[]{:S(2)}, u32[]{:S(2)}) async-start(bf16[16,128,128]{2,1,0:T(8,128)(2,1)} %broadcast_in_dim.31), calls=%async_computation | async-start | bytes 1048576 | tf_op jit(solution)/shard_map/all_to_all | solution.py:19
  12.1 44.5 %collective-permute-start = (bf16[96,4096]{1,0:T(8,128)(2,1)}, bf16[96,4096]{1,0:T(8,128)(2,1)}, u32[]{:S(2)}, u32[]{:S(2)}) collective-permute-start(bf16[96,4096]{1,0:T(8,128)(2,1)} %bitcast.46), channel_id=1, source_target_pairs={{0,256},{256,0},{1,257},{257,1},{2,258},{258,2},{3,259},{259,3},{4... | collective-permute-start | bytes 2359304 | tf_op jit(solution)/shard_map/ppermute | solution.py:285
  15.3 41.2 %collective-permute-start.1 = (bf16[96,4096]{1,0:T(8,128)(2,1)}, bf16[96,4096]{1,0:T(8,128)(2,1)}, u32[]{:S(2)}, u32[]{:S(2)}) collective-permute-start(bf16[96,4096]{1,0:T(8,128)(2,1)} %bitcast.49), channel_id=1, source_target_pairs={{0,256},{256,0},{1,257},{257,1},{2,258},{258,2},{3,259},{259,3},{4... | collective-permute-start | bytes 2359304 | tf_op jit(solution)/shard_map/ppermute | solution.py:285
  34.5 22.1 %collective-permute-start.2 = (bf16[1536,256]{1,0:T(8,128)(2,1)}, bf16[1536,256]{1,0:T(8,128)(2,1)}, u32[]{:S(2)}, u32[]{:S(2)}) collective-permute-start(bf16[1536,256]{1,0:T(8,128)(2,1)} %bitcast.12.refs_0_), channel_id=1, source_target_pairs={{0,32},{32,0},{64,96},{96,64},{128,160},{160,128},{192,224},{224,1... | collective-permute-start | bytes 2359304 | tf_op jit(solution)/shard_map/ppermute | solution.py:319
  42.7 30.6 %copy-start.11 = (bf16[4,4096]{1,0:T(4,128)(2,1)S(1)}, bf16[4,4096]{1,0:T(4,128)(2,1)}, u32[]{:S(2)}) copy-start(bf16[4,4096]{1,0:T(4,128)(2,1)} %param.15) | copy-start | bytes 98308
  42.7 30.8 %copy-start.12 = (f32[4096]{0:T(1024)S(1)}, f32[4096]{0:T(1024)}, u32[]{:S(2)}) copy-start(f32[4096]{0:T(1024)} %param.17) | copy-start | bytes 49156
  73.5 26.9 %copy-start.10 = (bf16[4,4096]{1,0:T(4,128)(2,1)}, bf16[4,4096]{1,0:T(4,128)(2,1)S(1)}, u32[]{:S(2)}) copy-start(bf16[4,4096]{1,0:T(4,128)(2,1)S(1)} %get-tuple-element.45) | copy-start | bytes 98308
  100.4 52.6 %copy-start.1 = (bf16[64,4224]{1,0:T(8,128)(2,1)}, bf16[64,4224]{1,0:T(8,128)(2,1)S(1)}, u32[]{:S(2)}) copy-start(bf16[64,4224]{1,0:T(8,128)(2,1)S(1)} %reshape.146.refs_0_.refs_10_) | copy-start | bytes 1622020
  100.4 14.2 %collective-permute-start.6 = (bf16[64,4224]{1,0:T(8,128)(2,1)S(1)}, bf16[64,4224]{1,0:T(8,128)(2,1)S(1)}, u32[]{:S(2)}, u32[]{:S(2)}) collective-permute-start(bf16[64,4224]{1,0:T(8,128)(2,1)S(1)} %reshape.146.refs_0_.refs_10_), channel_id=1, source_target_pairs={{32,0},{64,32},{96,64},{128,96},{160,128},{192,160},{224,192},{0,2... | collective-permute-start | bytes 1622024 | tf_op jit(solution)/shard_map/ppermute | solution.py:343
  104.1 15.4 %collective-permute-start.3 = (bf16[64,4224]{1,0:T(8,128)(2,1)S(1)}, bf16[64,4224]{1,0:T(8,128)(2,1)S(1)}, u32[]{:S(2)}, u32[]{:S(2)}) collective-permute-start(bf16[64,4224]{1,0:T(8,128)(2,1)S(1)} %reshape.146.refs_0_.refs_10_), channel_id=1, source_target_pairs={{0,32},{32,64},{64,96},{96,128},{128,160},{160,192},{192,224},{224... | collective-permute-start | bytes 1622024 | tf_op jit(solution)/shard_map/ppermute | solution.py:343
  114.6 27.8 %copy-start.5 = (bf16[64,4224]{1,0:T(8,128)(2,1)}, bf16[64,4224]{1,0:T(8,128)(2,1)S(1)}, u32[]{:S(2)}) copy-start(bf16[64,4224]{1,0:T(8,128)(2,1)S(1)} %collective-permute-done.6.refs_2_.refs_12_) | copy-start | bytes 1622020
  114.6 14.1 %collective-permute-start.7 = (bf16[64,4224]{1,0:T(8,128)(2,1)S(1)}, bf16[64,4224]{1,0:T(8,128)(2,1)S(1)}, u32[]{:S(2)}, u32[]{:S(2)}) collective-permute-start(bf16[64,4224]{1,0:T(8,128)(2,1)S(1)} %collective-permute-done.6.refs_2_.refs_12_), channel_id=1, source_target_pairs={{32,0},{64,32},{96,64},{128,96},{160,128},{192,160},{224,192},{0,2... | collective-permute-start | bytes 1622024 | tf_op jit(solution)/shard_map/ppermute | solution.py:343
  119.5 24.8 %copy-start.6 = (bf16[64,4224]{1,0:T(8,128)(2,1)}, bf16[64,4224]{1,0:T(8,128)(2,1)S(1)}, u32[]{:S(2)}) copy-start(bf16[64,4224]{1,0:T(8,128)(2,1)S(1)} %collective-permute-done.3.refs_1_.refs_11_) | copy-start | bytes 1622020
  119.5 14.5 %collective-permute-start.4 = (bf16[64,4224]{1,0:T(8,128)(2,1)S(1)}, bf16[64,4224]{1,0:T(8,128)(2,1)S(1)}, u32[]{:S(2)}, u32[]{:S(2)}) collective-permute-start(bf16[64,4224]{1,0:T(8,128)(2,1)S(1)} %collective-permute-done.3.refs_1_.refs_11_), channel_id=1, source_target_pairs={{0,32},{32,64},{64,96},{96,128},{128,160},{160,192},{192,224},{224... | collective-permute-start | bytes 1622024 | tf_op jit(solution)/shard_map/ppermute | solution.py:343
  128.6 15.6 %collective-permute-start.8 = (bf16[64,4224]{1,0:T(8,128)(2,1)S(1)}, bf16[64,4224]{1,0:T(8,128)(2,1)S(1)}, u32[]{:S(2)}, u32[]{:S(2)}) collective-permute-start(bf16[64,4224]{1,0:T(8,128)(2,1)S(1)} %collective-permute-done.7.refs_4_.refs_14_), channel_id=1, source_target_pairs={{32,0},{64,32},{96,64},{128,96},{160,128},{192,160},{224,192},{0,2... | collective-permute-start | bytes 1622024 | tf_op jit(solution)/shard_map/ppermute | solution.py:343
  134.0 15.7 %collective-permute-start.5 = (bf16[64,4224]{1,0:T(8,128)(2,1)S(1)}, bf16[64,4224]{1,0:T(8,128)(2,1)S(1)}, u32[]{:S(2)}, u32[]{:S(2)}) collective-permute-start(bf16[64,4224]{1,0:T(8,128)(2,1)S(1)} %collective-permute-done.4.refs_3_.refs_13_), channel_id=1, source_target_pairs={{0,32},{32,64},{64,96},{96,128},{128,160},{160,192},{192,224},{224... | collective-permute-start | bytes 1622024 | tf_op jit(solution)/shard_map/ppermute | solution.py:343
  135.9 23.0 %collective-permute-start.11 = (bf16[1536,256]{1,0:T(8,128)(2,1)}, bf16[1536,256]{1,0:T(8,128)(2,1)}, u32[]{:S(2)}, u32[]{:S(2)}) collective-permute-start(bf16[1536,256]{1,0:T(8,128)(2,1)} %bitcast.12.refs_0_), channel_id=1, source_target_pairs={{0,256},{256,0},{1,257},{257,1},{2,258},{258,2},{3,259},{259,3},{4... | collective-permute-start | bytes 2359304 | tf_op jit(solution)/shard_map/ppermute | solution.py:348
  142.3 32.7 %collective-permute-start.12 = (bf16[1536,256]{1,0:T(8,128)(2,1)}, bf16[1536,256]{1,0:T(8,128)(2,1)}, u32[]{:S(2)}, u32[]{:S(2)}) collective-permute-start(bf16[1536,256]{1,0:T(8,128)(2,1)} %collective-permute-done.2.refs_1_), channel_id=1, source_target_pairs={{0,256},{256,0},{1,257},{257,1},{2,258},{258,2},{3,259},{259,3},{4... | collective-permute-start | bytes 2359304 | tf_op jit(solution)/shard_map/ppermute | solution.py:348
  145.1 30.0 %collective-permute-start.10 = (bf16[32,4224]{1,0:T(8,128)(2,1)}, bf16[32,4224]{1,0:T(8,128)(2,1)S(1)}, u32[]{:S(2)}, u32[]{:S(2)}) collective-permute-start(bf16[32,4224]{1,0:T(8,128)(2,1)} %slice.25), channel_id=1, source_target_pairs={{32,0},{64,32},{96,64},{128,96},{160,128},{192,160},{224,192},{0,2... | collective-permute-start | bytes 811016 | tf_op jit(solution)/shard_map/ppermute | solution.py:347
  150.4 24.7 %collective-permute-start.9 = (bf16[32,4224]{1,0:T(8,128)(2,1)}, bf16[32,4224]{1,0:T(8,128)(2,1)}, u32[]{:S(2)}, u32[]{:S(2)}) collective-permute-start(bf16[32,4224]{1,0:T(8,128)(2,1)} %slice.24), channel_id=1, source_target_pairs={{0,32},{32,64},{64,96},{96,128},{128,160},{160,192},{192,224},{224... | collective-permute-start | bytes 811016 | tf_op jit(solution)/shard_map/ppermute | solution.py:346
  182.6 24.1 %all-to-all-start.6 = ((bf16[8,192,256]{2,1,0:T(8,128)(2,1)}), bf16[8,192,256]{2,1,0:T(8,128)(2,1)S(1)}, u32[]{:S(2)}, u32[]{:S(2)}) async-start(bf16[8,192,256]{2,1,0:T(8,128)(2,1)} %get-tuple-element.40), calls=%async_computation.6 | async-start | bytes 1572864 | tf_op jit(solution)/shard_map/all_to_all | solution.py:19
  241.1 10.4 %all-to-all-start.8 = ((bf16[8,4,1024]{2,1,0:T(4,128)(2,1)}), bf16[8,4,1024]{2,1,0:T(4,128)(2,1)S(1)}, u32[]{:S(2)}, u32[]{:S(2)}) async-start(bf16[8,4,1024]{2,1,0:T(4,128)(2,1)} %reshape.149), calls=%async_computation.8 | async-start | bytes 131072 | tf_op jit(solution)/shard_map/all_to_all | solution.py:19
  (6 other events, 56.8 us)

commit v6 on v5

v6 whole, which is shorter than its diff:
```python
import jax
import jax.numpy as jnp
import numpy as np
from jax import lax
from jax.experimental import pallas as pl
from jax.experimental.pallas import tpu as pltpu
from jax.sharding import Mesh, PartitionSpec as P

HEAD_WIDTH = 128
EXTRA = 128

CTX = ("zl", "ya", "yb")
EXP = ("x", "zh", "co")
EPS_NORM = 1e-06
NEG_LARGE = -1e30


def exchange(pieces, axis):
    return lax.all_to_all(pieces, axis, 0, 0, tiled=True)


def spread(value, axis, count):
    return exchange(jnp.broadcast_to(value[None], (count,) + value.shape), axis)


def added(pieces):
    return jnp.sum(pieces.astype(jnp.float32), axis=0)


def rows_dot(left, right):
    return lax.dot_general(
        left, right, (((1,), (1,)), ((), ())), preferred_element_type=jnp.float32
    )


def route(expert_ids, expert_gates, expert_count, slots):
    flat_ids = expert_ids.reshape(-1)
    tok_rows, top_count = expert_ids.shape
    owner_row = jnp.arange(tok_rows * top_count, dtype=jnp.int32) // top_count
    earlier = (flat_ids[:, None] == flat_ids[None, :]) & (owner_row[None, :] < owner_row[:, None])
    slot_ids = jnp.sum(earlier.astype(jnp.int32), axis=1).reshape(tok_rows, top_count)
    expert_hit = (
        expert_ids[None, None] == jnp.arange(expert_count, dtype=jnp.int32)[:, None, None, None]
    )
    slot_hit = slot_ids[None, None] == jnp.arange(slots, dtype=jnp.int32)[None, :, None, None]
    hits = expert_hit & slot_hit
    table = jnp.any(hits, axis=3).astype(jnp.bfloat16)
    mix = jnp.sum(jnp.where(hits, expert_gates[None, None], 0.0), axis=3)
    return table.reshape(expert_count * slots, tok_rows), mix.reshape(
        expert_count * slots, tok_rows
    )


def whole(shape):
    return pl.BlockSpec(shape, lambda *_: (0,) * len(shape))


def weight_rows(place_ref, refs, weight):
    units = refs[0].shape[0]
    for at, ref in enumerate(refs):
        turn = (0, 2, 1, 3)[at % 4]
        start = (at // 4 * 4 + (place_ref[0] ^ turn)) * units
        weight[pl.ds(pl.multiple_of(start, 32), units), :] = ref[...]


def gated(total, units):
    gate, upper = total[: 4 * units, :], total[4 * units :, :]
    return (gate / (1.0 + jnp.exp(-gate)) * upper).astype(jnp.bfloat16)


def accumulate(weight, rows, block_refs, total):
    start = 0
    for block in block_refs:
        rows[pl.ds(start, block.shape[0]), :] = block[...]
        start += block.shape[0]

    @pl.when(pl.program_id(0) == 0)
    def _():
        total[...] = jnp.zeros_like(total)

    total[...] += rows_dot(weight[...], rows[...])


def first_kernel(place_ref, *refs):
    blocks, weights, (out_ref, weight, rows, total) = refs[:-12], refs[-12:-4], refs[-4:]
    weight_rows(place_ref, weights, weight)
    accumulate(weight, rows, blocks, total)

    @pl.when(pl.program_id(0) == pl.num_programs(0) - 1)
    def _():
        out_ref[...] = gated(total, weights[0].shape[0])


def last_kernel(count, place_ref, *refs):
    blocks, weights, first = refs[:count], refs[count : count + 8], refs[count + 8]
    extras, (out_ref, extra_ref, weight, rows, total, tags) = refs[count + 9 : -6], refs[-6:]
    weight_rows(place_ref, weights, weight)
    accumulate(weight, rows, blocks, total)

    @pl.when(pl.program_id(0) == pl.num_programs(0) - 1)
    def _():
        hidden = jnp.concatenate([first[...], gated(total, weights[0].shape[0])], axis=1)
        slots = hidden.shape[1]
        peers = out_ref.shape[0]
        each = slots // peers
        start = 0
        for extra in extras:
            tags[pl.ds(start, extra.shape[0]), :] = extra[...]
            start += extra.shape[0]
        held = lax.broadcasted_iota(jnp.int32, (slots, slots), 0)
        turn = held // each
        away = jnp.where(turn % 2 == 1, peers - (turn + 1) // 2, turn // 2)
        goal = (place_ref[1] + away) % peers * each + held % each
        column = lax.broadcasted_iota(jnp.int32, (slots, slots), 1)
        move = jnp.where(goal == column, 1.0, 0.0).astype(jnp.bfloat16)
        hidden = jnp.dot(hidden, move, preferred_element_type=jnp.float32).astype(jnp.bfloat16)
        for peer in range(peers):
            out_ref[peer] = hidden
        extra_ref[...] = lax.dot_general(
            move, tags[...], (((0,), (0,)), ((), ())), preferred_element_type=jnp.float32
        ).astype(jnp.bfloat16)


def row_specs(blocks, weights, step):
    return [pl.BlockSpec((b.shape[0], step), lambda k, *_: (0, k)) for b in blocks] + [
        pl.BlockSpec((w.shape[0], step), lambda k, *_: (0, k)) for w in weights
    ]


def held_scratch(units, count, step):
    return [
        pltpu.VMEM((8 * units, step), jnp.bfloat16),
        pltpu.VMEM((count, step), jnp.bfloat16),
        pltpu.VMEM((8 * units, count), jnp.float32),
    ]


def cost(units, count, width):
    return pl.CostEstimate(
        flops=16 * units * count * width,
        bytes_accessed=2 * (count + 8 * units) * width,
        transcendentals=0,
    )


def first_hidden(place, blocks, weights, width):
    units, step = weights[0].shape[0], 1024
    count = sum(b.shape[0] for b in blocks)
    return pl.pallas_call(
        first_kernel,
        out_shape=jax.ShapeDtypeStruct((4 * units, count), jnp.bfloat16),
        grid_spec=pltpu.PrefetchScalarGridSpec(
            num_scalar_prefetch=1,
            grid=(width // step,),
            in_specs=row_specs(blocks, weights, step),
            out_specs=whole((4 * units, count)),
            scratch_shapes=held_scratch(units, count, step),
        ),
        compiler_params=pltpu.CompilerParams(vmem_limit_bytes=60 * 2**20),
        cost_estimate=cost(units, count, width),
    )(place, *blocks, *weights)


def last_hidden(place, blocks, weights, first, every, width, peers):
    units, step = weights[0].shape[0], 1024
    count = sum(b.shape[0] for b in blocks)
    slots = sum(b.shape[0] for b in every)
    pieces = (peers, 4 * units, slots)
    return pl.pallas_call(
        lambda *refs: last_kernel(len(blocks), *refs),
        out_shape=(
            jax.ShapeDtypeStruct(pieces, jnp.bfloat16),
            jax.ShapeDtypeStruct((slots, EXTRA), jnp.bfloat16),
        ),
        grid_spec=pltpu.PrefetchScalarGridSpec(
            num_scalar_prefetch=1,
            grid=(width // step,),
            in_specs=row_specs(blocks, weights, step)
            + [whole(first.shape)]
            + [
                pl.BlockSpec((b.shape[0], EXTRA), lambda k, *_: (0, width // EXTRA))
                for b in every
            ],
            out_specs=(whole(pieces), whole((slots, EXTRA))),
            scratch_shapes=held_scratch(units, count, step)
            + [pltpu.VMEM((slots, EXTRA), jnp.bfloat16)],
        ),
        compiler_params=pltpu.CompilerParams(vmem_limit_bytes=60 * 2**20),
        cost_estimate=cost(units, count, width),
    )(place, *blocks, *weights, first, *every)


def down_kernel(hidden_ref, extra_ref, *refs):
    weights, out_ref, stacked, held, arrived = refs[:4], refs[4], refs[5], refs[6], refs[7]
    copies = [
        pltpu.make_async_copy(weight, held.at[i], arrived.at[i]) for i, weight in enumerate(weights)
    ]
    for copy in copies:
        copy.start()
    peers, units, count = hidden_ref.shape
    half = units // 2
    for peer in range(peers):
        for z in range(2):
            rows = pl.ds((z * peers + peer) * half, half)
            stacked[rows, :] = hidden_ref[peer, z * half : (z + 1) * half, :]
    each = count // peers
    to = lax.broadcasted_iota(jnp.int32, (count, count), 0)
    source = (to % (2 * peers)) // 2 * each + to // (2 * peers) * 2 + to % 2
    column = lax.broadcasted_iota(jnp.int32, (count, count), 1)
    move = jnp.where(source == column, 1.0, 0.0).astype(jnp.bfloat16)
    rows = rows_dot(move, stacked[...]).astype(jnp.bfloat16)
    cols = held.shape[2]
    extra = jnp.dot(move, extra_ref[...], preferred_element_type=jnp.float32)
    out_ref[:, 4 * cols :] = extra.astype(jnp.bfloat16)
    for i, copy in enumerate(copies):
        copy.wait()
        result = jnp.dot(rows, held[i], preferred_element_type=jnp.float32)
        out_ref[:, i * cols : (i + 1) * cols] = result.astype(jnp.bfloat16)


def down_slots(hidden, extra, weights):
    peers, units, count = hidden.shape
    deep, cols = weights[0].shape
    out = (count, 4 * cols + EXTRA)
    return pl.pallas_call(
        down_kernel,
        out_shape=jax.ShapeDtypeStruct(out, jnp.bfloat16),
        grid=(1,),
        in_specs=[whole(hidden.shape), whole(extra.shape)]
        + [pl.BlockSpec(memory_space=pl.ANY)] * 4,
        out_specs=whole(out),
        scratch_shapes=[
            pltpu.VMEM((deep, count), jnp.bfloat16),
            pltpu.VMEM((4, deep, cols), jnp.bfloat16),
            pltpu.SemaphoreType.DMA((4,)),
        ],
        compiler_params=pltpu.CompilerParams(vmem_limit_bytes=60 * 2**20),
        cost_estimate=pl.CostEstimate(
            flops=8 * deep * count * cols, bytes_accessed=8 * deep * cols, transcendentals=0
        ),
    )(hidden, extra, *weights)


def on_device(
    queries,
    keys,
    values,
    residual,
    out_weight,
    norm_gain,
    expert_ids,
    expert_gates,
    w_gate,
    w_up,
    w_down,
):
    n_zl, n_ya, n_yb = lax.axis_size("zl"), lax.axis_size("ya"), lax.axis_size("yb")
    n_x, n_zh, n_co = lax.axis_size("x"), lax.axis_size("zh"), lax.axis_size("co")
    zl, ya, yb, x_pos, co = (lax.axis_index(a) for a in ("zl", "ya", "yb", "x", "co"))
    ctx_count, expert_count = n_zl * n_ya * n_yb, n_x * n_zh * n_co
    width = residual.shape[1]
    tok_dev, top_count = expert_ids.shape
    slots = 2
    tok_block = queries.shape[0]
    heads = queries.shape[1] // HEAD_WIDTH
    swap = [(0, 1), (1, 0)]
    gate_own, up_own, down_own = w_gate[0].T, w_up[0].T, w_down[0]

    gate_z, up_z = lax.ppermute(gate_own, "zl", swap), lax.ppermute(up_own, "zl", swap)
    gate_y, up_y = lax.ppermute(gate_own, "yb", swap), lax.ppermute(up_own, "yb", swap)

    mine = jnp.where(co == 0, keys, values)
    mine = lax.dynamic_slice_in_dim(mine, x_pos * HEAD_WIDTH, HEAD_WIDTH, 1)
    gathered = spread(mine, CTX, ctx_count).reshape(ctx_count * tok_block, HEAD_WIDTH)

    table, mix = route(expert_ids, expert_gates, expert_count, slots)
    places = n_ya * tok_dev
    own_place = jnp.arange(places, dtype=jnp.int32) // tok_dev == ya
    mix = jnp.where(own_place[None, :], jnp.tile(mix, (1, n_ya)), 0.0)
    mix_high = mix.astype(jnp.bfloat16)
    mix_low = (mix - mix_high.astype(jnp.float32)).astype(jnp.bfloat16)
    extra = jnp.concatenate([mix_high, mix_low], axis=1)
    extra = jnp.pad(extra, ((0, 0), (0, EXTRA - extra.shape[1])))
    key_all, value_all = spread(gathered, "co", n_co)

    order = np.arange(tok_block).reshape(n_x, n_zh, n_co, tok_dev).transpose(2, 0, 1, 3)
    split = queries.reshape(n_x, n_zh, n_co, tok_dev, heads, HEAD_WIDTH)
    query_rows = jnp.transpose(split, (4, 2, 0, 1, 3, 5)).reshape(heads * tok_block, HEAD_WIDTH)
    query_pos = ((zl * n_ya + ya) * n_yb + yb) * tok_block + jnp.asarray(
        np.tile(order.reshape(-1), heads), jnp.int32
    )
    key_pos = jnp.arange(key_all.shape[0], dtype=jnp.int32)
    allowed = key_pos[None, :] <= query_pos[:, None]
    scores = rows_dot(query_rows, key_all) * (1.0 / HEAD_WIDTH**0.5)
    scores = jnp.where(allowed, scores, NEG_LARGE)
    weights = jnp.exp(scores - jnp.max(scores, axis=1, keepdims=True))
    total = jnp.sum(weights, axis=1, keepdims=True)
    numer = jnp.dot(weights.astype(jnp.bfloat16), value_all, preferred_element_type=jnp.float32)
    done = (numer / total).astype(jnp.bfloat16).reshape(heads, tok_block, HEAD_WIDTH)
    heads_out = jnp.transpose(done, (1, 0, 2)).reshape(tok_block, heads * HEAD_WIDTH)

    heads_out, down_own = lax.optimization_barrier((heads_out, down_own))
    down_y = lax.ppermute(down_own, "yb", swap)

    partial = jnp.dot(heads_out, out_weight, preferred_element_type=jnp.float32)
    partial = partial.astype(jnp.bfloat16).reshape(n_co, tok_block // n_co, width)
    partial = added(exchange(partial, "co")).astype(jnp.bfloat16)
    partial, gate_z, up_z = lax.optimization_barrier((partial, gate_z, up_z))
    gate_zy = lax.ppermute(gate_z, "yb", swap)
    partial = added(exchange(partial.reshape(n_x, -1, width), "x")).astype(jnp.bfloat16)
    partial, gate_y, up_y, down_y = lax.optimization_barrier((partial, gate_y, up_y, down_y))
    projected = added(exchange(partial.reshape(n_zh, tok_dev, width), "zh"))
    mixed = (residual.astype(jnp.float32) + projected).astype(jnp.bfloat16)

    stream = mixed.astype(jnp.float32)
    mean_sq = jnp.mean(stream * stream, axis=1, keepdims=True)
    normed = (stream * lax.rsqrt(mean_sq + EPS_NORM) * norm_gain[None, :]).astype(jnp.bfloat16)

    normed, gate_zy, up_z = lax.optimization_barrier((normed, gate_zy, up_z))
    up_zy = lax.ppermute(up_z, "yb", swap)
    outgoing = jnp.dot(table, normed, preferred_element_type=jnp.float32).astype(jnp.bfloat16)
    outgoing = jnp.concatenate([outgoing, extra], axis=1)
    arrived = exchange(outgoing.reshape(expert_count, slots, width + EXTRA), EXP)
    arrived = arrived.reshape(expert_count * slots, width + EXTRA)

    arrived, down_own, up_zy = lax.optimization_barrier((arrived, down_own, up_zy))
    after = [(i, (i + 1) % n_ya) for i in range(n_ya)]
    before = [(b, a) for a, b in after]
    left, right = lax.ppermute(arrived, "ya", after), lax.ppermute(arrived, "ya", before)
    down_z = lax.ppermute(down_own, "zl", swap)
    left, right, down_z, down_y = lax.optimization_barrier((left, right, down_z, down_y))
    part = arrived.shape[0] // 2
    last = [lax.ppermute(left[:part], "ya", after), lax.ppermute(right[part:], "ya", before)]
    down_zy = lax.ppermute(down_y, "zl", swap)
    weights = (gate_own, gate_z, gate_y, gate_zy, up_own, up_z, up_y, up_zy)
    blocks = [arrived, left, right]
    place = jnp.stack([zl * 2 + yb, ya])
    first = first_hidden(place, blocks, weights, width)
    last, first, down_zy = lax.optimization_barrier((last, first, down_zy))

    hidden, extra = last_hidden(place, last, weights, first, blocks + last, width, n_ya)
    hidden = exchange(hidden, "ya")

    result = down_slots(hidden, extra, (down_own, down_y, down_z, down_zy))
    cols = result.shape[1] - EXTRA
    result = exchange(result.reshape(expert_count, -1, cols + EXTRA), EXP)
    result = result.reshape(-1, cols + EXTRA)
    tokens = lax.dot_general(
        result[:, cols : cols + 2 * places],
        result[:, :cols],
        (((0,), (0,)), ((), ())),
        preferred_element_type=jnp.float32,
    )
    tokens = (tokens[:places] + tokens[places:]).astype(jnp.bfloat16)
    tokens = exchange(tokens.reshape(n_ya, tok_dev, cols), "ya")
    tokens = tokens.reshape(n_ya, tok_dev, n_zl, n_yb, cols // 4)
    tokens = jnp.where(zl == 0, tokens, tokens[:, :, ::-1])
    tokens = jnp.where(yb == 0, tokens, tokens[:, :, :, ::-1])
    tokens = tokens.transpose(1, 2, 0, 3, 4)
    return (mixed, tokens.reshape(tok_dev, width))


def solution(mesh):
    fine = Mesh(mesh.devices.reshape(2, 4, 2, 4, 4, 2), CTX + EXP)
    return jax.shard_map(
        on_device,
        mesh=fine,
        in_specs=(
            P(CTX, EXP),
            P(CTX, None),
            P(CTX, None),
            P(CTX + EXP, None),
            P(EXP, None),
            P(),
            P(CTX + EXP, None),
            P(CTX + EXP, None),
            P(EXP, None, CTX),
            P(EXP, None, CTX),
            P(EXP, None, CTX),
        ),
        out_specs=(P(CTX + EXP, None), P(CTX + EXP, None)),
        check_vma=False,
    )
```

time: 255 us -> 285 us (1.12)
  waiting for transfers between devices: 63.7 us -> 101 us
  blocking collectives: 93.4 us -> 69.1 us
  starting transfers between devices: 59.3 us -> 75.3 us
    all_to_all x3 -> x5, waiting for transfers between devices: 31.7 us -> 62.1 us  [exchange(): return lax.all_to_all(pieces, axis, 0, 0, tiled=True)]
    all_to_all x6 -> x4, blocking collectives: 93.4 us -> 69.1 us  [exchange(): return lax.all_to_all(pieces, axis, 0, 0, tiled=True)]
    all_to_all x3 -> x5, starting transfers between devices: 16.7 us -> 37.3 us  [exchange(): return lax.all_to_all(pieces, axis, 0, 0, tiled=True)]
    ppermute x13, waiting for transfers between devices: 32 us -> 38.8 us  [the longest x1 21.9 us: on_device(): lax.ppermute(arrived, 'ya', before)]
    ppermute x13, starting transfers between devices: 42.6 us -> 38.1 us  [the longest x1 4.17 us: on_device(): lax.ppermute(gate_own, 'yb', swap)]
  transfers between devices with their start and end apart: 16 -> 18, of which waited for: 6 -> 9; matrix products, arithmetic and copies ran while one was open for 4% -> 4% of each run, Pallas kernels for 2% -> 2%
where the time goes in v6:
time: 285 us; the launch traced here: 283 us
  waiting for transfers between devices  101 us (35%)
  starting transfers between devices  75.3 us (26%)
  blocking collectives  69.1 us (24%)
  Pallas kernels  19.7 us (7%)
  local copies, waits for them, and re-layouts  8.34 us (3%)
  other arithmetic  6.1 us (2%)
    all_to_all x4, blocking collectives, exchange(): return lax.all_to_all(pieces, axis, 0, 0, tiled=True)  69.1 us
    all_to_all x5, waiting for transfers between devices, exchange(): return lax.all_to_all(pieces, axis, 0, 0, tiled=True)  62.1 us
    all_to_all x5, starting transfers between devices, exchange(): return lax.all_to_all(pieces, axis, 0, 0, tiled=True)  37.3 us
    ppermute x1, waiting for transfers between devices, on_device(): lax.ppermute(arrived, 'ya', before)  21.9 us
    ppermute x1, waiting for transfers between devices, on_device(): gate_zy = lax.ppermute(gate_z, 'yb', swap)  12.3 us
    pallas_call x1, Pallas kernels, last_hidden(): pl.pallas_call(lambda *refs: last_kernel(len(blocks), *refs), out_shape=(...  7.28 us
    pallas_call x1, Pallas kernels, first_hidden(): pl.pallas_call(first_kernel, out_shape=jax.ShapeDtypeStruct((4 * units, c...  7.02 us
  transfers between devices with their start and end apart: 18, of which 9 were waited for; matrix products, arithmetic and copies ran while one was open for 4% of the time, Pallas kernels for 2%

profile of v6, /device:TPU:1, one launch (start us, length us, event | category | flops | bytes accessed | tf_op | source)
XLA Modules:
  0.0 282.6 jit_solution(5179235109646091059)
XLA Ops:
  0.6 4.2 %collective-permute-start.2 = (bf16[96,4096]{1,0:T(8,128)(2,1)}, bf16[96,4096]{1,0:T(8,128)(2,1)}, u32[]{:S(2)}, u32[]{:S(2)}) collective-permute-start(bf16[96,4096]{1,0:T(8,128)(2,1)} %bitcast.45), channel_id=1, source_target_pairs={{0,32},{32,0},{1,33},{33,1},{2,34},{34,2},{3,35},{35,3},{4,36},{36... | collective-permute-start | bytes 2359304 | tf_op jit(solution)/shard_map/ppermute | solution.py:270
  4.8 4.0 %collective-permute-start = (bf16[96,4096]{1,0:T(8,128)(2,1)}, bf16[96,4096]{1,0:T(8,128)(2,1)}, u32[]{:S(2)}, u32[]{:S(2)}) collective-permute-start(bf16[96,4096]{1,0:T(8,128)(2,1)} %bitcast.46), channel_id=1, source_target_pairs={{0,256},{256,0},{1,257},{257,1},{2,258},{258,2},{3,259},{259,3},{4... | collective-permute-start | bytes 2359304 | tf_op jit(solution)/shard_map/ppermute | solution.py:269
  14.6 8.1 %all-to-all-start = ((bf16[16,128,128]{2,1,0:T(8,128)(2,1)}), bf16[16,128,128]{2,1,0:T(8,128)(2,1)S(1)}, u32[]{:S(2)}, u32[]{:S(2)}) async-start(bf16[16,128,128]{2,1,0:T(8,128)(2,1)} %broadcast_in_dim.34), calls=%async_computation | async-start | bytes 1048576 | tf_op jit(solution)/shard_map/all_to_all | solution.py:19
  26.8 27.0 %all-to-all-done = bf16[16,128,128]{2,1,0:T(8,128)(2,1)S(1)} async-done(((bf16[16,128,128]{2,1,0:T(8,128)(2,1)}), bf16[16,128,128]{2,1,0:T(8,128)(2,1)S(1)}, u32[]{:S(2)}, u32[]{:S(2)}) %all-to-all-start) | async-done | bytes 524320 | tf_op jit(solution)/shard_map/all_to_all | solution.py:19
  53.9 6.5 %all_to_all.45 = bf16[2,2048,128]{2,1,0:T(8,128)(2,1)S(1)} all-to-all(bf16[2,2048,128]{2,1,0:T(8,128)(2,1)S(1)} %broadcast_in_dim.36), channel_id=1, replica_groups=mesh['zl'=2,'ya'=4,'yb'=2,'x'=4,'zh'=4,'co'=2] {'co'}, dimensions={0} | all-to-all | bytes 2097152 | tf_op jit(solution)/shard_map/all_to_all | solution.py:19
  64.5 4.6 %all_to_all.46 = bf16[2,64,4096]{2,1,0:T(8,128)(2,1)S(1)} all-to-all(bf16[2,64,4096]{2,1,0:T(8,128)(2,1)S(1)} %bitcast.44), channel_id=1, replica_groups=mesh['zl'=2,'ya'=4,'yb'=2,'x'=4,'zh'=4,'co'=2] {'co'}, dimensions={0} | all-to-all | bytes 2097152 | tf_op jit(solution)/shard_map/all_to_all | solution.py:19
  70.3 4.0 %all-to-all-start.3 = ((bf16[4,16,4096]{2,1,0:T(8,128)(2,1)}), bf16[4,16,4096]{2,1,0:T(8,128)(2,1)S(1)}, u32[]{:S(2)}, u32[]{:S(2)}) async-start(bf16[4,16,4096]{2,1,0:T(8,128)(2,1)} %bitcast.56), calls=%async_computation.3 | async-start | bytes 1048576 | tf_op jit(solution)/shard_map/all_to_all | solution.py:19
  74.4 8.8 %all-to-all-done.3 = bf16[4,16,4096]{2,1,0:T(8,128)(2,1)S(1)} async-done(((bf16[4,16,4096]{2,1,0:T(8,128)(2,1)}), bf16[4,16,4096]{2,1,0:T(8,128)(2,1)S(1)}, u32[]{:S(2)}, u32[]{:S(2)}) %all-to-all-start.3) | async-done | bytes 524320 | tf_op jit(solution)/shard_map/all_to_all | solution.py:19
  84.0 9.1 %all-to-all-start.4 = ((bf16[4,4,4096]{2,1,0:T(4,128)(2,1)}), bf16[4,4,4096]{2,1,0:T(4,128)(2,1)S(1)}, u32[]{:S(2)}, u32[]{:S(2)}) async-start(bf16[4,4,4096]{2,1,0:T(4,128)(2,1)} %reshape.132), calls=%async_computation.4 | async-start | bytes 262144 | tf_op jit(solution)/shard_map/all_to_all | solution.py:19
  93.6 3.6 %collective-permute-start.5 = (bf16[96,4096]{1,0:T(8,128)(2,1)}, bf16[96,4096]{1,0:T(8,128)(2,1)S(1)}, u32[]{:S(2)}, u32[]{:S(2)}) collective-permute-start(bf16[96,4096]{1,0:T(8,128)(2,1)} %collective-permute-done.refs_4_), channel_id=1, source_target_pairs={{0,32},{32,0},{1,33},{33,1},{2,34},{34,2},{3,35},{35,3},{4,36},{36... | collective-permute-start | bytes 2359304 | tf_op jit(solution)/shard_map/ppermute | solution.py:309
  97.2 3.5 %all-to-all-done.4 = bf16[4,4,4096]{2,1,0:T(4,128)(2,1)S(1)} async-done(((bf16[4,4,4096]{2,1,0:T(4,128)(2,1)}), bf16[4,4,4096]{2,1,0:T(4,128)(2,1)S(1)}, u32[]{:S(2)}, u32[]{:S(2)}) %all-to-all-start.4) | async-done | bytes 131104 | tf_op jit(solution)/shard_map/all_to_all | solution.py:19
  101.1 12.3 %collective-permute-done.5.refs_6_ = bf16[96,4096]{1,0:T(8,128)(2,1)S(1)} collective-permute-done((bf16[96,4096]{1,0:T(8,128)(2,1)}, bf16[96,4096]{1,0:T(8,128)(2,1)S(1)}, u32[]{:S(2)}, u32[]{:S(2)}) %collective-permute-start.5) | collective-permute-done | bytes 786464 | tf_op jit(solution)/shard_map/ppermute | solution.py:309
  114.9 11.3 %all-to-all-start.5 = ((bf16[32,2,4224]{2,1,0:T(2,128)(2,1)}), bf16[32,2,4224]{2,1,0:T(2,128)(2,1)S(1)}, u32[]{:S(2)}, u32[]{:S(2)}) async-start(bf16[32,2,4224]{2,1,0:T(2,128)(2,1)} %reshape.134), calls=%async_computation.5 | async-start | bytes 1081344 | tf_op jit(solution)/shard_map/all_to_all | solution.py:19
  128.4 16.1 %all-to-all-done.5 = bf16[32,2,4224]{2,1,0:T(2,128)(2,1)S(1)} async-done(((bf16[32,2,4224]{2,1,0:T(2,128)(2,1)}), bf16[32,2,4224]{2,1,0:T(2,128)(2,1)S(1)}, u32[]{:S(2)}, u32[]{:S(2)}) %all-to-all-start.5) | async-done | bytes 540704 | tf_op jit(solution)/shard_map/all_to_all | solution.py:19
  149.5 3.7 %collective-permute-start.8 = (bf16[64,4224]{1,0:T(8,128)(2,1)S(1)}, bf16[64,4224]{1,0:T(8,128)(2,1)S(1)}, u32[]{:S(2)}, u32[]{:S(2)}) collective-permute-start(bf16[64,4224]{1,0:T(8,128)(2,1)S(1)} %reshape.135.refs_0_.refs_12_), channel_id=1, source_target_pairs={{64,0},{128,64},{192,128},{0,192},{65,1},{129,65},{193,129},{1,193... | collective-permute-start | bytes 1622024 | tf_op jit(solution)/shard_map/ppermute | solution.py:329
  155.7 21.9 %collective-permute-done.8.refs_2_.refs_14_ = bf16[64,4224]{1,0:T(8,128)(2,1)S(1)} collective-permute-done((bf16[64,4224]{1,0:T(8,128)(2,1)S(1)}, bf16[64,4224]{1,0:T(8,128)(2,1)S(1)}, u32[]{:S(2)}, u32[]{:S(2)}) %collective-permute-start.8) | collective-permute-done | bytes 540704 | tf_op jit(solution)/shard_map/ppermute | solution.py:329
  177.7 3.6 %collective-permute-start.12 = (bf16[1536,256]{1,0:T(8,128)(2,1)}, bf16[1536,256]{1,0:T(8,128)(2,1)}, u32[]{:S(2)}, u32[]{:S(2)}) collective-permute-start(bf16[1536,256]{1,0:T(8,128)(2,1)} %collective-permute-done.4.refs_1_), channel_id=1, source_target_pairs={{0,256},{256,0},{1,257},{257,1},{2,258},{258,2},{3,259},{259,3},{4... | collective-permute-start | bytes 2359304 | tf_op jit(solution)/shard_map/ppermute | solution.py:334
  189.6 7.0 %shard_map.131.refs_11_ = bf16[384,192]{1,0:T(8,128)(2,1)} custom-call(s32[2]{0:T(128)} %pad_add_fusion.place_ref.refs_0_, bf16[64,4224]{1,0:T(8,128)(2,1)} %copy-done.1, bf16[64,4224]{1,0:T(8,128)(2,1)} %copy-done.3, bf16[64,4224]{1,0:T(8,128)(2,1)} %copy-done.2, bf16[96,4096]{1,0:T(8,128)(2,1)} %bitcast.47, bf16[96,4096]{1,0:T(8,128)(2,1)} %collective-permute-done.refs_4_, ...), custom_call_target="tpu_custom_call" | custom-call | flops 1207959552 | bytes 7864320 | tf_op jit(solution)/shard_map/pallas_call | solution.py:149
  198.5 7.3 %shard_map.132 = (bf16[4,384,256]{2,1,0:T(8,128)(2,1)}, bf16[256,128]{1,0:T(8,128)(2,1)}) custom-call(s32[2]{0:T(128)} %pad_add_fusion.place_ref.refs_0_, bf16[32,4224]{1,0:T(8,128)(2,1)} %collective-permute-done.10.refs_1_.refs_15_, bf16[32,4224]{1,0:T(8,128)(2,1)} %copy-done.5, bf16[96,4096]{1,0:T(8,128)(2,1)} %bitcast.48, ...), custom_call_target="tpu_custom_call" | custom-call | flops 402653184 | bytes 6815744 | tf_op jit(solution)/shard_map/pallas_call | solution.py:169
  205.8 20.7 %all_to_all.47.hidden_ref = bf16[4,384,256]{2,1,0:T(8,128)(2,1)} all-to-all(bf16[4,384,256]{2,1,0:T(8,128)(2,1)} %get-tuple-element.48), channel_id=1, replica_groups=mesh['zl'=2,'ya'=4,'yb'=2,'x'=4,'zh'=4,'co'=2] {'ya'}, dimensions={0} | all-to-all | bytes 1572864 | tf_op jit(solution)/shard_map/all_to_all | solution.py:19
  226.5 5.4 %shard_map.133 = bf16[256,1152]{1,0:T(8,128)(2,1)} custom-call(bf16[4,384,256]{2,1,0:T(8,128)(2,1)} %all_to_all.47.hidden_ref, bf16[256,128]{1,0:T(8,128)(2,1)} %get-tuple-element.49.extra_ref, bf16[1536,256]{1,0:T(8,128)(2,1)} %bitcast.9.refs_0_, bf16[1536,256]{1,0:T(8,128)(2,1)} %collective-permute-done.4.refs_1_, ...), custom_call_target="tpu_custom_call" | custom-call | flops 805306368 | bytes 3145728 | tf_op jit(solution)/shard_map/pallas_call | solution.py:225
  231.9 37.3 %all_to_all.48 = bf16[32,8,1152]{2,1,0:T(8,128)(2,1)S(1)} all-to-all(bf16[32,8,1152]{2,1,0:T(8,128)(2,1)} %bitcast.53), channel_id=1, replica_groups=mesh['zl'=2,'ya'=4,'yb'=2,'x'=4,'zh'=4,'co'=2] {'x','zh','co'}, dimensions={0} | all-to-all | bytes 1179648 | tf_op jit(solution)/shard_map/all_to_all | solution.py:19
  270.1 4.7 %all-to-all-start.8 = ((bf16[4,4,1024]{2,1,0:T(4,128)(2,1)}), bf16[4,4,1024]{2,1,0:T(4,128)(2,1)S(1)}, u32[]{:S(2)}, u32[]{:S(2)}) async-start(bf16[4,4,1024]{2,1,0:T(4,128)(2,1)} %reshape.138), calls=%async_computation.8 | async-start | bytes 65536 | tf_op jit(solution)/shard_map/all_to_all | solution.py:19
  274.8 6.7 %all-to-all-done.8 = bf16[4,4,1024]{2,1,0:T(4,128)(2,1)S(1)} async-done(((bf16[4,4,1024]{2,1,0:T(4,128)(2,1)}), bf16[4,4,1024]{2,1,0:T(4,128)(2,1)S(1)}, u32[]{:S(2)}, u32[]{:S(2)}) %all-to-all-start.8) | async-done | bytes 32800 | tf_op jit(solution)/shard_map/all_to_all | solution.py:19
  (89 shorter events, 40.0 us)
Async XLA Ops:
  0.6 63.4 %copy-start = (bf16[256,4096]{1,0:T(8,128)(2,1)S(1)}, bf16[256,4096]{1,0:T(8,128)(2,1)}, u32[]{:S(2)}) copy-start(bf16[256,4096]{1,0:T(8,128)(2,1)} %param.16) | copy-start | bytes 6291460
  0.6 82.6 %collective-permute-start.2 = (bf16[96,4096]{1,0:T(8,128)(2,1)}, bf16[96,4096]{1,0:T(8,128)(2,1)}, u32[]{:S(2)}, u32[]{:S(2)}) collective-permute-start(bf16[96,4096]{1,0:T(8,128)(2,1)} %bitcast.45), channel_id=1, source_target_pairs={{0,32},{32,0},{1,33},{33,1},{2,34},{34,2},{3,35},{35,3},{4,36},{36... | collective-permute-start | bytes 2359304 | tf_op jit(solution)/shard_map/ppermute | solution.py:270
  4.8 65.4 %collective-permute-start = (bf16[96,4096]{1,0:T(8,128)(2,1)}, bf16[96,4096]{1,0:T(8,128)(2,1)}, u32[]{:S(2)}, u32[]{:S(2)}) collective-permute-start(bf16[96,4096]{1,0:T(8,128)(2,1)} %bitcast.46), channel_id=1, source_target_pairs={{0,256},{256,0},{1,257},{257,1},{2,258},{258,2},{3,259},{259,3},{4... | collective-permute-start | bytes 2359304 | tf_op jit(solution)/shard_map/ppermute | solution.py:269
  8.8 74.5 %collective-permute-start.3 = (bf16[96,4096]{1,0:T(8,128)(2,1)}, bf16[96,4096]{1,0:T(8,128)(2,1)}, u32[]{:S(2)}, u32[]{:S(2)}) collective-permute-start(bf16[96,4096]{1,0:T(8,128)(2,1)} %bitcast.49), channel_id=1, source_target_pairs={{0,32},{32,0},{1,33},{33,1},{2,34},{34,2},{3,35},{35,3},{4,36},{36... | collective-permute-start | bytes 2359304 | tf_op jit(solution)/shard_map/ppermute | solution.py:270
  10.9 59.3 %collective-permute-start.1 = (bf16[96,4096]{1,0:T(8,128)(2,1)}, bf16[96,4096]{1,0:T(8,128)(2,1)}, u32[]{:S(2)}, u32[]{:S(2)}) collective-permute-start(bf16[96,4096]{1,0:T(8,128)(2,1)} %bitcast.50), channel_id=1, source_target_pairs={{0,256},{256,0},{1,257},{257,1},{2,258},{258,2},{3,259},{259,3},{4... | collective-permute-start | bytes 2359304 | tf_op jit(solution)/shard_map/ppermute | solution.py:269
  14.6 39.3 %all-to-all-start = ((bf16[16,128,128]{2,1,0:T(8,128)(2,1)}), bf16[16,128,128]{2,1,0:T(8,128)(2,1)S(1)}, u32[]{:S(2)}, u32[]{:S(2)}) async-start(bf16[16,128,128]{2,1,0:T(8,128)(2,1)} %broadcast_in_dim.34), calls=%async_computation | async-start | bytes 1048576 | tf_op jit(solution)/shard_map/all_to_all | solution.py:19
  61.9 21.4 %collective-permute-start.4 = (bf16[1536,256]{1,0:T(8,128)(2,1)}, bf16[1536,256]{1,0:T(8,128)(2,1)}, u32[]{:S(2)}, u32[]{:S(2)}) collective-permute-start(bf16[1536,256]{1,0:T(8,128)(2,1)} %bitcast.9.refs_0_), channel_id=1, source_target_pairs={{0,32},{32,0},{1,33},{33,1},{2,34},{34,2},{3,35},{35,3},{4,36},{36... | collective-permute-start | bytes 2359304 | tf_op jit(solution)/shard_map/ppermute | solution.py:303
  69.1 31.7 %copy-start.7 = (bf16[4,4096]{1,0:T(4,128)(2,1)S(1)}, bf16[4,4096]{1,0:T(4,128)(2,1)}, u32[]{:S(2)}) copy-start(bf16[4,4096]{1,0:T(4,128)(2,1)} %param.15) | copy-start | bytes 98308
  69.1 31.9 %copy-start.8 = (f32[4096]{0:T(1024)S(1)}, f32[4096]{0:T(1024)}, u32[]{:S(2)}) copy-start(f32[4096]{0:T(1024)} %param.17) | copy-start | bytes 49156
  70.3 12.9 %all-to-all-start.3 = ((bf16[4,16,4096]{2,1,0:T(8,128)(2,1)}), bf16[4,16,4096]{2,1,0:T(8,128)(2,1)S(1)}, u32[]{:S(2)}, u32[]{:S(2)}) async-start(bf16[4,16,4096]{2,1,0:T(8,128)(2,1)} %bitcast.56), calls=%async_computation.3 | async-start | bytes 1048576 | tf_op jit(solution)/shard_map/all_to_all | solution.py:19
  84.0 16.8 %all-to-all-start.4 = ((bf16[4,4,4096]{2,1,0:T(4,128)(2,1)}), bf16[4,4,4096]{2,1,0:T(4,128)(2,1)S(1)}, u32[]{:S(2)}, u32[]{:S(2)}) async-start(bf16[4,4,4096]{2,1,0:T(4,128)(2,1)} %reshape.132), calls=%async_computation.4 | async-start | bytes 262144 | tf_op jit(solution)/shard_map/all_to_all | solution.py:19
  93.6 19.8 %collective-permute-start.5 = (bf16[96,4096]{1,0:T(8,128)(2,1)}, bf16[96,4096]{1,0:T(8,128)(2,1)S(1)}, u32[]{:S(2)}, u32[]{:S(2)}) collective-permute-start(bf16[96,4096]{1,0:T(8,128)(2,1)} %collective-permute-done.refs_4_), channel_id=1, source_target_pairs={{0,32},{32,0},{1,33},{33,1},{2,34},{34,2},{3,35},{35,3},{4,36},{36... | collective-permute-start | bytes 2359304 | tf_op jit(solution)/shard_map/ppermute | solution.py:309
  101.0 43.7 %copy-start.6 = (bf16[4,4096]{1,0:T(4,128)(2,1)}, bf16[4,4096]{1,0:T(4,128)(2,1)S(1)}, u32[]{:S(2)}) copy-start(bf16[4,4096]{1,0:T(4,128)(2,1)S(1)} %get-tuple-element.53) | copy-start | bytes 98308
  113.5 15.0 %copy-start.4 = (bf16[96,4096]{1,0:T(8,128)(2,1)}, bf16[96,4096]{1,0:T(8,128)(2,1)S(1)}, u32[]{:S(2)}) copy-start(bf16[96,4096]{1,0:T(8,128)(2,1)S(1)} %collective-permute-done.5.refs_6_) | copy-start | bytes 2359300
  114.9 29.6 %all-to-all-start.5 = ((bf16[32,2,4224]{2,1,0:T(2,128)(2,1)}), bf16[32,2,4224]{2,1,0:T(2,128)(2,1)S(1)}, u32[]{:S(2)}, u32[]{:S(2)}) async-start(bf16[32,2,4224]{2,1,0:T(2,128)(2,1)} %reshape.134), calls=%async_computation.5 | async-start | bytes 1081344 | tf_op jit(solution)/shard_map/all_to_all | solution.py:19
  126.2 21.1 %collective-permute-start.6 = (bf16[96,4096]{1,0:T(8,128)(2,1)}, bf16[96,4096]{1,0:T(8,128)(2,1)}, u32[]{:S(2)}, u32[]{:S(2)}) collective-permute-start(bf16[96,4096]{1,0:T(8,128)(2,1)} %collective-permute-done.1.refs_8_), channel_id=1, source_target_pairs={{0,32},{32,0},{1,33},{33,1},{2,34},{34,2},{3,35},{35,3},{4,36},{36... | collective-permute-start | bytes 2359304 | tf_op jit(solution)/shard_map/ppermute | solution.py:320
  144.7 44.9 %copy-start.1 = (bf16[64,4224]{1,0:T(8,128)(2,1)}, bf16[64,4224]{1,0:T(8,128)(2,1)S(1)}, u32[]{:S(2)}) copy-start(bf16[64,4224]{1,0:T(8,128)(2,1)S(1)} %reshape.135.refs_0_.refs_12_) | copy-start | bytes 1622020
  147.3 30.4 %collective-permute-start.9 = (bf16[1536,256]{1,0:T(8,128)(2,1)}, bf16[1536,256]{1,0:T(8,128)(2,1)}, u32[]{:S(2)}, u32[]{:S(2)}) collective-permute-start(bf16[1536,256]{1,0:T(8,128)(2,1)} %bitcast.9.refs_0_), channel_id=1, source_target_pairs={{0,256},{256,0},{1,257},{257,1},{2,258},{258,2},{3,259},{259,3},{4... | collective-permute-start | bytes 2359304 | tf_op jit(solution)/shard_map/ppermute | solution.py:330
  149.5 28.1 %collective-permute-start.8 = (bf16[64,4224]{1,0:T(8,128)(2,1)S(1)}, bf16[64,4224]{1,0:T(8,128)(2,1)S(1)}, u32[]{:S(2)}, u32[]{:S(2)}) collective-permute-start(bf16[64,4224]{1,0:T(8,128)(2,1)S(1)} %reshape.135.refs_0_.refs_12_), channel_id=1, source_target_pairs={{64,0},{128,64},{192,128},{0,192},{65,1},{129,65},{193,129},{1,193... | collective-permute-start | bytes 1622024 | tf_op jit(solution)/shard_map/ppermute | solution.py:329
  153.3 24.4 %collective-permute-start.7 = (bf16[64,4224]{1,0:T(8,128)(2,1)S(1)}, bf16[64,4224]{1,0:T(8,128)(2,1)S(1)}, u32[]{:S(2)}, u32[]{:S(2)}) collective-permute-start(bf16[64,4224]{1,0:T(8,128)(2,1)S(1)} %reshape.135.refs_0_.refs_12_), channel_id=1, source_target_pairs={{0,64},{64,128},{128,192},{192,0},{1,65},{65,129},{129,193},{193,1... | collective-permute-start | bytes 1622024 | tf_op jit(solution)/shard_map/ppermute | solution.py:329
  177.7 20.8 %collective-permute-start.12 = (bf16[1536,256]{1,0:T(8,128)(2,1)}, bf16[1536,256]{1,0:T(8,128)(2,1)}, u32[]{:S(2)}, u32[]{:S(2)}) collective-permute-start(bf16[1536,256]{1,0:T(8,128)(2,1)} %collective-permute-done.4.refs_1_), channel_id=1, source_target_pairs={{0,256},{256,0},{1,257},{257,1},{2,258},{258,2},{3,259},{259,3},{4... | collective-permute-start | bytes 2359304 | tf_op jit(solution)/shard_map/ppermute | solution.py:334
  182.7 13.9 %collective-permute-start.11 = (bf16[32,4224]{1,0:T(8,128)(2,1)}, bf16[32,4224]{1,0:T(8,128)(2,1)S(1)}, u32[]{:S(2)}, u32[]{:S(2)}) collective-permute-start(bf16[32,4224]{1,0:T(8,128)(2,1)} %slice.19), channel_id=1, source_target_pairs={{64,0},{128,64},{192,128},{0,192},{65,1},{129,65},{193,129},{1,193... | collective-permute-start | bytes 811016 | tf_op jit(solution)/shard_map/ppermute | solution.py:333
  185.9 12.6 %collective-permute-start.10 = (bf16[32,4224]{1,0:T(8,128)(2,1)}, bf16[32,4224]{1,0:T(8,128)(2,1)}, u32[]{:S(2)}, u32[]{:S(2)}) collective-permute-start(bf16[32,4224]{1,0:T(8,128)(2,1)} %slice.18), channel_id=1, source_target_pairs={{0,64},{64,128},{128,192},{192,0},{1,65},{65,129},{129,193},{193,1... | collective-permute-start | bytes 811016 | tf_op jit(solution)/shard_map/ppermute | solution.py:333
  270.1 11.4 %all-to-all-start.8 = ((bf16[4,4,1024]{2,1,0:T(4,128)(2,1)}), bf16[4,4,1024]{2,1,0:T(4,128)(2,1)S(1)}, u32[]{:S(2)}, u32[]{:S(2)}) async-start(bf16[4,4,1024]{2,1,0:T(4,128)(2,1)} %reshape.138), calls=%async_computation.8 | async-start | bytes 65536 | tf_op jit(solution)/shard_map/all_to_all | solution.py:19
  (3 other events, 17.4 us)

commit v7 on v5

--- a/solution.py
+++ b/solution.py
@@ -101,15 +101,17 @@
         out_ref[...] = gated(total, weights[0].shape[0])
 
 
-def last_kernel(count, place_ref, *refs):
-    blocks, weights, first = refs[:count], refs[count : count + 4], refs[count + 4]
-    extras, (out_ref, extra_ref, weight, rows, total, tags) = refs[count + 5 : -6], refs[-6:]
+def last_kernel(count, parts, place_ref, *refs):
+    blocks, weights, refs = refs[:count], refs[count : count + 4], refs[count + 4 :]
+    done, extras = refs[:parts], refs[parts:-6]
+    out_ref, extra_ref, weight, rows, total, tags = refs[-6:]
     weight_rows(place_ref, weights, weight)
     accumulate(weight, rows, blocks, total)
 
     @pl.when(pl.program_id(0) == pl.num_programs(0) - 1)
     def _():
-        hidden = jnp.concatenate([first[...], gated(total, weights[0].shape[0])], axis=1)
+        held = [part[...] for part in done] + [gated(total, weights[0].shape[0])]
+        hidden = jnp.concatenate(held, axis=1)
         slots = hidden.shape[1]
         peers = out_ref.shape[0]
         each = slots // peers
@@ -178,7 +180,7 @@
     slots = sum(b.shape[0] for b in every)
     pieces = (peers, 2 * units, slots // 2)
     return pl.pallas_call(
-        lambda *refs: last_kernel(len(blocks), *refs),
+        lambda *refs: last_kernel(len(blocks), len(first), *refs),
         out_shape=(
             jax.ShapeDtypeStruct(pieces, jnp.bfloat16),
             jax.ShapeDtypeStruct((slots, EXTRA), jnp.bfloat16),
@@ -187,7 +189,7 @@
             num_scalar_prefetch=1,
             grid=(width // step,),
             in_specs=row_specs(blocks, weights, step)
-            + [whole(first.shape)]
+            + [whole(part.shape) for part in first]
             + [
                 pl.BlockSpec((b.shape[0], EXTRA), lambda k, *_: (0, width // EXTRA))
                 for b in every
@@ -198,27 +200,35 @@
         ),
         compiler_params=pltpu.CompilerParams(vmem_limit_bytes=60 * 2**20),
         cost_estimate=cost(units, count, width),
-    )(place, *blocks, *weights, first, *every)
+    )(place, *blocks, *weights, *first, *every)
 
 
 def down_kernel(half_ref, hidden_ref, extra_ref, *refs):
-    weights, out_ref, stacked, held, arrived = refs[:4], refs[4], refs[5], refs[6], refs[7]
+    weights, (out_ref, stacked, held, placed, arrived) = refs[:4], refs[4:]
+    peers, units, count = hidden_ref.shape
+    half = units // 2
+    moves = [
+        pltpu.make_async_copy(
+            hidden_ref.at[peer, pl.ds(z * half, half), :],
+            stacked.at[pl.ds((z * peers + peer) * half, half), :],
+            placed.at[z * peers + peer],
+        )
+        for z in range(2)
+        for peer in range(peers)
+    ]
     copies = [
         pltpu.make_async_copy(weight, held.at[i], arrived.at[i]) for i, weight in enumerate(weights)
     ]
-    for copy in copies:
+    for copy in moves + copies:
         copy.start()
-    peers, units, count = hidden_ref.shape
-    for peer in range(peers):
-        for z in range(2):
-            rows = pl.ds((z * peers + peer) * (units // 2), units // 2)
-            stacked[rows, :] = hidden_ref[peer, z * (units // 2) : (z + 1) * (units // 2), :]
     blocks = peers // 2
     each = count // blocks
     to = lax.broadcasted_iota(jnp.int32, (count, count), 0)
     source = (to % (2 * blocks)) // 2 * each + to // (2 * blocks) * 2 + to % 2
     column = lax.broadcasted_iota(jnp.int32, (count, count), 1)
     move = jnp.where(source == column, 1.0, 0.0).astype(jnp.bfloat16)
+    for copy in moves:
+        copy.wait()
     rows = rows_dot(move, stacked[...]).astype(jnp.bfloat16)
     cols = held.shape[2]
     extra = jnp.where(half_ref[0] == 0, extra_ref[:count, :], extra_ref[count:, :])
@@ -240,12 +250,13 @@
         grid_spec=pltpu.PrefetchScalarGridSpec(
             num_scalar_prefetch=1,
             grid=(1,),
-            in_specs=[whole(hidden.shape), whole(extra.shape)]
+            in_specs=[pl.BlockSpec(memory_space=pl.ANY), whole(extra.shape)]
             + [pl.BlockSpec(memory_space=pl.ANY)] * 4,
             out_specs=whole(out),
             scratch_shapes=[
                 pltpu.VMEM((deep, count), jnp.bfloat16),
                 pltpu.VMEM((4, deep, cols), jnp.bfloat16),
+                pltpu.SemaphoreType.DMA((2 * peers,)),
                 pltpu.SemaphoreType.DMA((4,)),
             ],
         ),
@@ -315,14 +326,12 @@
     done = (numer / total).astype(jnp.bfloat16).reshape(heads, tok_block, HEAD_WIDTH)
     heads_out = jnp.transpose(done, (1, 0, 2)).reshape(tok_block, heads * HEAD_WIDTH)
 
-    heads_out, down_own = lax.optimization_barrier((heads_out, down_own))
-    down_y = lax.ppermute(down_own, "y", swap_y)
-
     partial = jnp.dot(heads_out, out_weight, preferred_element_type=jnp.float32)
     partial = partial.astype(jnp.bfloat16).reshape(n_co, tok_block // n_co, width)
     partial = added(exchange(partial, "co")).astype(jnp.bfloat16)
     partial = added(exchange(partial.reshape(n_x, -1, width), "x")).astype(jnp.bfloat16)
-    partial, gate_z, up_z, down_y = lax.optimization_barrier((partial, gate_z, up_z, down_y))
+    partial, gate_z, up_z, down_own = lax.optimization_barrier((partial, gate_z, up_z, down_own))
+    down_y = lax.ppermute(down_own, "y", swap_y)
     projected = added(exchange(partial.reshape(n_zh, tok_dev, width), "zh"))
     mixed = (residual.astype(jnp.float32) + projected).astype(jnp.bfloat16)
 
@@ -338,20 +347,31 @@
     arrived, down_own, down_y = lax.optimization_barrier((arrived, down_own, down_y))
     after = [(i, (i + 1) % n_y) for i in range(n_y)]
     before = [(b, a) for a, b in after]
-    blocks, left, right = [arrived], arrived, arrived
-    for _ in range(n_y // 2 - 1):
-        left, right = lax.ppermute(left, "y", after), lax.ppermute(right, "y", before)
-        blocks += [left, right]
-    part = arrived.shape[0] // 2
-    blocks.append(lax.ppermute(left[:part], "y", after))
-    blocks.append(lax.ppermute(right[part:], "y", before))
-    down_z, down_zy = lax.ppermute(down_own, "zl", swap_z), lax.ppermute(down_y, "zl", swap_z)
     weights = (gate_own, gate_z, up_own, up_z)
-    first = first_hidden(zl, blocks[:5], weights, width)
-    last, first, down_z, down_zy = lax.optimization_barrier((blocks[5:], first, down_z, down_zy))
+
+    def onward(left, right):
+        return lax.ppermute(left, "y", after), lax.ppermute(right, "y", before)
+
+    one = onward(arrived, arrived)
+    two = onward(*one)
+    down_z = lax.ppermute(down_own, "zl", swap_z)
+    two, down_z, down_y = lax.optimization_barrier((two, down_z, down_y))
+    three = onward(*two)
+    down_zy = lax.ppermute(down_y, "zl", swap_z)
+    first = first_hidden(zl, (arrived,) + one + two, weights, width)
+    three, first = lax.optimization_barrier((three, first))
+    last = lax.ppermute(three[0], "y", after)
+    second = first_hidden(zl, three, weights, width)
+    last, second, down_zy = lax.optimization_barrier((last, second, down_zy))
 
     hidden, extra = last_hidden(
-        jnp.stack([zl, y_pos]), last, weights, first, blocks[:5] + last, width, n_y
+        jnp.stack([zl, y_pos]),
+        (last,),
+        weights,
+        (first, second),
+        (arrived,) + one + two + three + (last,),
+        width,
+        n_y,
     )
     hidden = exchange(hidden, "y")
 

time: 255 us -> 251 us (0.984)
  blocking collectives: 93.4 us -> 73.9 us
  Pallas kernels: 18 us -> 23.3 us
  waiting for transfers between devices: 63.7 us -> 67.9 us
  starting transfers between devices: 59.3 us -> 63.4 us
  other arithmetic: 5.49 us -> 8.08 us
    all_to_all x6 -> x5, blocking collectives: 93.4 us -> 73.9 us  [exchange(): return lax.all_to_all(pieces, axis, 0, 0, tiled=True)]
    all_to_all x3 -> x4, waiting for transfers between devices: 31.7 us -> 44.2 us  [exchange(): return lax.all_to_all(pieces, axis, 0, 0, tiled=True)]
    ppermute x10 -> x9, waiting for transfers between devices: 32 us -> 21 us  [the longest x6 13.3 us: onward(): return (lax.ppermute(left, 'y', after), lax.ppermute(right, 'y', before))]
    all_to_all x3 -> x4, starting transfers between devices: 16.7 us -> 24.9 us  [exchange(): return lax.all_to_all(pieces, axis, 0, 0, tiled=True)]
    ppermute x10 -> x9, starting transfers between devices: 34.5 us -> 29.7 us  [the longest x6 20.3 us: onward(): return (lax.ppermute(left, 'y', after), lax.ppermute(right, 'y', before))]
    pallas_call x1 -> x2, Pallas kernels: 5.88 us -> 10.6 us  [first_hidden(): pl.pallas_call(first_kernel, out_shape=jax.ShapeDtypeStruct((2 * units, c...]
    ppermute x1, waiting for transfers between devices: 0.01 us -> 2.69 us  [on_device(): down_y = lax.ppermute(down_own, 'y', swap_y)]
  transfers between devices with their start and end apart: 16 -> 16, of which waited for: 6 -> 11; matrix products, arithmetic and copies ran while one was open for 4% -> 5% of each run, Pallas kernels for 2% -> 4%
where the time goes in v7:
time: 251 us; the launch traced here: 249 us
  blocking collectives  73.9 us (29%)
  waiting for transfers between devices  67.9 us (27%)
  starting transfers between devices  63.4 us (25%)
  Pallas kernels  23.3 us (9%)
  local copies, waits for them, and re-layouts  9.02 us (4%)
  other arithmetic  8.08 us (3%)
  matrix products  2.81 us (1%)
    all_to_all x5, blocking collectives, exchange(): return lax.all_to_all(pieces, axis, 0, 0, tiled=True)  73.9 us
    all_to_all x4, waiting for transfers between devices, exchange(): return lax.all_to_all(pieces, axis, 0, 0, tiled=True)  44.2 us
    all_to_all x4, starting transfers between devices, exchange(): return lax.all_to_all(pieces, axis, 0, 0, tiled=True)  24.9 us
    ppermute x6, starting transfers between devices, onward(): return (lax.ppermute(left, 'y', after), lax.ppermute(right, 'y', before))  20.3 us
    ppermute x6, waiting for transfers between devices, onward(): return (lax.ppermute(left, 'y', after), lax.ppermute(right, 'y', before))  13.3 us
    pallas_call x2, Pallas kernels, first_hidden(): pl.pallas_call(first_kernel, out_shape=jax.ShapeDtypeStruct((2 * units, c...  10.6 us
    pallas_call x1, Pallas kernels, down_slots(): pl.pallas_call(down_kernel, out_shape=jax.ShapeDtypeStruct(out, jnp.bfloa...  6.41 us
    pallas_call x1, Pallas kernels, last_hidden(): pl.pallas_call(lambda *refs: last_kernel(len(blocks), len(first), *refs),...  6.36 us
  transfers between devices with their start and end apart: 16, of which 11 were waited for; matrix products, arithmetic and copies ran while one was open for 5% of the time, Pallas kernels for 4%

profile of v7, /device:TPU:1, one launch (start us, length us, event | category | flops | bytes accessed | tf_op | source)
XLA Modules:
  0.0 249.5 jit_solution(8067113307766270314)
XLA Ops:
  2.5 9.6 %all-to-all-start = ((bf16[16,128,128]{2,1,0:T(8,128)(2,1)}), bf16[16,128,128]{2,1,0:T(8,128)(2,1)S(1)}, u32[]{:S(2)}, u32[]{:S(2)}) async-start(bf16[16,128,128]{2,1,0:T(8,128)(2,1)} %broadcast_in_dim.31), calls=%async_computation | async-start | bytes 1048576 | tf_op jit(solution)/shard_map/all_to_all | solution.py:19
  25.9 7.1 %all_to_all.45 = bf16[2,2048,128]{2,1,0:T(8,128)(2,1)S(1)} all-to-all(bf16[2,2048,128]{2,1,0:T(8,128)(2,1)S(1)} %broadcast_in_dim.37), channel_id=1, replica_groups=mesh['zl'=2,'y'=8,'x'=4,'zh'=4,'co'=2] {'co'}, dimensions={0} | all-to-all | bytes 2097152 | tf_op jit(solution)/shard_map/all_to_all | solution.py:19
  35.0 5.4 %all_to_all.46 = bf16[2,64,4096]{2,1,0:T(8,128)(2,1)} all-to-all(bf16[2,64,4096]{2,1,0:T(8,128)(2,1)S(1)} %bitcast.53), channel_id=1, replica_groups=mesh['zl'=2,'y'=8,'x'=4,'zh'=4,'co'=2] {'co'}, dimensions={0} | all-to-all | bytes 2097152 | tf_op jit(solution)/shard_map/all_to_all | solution.py:19
  42.7 12.6 %all_to_all.47 = bf16[4,16,4096]{2,1,0:T(8,128)(2,1)S(1)} all-to-all(bf16[4,16,4096]{2,1,0:T(8,128)(2,1)} %bitcast.57), channel_id=1, replica_groups=mesh['zl'=2,'y'=8,'x'=4,'zh'=4,'co'=2] {'x'}, dimensions={0} | all-to-all | bytes 1048576 | tf_op jit(solution)/shard_map/all_to_all | solution.py:19
  55.5 16.2 %all_to_all.48 = bf16[4,4,4096]{2,1,0:T(4,128)(2,1)S(1)} all-to-all(bf16[4,4,4096]{2,1,0:T(4,128)(2,1)S(1)} %reshape.144), channel_id=1, replica_groups=mesh['zl'=2,'y'=8,'x'=4,'zh'=4,'co'=2] {'zh'}, dimensions={0} | all-to-all | bytes 262144 | tf_op jit(solution)/shard_map/all_to_all | solution.py:19
  74.8 6.8 %all-to-all-start.5 = ((bf16[32,2,4224]{2,1,0:T(2,128)(2,1)}), bf16[32,2,4224]{2,1,0:T(2,128)(2,1)S(1)}, u32[]{:S(2)}, u32[]{:S(2)}) async-start(bf16[32,2,4224]{2,1,0:T(2,128)(2,1)} %reshape.146), calls=%async_computation.5 | async-start | bytes 1081344 | tf_op jit(solution)/shard_map/all_to_all | solution.py:19
  81.6 3.5 %collective-permute-start.2 = (bf16[1536,256]{1,0:T(8,128)(2,1)}, bf16[1536,256]{1,0:T(8,128)(2,1)}, u32[]{:S(2)}, u32[]{:S(2)}) collective-permute-start(bf16[1536,256]{1,0:T(8,128)(2,1)} %bitcast.58), channel_id=1, source_target_pairs={{0,32},{32,0},{64,96},{96,64},{128,160},{160,128},{192,224},{224,1... | collective-permute-start | bytes 2359304 | tf_op jit(solution)/shard_map/ppermute | solution.py:334
  85.1 14.9 %all-to-all-done.5 = bf16[32,2,4224]{2,1,0:T(2,128)(2,1)S(1)} async-done(((bf16[32,2,4224]{2,1,0:T(2,128)(2,1)}), bf16[32,2,4224]{2,1,0:T(2,128)(2,1)S(1)}, u32[]{:S(2)}, u32[]{:S(2)}) %all-to-all-start.5) | async-done | bytes 540704 | tf_op jit(solution)/shard_map/all_to_all | solution.py:19
  112.2 6.6 %collective-permute-done.3.refs_1_.refs_9_ = bf16[64,4224]{1,0:T(8,128)(2,1)S(1)} collective-permute-done((bf16[64,4224]{1,0:T(8,128)(2,1)S(1)}, bf16[64,4224]{1,0:T(8,128)(2,1)S(1)}, u32[]{:S(2)}, u32[]{:S(2)}) %collective-permute-start.3) | collective-permute-done | bytes 540704 | tf_op jit(solution)/shard_map/ppermute | solution.py:353
  120.8 4.6 %collective-permute-start.6 = (bf16[64,4224]{1,0:T(8,128)(2,1)S(1)}, bf16[64,4224]{1,0:T(8,128)(2,1)}, u32[]{:S(2)}, u32[]{:S(2)}) collective-permute-start(bf16[64,4224]{1,0:T(8,128)(2,1)S(1)} %collective-permute-done.5.refs_2_.refs_10_), channel_id=1, source_target_pairs={{32,0},{64,32},{96,64},{128,96},{160,128},{192,160},{224,192},{0,2... | collective-permute-start | bytes 1622024 | tf_op jit(solution)/shard_map/ppermute | solution.py:353
  125.4 3.8 %collective-permute-done.7.refs_2_ = bf16[1536,256]{1,0:T(8,128)(2,1)S(1)} collective-permute-done((bf16[1536,256]{1,0:T(8,128)(2,1)}, bf16[1536,256]{1,0:T(8,128)(2,1)S(1)}, u32[]{:S(2)}, u32[]{:S(2)}) %collective-permute-start.7) | collective-permute-done | bytes 786464 | tf_op jit(solution)/shard_map/ppermute | solution.py:357
  129.2 4.8 %collective-permute-done.4.refs_3_.refs_11_ = bf16[64,4224]{1,0:T(8,128)(2,1)} collective-permute-done((bf16[64,4224]{1,0:T(8,128)(2,1)S(1)}, bf16[64,4224]{1,0:T(8,128)(2,1)}, u32[]{:S(2)}, u32[]{:S(2)}) %collective-permute-start.4) | collective-permute-done | bytes 540704 | tf_op jit(solution)/shard_map/ppermute | solution.py:353
  137.2 4.9 %collective-permute-start.9 = (bf16[64,4224]{1,0:T(8,128)(2,1)}, bf16[64,4224]{1,0:T(8,128)(2,1)}, u32[]{:S(2)}, u32[]{:S(2)}) collective-permute-start(bf16[64,4224]{1,0:T(8,128)(2,1)} %collective-permute-done.6.refs_4_.refs_12_), channel_id=1, source_target_pairs={{32,0},{64,32},{96,64},{128,96},{160,128},{192,160},{224,192},{0,2... | collective-permute-start | bytes 1622024 | tf_op jit(solution)/shard_map/ppermute | solution.py:353
  144.7 5.9 %shard_map.131.refs_6_ = bf16[192,320]{1,0:T(8,128)(2,1)} custom-call(s32[1]{0:T(128)} %bitcast.20.zl_ref, bf16[64,4224]{1,0:T(8,128)(2,1)} %copy-done.2, bf16[64,4224]{1,0:T(8,128)(2,1)} %copy-done.4, bf16[64,4224]{1,0:T(8,128)(2,1)} %copy-done.5, bf16[64,4224]{1,0:T(8,128)(2,1)} %collective-permute-done.4.refs_3_.refs_11_, ...), custom_call_target="tpu_custom_call" | custom-call | flops 1006632960 | bytes 5767168 | tf_op jit(solution)/shard_map/pallas_call | solution.py:162
  151.7 4.0 %collective-permute-start.10 = (bf16[64,4224]{1,0:T(8,128)(2,1)}, bf16[64,4224]{1,0:T(8,128)(2,1)S(1)}, u32[]{:S(2)}, u32[]{:S(2)}) collective-permute-start(bf16[64,4224]{1,0:T(8,128)(2,1)} %collective-permute-done.8.refs_0_.refs_13_), channel_id=1, source_target_pairs={{0,32},{32,64},{64,96},{96,128},{128,160},{160,192},{192,224},{224... | collective-permute-start | bytes 1622024 | tf_op jit(solution)/shard_map/ppermute | solution.py:363
  156.3 4.7 %shard_map.132.refs_7_ = bf16[192,128]{1,0:T(8,128)(2,1)} custom-call(s32[1]{0:T(128)} %bitcast.20.zl_ref, bf16[64,4224]{1,0:T(8,128)(2,1)} %collective-permute-done.8.refs_0_.refs_13_, bf16[64,4224]{1,0:T(8,128)(2,1)} %collective-permute-done.9.refs_1_.refs_14_, bf16[96,4096]{1,0:T(8,128)(2,1)} %bitcast.47, bf16[96,4096]{1,0:T(8,128)(2,1)} %copy-done.1, ...), custom_call_target="tpu_custom_call" | custom-call | flops 402653184 | bytes 4194304 | tf_op jit(solution)/shard_map/pallas_call | solution.py:162
  161.0 4.0 %collective-permute-done.10.refs_1_.refs_15_ = bf16[64,4224]{1,0:T(8,128)(2,1)S(1)} collective-permute-done((bf16[64,4224]{1,0:T(8,128)(2,1)}, bf16[64,4224]{1,0:T(8,128)(2,1)S(1)}, u32[]{:S(2)}, u32[]{:S(2)}) %collective-permute-start.10) | collective-permute-done | bytes 540704 | tf_op jit(solution)/shard_map/ppermute | solution.py:363
  165.8 6.4 %shard_map.133 = (bf16[8,192,256]{2,1,0:T(8,128)(2,1)}, bf16[512,128]{1,0:T(8,128)(2,1)}) custom-call(s32[2]{0:T(128)} %pad_add_fusion.refs_0_, bf16[64,4224]{1,0:T(8,128)(2,1)} %copy-done.6, bf16[96,4096]{1,0:T(8,128)(2,1)} %bitcast.48, bf16[96,4096]{1,0:T(8,128)(2,1)} %copy-done.1, bf16[96,4096]{1,0:T(8,128)(2,1)} %bitcast.52, ...), custom_call_target="tpu_custom_call" | custom-call | flops 201326592 | bytes 3670016 | tf_op jit(solution)/shard_map/pallas_call | solution.py:182
  172.2 5.2 %all-to-all-start.6 = ((bf16[8,192,256]{2,1,0:T(8,128)(2,1)}), bf16[8,192,256]{2,1,0:T(8,128)(2,1)S(1)}, u32[]{:S(2)}, u32[]{:S(2)}) async-start(bf16[8,192,256]{2,1,0:T(8,128)(2,1)} %get-tuple-element.42), calls=%async_computation.6 | async-start | bytes 1572864 | tf_op jit(solution)/shard_map/all_to_all | solution.py:19
  177.4 19.7 %all-to-all-done.6.hidden_ref = bf16[8,192,256]{2,1,0:T(8,128)(2,1)S(1)} async-done(((bf16[8,192,256]{2,1,0:T(8,128)(2,1)}), bf16[8,192,256]{2,1,0:T(8,128)(2,1)S(1)}, u32[]{:S(2)}, u32[]{:S(2)}) %all-to-all-start.6) | async-done | bytes 786464 | tf_op jit(solution)/shard_map/all_to_all | solution.py:19
  198.0 6.4 %shard_map.134 = bf16[256,1152]{1,0:T(8,128)(2,1)} custom-call(s32[1]{0:T(128)} %bitcast.19.half_ref, bf16[8,192,256]{2,1,0:T(8,128)(2,1)} %copy-done.3, bf16[512,128]{1,0:T(8,128)(2,1)} %get-tuple-element.43.extra_ref, bf16[1536,256]{1,0:T(8,128)(2,1)} %bitcast.60, bf16[1536,256]{1,0:T(8,128)(2,1)} %collective-permute-done.2.refs_1_, ...), custom_call_target="tpu_custom_call" | custom-call | flops 805306368 | bytes 3145728 | tf_op jit(solution)/shard_map/pallas_call | solution.py:247
  204.4 32.6 %all_to_all.49 = bf16[32,8,1152]{2,1,0:T(8,128)(2,1)S(1)} all-to-all(bf16[32,8,1152]{2,1,0:T(8,128)(2,1)} %bitcast.54), channel_id=1, replica_groups=mesh['zl'=2,'y'=8,'x'=4,'zh'=4,'co'=2] {'x','zh','co'}, dimensions={0} | all-to-all | bytes 1179648 | tf_op jit(solution)/shard_map/all_to_all | solution.py:19
  237.9 3.3 %all-to-all-start.8 = ((bf16[8,4,1024]{2,1,0:T(4,128)(2,1)}), bf16[8,4,1024]{2,1,0:T(4,128)(2,1)S(1)}, u32[]{:S(2)}, u32[]{:S(2)}) async-start(bf16[8,4,1024]{2,1,0:T(4,128)(2,1)} %reshape.150), calls=%async_computation.8 | async-start | bytes 131072 | tf_op jit(solution)/shard_map/all_to_all | solution.py:19
  241.3 7.1 %all-to-all-done.8 = bf16[8,4,1024]{2,1,0:T(4,128)(2,1)S(1)} async-done(((bf16[8,4,1024]{2,1,0:T(4,128)(2,1)}), bf16[8,4,1024]{2,1,0:T(4,128)(2,1)S(1)}, u32[]{:S(2)}, u32[]{:S(2)}) %all-to-all-start.8) | async-done | bytes 65568 | tf_op jit(solution)/shard_map/all_to_all | solution.py:19
  (87 shorter events, 48.4 us)
Async XLA Ops:
  0.6 33.9 %copy-start = (bf16[256,4096]{1,0:T(8,128)(2,1)S(1)}, bf16[256,4096]{1,0:T(8,128)(2,1)}, u32[]{:S(2)}) copy-start(bf16[256,4096]{1,0:T(8,128)(2,1)} %param.16) | copy-start | bytes 6291460
  2.5 23.3 %all-to-all-start = ((bf16[16,128,128]{2,1,0:T(8,128)(2,1)}), bf16[16,128,128]{2,1,0:T(8,128)(2,1)S(1)}, u32[]{:S(2)}, u32[]{:S(2)}) async-start(bf16[16,128,128]{2,1,0:T(8,128)(2,1)} %broadcast_in_dim.31), calls=%async_computation | async-start | bytes 1048576 | tf_op jit(solution)/shard_map/all_to_all | solution.py:19
  12.1 43.4 %collective-permute-start = (bf16[96,4096]{1,0:T(8,128)(2,1)}, bf16[96,4096]{1,0:T(8,128)(2,1)S(1)}, u32[]{:S(2)}, u32[]{:S(2)}) collective-permute-start(bf16[96,4096]{1,0:T(8,128)(2,1)} %bitcast.45), channel_id=1, source_target_pairs={{0,256},{256,0},{1,257},{257,1},{2,258},{258,2},{3,259},{259,3},{4... | collective-permute-start | bytes 2359304 | tf_op jit(solution)/shard_map/ppermute | solution.py:296
  15.3 40.1 %collective-permute-start.1 = (bf16[96,4096]{1,0:T(8,128)(2,1)}, bf16[96,4096]{1,0:T(8,128)(2,1)}, u32[]{:S(2)}, u32[]{:S(2)}) collective-permute-start(bf16[96,4096]{1,0:T(8,128)(2,1)} %bitcast.49), channel_id=1, source_target_pairs={{0,256},{256,0},{1,257},{257,1},{2,258},{258,2},{3,259},{259,3},{4... | collective-permute-start | bytes 2359304 | tf_op jit(solution)/shard_map/ppermute | solution.py:296
  22.6 10.4 %copy-start.9 = (bf16[4,4,2,4,2,128]{5,3,1,0,2,4:T(4,128)(2,1)S(1)}, bf16[4,4,2,4,2,128]{5,3,1,0,2,4:T(4,128)(2,1)}, u32[]{:S(2)}) copy-start(bf16[4,4,2,4,2,128]{5,3,1,0,2,4:T(4,128)(2,1)} %copy.32) | copy-start | bytes 196612
  55.4 19.4 %copy-start.1 = (bf16[96,4096]{1,0:T(8,128)(2,1)}, bf16[96,4096]{1,0:T(8,128)(2,1)S(1)}, u32[]{:S(2)}) copy-start(bf16[96,4096]{1,0:T(8,128)(2,1)S(1)} %collective-permute-done.refs_6_.refs_3_) | copy-start | bytes 2359300
  72.6 27.6 %copy-start.8 = (bf16[4,4096]{1,0:T(4,128)(2,1)}, bf16[4,4096]{1,0:T(4,128)(2,1)S(1)}, u32[]{:S(2)}) copy-start(bf16[4,4096]{1,0:T(4,128)(2,1)S(1)} %get-tuple-element.47) | copy-start | bytes 98308
  74.8 25.2 %all-to-all-start.5 = ((bf16[32,2,4224]{2,1,0:T(2,128)(2,1)}), bf16[32,2,4224]{2,1,0:T(2,128)(2,1)S(1)}, u32[]{:S(2)}, u32[]{:S(2)}) async-start(bf16[32,2,4224]{2,1,0:T(2,128)(2,1)} %reshape.146), calls=%async_computation.5 | async-start | bytes 1081344 | tf_op jit(solution)/shard_map/all_to_all | solution.py:19
  81.6 21.4 %collective-permute-start.2 = (bf16[1536,256]{1,0:T(8,128)(2,1)}, bf16[1536,256]{1,0:T(8,128)(2,1)}, u32[]{:S(2)}, u32[]{:S(2)}) collective-permute-start(bf16[1536,256]{1,0:T(8,128)(2,1)} %bitcast.58), channel_id=1, source_target_pairs={{0,32},{32,0},{64,96},{96,64},{128,160},{160,128},{192,224},{224,1... | collective-permute-start | bytes 2359304 | tf_op jit(solution)/shard_map/ppermute | solution.py:334
  100.3 44.5 %copy-start.2 = (bf16[64,4224]{1,0:T(8,128)(2,1)}, bf16[64,4224]{1,0:T(8,128)(2,1)S(1)}, u32[]{:S(2)}) copy-start(bf16[64,4224]{1,0:T(8,128)(2,1)S(1)} %reshape.147.refs_0_.refs_8_) | copy-start | bytes 1622020
  103.0 15.9 %collective-permute-start.3 = (bf16[64,4224]{1,0:T(8,128)(2,1)S(1)}, bf16[64,4224]{1,0:T(8,128)(2,1)S(1)}, u32[]{:S(2)}, u32[]{:S(2)}) collective-permute-start(bf16[64,4224]{1,0:T(8,128)(2,1)S(1)} %reshape.147.refs_0_.refs_8_), channel_id=1, source_target_pairs={{0,32},{32,64},{64,96},{96,128},{128,160},{160,192},{192,224},{224... | collective-permute-start | bytes 1622024 | tf_op jit(solution)/shard_map/ppermute | solution.py:353
  106.1 14.7 %collective-permute-start.5 = (bf16[64,4224]{1,0:T(8,128)(2,1)S(1)}, bf16[64,4224]{1,0:T(8,128)(2,1)S(1)}, u32[]{:S(2)}, u32[]{:S(2)}) collective-permute-start(bf16[64,4224]{1,0:T(8,128)(2,1)S(1)} %reshape.147.refs_0_.refs_8_), channel_id=1, source_target_pairs={{32,0},{64,32},{96,64},{128,96},{160,128},{192,160},{224,192},{0,2... | collective-permute-start | bytes 1622024 | tf_op jit(solution)/shard_map/ppermute | solution.py:353
  109.5 19.7 %collective-permute-start.7 = (bf16[1536,256]{1,0:T(8,128)(2,1)}, bf16[1536,256]{1,0:T(8,128)(2,1)S(1)}, u32[]{:S(2)}, u32[]{:S(2)}) collective-permute-start(bf16[1536,256]{1,0:T(8,128)(2,1)} %bitcast.59), channel_id=1, source_target_pairs={{0,256},{256,0},{1,257},{257,1},{2,258},{258,2},{3,259},{259,3},{4... | collective-permute-start | bytes 2359304 | tf_op jit(solution)/shard_map/ppermute | solution.py:357
  118.8 25.9 %copy-start.4 = (bf16[64,4224]{1,0:T(8,128)(2,1)}, bf16[64,4224]{1,0:T(8,128)(2,1)S(1)}, u32[]{:S(2)}) copy-start(bf16[64,4224]{1,0:T(8,128)(2,1)S(1)} %collective-permute-done.3.refs_1_.refs_9_) | copy-start | bytes 1622020
  118.8 15.1 %collective-permute-start.4 = (bf16[64,4224]{1,0:T(8,128)(2,1)S(1)}, bf16[64,4224]{1,0:T(8,128)(2,1)}, u32[]{:S(2)}, u32[]{:S(2)}) collective-permute-start(bf16[64,4224]{1,0:T(8,128)(2,1)S(1)} %collective-permute-done.3.refs_1_.refs_9_), channel_id=1, source_target_pairs={{0,32},{32,64},{64,96},{96,128},{128,160},{160,192},{192,224},{224... | collective-permute-start | bytes 1622024 | tf_op jit(solution)/shard_map/ppermute | solution.py:353
  120.8 23.9 %copy-start.5 = (bf16[64,4224]{1,0:T(8,128)(2,1)}, bf16[64,4224]{1,0:T(8,128)(2,1)S(1)}, u32[]{:S(2)}) copy-start(bf16[64,4224]{1,0:T(8,128)(2,1)S(1)} %collective-permute-done.5.refs_2_.refs_10_) | copy-start | bytes 1622020
  120.8 14.0 %collective-permute-start.6 = (bf16[64,4224]{1,0:T(8,128)(2,1)S(1)}, bf16[64,4224]{1,0:T(8,128)(2,1)}, u32[]{:S(2)}, u32[]{:S(2)}) collective-permute-start(bf16[64,4224]{1,0:T(8,128)(2,1)S(1)} %collective-permute-done.5.refs_2_.refs_10_), channel_id=1, source_target_pairs={{32,0},{64,32},{96,64},{128,96},{160,128},{192,160},{224,192},{0,2... | collective-permute-start | bytes 1622024 | tf_op jit(solution)/shard_map/ppermute | solution.py:353
  129.2 5.6 %copy-start.7 = (bf16[1536,256]{1,0:T(8,128)(2,1)}, bf16[1536,256]{1,0:T(8,128)(2,1)S(1)}, u32[]{:S(2)}) copy-start(bf16[1536,256]{1,0:T(8,128)(2,1)S(1)} %collective-permute-done.7.refs_2_) | copy-start | bytes 2359300
  134.7 15.9 %collective-permute-start.8 = (bf16[64,4224]{1,0:T(8,128)(2,1)}, bf16[64,4224]{1,0:T(8,128)(2,1)}, u32[]{:S(2)}, u32[]{:S(2)}) collective-permute-start(bf16[64,4224]{1,0:T(8,128)(2,1)} %collective-permute-done.4.refs_3_.refs_11_), channel_id=1, source_target_pairs={{0,32},{32,64},{64,96},{96,128},{128,160},{160,192},{192,224},{224... | collective-permute-start | bytes 1622024 | tf_op jit(solution)/shard_map/ppermute | solution.py:353
  137.2 14.5 %collective-permute-start.9 = (bf16[64,4224]{1,0:T(8,128)(2,1)}, bf16[64,4224]{1,0:T(8,128)(2,1)}, u32[]{:S(2)}, u32[]{:S(2)}) collective-permute-start(bf16[64,4224]{1,0:T(8,128)(2,1)} %collective-permute-done.6.refs_4_.refs_12_), channel_id=1, source_target_pairs={{32,0},{64,32},{96,64},{128,96},{160,128},{192,160},{224,192},{0,2... | collective-permute-start | bytes 1622024 | tf_op jit(solution)/shard_map/ppermute | solution.py:353
  142.1 18.9 %collective-permute-start.11 = (bf16[1536,256]{1,0:T(8,128)(2,1)}, bf16[1536,256]{1,0:T(8,128)(2,1)}, u32[]{:S(2)}, u32[]{:S(2)}) collective-permute-start(bf16[1536,256]{1,0:T(8,128)(2,1)} %collective-permute-done.2.refs_1_), channel_id=1, source_target_pairs={{0,256},{256,0},{1,257},{257,1},{2,258},{258,2},{3,259},{259,3},{4... | collective-permute-start | bytes 2359304 | tf_op jit(solution)/shard_map/ppermute | solution.py:360
  151.7 13.3 %collective-permute-start.10 = (bf16[64,4224]{1,0:T(8,128)(2,1)}, bf16[64,4224]{1,0:T(8,128)(2,1)S(1)}, u32[]{:S(2)}, u32[]{:S(2)}) collective-permute-start(bf16[64,4224]{1,0:T(8,128)(2,1)} %collective-permute-done.8.refs_0_.refs_13_), channel_id=1, source_target_pairs={{0,32},{32,64},{64,96},{96,128},{128,160},{160,192},{192,224},{224... | collective-permute-start | bytes 1622024 | tf_op jit(solution)/shard_map/ppermute | solution.py:363
  172.2 24.9 %all-to-all-start.6 = ((bf16[8,192,256]{2,1,0:T(8,128)(2,1)}), bf16[8,192,256]{2,1,0:T(8,128)(2,1)S(1)}, u32[]{:S(2)}, u32[]{:S(2)}) async-start(bf16[8,192,256]{2,1,0:T(8,128)(2,1)} %get-tuple-element.42), calls=%async_computation.6 | async-start | bytes 1572864 | tf_op jit(solution)/shard_map/all_to_all | solution.py:19
  237.9 10.5 %all-to-all-start.8 = ((bf16[8,4,1024]{2,1,0:T(4,128)(2,1)}), bf16[8,4,1024]{2,1,0:T(4,128)(2,1)S(1)}, u32[]{:S(2)}, u32[]{:S(2)}) async-start(bf16[8,4,1024]{2,1,0:T(4,128)(2,1)} %reshape.150), calls=%async_computation.8 | async-start | bytes 131072 | tf_op jit(solution)/shard_map/all_to_all | solution.py:19
  (2 other events, 1.8 us)

commit v8 on v7

--- a/solution.py
+++ b/solution.py
@@ -33,26 +33,88 @@
     )
 
 
-def route(expert_ids, expert_gates, expert_count, slots):
-    flat_ids = expert_ids.reshape(-1)
-    tok_rows, top_count = expert_ids.shape
-    owner_row = jnp.arange(tok_rows * top_count, dtype=jnp.int32) // top_count
-    earlier = (flat_ids[:, None] == flat_ids[None, :]) & (owner_row[None, :] < owner_row[:, None])
-    slot_ids = jnp.sum(earlier.astype(jnp.int32), axis=1).reshape(tok_rows, top_count)
-    expert_hit = (
-        expert_ids[None, None] == jnp.arange(expert_count, dtype=jnp.int32)[:, None, None, None]
-    )
-    slot_hit = slot_ids[None, None] == jnp.arange(slots, dtype=jnp.int32)[None, :, None, None]
-    hits = expert_hit & slot_hit
-    table = jnp.any(hits, axis=3).astype(jnp.bfloat16)
-    mix = jnp.sum(jnp.where(hits, expert_gates[None, None], 0.0), axis=3)
-    return table.reshape(expert_count * slots, tok_rows), mix.reshape(
-        expert_count * slots, tok_rows
-    )
-
-
 def whole(shape):
     return pl.BlockSpec(shape, lambda *_: (0,) * len(shape))
+
+
+def dispatch_kernel(place_ref, parts_ref, gain_ref, mixed_ref, out_ref):
+    parts, tokens, wide = parts_ref.shape
+    peers, rows = out_ref.shape[0], out_ref.shape[1]
+    width = wide - EXTRA
+    tok_dev = tokens // parts
+    top = EXTRA // 4
+    whole_sum = parts_ref[0].astype(jnp.float32)
+    for part in range(1, parts):
+        whole_sum += parts_ref[part].astype(jnp.float32)
+    mixed = whole_sum[:, :width].astype(jnp.bfloat16)
+    for part in range(parts):
+
+        @pl.when(place_ref[0] == part)
+        def _():
+            mixed_ref[...] = mixed[part * tok_dev : (part + 1) * tok_dev, :]
+
+    stream = mixed.astype(jnp.float32)
+    mean_sq = jnp.mean(stream * stream, axis=1, keepdims=True)
+    normed = (stream * lax.rsqrt(mean_sq + EPS_NORM) * gain_ref[...]).astype(jnp.bfloat16)
+
+    extra = whole_sum[:, width:]
+    named = extra[:, :top]
+    high, low = extra[:, top : 2 * top], extra[:, 2 * top : 3 * top]
+    place = place_ref[0]
+    hits, highs, lows = [], [], []
+    for peer in range(peers):
+        expert = peer // 2 * (2 * parts) + 2 * place + peer % 2
+        match = named == (expert + 1).astype(jnp.float32)
+        hits.append(jnp.sum(match.astype(jnp.float32), axis=1, keepdims=True))
+        highs.append(jnp.sum(jnp.where(match, high, 0.0), axis=1, keepdims=True))
+        lows.append(jnp.sum(jnp.where(match, low, 0.0), axis=1, keepdims=True))
+    token = lax.broadcasted_iota(jnp.int32, (tokens, tokens), 0)
+    other = lax.broadcasted_iota(jnp.int32, (tokens, tokens), 1)
+    earlier = (token // tok_dev == other // tok_dev) & (other < token)
+    row = lax.broadcasted_iota(jnp.int32, (rows, tokens), 0)
+    column = lax.broadcasted_iota(jnp.int32, (rows, tokens), 1)
+    from_block = row // 2 == column // tok_dev
+    lane = lax.broadcasted_iota(jnp.int32, (tokens, EXTRA), 1)
+    local = lax.broadcasted_iota(jnp.int32, (tokens, EXTRA), 0) % tok_dev
+    goal = place_ref[1] * tok_dev + local
+    for peer in range(peers):
+        hit = hits[peer]
+        hit_row = jnp.sum(jnp.where(token == other, hit, 0.0), axis=0, keepdims=True)
+        rank = jnp.sum(jnp.where(earlier, hit_row, 0.0), axis=1, keepdims=True)
+        rank_row = jnp.sum(jnp.where(token == other, rank, 0.0), axis=0, keepdims=True)
+        take = from_block & (hit_row > 0.5) & (rank_row == (row % 2).astype(jnp.float32))
+        take = jnp.where(take, 1.0, 0.0).astype(jnp.bfloat16)
+        sent = jnp.dot(take, normed, preferred_element_type=jnp.float32)
+        out_ref[peer, :, :width] = sent.astype(jnp.bfloat16)
+        tag = jnp.where(lane == goal, highs[peer], 0.0)
+        tag += jnp.where(lane == goal + 32, lows[peer], 0.0)
+        tag = jnp.dot(take, tag.astype(jnp.bfloat16), preferred_element_type=jnp.float32)
+        out_ref[peer, :, width:] = tag.astype(jnp.bfloat16)
+
+
+def dispatch_rows(place, parts, gain, peers):
+    count, tokens, wide = parts.shape
+    width = wide - EXTRA
+    out = (peers, 2 * count, wide)
+    return pl.pallas_call(
+        dispatch_kernel,
+        out_shape=(
+            jax.ShapeDtypeStruct((tokens // count, width), jnp.bfloat16),
+            jax.ShapeDtypeStruct(out, jnp.bfloat16),
+        ),
+        grid_spec=pltpu.PrefetchScalarGridSpec(
+            num_scalar_prefetch=1,
+            grid=(1,),
+            in_specs=[whole(parts.shape), whole((1, width))],
+            out_specs=(whole((tokens // count, width)), whole(out)),
+        ),
+        compiler_params=pltpu.CompilerParams(vmem_limit_bytes=24 * 2**20),
+        cost_estimate=pl.CostEstimate(
+            flops=2 * peers * 2 * count * tokens * wide,
+            bytes_accessed=4 * peers * count * wide,
+            transcendentals=0,
+        ),
+    )(place, parts, gain.reshape(1, width))
 
 
 def weight_rows(zl_ref, refs, weight):
@@ -224,7 +286,9 @@
     blocks = peers // 2
     each = count // blocks
     to = lax.broadcasted_iota(jnp.int32, (count, count), 0)
-    source = (to % (2 * blocks)) // 2 * each + to // (2 * blocks) * 2 + to % 2
+    owner = to // (2 * blocks)
+    source = owner // 8 * 16 + owner % 2 * 8 + owner % 8 // 2 * 2 + to % 2
+    source = (to % (2 * blocks)) // 2 * each + source
     column = lax.broadcasted_iota(jnp.int32, (count, count), 1)
     move = jnp.where(source == column, 1.0, 0.0).astype(jnp.bfloat16)
     for copy in moves:
@@ -286,7 +350,6 @@
     ctx_count, expert_count = n_zl * n_y, n_x * n_zh * n_co
     width = residual.shape[1]
     tok_dev, top_count = expert_ids.shape
-    slots = 2
     tok_block = queries.shape[0]
     heads = queries.shape[1] // HEAD_WIDTH
     swap_z = [(i, i ^ 1) for i in range(n_zl)]
@@ -299,15 +362,6 @@
     mine = lax.dynamic_slice_in_dim(mine, x_pos * HEAD_WIDTH, HEAD_WIDTH, 1)
     gathered = spread(mine, CTX, ctx_count).reshape(ctx_count * tok_block, HEAD_WIDTH)
 
-    table, mix = route(expert_ids, expert_gates, expert_count, slots)
-    places = n_y * tok_dev
-    own_place = jnp.arange(places, dtype=jnp.int32) // tok_dev == y_pos
-    mix = jnp.where(own_place[None, :], jnp.tile(mix, (1, n_y)), 0.0)
-    mix_high = mix.astype(jnp.bfloat16)
-    mix_low = (mix - mix_high.astype(jnp.float32)).astype(jnp.bfloat16)
-    extra = jnp.concatenate([mix_high, mix_low], axis=1)
-    extra = jnp.pad(extra, ((0, 0), (0, EXTRA - extra.shape[1])))
-    gathered, table, extra = lax.optimization_barrier((gathered, table, extra))
     key_all, value_all = spread(gathered, "co", n_co)
 
     order = np.arange(tok_block).reshape(n_x, n_zh, n_co, tok_dev).transpose(2, 0, 1, 3)
@@ -329,20 +383,23 @@
     partial = jnp.dot(heads_out, out_weight, preferred_element_type=jnp.float32)
     partial = partial.astype(jnp.bfloat16).reshape(n_co, tok_block // n_co, width)
     partial = added(exchange(partial, "co")).astype(jnp.bfloat16)
-    partial = added(exchange(partial.reshape(n_x, -1, width), "x")).astype(jnp.bfloat16)
+    partial = added(exchange(partial.reshape(n_x, -1, width), "x"))
     partial, gate_z, up_z, down_own = lax.optimization_barrier((partial, gate_z, up_z, down_own))
     down_y = lax.ppermute(down_own, "y", swap_y)
-    projected = added(exchange(partial.reshape(n_zh, tok_dev, width), "zh"))
-    mixed = (residual.astype(jnp.float32) + projected).astype(jnp.bfloat16)
-
-    stream = mixed.astype(jnp.float32)
-    mean_sq = jnp.mean(stream * stream, axis=1, keepdims=True)
-    normed = (stream * lax.rsqrt(mean_sq + EPS_NORM) * norm_gain[None, :]).astype(jnp.bfloat16)
-
-    outgoing = jnp.dot(table, normed, preferred_element_type=jnp.float32).astype(jnp.bfloat16)
-    outgoing = jnp.concatenate([outgoing, extra], axis=1)
-    arrived = exchange(outgoing.reshape(expert_count, slots, width + EXTRA), EXP)
-    arrived = arrived.reshape(expert_count * slots, width + EXTRA)
+    high = expert_gates.astype(jnp.bfloat16)
+    low = (expert_gates - high.astype(jnp.float32)).astype(jnp.bfloat16)
+    room = ((0, 0), (0, EXTRA // 4 - top_count))
+    own = [(expert_ids + 1).astype(jnp.bfloat16), high, low, jnp.zeros_like(low)]
+    own = jnp.concatenate([residual] + [jnp.pad(part, room) for part in own], axis=1)
+    mine = jnp.arange(n_zh, dtype=jnp.int32)[:, None, None] == lax.axis_index("zh")
+    own = jnp.where(mine, own[None], 0).reshape(n_zh * tok_dev, width + EXTRA)
+    partial = jnp.pad(partial, ((0, 0), (0, EXTRA))) + own.astype(jnp.float32)
+    parts = spread(partial.astype(jnp.bfloat16), "zh", n_zh)
+
+    places = n_y * tok_dev
+    place = jnp.stack([lax.axis_index("zh"), y_pos])
+    mixed, outgoing = dispatch_rows(place, parts, norm_gain, n_x * n_co)
+    arrived = exchange(outgoing, ("x", "co")).reshape(-1, width + EXTRA)
 
     arrived, down_own, down_y = lax.optimization_barrier((arrived, down_own, down_y))
     after = [(i, (i + 1) % n_y) for i in range(n_y)]

time: 251 us -> 244 us (0.972)
  blocking collectives: 73.9 us -> 41.8 us
  waiting for transfers between devices: 67.9 us -> 82.4 us
  starting transfers between devices: 63.4 us -> 75.2 us
    all_to_all x5 -> x3, blocking collectives: 73.9 us -> 41.8 us  [exchange(): return lax.all_to_all(pieces, axis, 0, 0, tiled=True)]
    all_to_all x4 -> x6, waiting for transfers between devices: 44.2 us -> 62.1 us  [exchange(): return lax.all_to_all(pieces, axis, 0, 0, tiled=True)]
    all_to_all x4 -> x6, starting transfers between devices: 24.9 us -> 36.1 us  [exchange(): return lax.all_to_all(pieces, axis, 0, 0, tiled=True)]
    ppermute x1, waiting for transfers between devices: 2.69 us -> 0.01 us  [on_device(): down_y = lax.ppermute(down_own, 'y', swap_y)]
  transfers between devices with their start and end apart: 16 -> 18, of which waited for: 11 -> 11; matrix products, arithmetic and copies ran while one was open for 5% -> 4% of each run, Pallas kernels for 4% -> 5%
where the time goes in v8:
time: 244 us; the launch traced here: 243 us
  waiting for transfers between devices  82.4 us (34%)
  starting transfers between devices  75.2 us (31%)
  blocking collectives  41.8 us (17%)
  Pallas kernels  25.6 us (10%)
  local copies, waits for them, and re-layouts  8.79 us (4%)
  other arithmetic  6.38 us (3%)
    all_to_all x6, waiting for transfers between devices, exchange(): return lax.all_to_all(pieces, axis, 0, 0, tiled=True)  62.1 us
    all_to_all x3, blocking collectives, exchange(): return lax.all_to_all(pieces, axis, 0, 0, tiled=True)  41.8 us
    all_to_all x6, starting transfers between devices, exchange(): return lax.all_to_all(pieces, axis, 0, 0, tiled=True)  36.1 us
    ppermute x6, starting transfers between devices, onward(): return (lax.ppermute(left, 'y', after), lax.ppermute(right, 'y', before))  20.3 us
    ppermute x6, waiting for transfers between devices, onward(): return (lax.ppermute(left, 'y', after), lax.ppermute(right, 'y', before))  12.1 us
    pallas_call x2, Pallas kernels, first_hidden(): pl.pallas_call(first_kernel, out_shape=jax.ShapeDtypeStruct((2 * units, c...  10.6 us
    pallas_call x1, Pallas kernels, last_hidden(): pl.pallas_call(lambda *refs: last_kernel(len(blocks), len(first), *refs),...  6.41 us
    pallas_call x1, Pallas kernels, down_slots(): pl.pallas_call(down_kernel, out_shape=jax.ShapeDtypeStruct(out, jnp.bfloa...  6.4 us
  transfers between devices with their start and end apart: 18, of which 11 were waited for; matrix products, arithmetic and copies ran while one was open for 4% of the time, Pallas kernels for 5%

profile of v8, /device:TPU:1, one launch (start us, length us, event | category | flops | bytes accessed | tf_op | source)
XLA Modules:
  0.0 242.9 jit_solution(8909594650262400472)
XLA Ops:
  2.5 9.6 %all-to-all-start = ((bf16[16,128,128]{2,1,0:T(8,128)(2,1)}), bf16[16,128,128]{2,1,0:T(8,128)(2,1)S(1)}, u32[]{:S(2)}, u32[]{:S(2)}) async-start(bf16[16,128,128]{2,1,0:T(8,128)(2,1)} %broadcast_in_dim.58), calls=%async_computation | async-start | bytes 1048576 | tf_op jit(solution)/shard_map/all_to_all | solution.py:19
  19.1 6.7 %all-to-all-done = bf16[16,128,128]{2,1,0:T(8,128)(2,1)S(1)} async-done(((bf16[16,128,128]{2,1,0:T(8,128)(2,1)}), bf16[16,128,128]{2,1,0:T(8,128)(2,1)S(1)}, u32[]{:S(2)}, u32[]{:S(2)}) %all-to-all-start) | async-done | bytes 524320 | tf_op jit(solution)/shard_map/all_to_all | solution.py:19
  25.9 7.1 %all_to_all.45 = bf16[2,2048,128]{2,1,0:T(8,128)(2,1)S(1)} all-to-all(bf16[2,2048,128]{2,1,0:T(8,128)(2,1)S(1)} %broadcast_in_dim.60), channel_id=1, replica_groups=mesh['zl'=2,'y'=8,'x'=4,'zh'=4,'co'=2] {'co'}, dimensions={0} | all-to-all | bytes 2097152 | tf_op jit(solution)/shard_map/all_to_all | solution.py:19
  35.1 5.5 %all_to_all.46 = bf16[2,64,4096]{2,1,0:T(8,128)(2,1)} all-to-all(bf16[2,64,4096]{2,1,0:T(8,128)(2,1)S(1)} %bitcast.57), channel_id=1, replica_groups=mesh['zl'=2,'y'=8,'x'=4,'zh'=4,'co'=2] {'co'}, dimensions={0} | all-to-all | bytes 2097152 | tf_op jit(solution)/shard_map/all_to_all | solution.py:19
  42.9 4.1 %all-to-all-start.3 = ((bf16[4,16,4096]{2,1,0:T(8,128)(2,1)}), bf16[4,16,4096]{2,1,0:T(8,128)(2,1)S(1)}, u32[]{:S(2)}, u32[]{:S(2)}) async-start(bf16[4,16,4096]{2,1,0:T(8,128)(2,1)} %bitcast.61), calls=%async_computation.3 | async-start | bytes 1048576 | tf_op jit(solution)/shard_map/all_to_all | solution.py:19
  49.6 6.4 %all-to-all-done.3 = bf16[4,16,4096]{2,1,0:T(8,128)(2,1)S(1)} async-done(((bf16[4,16,4096]{2,1,0:T(8,128)(2,1)}), bf16[4,16,4096]{2,1,0:T(8,128)(2,1)S(1)}, u32[]{:S(2)}, u32[]{:S(2)}) %all-to-all-start.3) | async-done | bytes 524320 | tf_op jit(solution)/shard_map/all_to_all | solution.py:19
  58.1 9.1 %all-to-all-start.4 = ((bf16[4,16,4224]{2,1,0:T(8,128)(2,1)}), bf16[4,16,4224]{2,1,0:T(8,128)(2,1)S(1)}, u32[]{:S(2)}, u32[]{:S(2)}) async-start(bf16[4,16,4224]{2,1,0:T(8,128)(2,1)} %broadcast_in_dim.69), calls=%async_computation.4 | async-start | bytes 1081344 | tf_op jit(solution)/shard_map/all_to_all | solution.py:19
  70.1 12.2 %all-to-all-done.4.parts_ref = bf16[4,16,4224]{2,1,0:T(8,128)(2,1)S(1)} async-done(((bf16[4,16,4224]{2,1,0:T(8,128)(2,1)}), bf16[4,16,4224]{2,1,0:T(8,128)(2,1)S(1)}, u32[]{:S(2)}, u32[]{:S(2)}) %all-to-all-start.4) | async-done | bytes 540704 | tf_op jit(solution)/shard_map/all_to_all | solution.py:19
  84.5 4.8 %all-to-all-start.5 = ((bf16[8,8,4224]{2,1,0:T(8,128)(2,1)}), bf16[8,8,4224]{2,1,0:T(8,128)(2,1)S(1)}, u32[]{:S(2)}, u32[]{:S(2)}) async-start(bf16[8,8,4224]{2,1,0:T(8,128)(2,1)} %get-tuple-element.25), calls=%async_computation.5 | async-start | bytes 1081344 | tf_op jit(solution)/shard_map/all_to_all | solution.py:19
  89.4 9.7 %all-to-all-done.5 = bf16[8,8,4224]{2,1,0:T(8,128)(2,1)S(1)} async-done(((bf16[8,8,4224]{2,1,0:T(8,128)(2,1)}), bf16[8,8,4224]{2,1,0:T(8,128)(2,1)S(1)}, u32[]{:S(2)}, u32[]{:S(2)}) %all-to-all-start.5) | async-done | bytes 540704 | tf_op jit(solution)/shard_map/all_to_all | solution.py:19
  108.6 6.4 %collective-permute-done.3.refs_1_.refs_9_ = bf16[64,4224]{1,0:T(8,128)(2,1)S(1)} collective-permute-done((bf16[64,4224]{1,0:T(8,128)(2,1)S(1)}, bf16[64,4224]{1,0:T(8,128)(2,1)S(1)}, u32[]{:S(2)}, u32[]{:S(2)}) %collective-permute-start.3) | collective-permute-done | bytes 540704 | tf_op jit(solution)/shard_map/ppermute | solution.py:410
  117.0 4.6 %collective-permute-start.6 = (bf16[64,4224]{1,0:T(8,128)(2,1)S(1)}, bf16[64,4224]{1,0:T(8,128)(2,1)}, u32[]{:S(2)}, u32[]{:S(2)}) collective-permute-start(bf16[64,4224]{1,0:T(8,128)(2,1)S(1)} %collective-permute-done.5.refs_2_.refs_10_), channel_id=1, source_target_pairs={{32,0},{64,32},{96,64},{128,96},{160,128},{192,160},{224,192},{0,2... | collective-permute-start | bytes 1622024 | tf_op jit(solution)/shard_map/ppermute | solution.py:410
  125.4 4.9 %collective-permute-done.4.refs_3_.refs_11_ = bf16[64,4224]{1,0:T(8,128)(2,1)} collective-permute-done((bf16[64,4224]{1,0:T(8,128)(2,1)S(1)}, bf16[64,4224]{1,0:T(8,128)(2,1)}, u32[]{:S(2)}, u32[]{:S(2)}) %collective-permute-start.4) | collective-permute-done | bytes 540704 | tf_op jit(solution)/shard_map/ppermute | solution.py:410
  133.4 5.0 %collective-permute-start.9 = (bf16[64,4224]{1,0:T(8,128)(2,1)}, bf16[64,4224]{1,0:T(8,128)(2,1)}, u32[]{:S(2)}, u32[]{:S(2)}) collective-permute-start(bf16[64,4224]{1,0:T(8,128)(2,1)} %collective-permute-done.6.refs_4_.refs_12_), channel_id=1, source_target_pairs={{32,0},{64,32},{96,64},{128,96},{160,128},{192,160},{224,192},{0,2... | collective-permute-start | bytes 1622024 | tf_op jit(solution)/shard_map/ppermute | solution.py:410
  142.2 5.9 %shard_map.132.refs_6_ = bf16[192,320]{1,0:T(8,128)(2,1)} custom-call(s32[1]{0:T(128)} %bitcast.20.zl_ref, bf16[64,4224]{1,0:T(8,128)(2,1)} %bitcast.55, bf16[64,4224]{1,0:T(8,128)(2,1)} %copy-done.5, bf16[64,4224]{1,0:T(8,128)(2,1)} %copy-done.6, bf16[64,4224]{1,0:T(8,128)(2,1)} %collective-permute-done.4.refs_3_.refs_11_, ...), custom_call_target="tpu_custom_call" | custom-call | flops 1006632960 | bytes 5767168 | tf_op jit(solution)/shard_map/pallas_call | solution.py:224
  148.1 3.9 %collective-permute-start.10 = (bf16[64,4224]{1,0:T(8,128)(2,1)}, bf16[64,4224]{1,0:T(8,128)(2,1)S(1)}, u32[]{:S(2)}, u32[]{:S(2)}) collective-permute-start(bf16[64,4224]{1,0:T(8,128)(2,1)} %collective-permute-done.8.refs_0_.refs_13_), channel_id=1, source_target_pairs={{0,32},{32,64},{64,96},{96,128},{128,160},{160,192},{192,224},{224... | collective-permute-start | bytes 1622024 | tf_op jit(solution)/shard_map/ppermute | solution.py:420
  152.6 4.7 %shard_map.133.refs_7_ = bf16[192,128]{1,0:T(8,128)(2,1)} custom-call(s32[1]{0:T(128)} %bitcast.20.zl_ref, bf16[64,4224]{1,0:T(8,128)(2,1)} %collective-permute-done.8.refs_0_.refs_13_, bf16[64,4224]{1,0:T(8,128)(2,1)} %collective-permute-done.9.refs_1_.refs_14_, bf16[96,4096]{1,0:T(8,128)(2,1)} %bitcast.47, bf16[96,4096]{1,0:T(8,128)(2,1)} %copy-done.2, ...), custom_call_target="tpu_custom_call" | custom-call | flops 402653184 | bytes 4194304 | tf_op jit(solution)/shard_map/pallas_call | solution.py:224
  157.2 4.3 %collective-permute-done.10.refs_1_.refs_15_ = bf16[64,4224]{1,0:T(8,128)(2,1)S(1)} collective-permute-done((bf16[64,4224]{1,0:T(8,128)(2,1)}, bf16[64,4224]{1,0:T(8,128)(2,1)S(1)}, u32[]{:S(2)}, u32[]{:S(2)}) %collective-permute-start.10) | collective-permute-done | bytes 540704 | tf_op jit(solution)/shard_map/ppermute | solution.py:420
  162.4 6.4 %shard_map.134 = (bf16[8,192,256]{2,1,0:T(8,128)(2,1)}, bf16[512,128]{1,0:T(8,128)(2,1)}) custom-call(s32[2]{0:T(128)} %pad_add_fusion.1.refs_0_, bf16[64,4224]{1,0:T(8,128)(2,1)} %copy-done.7, bf16[96,4096]{1,0:T(8,128)(2,1)} %bitcast.48, bf16[96,4096]{1,0:T(8,128)(2,1)} %copy-done.2, bf16[96,4096]{1,0:T(8,128)(2,1)} %bitcast.52, ...), custom_call_target="tpu_custom_call" | custom-call | flops 201326592 | bytes 3670016 | tf_op jit(solution)/shard_map/pallas_call | solution.py:244
  168.8 5.1 %all-to-all-start.6 = ((bf16[8,192,256]{2,1,0:T(8,128)(2,1)}), bf16[8,192,256]{2,1,0:T(8,128)(2,1)S(1)}, u32[]{:S(2)}, u32[]{:S(2)}) async-start(bf16[8,192,256]{2,1,0:T(8,128)(2,1)} %get-tuple-element.40), calls=%async_computation.6 | async-start | bytes 1572864 | tf_op jit(solution)/shard_map/all_to_all | solution.py:19
  173.9 20.0 %all-to-all-done.6.hidden_ref = bf16[8,192,256]{2,1,0:T(8,128)(2,1)S(1)} async-done(((bf16[8,192,256]{2,1,0:T(8,128)(2,1)}), bf16[8,192,256]{2,1,0:T(8,128)(2,1)S(1)}, u32[]{:S(2)}, u32[]{:S(2)}) %all-to-all-start.6) | async-done | bytes 786464 | tf_op jit(solution)/shard_map/all_to_all | solution.py:19
  194.8 6.4 %shard_map.135 = bf16[256,1152]{1,0:T(8,128)(2,1)} custom-call(s32[1]{0:T(128)} %bitcast.19.half_ref, bf16[8,192,256]{2,1,0:T(8,128)(2,1)} %copy-done.4, bf16[512,128]{1,0:T(8,128)(2,1)} %get-tuple-element.41.extra_ref, bf16[1536,256]{1,0:T(8,128)(2,1)} %bitcast.64, bf16[1536,256]{1,0:T(8,128)(2,1)} %collective-permute-done.2.refs_1_, ...), custom_call_target="tpu_custom_call" | custom-call | flops 805306368 | bytes 3145728 | tf_op jit(solution)/shard_map/pallas_call | solution.py:311
  201.2 29.2 %all_to_all.47 = bf16[32,8,1152]{2,1,0:T(8,128)(2,1)S(1)} all-to-all(bf16[32,8,1152]{2,1,0:T(8,128)(2,1)} %bitcast.58), channel_id=1, replica_groups=mesh['zl'=2,'y'=8,'x'=4,'zh'=4,'co'=2] {'x','zh','co'}, dimensions={0} | all-to-all | bytes 1179648 | tf_op jit(solution)/shard_map/all_to_all | solution.py:19
  234.6 7.1 %all-to-all-done.8 = bf16[8,4,1024]{2,1,0:T(4,128)(2,1)S(1)} async-done(((bf16[8,4,1024]{2,1,0:T(4,128)(2,1)}), bf16[8,4,1024]{2,1,0:T(4,128)(2,1)S(1)}, u32[]{:S(2)}, u32[]{:S(2)}) %all-to-all-start.8) | async-done | bytes 65568 | tf_op jit(solution)/shard_map/all_to_all | solution.py:19
  (85 shorter events, 52.7 us)
Async XLA Ops:
  0.6 33.9 %copy-start = (bf16[256,4096]{1,0:T(8,128)(2,1)S(1)}, bf16[256,4096]{1,0:T(8,128)(2,1)}, u32[]{:S(2)}) copy-start(bf16[256,4096]{1,0:T(8,128)(2,1)} %param.16) | copy-start | bytes 6291460
  2.5 23.3 %all-to-all-start = ((bf16[16,128,128]{2,1,0:T(8,128)(2,1)}), bf16[16,128,128]{2,1,0:T(8,128)(2,1)S(1)}, u32[]{:S(2)}, u32[]{:S(2)}) async-start(bf16[16,128,128]{2,1,0:T(8,128)(2,1)} %broadcast_in_dim.58), calls=%async_computation | async-start | bytes 1048576 | tf_op jit(solution)/shard_map/all_to_all | solution.py:19
  12.1 44.0 %collective-permute-start = (bf16[96,4096]{1,0:T(8,128)(2,1)}, bf16[96,4096]{1,0:T(8,128)(2,1)S(1)}, u32[]{:S(2)}, u32[]{:S(2)}) collective-permute-start(bf16[96,4096]{1,0:T(8,128)(2,1)} %bitcast.45), channel_id=1, source_target_pairs={{0,256},{256,0},{1,257},{257,1},{2,258},{258,2},{3,259},{259,3},{4... | collective-permute-start | bytes 2359304 | tf_op jit(solution)/shard_map/ppermute | solution.py:359
  15.4 40.7 %collective-permute-start.1 = (bf16[96,4096]{1,0:T(8,128)(2,1)}, bf16[96,4096]{1,0:T(8,128)(2,1)}, u32[]{:S(2)}, u32[]{:S(2)}) collective-permute-start(bf16[96,4096]{1,0:T(8,128)(2,1)} %bitcast.49), channel_id=1, source_target_pairs={{0,256},{256,0},{1,257},{257,1},{2,258},{258,2},{3,259},{259,3},{4... | collective-permute-start | bytes 2359304 | tf_op jit(solution)/shard_map/ppermute | solution.py:359
  42.9 39.4 %copy-start.1 = (f32[4096]{0:T(1024)S(1)}, f32[4096]{0:T(1024)}, u32[]{:S(2)}) copy-start(f32[4096]{0:T(1024)} %param.17) | copy-start | bytes 49156
  42.9 13.0 %all-to-all-start.3 = ((bf16[4,16,4096]{2,1,0:T(8,128)(2,1)}), bf16[4,16,4096]{2,1,0:T(8,128)(2,1)S(1)}, u32[]{:S(2)}, u32[]{:S(2)}) async-start(bf16[4,16,4096]{2,1,0:T(8,128)(2,1)} %bitcast.61), calls=%async_computation.3 | async-start | bytes 1048576 | tf_op jit(solution)/shard_map/all_to_all | solution.py:19
  56.1 86.1 %copy-start.2 = (bf16[96,4096]{1,0:T(8,128)(2,1)}, bf16[96,4096]{1,0:T(8,128)(2,1)S(1)}, u32[]{:S(2)}) copy-start(bf16[96,4096]{1,0:T(8,128)(2,1)S(1)} %collective-permute-done.refs_6_.refs_3_) | copy-start | bytes 2359300
  58.1 24.3 %all-to-all-start.4 = ((bf16[4,16,4224]{2,1,0:T(8,128)(2,1)}), bf16[4,16,4224]{2,1,0:T(8,128)(2,1)S(1)}, u32[]{:S(2)}, u32[]{:S(2)}) async-start(bf16[4,16,4224]{2,1,0:T(8,128)(2,1)} %broadcast_in_dim.69), calls=%async_computation.4 | async-start | bytes 1081344 | tf_op jit(solution)/shard_map/all_to_all | solution.py:19
  67.2 22.2 %collective-permute-start.2 = (bf16[1536,256]{1,0:T(8,128)(2,1)}, bf16[1536,256]{1,0:T(8,128)(2,1)}, u32[]{:S(2)}, u32[]{:S(2)}) collective-permute-start(bf16[1536,256]{1,0:T(8,128)(2,1)} %bitcast.62), channel_id=1, source_target_pairs={{0,32},{32,0},{64,96},{96,64},{128,160},{160,128},{192,224},{224,1... | collective-permute-start | bytes 2359304 | tf_op jit(solution)/shard_map/ppermute | solution.py:388
  84.5 14.5 %all-to-all-start.5 = ((bf16[8,8,4224]{2,1,0:T(8,128)(2,1)}), bf16[8,8,4224]{2,1,0:T(8,128)(2,1)S(1)}, u32[]{:S(2)}, u32[]{:S(2)}) async-start(bf16[8,8,4224]{2,1,0:T(8,128)(2,1)} %get-tuple-element.25), calls=%async_computation.5 | async-start | bytes 1081344 | tf_op jit(solution)/shard_map/all_to_all | solution.py:19
  99.0 43.1 %copy-start.3 = (bf16[8,8,4224]{2,1,0:T(8,128)(2,1)}, bf16[8,8,4224]{2,1,0:T(8,128)(2,1)S(1)}, u32[]{:S(2)}) copy-start(bf16[8,8,4224]{2,1,0:T(8,128)(2,1)S(1)} %all-to-all-done.5) | copy-start | bytes 1622020
  99.1 16.0 %collective-permute-start.3 = (bf16[64,4224]{1,0:T(8,128)(2,1)S(1)}, bf16[64,4224]{1,0:T(8,128)(2,1)S(1)}, u32[]{:S(2)}, u32[]{:S(2)}) collective-permute-start(bf16[64,4224]{1,0:T(8,128)(2,1)S(1)} %bitcast.53), channel_id=1, source_target_pairs={{0,32},{32,64},{64,96},{96,128},{128,160},{160,192},{192,224},{224... | collective-permute-start | bytes 1622024 | tf_op jit(solution)/shard_map/ppermute | solution.py:410
  101.9 15.1 %collective-permute-start.5 = (bf16[64,4224]{1,0:T(8,128)(2,1)S(1)}, bf16[64,4224]{1,0:T(8,128)(2,1)S(1)}, u32[]{:S(2)}, u32[]{:S(2)}) collective-permute-start(bf16[64,4224]{1,0:T(8,128)(2,1)S(1)} %bitcast.54), channel_id=1, source_target_pairs={{32,0},{64,32},{96,64},{128,96},{160,128},{192,160},{224,192},{0,2... | collective-permute-start | bytes 1622024 | tf_op jit(solution)/shard_map/ppermute | solution.py:410
  105.5 19.8 %collective-permute-start.7 = (bf16[1536,256]{1,0:T(8,128)(2,1)}, bf16[1536,256]{1,0:T(8,128)(2,1)S(1)}, u32[]{:S(2)}, u32[]{:S(2)}) collective-permute-start(bf16[1536,256]{1,0:T(8,128)(2,1)} %bitcast.63), channel_id=1, source_target_pairs={{0,256},{256,0},{1,257},{257,1},{2,258},{258,2},{3,259},{259,3},{4... | collective-permute-start | bytes 2359304 | tf_op jit(solution)/shard_map/ppermute | solution.py:414
  115.1 27.1 %copy-start.5 = (bf16[64,4224]{1,0:T(8,128)(2,1)}, bf16[64,4224]{1,0:T(8,128)(2,1)S(1)}, u32[]{:S(2)}) copy-start(bf16[64,4224]{1,0:T(8,128)(2,1)S(1)} %collective-permute-done.3.refs_1_.refs_9_) | copy-start | bytes 1622020
  115.1 15.2 %collective-permute-start.4 = (bf16[64,4224]{1,0:T(8,128)(2,1)S(1)}, bf16[64,4224]{1,0:T(8,128)(2,1)}, u32[]{:S(2)}, u32[]{:S(2)}) collective-permute-start(bf16[64,4224]{1,0:T(8,128)(2,1)S(1)} %collective-permute-done.3.refs_1_.refs_9_), channel_id=1, source_target_pairs={{0,32},{32,64},{64,96},{96,128},{128,160},{160,192},{192,224},{224... | collective-permute-start | bytes 1622024 | tf_op jit(solution)/shard_map/ppermute | solution.py:410
  117.0 13.3 %copy-start.6 = (bf16[64,4224]{1,0:T(8,128)(2,1)}, bf16[64,4224]{1,0:T(8,128)(2,1)S(1)}, u32[]{:S(2)}) copy-start(bf16[64,4224]{1,0:T(8,128)(2,1)S(1)} %collective-permute-done.5.refs_2_.refs_10_) | copy-start | bytes 1622020
  117.0 14.1 %collective-permute-start.6 = (bf16[64,4224]{1,0:T(8,128)(2,1)S(1)}, bf16[64,4224]{1,0:T(8,128)(2,1)}, u32[]{:S(2)}, u32[]{:S(2)}) collective-permute-start(bf16[64,4224]{1,0:T(8,128)(2,1)S(1)} %collective-permute-done.5.refs_2_.refs_10_), channel_id=1, source_target_pairs={{32,0},{64,32},{96,64},{128,96},{160,128},{192,160},{224,192},{0,2... | collective-permute-start | bytes 1622024 | tf_op jit(solution)/shard_map/ppermute | solution.py:410
  131.1 17.0 %collective-permute-start.8 = (bf16[64,4224]{1,0:T(8,128)(2,1)}, bf16[64,4224]{1,0:T(8,128)(2,1)}, u32[]{:S(2)}, u32[]{:S(2)}) collective-permute-start(bf16[64,4224]{1,0:T(8,128)(2,1)} %collective-permute-done.4.refs_3_.refs_11_), channel_id=1, source_target_pairs={{0,32},{32,64},{64,96},{96,128},{128,160},{160,192},{192,224},{224... | collective-permute-start | bytes 1622024 | tf_op jit(solution)/shard_map/ppermute | solution.py:410
  133.4 14.7 %collective-permute-start.9 = (bf16[64,4224]{1,0:T(8,128)(2,1)}, bf16[64,4224]{1,0:T(8,128)(2,1)}, u32[]{:S(2)}, u32[]{:S(2)}) collective-permute-start(bf16[64,4224]{1,0:T(8,128)(2,1)} %collective-permute-done.6.refs_4_.refs_12_), channel_id=1, source_target_pairs={{32,0},{64,32},{96,64},{128,96},{160,128},{192,160},{224,192},{0,2... | collective-permute-start | bytes 1622024 | tf_op jit(solution)/shard_map/ppermute | solution.py:410
  138.4 18.8 %collective-permute-start.11 = (bf16[1536,256]{1,0:T(8,128)(2,1)}, bf16[1536,256]{1,0:T(8,128)(2,1)}, u32[]{:S(2)}, u32[]{:S(2)}) collective-permute-start(bf16[1536,256]{1,0:T(8,128)(2,1)} %collective-permute-done.2.refs_1_), channel_id=1, source_target_pairs={{0,256},{256,0},{1,257},{257,1},{2,258},{258,2},{3,259},{259,3},{4... | collective-permute-start | bytes 2359304 | tf_op jit(solution)/shard_map/ppermute | solution.py:417
  148.1 13.5 %collective-permute-start.10 = (bf16[64,4224]{1,0:T(8,128)(2,1)}, bf16[64,4224]{1,0:T(8,128)(2,1)S(1)}, u32[]{:S(2)}, u32[]{:S(2)}) collective-permute-start(bf16[64,4224]{1,0:T(8,128)(2,1)} %collective-permute-done.8.refs_0_.refs_13_), channel_id=1, source_target_pairs={{0,32},{32,64},{64,96},{96,128},{128,160},{160,192},{192,224},{224... | collective-permute-start | bytes 1622024 | tf_op jit(solution)/shard_map/ppermute | solution.py:420
  168.8 25.0 %all-to-all-start.6 = ((bf16[8,192,256]{2,1,0:T(8,128)(2,1)}), bf16[8,192,256]{2,1,0:T(8,128)(2,1)S(1)}, u32[]{:S(2)}, u32[]{:S(2)}) async-start(bf16[8,192,256]{2,1,0:T(8,128)(2,1)} %get-tuple-element.40), calls=%async_computation.6 | async-start | bytes 1572864 | tf_op jit(solution)/shard_map/all_to_all | solution.py:19
  231.3 10.5 %all-to-all-start.8 = ((bf16[8,4,1024]{2,1,0:T(4,128)(2,1)}), bf16[8,4,1024]{2,1,0:T(4,128)(2,1)S(1)}, u32[]{:S(2)}, u32[]{:S(2)}) async-start(bf16[8,4,1024]{2,1,0:T(4,128)(2,1)} %reshape.77), calls=%async_computation.8 | async-start | bytes 131072 | tf_op jit(solution)/shard_map/all_to_all | solution.py:19
  (6 other events, 43.7 us)

commit v9 on v8

--- a/solution.py
+++ b/solution.py
@@ -181,10 +181,10 @@
         for extra in extras:
             tags[pl.ds(start, extra.shape[0]), :] = extra[...]
             start += extra.shape[0]
-        held = lax.broadcasted_iota(jnp.int32, (slots, slots), 0)
-        turn = held // each
-        away = jnp.where(turn % 2 == 1, peers - (turn + 1) // 2, turn // 2)
-        goal = (place_ref[1] + away) % peers * each + held % each
+        held = lax.broadcasted_iota(jnp.int32, (slots, 1), 0)
+        turn = held >> (each.bit_length() - 1)
+        away = jnp.where(turn & 1 == 1, peers - ((turn + 1) >> 1), turn >> 1)
+        goal = ((place_ref[1] + away) & (peers - 1)) * each + (held & (each - 1))
         column = lax.broadcasted_iota(jnp.int32, (slots, slots), 1)
         move = jnp.where(goal == column, 1.0, 0.0).astype(jnp.bfloat16)
         hidden = jnp.dot(hidden, move, preferred_element_type=jnp.float32).astype(jnp.bfloat16)
@@ -231,7 +231,7 @@
             out_specs=whole((2 * units, count)),
             scratch_shapes=held_scratch(units, count, step),
         ),
-        compiler_params=pltpu.CompilerParams(vmem_limit_bytes=60 * 2**20),
+        compiler_params=pltpu.CompilerParams(vmem_limit_bytes=24 * 2**20),
         cost_estimate=cost(units, count, width),
     )(zl.reshape(1), *blocks, *weights)
 
@@ -260,7 +260,7 @@
             scratch_shapes=held_scratch(units, count, step)
             + [pltpu.VMEM((slots, EXTRA), jnp.bfloat16)],
         ),
-        compiler_params=pltpu.CompilerParams(vmem_limit_bytes=60 * 2**20),
+        compiler_params=pltpu.CompilerParams(vmem_limit_bytes=24 * 2**20),
         cost_estimate=cost(units, count, width),
     )(place, *blocks, *weights, *first, *every)
 
@@ -285,10 +285,10 @@
         copy.start()
     blocks = peers // 2
     each = count // blocks
-    to = lax.broadcasted_iota(jnp.int32, (count, count), 0)
-    owner = to // (2 * blocks)
-    source = owner // 8 * 16 + owner % 2 * 8 + owner % 8 // 2 * 2 + to % 2
-    source = (to % (2 * blocks)) // 2 * each + source
+    to = lax.broadcasted_iota(jnp.int32, (count, 1), 0)
+    owner = to >> blocks.bit_length()
+    source = (owner >> 3) * 16 + (owner & 1) * 8 + ((owner & 7) >> 1) * 2 + (to & 1)
+    source = ((to & (2 * blocks - 1)) >> 1) * each + source
     column = lax.broadcasted_iota(jnp.int32, (count, count), 1)
     move = jnp.where(source == column, 1.0, 0.0).astype(jnp.bfloat16)
     for copy in moves:

time: 244 us -> 242 us (level)
  Pallas kernels: 25.6 us -> 21.8 us
  other arithmetic: 6.38 us -> 3.56 us
  waiting for transfers between devices: 82.4 us -> 85.1 us
    unnamed x24 -> x28, local copies, waits for them, and re-layouts: 1.83 us -> 5.29 us
  transfers between devices with their start and end apart: 18 -> 18, of which waited for: 11 -> 13; matrix products, arithmetic and copies ran while one was open for 4% -> 2% of each run, Pallas kernels for 5% -> 4%
where the time goes in v9:
time: 242 us; the launch traced here: 241 us
  waiting for transfers between devices  85.1 us (35%)
  starting transfers between devices  76.4 us (32%)
  blocking collectives  40.7 us (17%)
  Pallas kernels  21.8 us (9%)
  local copies, waits for them, and re-layouts  10 us (4%)
  other arithmetic  3.56 us (1%)
    all_to_all x6, waiting for transfers between devices, exchange(): return lax.all_to_all(pieces, axis, 0, 0, tiled=True)  64.1 us
    all_to_all x3, blocking collectives, exchange(): return lax.all_to_all(pieces, axis, 0, 0, tiled=True)  40.7 us
    all_to_all x6, starting transfers between devices, exchange(): return lax.all_to_all(pieces, axis, 0, 0, tiled=True)  35.9 us
    ppermute x6, starting transfers between devices, onward(): return (lax.ppermute(left, 'y', after), lax.ppermute(right, 'y', before))  20.2 us
    ppermute x6, waiting for transfers between devices, onward(): return (lax.ppermute(left, 'y', after), lax.ppermute(right, 'y', before))  10 us
    pallas_call x2, Pallas kernels, first_hidden(): pl.pallas_call(first_kernel, out_shape=jax.ShapeDtypeStruct((2 * units, c...  8.99 us
    pallas_call x1, Pallas kernels, down_slots(): pl.pallas_call(down_kernel, out_shape=jax.ShapeDtypeStruct(out, jnp.bfloa...  6.42 us
    unnamed x28, local copies, waits for them, and re-layouts  5.29 us
  transfers between devices with their start and end apart: 18, of which 13 were waited for; matrix products, arithmetic and copies ran while one was open for 2% of the time, Pallas kernels for 4%

profile of v9, /device:TPU:1, one launch (start us, length us, event | category | flops | bytes accessed | tf_op | source)
XLA Modules:
  0.0 240.5 jit_solution(2424480202029089392)
XLA Ops:
  2.5 9.6 %all-to-all-start = ((bf16[16,128,128]{2,1,0:T(8,128)(2,1)}), bf16[16,128,128]{2,1,0:T(8,128)(2,1)S(1)}, u32[]{:S(2)}, u32[]{:S(2)}) async-start(bf16[16,128,128]{2,1,0:T(8,128)(2,1)} %broadcast_in_dim.58), calls=%async_computation | async-start | bytes 1048576 | tf_op jit(solution)/shard_map/all_to_all | solution.py:19
  19.1 6.7 %all-to-all-done = bf16[16,128,128]{2,1,0:T(8,128)(2,1)S(1)} async-done(((bf16[16,128,128]{2,1,0:T(8,128)(2,1)}), bf16[16,128,128]{2,1,0:T(8,128)(2,1)S(1)}, u32[]{:S(2)}, u32[]{:S(2)}) %all-to-all-start) | async-done | bytes 524320 | tf_op jit(solution)/shard_map/all_to_all | solution.py:19
  25.9 7.1 %all_to_all.45 = bf16[2,2048,128]{2,1,0:T(8,128)(2,1)S(1)} all-to-all(bf16[2,2048,128]{2,1,0:T(8,128)(2,1)S(1)} %broadcast_in_dim.60), channel_id=1, replica_groups=mesh['zl'=2,'y'=8,'x'=4,'zh'=4,'co'=2] {'co'}, dimensions={0} | all-to-all | bytes 2097152 | tf_op jit(solution)/shard_map/all_to_all | solution.py:19
  35.0 4.7 %all_to_all.46 = bf16[2,64,4096]{2,1,0:T(8,128)(2,1)S(1)} all-to-all(bf16[2,64,4096]{2,1,0:T(8,128)(2,1)S(1)} %bitcast.57), channel_id=1, replica_groups=mesh['zl'=2,'y'=8,'x'=4,'zh'=4,'co'=2] {'co'}, dimensions={0} | all-to-all | bytes 2097152 | tf_op jit(solution)/shard_map/all_to_all | solution.py:19
  40.9 4.1 %all-to-all-start.3 = ((bf16[4,16,4096]{2,1,0:T(8,128)(2,1)}), bf16[4,16,4096]{2,1,0:T(8,128)(2,1)S(1)}, u32[]{:S(2)}, u32[]{:S(2)}) async-start(bf16[4,16,4096]{2,1,0:T(8,128)(2,1)} %bitcast.61), calls=%async_computation.3 | async-start | bytes 1048576 | tf_op jit(solution)/shard_map/all_to_all | solution.py:19
  45.3 8.6 %all-to-all-done.3 = bf16[4,16,4096]{2,1,0:T(8,128)(2,1)S(1)} async-done(((bf16[4,16,4096]{2,1,0:T(8,128)(2,1)}), bf16[4,16,4096]{2,1,0:T(8,128)(2,1)S(1)}, u32[]{:S(2)}, u32[]{:S(2)}) %all-to-all-start.3) | async-done | bytes 524320 | tf_op jit(solution)/shard_map/all_to_all | solution.py:19
  55.6 9.1 %all-to-all-start.4 = ((bf16[4,16,4224]{2,1,0:T(8,128)(2,1)}), bf16[4,16,4224]{2,1,0:T(8,128)(2,1)S(1)}, u32[]{:S(2)}, u32[]{:S(2)}) async-start(bf16[4,16,4224]{2,1,0:T(8,128)(2,1)} %broadcast_in_dim.69), calls=%async_computation.4 | async-start | bytes 1081344 | tf_op jit(solution)/shard_map/all_to_all | solution.py:19
  67.8 12.0 %all-to-all-done.4.parts_ref = bf16[4,16,4224]{2,1,0:T(8,128)(2,1)S(1)} async-done(((bf16[4,16,4224]{2,1,0:T(8,128)(2,1)}), bf16[4,16,4224]{2,1,0:T(8,128)(2,1)S(1)}, u32[]{:S(2)}, u32[]{:S(2)}) %all-to-all-start.4) | async-done | bytes 540704 | tf_op jit(solution)/shard_map/all_to_all | solution.py:19
  82.2 5.4 %all-to-all-start.5 = ((bf16[8,8,4224]{2,1,0:T(8,128)(2,1)}), bf16[8,8,4224]{2,1,0:T(8,128)(2,1)S(1)}, u32[]{:S(2)}, u32[]{:S(2)}) async-start(bf16[8,8,4224]{2,1,0:T(8,128)(2,1)} %copy-done.5), calls=%async_computation.5 | async-start | bytes 1081344 | tf_op jit(solution)/shard_map/all_to_all | solution.py:19
  87.5 9.7 %all-to-all-done.5 = bf16[8,8,4224]{2,1,0:T(8,128)(2,1)S(1)} async-done(((bf16[8,8,4224]{2,1,0:T(8,128)(2,1)}), bf16[8,8,4224]{2,1,0:T(8,128)(2,1)S(1)}, u32[]{:S(2)}, u32[]{:S(2)}) %all-to-all-start.5) | async-done | bytes 540704 | tf_op jit(solution)/shard_map/all_to_all | solution.py:19
  103.7 4.1 %collective-permute-start.7 = (bf16[1536,256]{1,0:T(8,128)(2,1)}, bf16[1536,256]{1,0:T(8,128)(2,1)S(1)}, u32[]{:S(2)}, u32[]{:S(2)}) collective-permute-start(bf16[1536,256]{1,0:T(8,128)(2,1)} %bitcast.63), channel_id=1, source_target_pairs={{0,256},{256,0},{1,257},{257,1},{2,258},{258,2},{3,259},{259,3},{4... | collective-permute-start | bytes 2359304 | tf_op jit(solution)/shard_map/ppermute | solution.py:414
  107.7 5.4 %collective-permute-done.3.refs_1_.refs_9_ = bf16[64,4224]{1,0:T(8,128)(2,1)S(1)} collective-permute-done((bf16[64,4224]{1,0:T(8,128)(2,1)S(1)}, bf16[64,4224]{1,0:T(8,128)(2,1)S(1)}, u32[]{:S(2)}, u32[]{:S(2)}) %collective-permute-start.3) | collective-permute-done | bytes 540704 | tf_op jit(solution)/shard_map/ppermute | solution.py:410
  115.6 4.1 %collective-permute-start.6 = (bf16[64,4224]{1,0:T(8,128)(2,1)S(1)}, bf16[64,4224]{1,0:T(8,128)(2,1)S(1)}, u32[]{:S(2)}, u32[]{:S(2)}) collective-permute-start(bf16[64,4224]{1,0:T(8,128)(2,1)S(1)} %collective-permute-done.5.refs_2_.refs_10_), channel_id=1, source_target_pairs={{32,0},{64,32},{96,64},{128,96},{160,128},{192,160},{224,192},{0,2... | collective-permute-start | bytes 1622024 | tf_op jit(solution)/shard_map/ppermute | solution.py:410
  119.7 5.0 %collective-permute-done.7.refs_2_ = bf16[1536,256]{1,0:T(8,128)(2,1)S(1)} collective-permute-done((bf16[1536,256]{1,0:T(8,128)(2,1)}, bf16[1536,256]{1,0:T(8,128)(2,1)S(1)}, u32[]{:S(2)}, u32[]{:S(2)}) %collective-permute-start.7) | collective-permute-done | bytes 786464 | tf_op jit(solution)/shard_map/ppermute | solution.py:414
  132.5 3.9 %collective-permute-start.9 = (bf16[64,4224]{1,0:T(8,128)(2,1)S(1)}, bf16[64,4224]{1,0:T(8,128)(2,1)S(1)}, u32[]{:S(2)}, u32[]{:S(2)}) collective-permute-start(bf16[64,4224]{1,0:T(8,128)(2,1)S(1)} %collective-permute-done.6.refs_4_.refs_12_), channel_id=1, source_target_pairs={{32,0},{64,32},{96,64},{128,96},{160,128},{192,160},{224,192},{0,2... | collective-permute-start | bytes 1622024 | tf_op jit(solution)/shard_map/ppermute | solution.py:410
  136.4 4.7 %collective-permute-start.11 = (bf16[1536,256]{1,0:T(8,128)(2,1)}, bf16[1536,256]{1,0:T(8,128)(2,1)S(1)}, u32[]{:S(2)}, u32[]{:S(2)}) collective-permute-start(bf16[1536,256]{1,0:T(8,128)(2,1)} %collective-permute-done.2.refs_1_), channel_id=1, source_target_pairs={{0,256},{256,0},{1,257},{257,1},{2,258},{258,2},{3,259},{259,3},{4... | collective-permute-start | bytes 2359304 | tf_op jit(solution)/shard_map/ppermute | solution.py:417
  142.3 5.1 %shard_map.132.refs_6_ = bf16[192,320]{1,0:T(8,128)(2,1)S(1)} custom-call(s32[1]{0:T(128)} %bitcast.20.zl_ref, bf16[64,4224]{1,0:T(8,128)(2,1)S(1)} %bitcast.54, bf16[64,4224]{1,0:T(8,128)(2,1)S(1)} %collective-permute-done.3.refs_1_.refs_9_, bf16[64,4224]{1,0:T(8,128)(2,1)S(1)} %collective-permute-done.5.refs_2_.refs_10_, ...), custom_call_target="tpu_custom_call" | custom-call | flops 1006632960 | bytes 5767168 | tf_op jit(solution)/shard_map/pallas_call | solution.py:224
  157.2 3.9 %collective-permute-done.10.refs_1_.refs_15_ = bf16[64,4224]{1,0:T(8,128)(2,1)S(1)} collective-permute-done((bf16[64,4224]{1,0:T(8,128)(2,1)S(1)}, bf16[64,4224]{1,0:T(8,128)(2,1)S(1)}, u32[]{:S(2)}, u32[]{:S(2)}) %collective-permute-start.10) | collective-permute-done | bytes 540704 | tf_op jit(solution)/shard_map/ppermute | solution.py:420
  161.1 4.9 %shard_map.134 = (bf16[8,192,256]{2,1,0:T(8,128)(2,1)S(1)}, bf16[512,128]{1,0:T(8,128)(2,1)S(1)}) custom-call(s32[2]{0:T(128)S(1)} %pad_add_fusion.1.refs_0_, bf16[64,4224]{1,0:T(8,128)(2,1)S(1)} %collective-permute-done.10.refs_1_.refs_15_, bf16[96,4096]{1,0:T(8,128)(2,1)S(1)} %bitcast.47, bf16[96,4096]{1,0:T(8,128)(2,1)} %collective-permute-done.refs_6_.refs_3_, ...), custom_call_target="tpu_custom_call" | custom-call | flops 201326592 | bytes 3670016 | tf_op jit(solution)/shard_map/pallas_call | solution.py:244
  167.5 4.4 %all-to-all-start.6 = ((bf16[8,192,256]{2,1,0:T(8,128)(2,1)}), bf16[8,192,256]{2,1,0:T(8,128)(2,1)S(1)}, u32[]{:S(2)}, u32[]{:S(2)}) async-start(bf16[8,192,256]{2,1,0:T(8,128)(2,1)} %copy-done.4), calls=%async_computation.6 | async-start | bytes 1572864 | tf_op jit(solution)/shard_map/all_to_all | solution.py:19
  171.9 20.0 %all-to-all-done.6.hidden_ref = bf16[8,192,256]{2,1,0:T(8,128)(2,1)S(1)} async-done(((bf16[8,192,256]{2,1,0:T(8,128)(2,1)}), bf16[8,192,256]{2,1,0:T(8,128)(2,1)S(1)}, u32[]{:S(2)}, u32[]{:S(2)}) %all-to-all-start.6) | async-done | bytes 786464 | tf_op jit(solution)/shard_map/all_to_all | solution.py:19
  192.7 6.4 %shard_map.135 = bf16[256,1152]{1,0:T(8,128)(2,1)} custom-call(s32[1]{0:T(128)} %bitcast.19.half_ref, bf16[8,192,256]{2,1,0:T(8,128)(2,1)} %copy-done.8, bf16[512,128]{1,0:T(8,128)(2,1)} %copy-done.6, bf16[1536,256]{1,0:T(8,128)(2,1)} %bitcast.64, bf16[1536,256]{1,0:T(8,128)(2,1)} %collective-permute-done.2.refs_1_, bf16[1536,256]{1,0:T(8,128)(2,1)} %copy-done.9, ...), custom_call_target="tpu_custom_call" | custom-call | flops 805306368 | bytes 3145728 | tf_op jit(solution)/shard_map/pallas_call | solution.py:311
  199.2 28.9 %all_to_all.47 = bf16[32,8,1152]{2,1,0:T(8,128)(2,1)S(1)} all-to-all(bf16[32,8,1152]{2,1,0:T(8,128)(2,1)} %bitcast.58), channel_id=1, replica_groups=mesh['zl'=2,'y'=8,'x'=4,'zh'=4,'co'=2] {'x','zh','co'}, dimensions={0} | all-to-all | bytes 1179648 | tf_op jit(solution)/shard_map/all_to_all | solution.py:19
  232.3 7.1 %all-to-all-done.8 = bf16[8,4,1024]{2,1,0:T(4,128)(2,1)S(1)} async-done(((bf16[8,4,1024]{2,1,0:T(4,128)(2,1)}), bf16[8,4,1024]{2,1,0:T(4,128)(2,1)S(1)}, u32[]{:S(2)}, u32[]{:S(2)}) %all-to-all-start.8) | async-done | bytes 65568 | tf_op jit(solution)/shard_map/all_to_all | solution.py:19
  (89 shorter events, 54.6 us)
Async XLA Ops:
  0.6 33.9 %copy-start = (bf16[256,4096]{1,0:T(8,128)(2,1)S(1)}, bf16[256,4096]{1,0:T(8,128)(2,1)}, u32[]{:S(2)}) copy-start(bf16[256,4096]{1,0:T(8,128)(2,1)} %param.16) | copy-start | bytes 6291460
  2.5 23.3 %all-to-all-start = ((bf16[16,128,128]{2,1,0:T(8,128)(2,1)}), bf16[16,128,128]{2,1,0:T(8,128)(2,1)S(1)}, u32[]{:S(2)}, u32[]{:S(2)}) async-start(bf16[16,128,128]{2,1,0:T(8,128)(2,1)} %broadcast_in_dim.58), calls=%async_computation | async-start | bytes 1048576 | tf_op jit(solution)/shard_map/all_to_all | solution.py:19
  12.1 41.9 %collective-permute-start = (bf16[96,4096]{1,0:T(8,128)(2,1)}, bf16[96,4096]{1,0:T(8,128)(2,1)}, u32[]{:S(2)}, u32[]{:S(2)}) collective-permute-start(bf16[96,4096]{1,0:T(8,128)(2,1)} %bitcast.44), channel_id=1, source_target_pairs={{0,256},{256,0},{1,257},{257,1},{2,258},{258,2},{3,259},{259,3},{4... | collective-permute-start | bytes 2359304 | tf_op jit(solution)/shard_map/ppermute | solution.py:359
  15.3 39.3 %collective-permute-start.1 = (bf16[96,4096]{1,0:T(8,128)(2,1)}, bf16[96,4096]{1,0:T(8,128)(2,1)}, u32[]{:S(2)}, u32[]{:S(2)}) collective-permute-start(bf16[96,4096]{1,0:T(8,128)(2,1)} %bitcast.48), channel_id=1, source_target_pairs={{0,256},{256,0},{1,257},{257,1},{2,258},{258,2},{3,259},{259,3},{4... | collective-permute-start | bytes 2359304 | tf_op jit(solution)/shard_map/ppermute | solution.py:359
  35.0 10.0 %copy-start.12 = (s32[4,8]{1,0:T(4,128)S(1)}, s32[4,8]{1,0:T(4,128)}, u32[]{:S(2)}) copy-start(s32[4,8]{1,0:T(4,128)} %param.18) | copy-start | bytes 388
  35.0 10.1 %copy-start.11 = (bf16[4,4096]{1,0:T(4,128)(2,1)S(1)}, bf16[4,4096]{1,0:T(4,128)(2,1)}, u32[]{:S(2)}) copy-start(bf16[4,4096]{1,0:T(4,128)(2,1)} %param.15) | copy-start | bytes 98308
  40.9 39.0 %copy-start.7 = (f32[4096]{0:T(1024)S(1)}, f32[4096]{0:T(1024)}, u32[]{:S(2)}) copy-start(f32[4096]{0:T(1024)} %param.17) | copy-start | bytes 49156
  40.9 13.1 %all-to-all-start.3 = ((bf16[4,16,4096]{2,1,0:T(8,128)(2,1)}), bf16[4,16,4096]{2,1,0:T(8,128)(2,1)S(1)}, u32[]{:S(2)}, u32[]{:S(2)}) async-start(bf16[4,16,4096]{2,1,0:T(8,128)(2,1)} %bitcast.61), calls=%async_computation.3 | async-start | bytes 1048576 | tf_op jit(solution)/shard_map/all_to_all | solution.py:19
  54.0 87.2 %copy-start.1 = (bf16[1,4096,96]{1,2,0:T(8,128)(2,1)S(1)}, bf16[1,4096,96]{1,2,0:T(8,128)(2,1)}, u32[]{:S(2)}) copy-start(bf16[1,4096,96]{1,2,0:T(8,128)(2,1)} %param.20) | copy-start | bytes 2359300
  55.6 24.3 %all-to-all-start.4 = ((bf16[4,16,4224]{2,1,0:T(8,128)(2,1)}), bf16[4,16,4224]{2,1,0:T(8,128)(2,1)S(1)}, u32[]{:S(2)}, u32[]{:S(2)}) async-start(bf16[4,16,4224]{2,1,0:T(8,128)(2,1)} %broadcast_in_dim.69), calls=%async_computation.4 | async-start | bytes 1081344 | tf_op jit(solution)/shard_map/all_to_all | solution.py:19
  64.7 22.8 %collective-permute-start.2 = (bf16[1536,256]{1,0:T(8,128)(2,1)}, bf16[1536,256]{1,0:T(8,128)(2,1)}, u32[]{:S(2)}, u32[]{:S(2)}) collective-permute-start(bf16[1536,256]{1,0:T(8,128)(2,1)} %bitcast.62), channel_id=1, source_target_pairs={{0,32},{32,0},{64,96},{96,64},{128,160},{160,128},{192,224},{224,1... | collective-permute-start | bytes 2359304 | tf_op jit(solution)/shard_map/ppermute | solution.py:388
  82.2 15.0 %all-to-all-start.5 = ((bf16[8,8,4224]{2,1,0:T(8,128)(2,1)}), bf16[8,8,4224]{2,1,0:T(8,128)(2,1)S(1)}, u32[]{:S(2)}, u32[]{:S(2)}) async-start(bf16[8,8,4224]{2,1,0:T(8,128)(2,1)} %copy-done.5), calls=%async_computation.5 | async-start | bytes 1081344 | tf_op jit(solution)/shard_map/all_to_all | solution.py:19
  97.2 16.0 %collective-permute-start.3 = (bf16[64,4224]{1,0:T(8,128)(2,1)S(1)}, bf16[64,4224]{1,0:T(8,128)(2,1)S(1)}, u32[]{:S(2)}, u32[]{:S(2)}) collective-permute-start(bf16[64,4224]{1,0:T(8,128)(2,1)S(1)} %bitcast.52), channel_id=1, source_target_pairs={{0,32},{32,64},{64,96},{96,128},{128,160},{160,192},{192,224},{224... | collective-permute-start | bytes 1622024 | tf_op jit(solution)/shard_map/ppermute | solution.py:410
  100.8 14.8 %collective-permute-start.5 = (bf16[64,4224]{1,0:T(8,128)(2,1)S(1)}, bf16[64,4224]{1,0:T(8,128)(2,1)S(1)}, u32[]{:S(2)}, u32[]{:S(2)}) collective-permute-start(bf16[64,4224]{1,0:T(8,128)(2,1)S(1)} %bitcast.53), channel_id=1, source_target_pairs={{32,0},{64,32},{96,64},{128,96},{160,128},{192,160},{224,192},{0,2... | collective-permute-start | bytes 1622024 | tf_op jit(solution)/shard_map/ppermute | solution.py:410
  103.7 21.0 %collective-permute-start.7 = (bf16[1536,256]{1,0:T(8,128)(2,1)}, bf16[1536,256]{1,0:T(8,128)(2,1)S(1)}, u32[]{:S(2)}, u32[]{:S(2)}) collective-permute-start(bf16[1536,256]{1,0:T(8,128)(2,1)} %bitcast.63), channel_id=1, source_target_pairs={{0,256},{256,0},{1,257},{257,1},{2,258},{258,2},{3,259},{259,3},{4... | collective-permute-start | bytes 2359304 | tf_op jit(solution)/shard_map/ppermute | solution.py:414
  113.2 15.1 %collective-permute-start.4 = (bf16[64,4224]{1,0:T(8,128)(2,1)S(1)}, bf16[64,4224]{1,0:T(8,128)(2,1)S(1)}, u32[]{:S(2)}, u32[]{:S(2)}) collective-permute-start(bf16[64,4224]{1,0:T(8,128)(2,1)S(1)} %collective-permute-done.3.refs_1_.refs_9_), channel_id=1, source_target_pairs={{0,32},{32,64},{64,96},{96,128},{128,160},{160,192},{192,224},{224... | collective-permute-start | bytes 1622024 | tf_op jit(solution)/shard_map/ppermute | solution.py:410
  115.6 13.6 %collective-permute-start.6 = (bf16[64,4224]{1,0:T(8,128)(2,1)S(1)}, bf16[64,4224]{1,0:T(8,128)(2,1)S(1)}, u32[]{:S(2)}, u32[]{:S(2)}) collective-permute-start(bf16[64,4224]{1,0:T(8,128)(2,1)S(1)} %collective-permute-done.5.refs_2_.refs_10_), channel_id=1, source_target_pairs={{32,0},{64,32},{96,64},{128,96},{160,128},{192,160},{224,192},{0,2... | collective-permute-start | bytes 1622024 | tf_op jit(solution)/shard_map/ppermute | solution.py:410
  124.7 16.5 %copy-start.9 = (bf16[1536,256]{1,0:T(8,128)(2,1)}, bf16[1536,256]{1,0:T(8,128)(2,1)S(1)}, u32[]{:S(2)}) copy-start(bf16[1536,256]{1,0:T(8,128)(2,1)S(1)} %collective-permute-done.7.refs_2_) | copy-start | bytes 2359300
  129.2 18.2 %collective-permute-start.8 = (bf16[64,4224]{1,0:T(8,128)(2,1)S(1)}, bf16[64,4224]{1,0:T(8,128)(2,1)S(1)}, u32[]{:S(2)}, u32[]{:S(2)}) collective-permute-start(bf16[64,4224]{1,0:T(8,128)(2,1)S(1)} %collective-permute-done.4.refs_3_.refs_11_), channel_id=1, source_target_pairs={{0,32},{32,64},{64,96},{96,128},{128,160},{160,192},{192,224},{224... | collective-permute-start | bytes 1622024 | tf_op jit(solution)/shard_map/ppermute | solution.py:410
  132.5 14.9 %collective-permute-start.9 = (bf16[64,4224]{1,0:T(8,128)(2,1)S(1)}, bf16[64,4224]{1,0:T(8,128)(2,1)S(1)}, u32[]{:S(2)}, u32[]{:S(2)}) collective-permute-start(bf16[64,4224]{1,0:T(8,128)(2,1)S(1)} %collective-permute-done.6.refs_4_.refs_12_), channel_id=1, source_target_pairs={{32,0},{64,32},{96,64},{128,96},{160,128},{192,160},{224,192},{0,2... | collective-permute-start | bytes 1622024 | tf_op jit(solution)/shard_map/ppermute | solution.py:410
  136.4 19.8 %collective-permute-start.11 = (bf16[1536,256]{1,0:T(8,128)(2,1)}, bf16[1536,256]{1,0:T(8,128)(2,1)S(1)}, u32[]{:S(2)}, u32[]{:S(2)}) collective-permute-start(bf16[1536,256]{1,0:T(8,128)(2,1)} %collective-permute-done.2.refs_1_), channel_id=1, source_target_pairs={{0,256},{256,0},{1,257},{257,1},{2,258},{258,2},{3,259},{259,3},{4... | collective-permute-start | bytes 2359304 | tf_op jit(solution)/shard_map/ppermute | solution.py:417
  147.4 13.7 %collective-permute-start.10 = (bf16[64,4224]{1,0:T(8,128)(2,1)S(1)}, bf16[64,4224]{1,0:T(8,128)(2,1)S(1)}, u32[]{:S(2)}, u32[]{:S(2)}) collective-permute-start(bf16[64,4224]{1,0:T(8,128)(2,1)S(1)} %collective-permute-done.8.refs_0_.refs_13_), channel_id=1, source_target_pairs={{0,32},{32,64},{64,96},{96,128},{128,160},{160,192},{192,224},{224... | collective-permute-start | bytes 1622024 | tf_op jit(solution)/shard_map/ppermute | solution.py:420
  167.5 24.3 %all-to-all-start.6 = ((bf16[8,192,256]{2,1,0:T(8,128)(2,1)}), bf16[8,192,256]{2,1,0:T(8,128)(2,1)S(1)}, u32[]{:S(2)}, u32[]{:S(2)}) async-start(bf16[8,192,256]{2,1,0:T(8,128)(2,1)} %copy-done.4), calls=%async_computation.6 | async-start | bytes 1572864 | tf_op jit(solution)/shard_map/all_to_all | solution.py:19
  228.9 10.5 %all-to-all-start.8 = ((bf16[8,4,1024]{2,1,0:T(4,128)(2,1)}), bf16[8,4,1024]{2,1,0:T(4,128)(2,1)S(1)}, u32[]{:S(2)}, u32[]{:S(2)}) async-start(bf16[8,4,1024]{2,1,0:T(4,128)(2,1)} %reshape.77), calls=%async_computation.8 | async-start | bytes 131072 | tf_op jit(solution)/shard_map/all_to_all | solution.py:19
  (8 other events, 23.8 us)

commit v10 on v9

--- a/solution.py
+++ b/solution.py
@@ -406,30 +406,35 @@
     before = [(b, a) for a, b in after]
     weights = (gate_own, gate_z, up_own, up_z)
 
-    def onward(left, right):
-        return lax.ppermute(left, "y", after), lax.ppermute(right, "y", before)
-
-    one = onward(arrived, arrived)
-    two = onward(*one)
+    def rightward(value):
+        return lax.ppermute(value, "y", after)
+
+    def leftward(value):
+        return lax.ppermute(value, "y", before)
+
+    left_one, right_one = rightward(arrived), leftward(arrived)
+    left_two, right_two = rightward(left_one), leftward(right_one)
     down_z = lax.ppermute(down_own, "zl", swap_z)
-    two, down_z, down_y = lax.optimization_barrier((two, down_z, down_y))
-    three = onward(*two)
+    right_two, down_z, down_y = lax.optimization_barrier((right_two, down_z, down_y))
+    left_three, right_three = rightward(left_two), leftward(right_two)
+    last = rightward(left_three)
     down_zy = lax.ppermute(down_y, "zl", swap_z)
-    first = first_hidden(zl, (arrived,) + one + two, weights, width)
-    three, first = lax.optimization_barrier((three, first))
-    last = lax.ppermute(three[0], "y", after)
-    second = first_hidden(zl, three, weights, width)
-    last, second, down_zy = lax.optimization_barrier((last, second, down_zy))
+    near = (arrived, left_one, right_one, left_two, right_two)
+    far = (left_three, right_three)
+    first = first_hidden(zl, near, weights, width)
+    second = first_hidden(zl, far, weights, width)
+    last, first, second = lax.optimization_barrier((last, first, second))
 
     hidden, extra = last_hidden(
         jnp.stack([zl, y_pos]),
         (last,),
         weights,
         (first, second),
-        (arrived,) + one + two + three + (last,),
+        near + far + (last,),
         width,
         n_y,
     )
+    hidden, down_zy = lax.optimization_barrier((hidden, down_zy))
     hidden = exchange(hidden, "y")
 
     result = down_slots(y_pos % 2, hidden, extra, (down_own, down_y, down_z, down_zy))

time: 242 us -> 239 us (0.988)
  starting transfers between devices: 76.4 us -> 73.5 us
    unnamed x28 -> x26, local copies, waits for them, and re-layouts: 5.29 us -> 4.4 us
  transfers between devices with their start and end apart: 18 -> 18, of which waited for: 13 -> 12; matrix products, arithmetic and copies ran while one was open for 2% -> 2% of each run, Pallas kernels for 4% -> 6%
where the time goes in v10:
time: 239 us; the launch traced here: 237 us
  waiting for transfers between devices  85.4 us (36%)
  starting transfers between devices  73.5 us (31%)
  blocking collectives  41 us (17%)
  Pallas kernels  21.8 us (9%)
  local copies, waits for them, and re-layouts  9.17 us (4%)
  other arithmetic  3.57 us (1%)
    all_to_all x6, waiting for transfers between devices, exchange(): return lax.all_to_all(pieces, axis, 0, 0, tiled=True)  64.1 us
    all_to_all x3, blocking collectives, exchange(): return lax.all_to_all(pieces, axis, 0, 0, tiled=True)  41 us
    all_to_all x6, starting transfers between devices, exchange(): return lax.all_to_all(pieces, axis, 0, 0, tiled=True)  36.3 us
    ppermute x4, waiting for transfers between devices, rightward(): return lax.ppermute(value, 'y', after)  14.7 us
    ppermute x3, starting transfers between devices, leftward(): return lax.ppermute(value, 'y', before)  11.7 us
    ppermute x4, starting transfers between devices, rightward(): return lax.ppermute(value, 'y', after)  9.86 us
    pallas_call x2, Pallas kernels, first_hidden(): pl.pallas_call(first_kernel, out_shape=jax.ShapeDtypeStruct((2 * units, c...  8.99 us
    pallas_call x1, Pallas kernels, down_slots(): pl.pallas_call(down_kernel, out_shape=jax.ShapeDtypeStruct(out, jnp.bfloa...  6.44 us
  transfers between devices with their start and end apart: 18, of which 12 were waited for; matrix products, arithmetic and copies ran while one was open for 2% of the time, Pallas kernels for 6%

profile of v10, /device:TPU:1, one launch (start us, length us, event | category | flops | bytes accessed | tf_op | source)
XLA Modules:
  0.0 237.3 jit_solution(8867230318318431613)
XLA Ops:
  2.5 9.6 %all-to-all-start = ((bf16[16,128,128]{2,1,0:T(8,128)(2,1)}), bf16[16,128,128]{2,1,0:T(8,128)(2,1)S(1)}, u32[]{:S(2)}, u32[]{:S(2)}) async-start(bf16[16,128,128]{2,1,0:T(8,128)(2,1)} %broadcast_in_dim.58), calls=%async_computation | async-start | bytes 1048576 | tf_op jit(solution)/shard_map/all_to_all | solution.py:19
  19.1 6.7 %all-to-all-done = bf16[16,128,128]{2,1,0:T(8,128)(2,1)S(1)} async-done(((bf16[16,128,128]{2,1,0:T(8,128)(2,1)}), bf16[16,128,128]{2,1,0:T(8,128)(2,1)S(1)}, u32[]{:S(2)}, u32[]{:S(2)}) %all-to-all-start) | async-done | bytes 524320 | tf_op jit(solution)/shard_map/all_to_all | solution.py:19
  25.9 7.1 %all_to_all.45 = bf16[2,2048,128]{2,1,0:T(8,128)(2,1)S(1)} all-to-all(bf16[2,2048,128]{2,1,0:T(8,128)(2,1)S(1)} %broadcast_in_dim.60), channel_id=1, replica_groups=mesh['zl'=2,'y'=8,'x'=4,'zh'=4,'co'=2] {'co'}, dimensions={0} | all-to-all | bytes 2097152 | tf_op jit(solution)/shard_map/all_to_all | solution.py:19
  35.0 4.7 %all_to_all.46 = bf16[2,64,4096]{2,1,0:T(8,128)(2,1)S(1)} all-to-all(bf16[2,64,4096]{2,1,0:T(8,128)(2,1)S(1)} %bitcast.57), channel_id=1, replica_groups=mesh['zl'=2,'y'=8,'x'=4,'zh'=4,'co'=2] {'co'}, dimensions={0} | all-to-all | bytes 2097152 | tf_op jit(solution)/shard_map/all_to_all | solution.py:19
  40.9 4.1 %all-to-all-start.3 = ((bf16[4,16,4096]{2,1,0:T(8,128)(2,1)}), bf16[4,16,4096]{2,1,0:T(8,128)(2,1)S(1)}, u32[]{:S(2)}, u32[]{:S(2)}) async-start(bf16[4,16,4096]{2,1,0:T(8,128)(2,1)} %bitcast.61), calls=%async_computation.3 | async-start | bytes 1048576 | tf_op jit(solution)/shard_map/all_to_all | solution.py:19
  45.3 8.6 %all-to-all-done.3 = bf16[4,16,4096]{2,1,0:T(8,128)(2,1)S(1)} async-done(((bf16[4,16,4096]{2,1,0:T(8,128)(2,1)}), bf16[4,16,4096]{2,1,0:T(8,128)(2,1)S(1)}, u32[]{:S(2)}, u32[]{:S(2)}) %all-to-all-start.3) | async-done | bytes 524320 | tf_op jit(solution)/shard_map/all_to_all | solution.py:19
  55.6 9.1 %all-to-all-start.4 = ((bf16[4,16,4224]{2,1,0:T(8,128)(2,1)}), bf16[4,16,4224]{2,1,0:T(8,128)(2,1)S(1)}, u32[]{:S(2)}, u32[]{:S(2)}) async-start(bf16[4,16,4224]{2,1,0:T(8,128)(2,1)} %broadcast_in_dim.69), calls=%async_computation.4 | async-start | bytes 1081344 | tf_op jit(solution)/shard_map/all_to_all | solution.py:19
  67.8 12.0 %all-to-all-done.4.parts_ref = bf16[4,16,4224]{2,1,0:T(8,128)(2,1)S(1)} async-done(((bf16[4,16,4224]{2,1,0:T(8,128)(2,1)}), bf16[4,16,4224]{2,1,0:T(8,128)(2,1)S(1)}, u32[]{:S(2)}, u32[]{:S(2)}) %all-to-all-start.4) | async-done | bytes 540704 | tf_op jit(solution)/shard_map/all_to_all | solution.py:19
  82.2 5.4 %all-to-all-start.5 = ((bf16[8,8,4224]{2,1,0:T(8,128)(2,1)}), bf16[8,8,4224]{2,1,0:T(8,128)(2,1)S(1)}, u32[]{:S(2)}, u32[]{:S(2)}) async-start(bf16[8,8,4224]{2,1,0:T(8,128)(2,1)} %copy-done.5), calls=%async_computation.5 | async-start | bytes 1081344 | tf_op jit(solution)/shard_map/all_to_all | solution.py:19
  87.5 9.7 %all-to-all-done.5 = bf16[8,8,4224]{2,1,0:T(8,128)(2,1)S(1)} async-done(((bf16[8,8,4224]{2,1,0:T(8,128)(2,1)}), bf16[8,8,4224]{2,1,0:T(8,128)(2,1)S(1)}, u32[]{:S(2)}, u32[]{:S(2)}) %all-to-all-start.5) | async-done | bytes 540704 | tf_op jit(solution)/shard_map/all_to_all | solution.py:19
  103.7 9.5 %collective-permute-done.3.refs_1_.refs_9_ = bf16[64,4224]{1,0:T(8,128)(2,1)S(1)} collective-permute-done((bf16[64,4224]{1,0:T(8,128)(2,1)S(1)}, bf16[64,4224]{1,0:T(8,128)(2,1)S(1)}, u32[]{:S(2)}, u32[]{:S(2)}) %collective-permute-start.3) | collective-permute-done | bytes 540704 | tf_op jit(solution)/shard_map/ppermute | solution.py:410
  115.6 3.9 %collective-permute-start.9 = (bf16[1536,256]{1,0:T(8,128)(2,1)}, bf16[1536,256]{1,0:T(8,128)(2,1)S(1)}, u32[]{:S(2)}, u32[]{:S(2)}) collective-permute-start(bf16[1536,256]{1,0:T(8,128)(2,1)} %bitcast.63), channel_id=1, source_target_pairs={{0,256},{256,0},{1,257},{257,1},{2,258},{258,2},{3,259},{259,3},{4... | collective-permute-start | bytes 2359304 | tf_op jit(solution)/shard_map/ppermute | solution.py:417
  119.5 4.6 %collective-permute-start.8 = (bf16[64,4224]{1,0:T(8,128)(2,1)S(1)}, bf16[64,4224]{1,0:T(8,128)(2,1)S(1)}, u32[]{:S(2)}, u32[]{:S(2)}) collective-permute-start(bf16[64,4224]{1,0:T(8,128)(2,1)S(1)} %collective-permute-done.7.refs_2_.refs_10_), channel_id=1, source_target_pairs={{32,0},{64,32},{96,64},{128,96},{160,128},{192,160},{224,192},{0,2... | collective-permute-start | bytes 1622024 | tf_op jit(solution)/shard_map/ppermute | solution.py:413
  124.1 4.2 %collective-permute-done.4.refs_3_.refs_11_ = bf16[64,4224]{1,0:T(8,128)(2,1)S(1)} collective-permute-done((bf16[64,4224]{1,0:T(8,128)(2,1)S(1)}, bf16[64,4224]{1,0:T(8,128)(2,1)S(1)}, u32[]{:S(2)}, u32[]{:S(2)}) %collective-permute-start.4) | collective-permute-done | bytes 540704 | tf_op jit(solution)/shard_map/ppermute | solution.py:410
  130.2 5.5 %collective-permute-done.9.refs_2_ = bf16[1536,256]{1,0:T(8,128)(2,1)S(1)} collective-permute-done((bf16[1536,256]{1,0:T(8,128)(2,1)}, bf16[1536,256]{1,0:T(8,128)(2,1)S(1)}, u32[]{:S(2)}, u32[]{:S(2)}) %collective-permute-start.9) | collective-permute-done | bytes 786464 | tf_op jit(solution)/shard_map/ppermute | solution.py:417
  139.2 4.3 %collective-permute-start.10 = (bf16[64,4224]{1,0:T(8,128)(2,1)S(1)}, bf16[64,4224]{1,0:T(8,128)(2,1)S(1)}, u32[]{:S(2)}, u32[]{:S(2)}) collective-permute-start(bf16[64,4224]{1,0:T(8,128)(2,1)S(1)} %collective-permute-done.8.refs_4_.refs_12_), channel_id=1, source_target_pairs={{32,0},{64,32},{96,64},{128,96},{160,128},{192,160},{224,192},{0,2... | collective-permute-start | bytes 1622024 | tf_op jit(solution)/shard_map/ppermute | solution.py:413
  146.6 5.1 %shard_map.132.refs_6_ = bf16[192,320]{1,0:T(8,128)(2,1)S(1)} custom-call(s32[1]{0:T(128)} %bitcast.20.zl_ref, bf16[64,4224]{1,0:T(8,128)(2,1)S(1)} %bitcast.54, bf16[64,4224]{1,0:T(8,128)(2,1)S(1)} %collective-permute-done.3.refs_1_.refs_9_, bf16[64,4224]{1,0:T(8,128)(2,1)S(1)} %collective-permute-done.7.refs_2_.refs_10_, ...), custom_call_target="tpu_custom_call" | custom-call | flops 1006632960 | bytes 5767168 | tf_op jit(solution)/shard_map/pallas_call | solution.py:224
  152.3 3.9 %shard_map.133.refs_7_ = bf16[192,128]{1,0:T(8,128)(2,1)S(1)} custom-call(s32[1]{0:T(128)} %bitcast.20.zl_ref, bf16[64,4224]{1,0:T(8,128)(2,1)S(1)} %collective-permute-done.5.refs_0_.refs_13_, bf16[64,4224]{1,0:T(8,128)(2,1)S(1)} %collective-permute-done.10.refs_1_.refs_14_, bf16[96,4096]{1,0:T(8,128)(2,1)S(1)} %bitcast.46, ...), custom_call_target="tpu_custom_call" | custom-call | flops 402653184 | bytes 4194304 | tf_op jit(solution)/shard_map/pallas_call | solution.py:224
  157.1 4.9 %shard_map.134 = (bf16[8,192,256]{2,1,0:T(8,128)(2,1)S(1)}, bf16[512,128]{1,0:T(8,128)(2,1)S(1)}) custom-call(s32[2]{0:T(128)S(1)} %pad_add_fusion.1.refs_0_, bf16[64,4224]{1,0:T(8,128)(2,1)S(1)} %collective-permute-done.6.refs_1_.refs_15_, bf16[96,4096]{1,0:T(8,128)(2,1)S(1)} %bitcast.47, bf16[96,4096]{1,0:T(8,128)(2,1)} %collective-permute-done.refs_6_.refs_3_, ...), custom_call_target="tpu_custom_call" | custom-call | flops 201326592 | bytes 3670016 | tf_op jit(solution)/shard_map/pallas_call | solution.py:244
  163.6 4.7 %all-to-all-start.6 = ((bf16[8,192,256]{2,1,0:T(8,128)(2,1)}), bf16[8,192,256]{2,1,0:T(8,128)(2,1)S(1)}, u32[]{:S(2)}, u32[]{:S(2)}) async-start(bf16[8,192,256]{2,1,0:T(8,128)(2,1)} %copy-done.4), calls=%async_computation.6 | async-start | bytes 1572864 | tf_op jit(solution)/shard_map/all_to_all | solution.py:19
  168.3 20.0 %all-to-all-done.6.hidden_ref = bf16[8,192,256]{2,1,0:T(8,128)(2,1)S(1)} async-done(((bf16[8,192,256]{2,1,0:T(8,128)(2,1)}), bf16[8,192,256]{2,1,0:T(8,128)(2,1)S(1)}, u32[]{:S(2)}, u32[]{:S(2)}) %all-to-all-start.6) | async-done | bytes 786464 | tf_op jit(solution)/shard_map/all_to_all | solution.py:19
  189.2 6.4 %shard_map.135 = bf16[256,1152]{1,0:T(8,128)(2,1)} custom-call(s32[1]{0:T(128)} %bitcast.19.half_ref, bf16[8,192,256]{2,1,0:T(8,128)(2,1)} %copy-done.8, bf16[512,128]{1,0:T(8,128)(2,1)} %copy-done.6, bf16[1536,256]{1,0:T(8,128)(2,1)} %bitcast.64, bf16[1536,256]{1,0:T(8,128)(2,1)} %collective-permute-done.2.refs_1_, bf16[1536,256]{1,0:T(8,128)(2,1)} %copy-done.9, ...), custom_call_target="tpu_custom_call" | custom-call | flops 805306368 | bytes 3145728 | tf_op jit(solution)/shard_map/pallas_call | solution.py:311
  195.6 29.1 %all_to_all.47 = bf16[32,8,1152]{2,1,0:T(8,128)(2,1)S(1)} all-to-all(bf16[32,8,1152]{2,1,0:T(8,128)(2,1)} %bitcast.58), channel_id=1, replica_groups=mesh['zl'=2,'y'=8,'x'=4,'zh'=4,'co'=2] {'x','zh','co'}, dimensions={0} | all-to-all | bytes 1179648 | tf_op jit(solution)/shard_map/all_to_all | solution.py:19
  229.0 7.1 %all-to-all-done.8 = bf16[8,4,1024]{2,1,0:T(4,128)(2,1)S(1)} async-done(((bf16[8,4,1024]{2,1,0:T(4,128)(2,1)}), bf16[8,4,1024]{2,1,0:T(4,128)(2,1)S(1)}, u32[]{:S(2)}, u32[]{:S(2)}) %all-to-all-start.8) | async-done | bytes 65568 | tf_op jit(solution)/shard_map/all_to_all | solution.py:19
  (87 shorter events, 45.9 us)
Async XLA Ops:
  0.6 33.9 %copy-start = (bf16[256,4096]{1,0:T(8,128)(2,1)S(1)}, bf16[256,4096]{1,0:T(8,128)(2,1)}, u32[]{:S(2)}) copy-start(bf16[256,4096]{1,0:T(8,128)(2,1)} %param.16) | copy-start | bytes 6291460
  2.5 23.3 %all-to-all-start = ((bf16[16,128,128]{2,1,0:T(8,128)(2,1)}), bf16[16,128,128]{2,1,0:T(8,128)(2,1)S(1)}, u32[]{:S(2)}, u32[]{:S(2)}) async-start(bf16[16,128,128]{2,1,0:T(8,128)(2,1)} %broadcast_in_dim.58), calls=%async_computation | async-start | bytes 1048576 | tf_op jit(solution)/shard_map/all_to_all | solution.py:19
  12.1 41.9 %collective-permute-start = (bf16[96,4096]{1,0:T(8,128)(2,1)}, bf16[96,4096]{1,0:T(8,128)(2,1)}, u32[]{:S(2)}, u32[]{:S(2)}) collective-permute-start(bf16[96,4096]{1,0:T(8,128)(2,1)} %bitcast.44), channel_id=1, source_target_pairs={{0,256},{256,0},{1,257},{257,1},{2,258},{258,2},{3,259},{259,3},{4... | collective-permute-start | bytes 2359304 | tf_op jit(solution)/shard_map/ppermute | solution.py:359
  15.3 39.3 %collective-permute-start.1 = (bf16[96,4096]{1,0:T(8,128)(2,1)}, bf16[96,4096]{1,0:T(8,128)(2,1)}, u32[]{:S(2)}, u32[]{:S(2)}) collective-permute-start(bf16[96,4096]{1,0:T(8,128)(2,1)} %bitcast.48), channel_id=1, source_target_pairs={{0,256},{256,0},{1,257},{257,1},{2,258},{258,2},{3,259},{259,3},{4... | collective-permute-start | bytes 2359304 | tf_op jit(solution)/shard_map/ppermute | solution.py:359
  35.0 10.0 %copy-start.12 = (f32[4,8]{1,0:T(4,128)S(1)}, f32[4,8]{1,0:T(4,128)}, u32[]{:S(2)}) copy-start(f32[4,8]{1,0:T(4,128)} %param.19) | copy-start | bytes 388
  35.0 10.0 %copy-start.11 = (s32[4,8]{1,0:T(4,128)S(1)}, s32[4,8]{1,0:T(4,128)}, u32[]{:S(2)}) copy-start(s32[4,8]{1,0:T(4,128)} %param.18) | copy-start | bytes 388
  35.0 10.1 %copy-start.10 = (bf16[4,4096]{1,0:T(4,128)(2,1)S(1)}, bf16[4,4096]{1,0:T(4,128)(2,1)}, u32[]{:S(2)}) copy-start(bf16[4,4096]{1,0:T(4,128)(2,1)} %param.15) | copy-start | bytes 98308
  40.9 39.0 %copy-start.7 = (f32[4096]{0:T(1024)S(1)}, f32[4096]{0:T(1024)}, u32[]{:S(2)}) copy-start(f32[4096]{0:T(1024)} %param.17) | copy-start | bytes 49156
  40.9 13.1 %all-to-all-start.3 = ((bf16[4,16,4096]{2,1,0:T(8,128)(2,1)}), bf16[4,16,4096]{2,1,0:T(8,128)(2,1)S(1)}, u32[]{:S(2)}, u32[]{:S(2)}) async-start(bf16[4,16,4096]{2,1,0:T(8,128)(2,1)} %bitcast.61), calls=%async_computation.3 | async-start | bytes 1048576 | tf_op jit(solution)/shard_map/all_to_all | solution.py:19
  54.0 91.5 %copy-start.1 = (bf16[1,4096,96]{1,2,0:T(8,128)(2,1)S(1)}, bf16[1,4096,96]{1,2,0:T(8,128)(2,1)}, u32[]{:S(2)}) copy-start(bf16[1,4096,96]{1,2,0:T(8,128)(2,1)} %param.20) | copy-start | bytes 2359300
  55.6 24.3 %all-to-all-start.4 = ((bf16[4,16,4224]{2,1,0:T(8,128)(2,1)}), bf16[4,16,4224]{2,1,0:T(8,128)(2,1)S(1)}, u32[]{:S(2)}, u32[]{:S(2)}) async-start(bf16[4,16,4224]{2,1,0:T(8,128)(2,1)} %broadcast_in_dim.69), calls=%async_computation.4 | async-start | bytes 1081344 | tf_op jit(solution)/shard_map/all_to_all | solution.py:19
  64.7 22.8 %collective-permute-start.2 = (bf16[1536,256]{1,0:T(8,128)(2,1)}, bf16[1536,256]{1,0:T(8,128)(2,1)}, u32[]{:S(2)}, u32[]{:S(2)}) collective-permute-start(bf16[1536,256]{1,0:T(8,128)(2,1)} %bitcast.62), channel_id=1, source_target_pairs={{0,32},{32,0},{64,96},{96,64},{128,160},{160,128},{192,224},{224,1... | collective-permute-start | bytes 2359304 | tf_op jit(solution)/shard_map/ppermute | solution.py:388
  82.2 15.0 %all-to-all-start.5 = ((bf16[8,8,4224]{2,1,0:T(8,128)(2,1)}), bf16[8,8,4224]{2,1,0:T(8,128)(2,1)S(1)}, u32[]{:S(2)}, u32[]{:S(2)}) async-start(bf16[8,8,4224]{2,1,0:T(8,128)(2,1)} %copy-done.5), calls=%async_computation.5 | async-start | bytes 1081344 | tf_op jit(solution)/shard_map/all_to_all | solution.py:19
  97.2 16.0 %collective-permute-start.3 = (bf16[64,4224]{1,0:T(8,128)(2,1)S(1)}, bf16[64,4224]{1,0:T(8,128)(2,1)S(1)}, u32[]{:S(2)}, u32[]{:S(2)}) collective-permute-start(bf16[64,4224]{1,0:T(8,128)(2,1)S(1)} %bitcast.52), channel_id=1, source_target_pairs={{0,32},{32,64},{64,96},{96,128},{128,160},{160,192},{192,224},{224... | collective-permute-start | bytes 1622024 | tf_op jit(solution)/shard_map/ppermute | solution.py:410
  100.8 18.7 %collective-permute-start.7 = (bf16[64,4224]{1,0:T(8,128)(2,1)S(1)}, bf16[64,4224]{1,0:T(8,128)(2,1)S(1)}, u32[]{:S(2)}, u32[]{:S(2)}) collective-permute-start(bf16[64,4224]{1,0:T(8,128)(2,1)S(1)} %bitcast.53), channel_id=1, source_target_pairs={{32,0},{64,32},{96,64},{128,96},{160,128},{192,160},{224,192},{0,2... | collective-permute-start | bytes 1622024 | tf_op jit(solution)/shard_map/ppermute | solution.py:413
  113.2 15.1 %collective-permute-start.4 = (bf16[64,4224]{1,0:T(8,128)(2,1)S(1)}, bf16[64,4224]{1,0:T(8,128)(2,1)S(1)}, u32[]{:S(2)}, u32[]{:S(2)}) collective-permute-start(bf16[64,4224]{1,0:T(8,128)(2,1)S(1)} %collective-permute-done.3.refs_1_.refs_9_), channel_id=1, source_target_pairs={{0,32},{32,64},{64,96},{96,128},{128,160},{160,192},{192,224},{224... | collective-permute-start | bytes 1622024 | tf_op jit(solution)/shard_map/ppermute | solution.py:410
  115.6 20.1 %collective-permute-start.9 = (bf16[1536,256]{1,0:T(8,128)(2,1)}, bf16[1536,256]{1,0:T(8,128)(2,1)S(1)}, u32[]{:S(2)}, u32[]{:S(2)}) collective-permute-start(bf16[1536,256]{1,0:T(8,128)(2,1)} %bitcast.63), channel_id=1, source_target_pairs={{0,256},{256,0},{1,257},{257,1},{2,258},{258,2},{3,259},{259,3},{4... | collective-permute-start | bytes 2359304 | tf_op jit(solution)/shard_map/ppermute | solution.py:417
  119.5 16.2 %collective-permute-start.8 = (bf16[64,4224]{1,0:T(8,128)(2,1)S(1)}, bf16[64,4224]{1,0:T(8,128)(2,1)S(1)}, u32[]{:S(2)}, u32[]{:S(2)}) collective-permute-start(bf16[64,4224]{1,0:T(8,128)(2,1)S(1)} %collective-permute-done.7.refs_2_.refs_10_), channel_id=1, source_target_pairs={{32,0},{64,32},{96,64},{128,96},{160,128},{192,160},{224,192},{0,2... | collective-permute-start | bytes 1622024 | tf_op jit(solution)/shard_map/ppermute | solution.py:413
  128.3 15.2 %collective-permute-start.5 = (bf16[64,4224]{1,0:T(8,128)(2,1)S(1)}, bf16[64,4224]{1,0:T(8,128)(2,1)S(1)}, u32[]{:S(2)}, u32[]{:S(2)}) collective-permute-start(bf16[64,4224]{1,0:T(8,128)(2,1)S(1)} %collective-permute-done.4.refs_3_.refs_11_), channel_id=1, source_target_pairs={{0,32},{32,64},{64,96},{96,128},{128,160},{160,192},{192,224},{224... | collective-permute-start | bytes 1622024 | tf_op jit(solution)/shard_map/ppermute | solution.py:410
  135.7 27.9 %collective-permute-start.11 = (bf16[1536,256]{1,0:T(8,128)(2,1)}, bf16[1536,256]{1,0:T(8,128)(2,1)}, u32[]{:S(2)}, u32[]{:S(2)}) collective-permute-start(bf16[1536,256]{1,0:T(8,128)(2,1)} %collective-permute-done.2.refs_1_), channel_id=1, source_target_pairs={{0,256},{256,0},{1,257},{257,1},{2,258},{258,2},{3,259},{259,3},{4... | collective-permute-start | bytes 2359304 | tf_op jit(solution)/shard_map/ppermute | solution.py:421
  139.2 13.1 %collective-permute-start.10 = (bf16[64,4224]{1,0:T(8,128)(2,1)S(1)}, bf16[64,4224]{1,0:T(8,128)(2,1)S(1)}, u32[]{:S(2)}, u32[]{:S(2)}) collective-permute-start(bf16[64,4224]{1,0:T(8,128)(2,1)S(1)} %collective-permute-done.8.refs_4_.refs_12_), channel_id=1, source_target_pairs={{32,0},{64,32},{96,64},{128,96},{160,128},{192,160},{224,192},{0,2... | collective-permute-start | bytes 1622024 | tf_op jit(solution)/shard_map/ppermute | solution.py:413
  143.5 13.7 %collective-permute-start.6 = (bf16[64,4224]{1,0:T(8,128)(2,1)S(1)}, bf16[64,4224]{1,0:T(8,128)(2,1)S(1)}, u32[]{:S(2)}, u32[]{:S(2)}) collective-permute-start(bf16[64,4224]{1,0:T(8,128)(2,1)S(1)} %collective-permute-done.5.refs_0_.refs_13_), channel_id=1, source_target_pairs={{0,32},{32,64},{64,96},{96,128},{128,160},{160,192},{192,224},{224... | collective-permute-start | bytes 1622024 | tf_op jit(solution)/shard_map/ppermute | solution.py:410
  163.6 24.7 %all-to-all-start.6 = ((bf16[8,192,256]{2,1,0:T(8,128)(2,1)}), bf16[8,192,256]{2,1,0:T(8,128)(2,1)S(1)}, u32[]{:S(2)}, u32[]{:S(2)}) async-start(bf16[8,192,256]{2,1,0:T(8,128)(2,1)} %copy-done.4), calls=%async_computation.6 | async-start | bytes 1572864 | tf_op jit(solution)/shard_map/all_to_all | solution.py:19
  225.7 10.5 %all-to-all-start.8 = ((bf16[8,4,1024]{2,1,0:T(4,128)(2,1)}), bf16[8,4,1024]{2,1,0:T(4,128)(2,1)S(1)}, u32[]{:S(2)}, u32[]{:S(2)}) async-start(bf16[8,4,1024]{2,1,0:T(4,128)(2,1)} %reshape.77), calls=%async_computation.8 | async-start | bytes 131072 | tf_op jit(solution)/shard_map/all_to_all | solution.py:19
  (7 other events, 19.7 us)

commit v11 on v10

--- a/solution.py
+++ b/solution.py
@@ -266,23 +266,18 @@
 
 
 def down_kernel(half_ref, hidden_ref, extra_ref, *refs):
-    weights, (out_ref, stacked, held, placed, arrived) = refs[:4], refs[4:]
+    weights, (out_ref, stacked, held, arrived) = refs[:4], refs[4:]
     peers, units, count = hidden_ref.shape
     half = units // 2
-    moves = [
-        pltpu.make_async_copy(
-            hidden_ref.at[peer, pl.ds(z * half, half), :],
-            stacked.at[pl.ds((z * peers + peer) * half, half), :],
-            placed.at[z * peers + peer],
-        )
-        for z in range(2)
-        for peer in range(peers)
-    ]
     copies = [
         pltpu.make_async_copy(weight, held.at[i], arrived.at[i]) for i, weight in enumerate(weights)
     ]
-    for copy in moves + copies:
+    for copy in copies:
         copy.start()
+    for peer in range(peers):
+        for z in range(2):
+            rows = pl.ds((z * peers + peer) * half, half)
+            stacked[rows, :] = hidden_ref[peer, z * half : (z + 1) * half, :]
     blocks = peers // 2
     each = count // blocks
     to = lax.broadcasted_iota(jnp.int32, (count, 1), 0)
@@ -291,8 +286,6 @@
     source = ((to & (2 * blocks - 1)) >> 1) * each + source
     column = lax.broadcasted_iota(jnp.int32, (count, count), 1)
     move = jnp.where(source == column, 1.0, 0.0).astype(jnp.bfloat16)
-    for copy in moves:
-        copy.wait()
     rows = rows_dot(move, stacked[...]).astype(jnp.bfloat16)
     cols = held.shape[2]
     extra = jnp.where(half_ref[0] == 0, extra_ref[:count, :], extra_ref[count:, :])
@@ -314,17 +307,16 @@
         grid_spec=pltpu.PrefetchScalarGridSpec(
             num_scalar_prefetch=1,
             grid=(1,),
-            in_specs=[pl.BlockSpec(memory_space=pl.ANY), whole(extra.shape)]
+            in_specs=[whole(hidden.shape), whole(extra.shape)]
             + [pl.BlockSpec(memory_space=pl.ANY)] * 4,
             out_specs=whole(out),
             scratch_shapes=[
                 pltpu.VMEM((deep, count), jnp.bfloat16),
                 pltpu.VMEM((4, deep, cols), jnp.bfloat16),
-                pltpu.SemaphoreType.DMA((2 * peers,)),
                 pltpu.SemaphoreType.DMA((4,)),
             ],
         ),
-        compiler_params=pltpu.CompilerParams(vmem_limit_bytes=60 * 2**20),
+        compiler_params=pltpu.CompilerParams(vmem_limit_bytes=24 * 2**20),
         cost_estimate=pl.CostEstimate(
             flops=8 * deep * count * cols, bytes_accessed=8 * deep * cols, transcendentals=0
         ),

time: 239 us -> 238 us (level)
  local copies, waits for them, and re-layouts: 9.17 us -> 12.8 us
  Pallas kernels: 21.8 us -> 18.3 us
    unnamed x26 -> x30, local copies, waits for them, and re-layouts: 4.4 us -> 8.09 us
    pallas_call x1, Pallas kernels: 6.44 us -> 2.88 us  [down_slots(): pl.pallas_call(down_kernel, out_shape=jax.ShapeDtypeStruct(out, jnp.bfloa...]
  transfers between devices with their start and end apart: 18 -> 18, of which waited for: 12 -> 12; matrix products, arithmetic and copies ran while one was open for 2% -> 2% of each run, Pallas kernels for 6% -> 7%
where the time goes in v11:
time: 238 us; the launch traced here: 236 us
  waiting for transfers between devices  85.5 us (36%)
  starting transfers between devices  73.4 us (31%)
  blocking collectives  39.9 us (17%)
  Pallas kernels  18.3 us (8%)
  local copies, waits for them, and re-layouts  12.8 us (5%)
  other arithmetic  3.56 us (1%)
    all_to_all x6, waiting for transfers between devices, exchange(): return lax.all_to_all(pieces, axis, 0, 0, tiled=True)  64.1 us
    all_to_all x3, blocking collectives, exchange(): return lax.all_to_all(pieces, axis, 0, 0, tiled=True)  39.9 us
    all_to_all x6, starting transfers between devices, exchange(): return lax.all_to_all(pieces, axis, 0, 0, tiled=True)  36.1 us
    ppermute x4, waiting for transfers between devices, rightward(): return lax.ppermute(value, 'y', after)  14.8 us
    ppermute x3, starting transfers between devices, leftward(): return lax.ppermute(value, 'y', before)  11.7 us
    ppermute x4, starting transfers between devices, rightward(): return lax.ppermute(value, 'y', after)  9.86 us
    pallas_call x2, Pallas kernels, first_hidden(): pl.pallas_call(first_kernel, out_shape=jax.ShapeDtypeStruct((2 * units, c...  8.99 us
    unnamed x30, local copies, waits for them, and re-layouts  8.09 us
  transfers between devices with their start and end apart: 18, of which 12 were waited for; matrix products, arithmetic and copies ran while one was open for 2% of the time, Pallas kernels for 7%

profile of v11, /device:TPU:1, one launch (start us, length us, event | category | flops | bytes accessed | tf_op | source)
XLA Modules:
  0.0 236.3 jit_solution(12940927028170630893)
XLA Ops:
  2.5 9.6 %all-to-all-start = ((bf16[16,128,128]{2,1,0:T(8,128)(2,1)}), bf16[16,128,128]{2,1,0:T(8,128)(2,1)S(1)}, u32[]{:S(2)}, u32[]{:S(2)}) async-start(bf16[16,128,128]{2,1,0:T(8,128)(2,1)} %broadcast_in_dim.58), calls=%async_computation | async-start | bytes 1048576 | tf_op jit(solution)/shard_map/all_to_all | solution.py:19
  19.1 6.7 %all-to-all-done = bf16[16,128,128]{2,1,0:T(8,128)(2,1)S(1)} async-done(((bf16[16,128,128]{2,1,0:T(8,128)(2,1)}), bf16[16,128,128]{2,1,0:T(8,128)(2,1)S(1)}, u32[]{:S(2)}, u32[]{:S(2)}) %all-to-all-start) | async-done | bytes 524320 | tf_op jit(solution)/shard_map/all_to_all | solution.py:19
  25.9 7.1 %all_to_all.45 = bf16[2,2048,128]{2,1,0:T(8,128)(2,1)S(1)} all-to-all(bf16[2,2048,128]{2,1,0:T(8,128)(2,1)S(1)} %broadcast_in_dim.60), channel_id=1, replica_groups=mesh['zl'=2,'y'=8,'x'=4,'zh'=4,'co'=2] {'co'}, dimensions={0} | all-to-all | bytes 2097152 | tf_op jit(solution)/shard_map/all_to_all | solution.py:19
  35.0 4.7 %all_to_all.46 = bf16[2,64,4096]{2,1,0:T(8,128)(2,1)S(1)} all-to-all(bf16[2,64,4096]{2,1,0:T(8,128)(2,1)S(1)} %bitcast.61), channel_id=1, replica_groups=mesh['zl'=2,'y'=8,'x'=4,'zh'=4,'co'=2] {'co'}, dimensions={0} | all-to-all | bytes 2097152 | tf_op jit(solution)/shard_map/all_to_all | solution.py:19
  40.9 4.1 %all-to-all-start.3 = ((bf16[4,16,4096]{2,1,0:T(8,128)(2,1)}), bf16[4,16,4096]{2,1,0:T(8,128)(2,1)S(1)}, u32[]{:S(2)}, u32[]{:S(2)}) async-start(bf16[4,16,4096]{2,1,0:T(8,128)(2,1)} %bitcast.64), calls=%async_computation.3 | async-start | bytes 1048576 | tf_op jit(solution)/shard_map/all_to_all | solution.py:19
  45.3 8.6 %all-to-all-done.3 = bf16[4,16,4096]{2,1,0:T(8,128)(2,1)S(1)} async-done(((bf16[4,16,4096]{2,1,0:T(8,128)(2,1)}), bf16[4,16,4096]{2,1,0:T(8,128)(2,1)S(1)}, u32[]{:S(2)}, u32[]{:S(2)}) %all-to-all-start.3) | async-done | bytes 524320 | tf_op jit(solution)/shard_map/all_to_all | solution.py:19
  55.6 9.1 %all-to-all-start.4 = ((bf16[4,16,4224]{2,1,0:T(8,128)(2,1)}), bf16[4,16,4224]{2,1,0:T(8,128)(2,1)S(1)}, u32[]{:S(2)}, u32[]{:S(2)}) async-start(bf16[4,16,4224]{2,1,0:T(8,128)(2,1)} %broadcast_in_dim.69), calls=%async_computation.4 | async-start | bytes 1081344 | tf_op jit(solution)/shard_map/all_to_all | solution.py:19
  67.8 12.0 %all-to-all-done.4.parts_ref = bf16[4,16,4224]{2,1,0:T(8,128)(2,1)S(1)} async-done(((bf16[4,16,4224]{2,1,0:T(8,128)(2,1)}), bf16[4,16,4224]{2,1,0:T(8,128)(2,1)S(1)}, u32[]{:S(2)}, u32[]{:S(2)}) %all-to-all-start.4) | async-done | bytes 540704 | tf_op jit(solution)/shard_map/all_to_all | solution.py:19
  82.2 5.4 %all-to-all-start.5 = ((bf16[8,8,4224]{2,1,0:T(8,128)(2,1)}), bf16[8,8,4224]{2,1,0:T(8,128)(2,1)S(1)}, u32[]{:S(2)}, u32[]{:S(2)}) async-start(bf16[8,8,4224]{2,1,0:T(8,128)(2,1)} %copy-done.10), calls=%async_computation.5 | async-start | bytes 1081344 | tf_op jit(solution)/shard_map/all_to_all | solution.py:19
  87.5 9.7 %all-to-all-done.5 = bf16[8,8,4224]{2,1,0:T(8,128)(2,1)S(1)} async-done(((bf16[8,8,4224]{2,1,0:T(8,128)(2,1)}), bf16[8,8,4224]{2,1,0:T(8,128)(2,1)S(1)}, u32[]{:S(2)}, u32[]{:S(2)}) %all-to-all-start.5) | async-done | bytes 540704 | tf_op jit(solution)/shard_map/all_to_all | solution.py:19
  97.2 3.6 %collective-permute-start.3 = (bf16[64,4224]{1,0:T(8,128)(2,1)S(1)}, bf16[64,4224]{1,0:T(8,128)(2,1)S(1)}, u32[]{:S(2)}, u32[]{:S(2)}) collective-permute-start(bf16[64,4224]{1,0:T(8,128)(2,1)S(1)} %bitcast.52), channel_id=1, source_target_pairs={{0,32},{32,64},{64,96},{96,128},{128,160},{160,192},{192,224},{224... | collective-permute-start | bytes 1622024 | tf_op jit(solution)/shard_map/ppermute | solution.py:402
  103.7 9.5 %collective-permute-done.3.refs_1_.refs_9_ = bf16[64,4224]{1,0:T(8,128)(2,1)S(1)} collective-permute-done((bf16[64,4224]{1,0:T(8,128)(2,1)S(1)}, bf16[64,4224]{1,0:T(8,128)(2,1)S(1)}, u32[]{:S(2)}, u32[]{:S(2)}) %collective-permute-start.3) | collective-permute-done | bytes 540704 | tf_op jit(solution)/shard_map/ppermute | solution.py:402
  115.6 3.9 %collective-permute-start.9 = (bf16[1536,256]{1,0:T(8,128)(2,1)}, bf16[1536,256]{1,0:T(8,128)(2,1)S(1)}, u32[]{:S(2)}, u32[]{:S(2)}) collective-permute-start(bf16[1536,256]{1,0:T(8,128)(2,1)} %bitcast.58), channel_id=1, source_target_pairs={{0,256},{256,0},{1,257},{257,1},{2,258},{258,2},{3,259},{259,3},{4... | collective-permute-start | bytes 2359304 | tf_op jit(solution)/shard_map/ppermute | solution.py:409
  119.5 4.6 %collective-permute-start.8 = (bf16[64,4224]{1,0:T(8,128)(2,1)S(1)}, bf16[64,4224]{1,0:T(8,128)(2,1)S(1)}, u32[]{:S(2)}, u32[]{:S(2)}) collective-permute-start(bf16[64,4224]{1,0:T(8,128)(2,1)S(1)} %collective-permute-done.7.refs_2_.refs_10_), channel_id=1, source_target_pairs={{32,0},{64,32},{96,64},{128,96},{160,128},{192,160},{224,192},{0,2... | collective-permute-start | bytes 1622024 | tf_op jit(solution)/shard_map/ppermute | solution.py:405
  124.1 4.2 %collective-permute-done.4.refs_3_.refs_11_ = bf16[64,4224]{1,0:T(8,128)(2,1)S(1)} collective-permute-done((bf16[64,4224]{1,0:T(8,128)(2,1)S(1)}, bf16[64,4224]{1,0:T(8,128)(2,1)S(1)}, u32[]{:S(2)}, u32[]{:S(2)}) %collective-permute-start.4) | collective-permute-done | bytes 540704 | tf_op jit(solution)/shard_map/ppermute | solution.py:402
  130.2 5.5 %collective-permute-done.9.refs_2_ = bf16[1536,256]{1,0:T(8,128)(2,1)S(1)} collective-permute-done((bf16[1536,256]{1,0:T(8,128)(2,1)}, bf16[1536,256]{1,0:T(8,128)(2,1)S(1)}, u32[]{:S(2)}, u32[]{:S(2)}) %collective-permute-start.9) | collective-permute-done | bytes 786464 | tf_op jit(solution)/shard_map/ppermute | solution.py:409
  140.1 4.3 %collective-permute-start.10 = (bf16[64,4224]{1,0:T(8,128)(2,1)S(1)}, bf16[64,4224]{1,0:T(8,128)(2,1)S(1)}, u32[]{:S(2)}, u32[]{:S(2)}) collective-permute-start(bf16[64,4224]{1,0:T(8,128)(2,1)S(1)} %collective-permute-done.8.refs_4_.refs_12_), channel_id=1, source_target_pairs={{32,0},{64,32},{96,64},{128,96},{160,128},{192,160},{224,192},{0,2... | collective-permute-start | bytes 1622024 | tf_op jit(solution)/shard_map/ppermute | solution.py:405
  147.5 5.1 %shard_map.132.refs_6_ = bf16[192,320]{1,0:T(8,128)(2,1)S(1)} custom-call(s32[1]{0:T(128)} %bitcast.20.zl_ref, bf16[64,4224]{1,0:T(8,128)(2,1)S(1)} %bitcast.54, bf16[64,4224]{1,0:T(8,128)(2,1)S(1)} %collective-permute-done.3.refs_1_.refs_9_, bf16[64,4224]{1,0:T(8,128)(2,1)S(1)} %collective-permute-done.7.refs_2_.refs_10_, ...), custom_call_target="tpu_custom_call" | custom-call | flops 1006632960 | bytes 5767168 | tf_op jit(solution)/shard_map/pallas_call | solution.py:224
  153.1 3.9 %shard_map.133.refs_7_ = bf16[192,128]{1,0:T(8,128)(2,1)S(1)} custom-call(s32[1]{0:T(128)} %bitcast.20.zl_ref, bf16[64,4224]{1,0:T(8,128)(2,1)S(1)} %collective-permute-done.5.refs_0_.refs_13_, bf16[64,4224]{1,0:T(8,128)(2,1)S(1)} %collective-permute-done.10.refs_1_.refs_14_, bf16[96,4096]{1,0:T(8,128)(2,1)S(1)} %bitcast.46, ...), custom_call_target="tpu_custom_call" | custom-call | flops 402653184 | bytes 4194304 | tf_op jit(solution)/shard_map/pallas_call | solution.py:224
  158.0 4.9 %shard_map.134 = (bf16[8,192,256]{2,1,0:T(8,128)(2,1)S(1)}, bf16[512,128]{1,0:T(8,128)(2,1)S(1)}) custom-call(s32[2]{0:T(128)S(1)} %pad_add_fusion.1.refs_0_, bf16[64,4224]{1,0:T(8,128)(2,1)S(1)} %collective-permute-done.6.refs_1_.refs_15_, bf16[96,4096]{1,0:T(8,128)(2,1)S(1)} %bitcast.47, bf16[96,4096]{1,0:T(8,128)(2,1)} %collective-permute-done.refs_6_.refs_3_, ...), custom_call_target="tpu_custom_call" | custom-call | flops 201326592 | bytes 3670016 | tf_op jit(solution)/shard_map/pallas_call | solution.py:244
  164.8 4.6 %all-to-all-start.6 = ((bf16[8,192,256]{2,1,0:T(8,128)(2,1)}), bf16[8,192,256]{2,1,0:T(8,128)(2,1)S(1)}, u32[]{:S(2)}, u32[]{:S(2)}) async-start(bf16[8,192,256]{2,1,0:T(8,128)(2,1)} %copy-done.9), calls=%async_computation.6 | async-start | bytes 1572864 | tf_op jit(solution)/shard_map/all_to_all | solution.py:19
  169.4 20.0 %all-to-all-done.6.hidden_ref = bf16[8,192,256]{2,1,0:T(8,128)(2,1)S(1)} async-done(((bf16[8,192,256]{2,1,0:T(8,128)(2,1)}), bf16[8,192,256]{2,1,0:T(8,128)(2,1)S(1)}, u32[]{:S(2)}, u32[]{:S(2)}) %all-to-all-start.6) | async-done | bytes 786464 | tf_op jit(solution)/shard_map/all_to_all | solution.py:19
  195.7 28.1 %all_to_all.47 = bf16[32,8,1152]{2,1,0:T(8,128)(2,1)S(1)} all-to-all(bf16[32,8,1152]{2,1,0:T(8,128)(2,1)S(1)} %bitcast.56), channel_id=1, replica_groups=mesh['zl'=2,'y'=8,'x'=4,'zh'=4,'co'=2] {'x','zh','co'}, dimensions={0} | all-to-all | bytes 1179648 | tf_op jit(solution)/shard_map/all_to_all | solution.py:19
  228.1 7.1 %all-to-all-done.8 = bf16[8,4,1024]{2,1,0:T(4,128)(2,1)S(1)} async-done(((bf16[8,4,1024]{2,1,0:T(4,128)(2,1)}), bf16[8,4,1024]{2,1,0:T(4,128)(2,1)S(1)}, u32[]{:S(2)}, u32[]{:S(2)}) %all-to-all-start.8) | async-done | bytes 65568 | tf_op jit(solution)/shard_map/all_to_all | solution.py:19
  (91 shorter events, 48.9 us)
Async XLA Ops:
  0.6 33.9 %copy-start = (bf16[256,4096]{1,0:T(8,128)(2,1)S(1)}, bf16[256,4096]{1,0:T(8,128)(2,1)}, u32[]{:S(2)}) copy-start(bf16[256,4096]{1,0:T(8,128)(2,1)} %param.16) | copy-start | bytes 6291460
  2.5 23.3 %all-to-all-start = ((bf16[16,128,128]{2,1,0:T(8,128)(2,1)}), bf16[16,128,128]{2,1,0:T(8,128)(2,1)S(1)}, u32[]{:S(2)}, u32[]{:S(2)}) async-start(bf16[16,128,128]{2,1,0:T(8,128)(2,1)} %broadcast_in_dim.58), calls=%async_computation | async-start | bytes 1048576 | tf_op jit(solution)/shard_map/all_to_all | solution.py:19
  12.1 41.9 %collective-permute-start = (bf16[96,4096]{1,0:T(8,128)(2,1)}, bf16[96,4096]{1,0:T(8,128)(2,1)}, u32[]{:S(2)}, u32[]{:S(2)}) collective-permute-start(bf16[96,4096]{1,0:T(8,128)(2,1)} %bitcast.44), channel_id=1, source_target_pairs={{0,256},{256,0},{1,257},{257,1},{2,258},{258,2},{3,259},{259,3},{4... | collective-permute-start | bytes 2359304 | tf_op jit(solution)/shard_map/ppermute | solution.py:351
  15.3 39.3 %collective-permute-start.1 = (bf16[96,4096]{1,0:T(8,128)(2,1)}, bf16[96,4096]{1,0:T(8,128)(2,1)}, u32[]{:S(2)}, u32[]{:S(2)}) collective-permute-start(bf16[96,4096]{1,0:T(8,128)(2,1)} %bitcast.48), channel_id=1, source_target_pairs={{0,256},{256,0},{1,257},{257,1},{2,258},{258,2},{3,259},{259,3},{4... | collective-permute-start | bytes 2359304 | tf_op jit(solution)/shard_map/ppermute | solution.py:351
  35.0 10.0 %copy-start.14 = (f32[4,8]{1,0:T(4,128)S(1)}, f32[4,8]{1,0:T(4,128)}, u32[]{:S(2)}) copy-start(f32[4,8]{1,0:T(4,128)} %param.19) | copy-start | bytes 388
  35.0 10.0 %copy-start.13 = (s32[4,8]{1,0:T(4,128)S(1)}, s32[4,8]{1,0:T(4,128)}, u32[]{:S(2)}) copy-start(s32[4,8]{1,0:T(4,128)} %param.18) | copy-start | bytes 388
  35.0 10.1 %copy-start.12 = (bf16[4,4096]{1,0:T(4,128)(2,1)S(1)}, bf16[4,4096]{1,0:T(4,128)(2,1)}, u32[]{:S(2)}) copy-start(bf16[4,4096]{1,0:T(4,128)(2,1)} %param.15) | copy-start | bytes 98308
  40.9 39.0 %copy-start.11 = (f32[4096]{0:T(1024)S(1)}, f32[4096]{0:T(1024)}, u32[]{:S(2)}) copy-start(f32[4096]{0:T(1024)} %param.17) | copy-start | bytes 49156
  40.9 13.0 %all-to-all-start.3 = ((bf16[4,16,4096]{2,1,0:T(8,128)(2,1)}), bf16[4,16,4096]{2,1,0:T(8,128)(2,1)S(1)}, u32[]{:S(2)}, u32[]{:S(2)}) async-start(bf16[4,16,4096]{2,1,0:T(8,128)(2,1)} %bitcast.64), calls=%async_computation.3 | async-start | bytes 1048576 | tf_op jit(solution)/shard_map/all_to_all | solution.py:19
  54.0 92.4 %copy-start.1 = (bf16[1,4096,96]{1,2,0:T(8,128)(2,1)S(1)}, bf16[1,4096,96]{1,2,0:T(8,128)(2,1)}, u32[]{:S(2)}) copy-start(bf16[1,4096,96]{1,2,0:T(8,128)(2,1)} %param.20) | copy-start | bytes 2359300
  55.6 24.3 %all-to-all-start.4 = ((bf16[4,16,4224]{2,1,0:T(8,128)(2,1)}), bf16[4,16,4224]{2,1,0:T(8,128)(2,1)S(1)}, u32[]{:S(2)}, u32[]{:S(2)}) async-start(bf16[4,16,4224]{2,1,0:T(8,128)(2,1)} %broadcast_in_dim.69), calls=%async_computation.4 | async-start | bytes 1081344 | tf_op jit(solution)/shard_map/all_to_all | solution.py:19
  64.7 22.8 %collective-permute-start.2 = (bf16[1536,256]{1,0:T(8,128)(2,1)}, bf16[1536,256]{1,0:T(8,128)(2,1)}, u32[]{:S(2)}, u32[]{:S(2)}) collective-permute-start(bf16[1536,256]{1,0:T(8,128)(2,1)} %bitcast.57), channel_id=1, source_target_pairs={{0,32},{32,0},{64,96},{96,64},{128,160},{160,128},{192,224},{224,1... | collective-permute-start | bytes 2359304 | tf_op jit(solution)/shard_map/ppermute | solution.py:380
  82.2 15.0 %all-to-all-start.5 = ((bf16[8,8,4224]{2,1,0:T(8,128)(2,1)}), bf16[8,8,4224]{2,1,0:T(8,128)(2,1)S(1)}, u32[]{:S(2)}, u32[]{:S(2)}) async-start(bf16[8,8,4224]{2,1,0:T(8,128)(2,1)} %copy-done.10), calls=%async_computation.5 | async-start | bytes 1081344 | tf_op jit(solution)/shard_map/all_to_all | solution.py:19
  97.2 16.0 %collective-permute-start.3 = (bf16[64,4224]{1,0:T(8,128)(2,1)S(1)}, bf16[64,4224]{1,0:T(8,128)(2,1)S(1)}, u32[]{:S(2)}, u32[]{:S(2)}) collective-permute-start(bf16[64,4224]{1,0:T(8,128)(2,1)S(1)} %bitcast.52), channel_id=1, source_target_pairs={{0,32},{32,64},{64,96},{96,128},{128,160},{160,192},{192,224},{224... | collective-permute-start | bytes 1622024 | tf_op jit(solution)/shard_map/ppermute | solution.py:402
  100.8 18.7 %collective-permute-start.7 = (bf16[64,4224]{1,0:T(8,128)(2,1)S(1)}, bf16[64,4224]{1,0:T(8,128)(2,1)S(1)}, u32[]{:S(2)}, u32[]{:S(2)}) collective-permute-start(bf16[64,4224]{1,0:T(8,128)(2,1)S(1)} %bitcast.53), channel_id=1, source_target_pairs={{32,0},{64,32},{96,64},{128,96},{160,128},{192,160},{224,192},{0,2... | collective-permute-start | bytes 1622024 | tf_op jit(solution)/shard_map/ppermute | solution.py:405
  113.2 15.1 %collective-permute-start.4 = (bf16[64,4224]{1,0:T(8,128)(2,1)S(1)}, bf16[64,4224]{1,0:T(8,128)(2,1)S(1)}, u32[]{:S(2)}, u32[]{:S(2)}) collective-permute-start(bf16[64,4224]{1,0:T(8,128)(2,1)S(1)} %collective-permute-done.3.refs_1_.refs_9_), channel_id=1, source_target_pairs={{0,32},{32,64},{64,96},{96,128},{128,160},{160,192},{192,224},{224... | collective-permute-start | bytes 1622024 | tf_op jit(solution)/shard_map/ppermute | solution.py:402
  115.6 20.1 %collective-permute-start.9 = (bf16[1536,256]{1,0:T(8,128)(2,1)}, bf16[1536,256]{1,0:T(8,128)(2,1)S(1)}, u32[]{:S(2)}, u32[]{:S(2)}) collective-permute-start(bf16[1536,256]{1,0:T(8,128)(2,1)} %bitcast.58), channel_id=1, source_target_pairs={{0,256},{256,0},{1,257},{257,1},{2,258},{258,2},{3,259},{259,3},{4... | collective-permute-start | bytes 2359304 | tf_op jit(solution)/shard_map/ppermute | solution.py:409
  119.5 17.1 %collective-permute-start.8 = (bf16[64,4224]{1,0:T(8,128)(2,1)S(1)}, bf16[64,4224]{1,0:T(8,128)(2,1)S(1)}, u32[]{:S(2)}, u32[]{:S(2)}) collective-permute-start(bf16[64,4224]{1,0:T(8,128)(2,1)S(1)} %collective-permute-done.7.refs_2_.refs_10_), channel_id=1, source_target_pairs={{32,0},{64,32},{96,64},{128,96},{160,128},{192,160},{224,192},{0,2... | collective-permute-start | bytes 1622024 | tf_op jit(solution)/shard_map/ppermute | solution.py:405
  128.3 16.1 %collective-permute-start.5 = (bf16[64,4224]{1,0:T(8,128)(2,1)S(1)}, bf16[64,4224]{1,0:T(8,128)(2,1)S(1)}, u32[]{:S(2)}, u32[]{:S(2)}) collective-permute-start(bf16[64,4224]{1,0:T(8,128)(2,1)S(1)} %collective-permute-done.4.refs_3_.refs_11_), channel_id=1, source_target_pairs={{0,32},{32,64},{64,96},{96,128},{128,160},{160,192},{192,224},{224... | collective-permute-start | bytes 1622024 | tf_op jit(solution)/shard_map/ppermute | solution.py:402
  136.6 27.2 %collective-permute-start.11 = (bf16[1536,256]{1,0:T(8,128)(2,1)}, bf16[1536,256]{1,0:T(8,128)(2,1)S(1)}, u32[]{:S(2)}, u32[]{:S(2)}) collective-permute-start(bf16[1536,256]{1,0:T(8,128)(2,1)} %collective-permute-done.2.refs_1_), channel_id=1, source_target_pairs={{0,256},{256,0},{1,257},{257,1},{2,258},{258,2},{3,259},{259,3},{4... | collective-permute-start | bytes 2359304 | tf_op jit(solution)/shard_map/ppermute | solution.py:413
  140.1 13.0 %collective-permute-start.10 = (bf16[64,4224]{1,0:T(8,128)(2,1)S(1)}, bf16[64,4224]{1,0:T(8,128)(2,1)S(1)}, u32[]{:S(2)}, u32[]{:S(2)}) collective-permute-start(bf16[64,4224]{1,0:T(8,128)(2,1)S(1)} %collective-permute-done.8.refs_4_.refs_12_), channel_id=1, source_target_pairs={{32,0},{64,32},{96,64},{128,96},{160,128},{192,160},{224,192},{0,2... | collective-permute-start | bytes 1622024 | tf_op jit(solution)/shard_map/ppermute | solution.py:405
  144.4 13.7 %collective-permute-start.6 = (bf16[64,4224]{1,0:T(8,128)(2,1)S(1)}, bf16[64,4224]{1,0:T(8,128)(2,1)S(1)}, u32[]{:S(2)}, u32[]{:S(2)}) collective-permute-start(bf16[64,4224]{1,0:T(8,128)(2,1)S(1)} %collective-permute-done.5.refs_0_.refs_13_), channel_id=1, source_target_pairs={{0,32},{32,64},{64,96},{96,128},{128,160},{160,192},{192,224},{224... | collective-permute-start | bytes 1622024 | tf_op jit(solution)/shard_map/ppermute | solution.py:402
  164.8 24.6 %all-to-all-start.6 = ((bf16[8,192,256]{2,1,0:T(8,128)(2,1)}), bf16[8,192,256]{2,1,0:T(8,128)(2,1)S(1)}, u32[]{:S(2)}, u32[]{:S(2)}) async-start(bf16[8,192,256]{2,1,0:T(8,128)(2,1)} %copy-done.9), calls=%async_computation.6 | async-start | bytes 1572864 | tf_op jit(solution)/shard_map/all_to_all | solution.py:19
  224.7 10.5 %all-to-all-start.8 = ((bf16[8,4,1024]{2,1,0:T(4,128)(2,1)}), bf16[8,4,1024]{2,1,0:T(4,128)(2,1)S(1)}, u32[]{:S(2)}, u32[]{:S(2)}) async-start(bf16[8,4,1024]{2,1,0:T(4,128)(2,1)} %reshape.77), calls=%async_computation.8 | async-start | bytes 131072 | tf_op jit(solution)/shard_map/all_to_all | solution.py:19
  (9 other events, 13.6 us)

commit v12 on v11

--- a/solution.py
+++ b/solution.py
@@ -426,7 +426,6 @@
         width,
         n_y,
     )
-    hidden, down_zy = lax.optimization_barrier((hidden, down_zy))
     hidden = exchange(hidden, "y")
 
     result = down_slots(y_pos % 2, hidden, extra, (down_own, down_y, down_z, down_zy))

time: 238 us -> 237 us (level)
  starting transfers between devices: 73.4 us -> 76.9 us
  waiting for transfers between devices: 85.5 us -> 82.5 us
    all_to_all x6, waiting for transfers between devices: 64.1 us -> 46.9 us  [exchange(): return lax.all_to_all(pieces, axis, 0, 0, tiled=True)]
    ppermute x1, waiting for transfers between devices: 0.01 us -> 13.4 us  [on_device(): down_zy = lax.ppermute(down_y, 'zl', swap_z)]
    all_to_all x6, starting transfers between devices: 36.1 us -> 39.1 us  [exchange(): return lax.all_to_all(pieces, axis, 0, 0, tiled=True)]
    unnamed x30 -> x26, local copies, waits for them, and re-layouts: 8.09 us -> 6.08 us
  transfers between devices with their start and end apart: 18 -> 18, of which waited for: 12 -> 13; matrix products, arithmetic and copies ran while one was open for 2% -> 2% of each run, Pallas kernels for 7% -> 4%
where the time goes in v12:
time: 237 us; the launch traced here: 236 us
  waiting for transfers between devices  82.5 us (35%)
  starting transfers between devices  76.9 us (32%)
  blocking collectives  40.8 us (17%)
  Pallas kernels  18.3 us (8%)
  local copies, waits for them, and re-layouts  10.8 us (5%)
  other arithmetic  3.57 us (2%)
    all_to_all x6, waiting for transfers between devices, exchange(): return lax.all_to_all(pieces, axis, 0, 0, tiled=True)  46.9 us
    all_to_all x3, blocking collectives, exchange(): return lax.all_to_all(pieces, axis, 0, 0, tiled=True)  40.8 us
    all_to_all x6, starting transfers between devices, exchange(): return lax.all_to_all(pieces, axis, 0, 0, tiled=True)  39.1 us
    ppermute x4, waiting for transfers between devices, rightward(): return lax.ppermute(value, 'y', after)  15.9 us
    ppermute x1, waiting for transfers between devices, on_device(): down_zy = lax.ppermute(down_y, 'zl', swap_z)  13.4 us
    ppermute x3, starting transfers between devices, leftward(): return lax.ppermute(value, 'y', before)  12.1 us
    ppermute x4, starting transfers between devices, rightward(): return lax.ppermute(value, 'y', after)  9.85 us
    pallas_call x2, Pallas kernels, first_hidden(): pl.pallas_call(first_kernel, out_shape=jax.ShapeDtypeStruct((2 * units, c...  9.03 us
  transfers between devices with their start and end apart: 18, of which 13 were waited for; matrix products, arithmetic and copies ran while one was open for 2% of the time, Pallas kernels for 4%

profile of v12, /device:TPU:1, one launch (start us, length us, event | category | flops | bytes accessed | tf_op | source)
XLA Modules:
  0.0 235.7 jit_solution(18307539122783464179)
XLA Ops:
  2.5 9.6 %all-to-all-start = ((bf16[16,128,128]{2,1,0:T(8,128)(2,1)}), bf16[16,128,128]{2,1,0:T(8,128)(2,1)S(1)}, u32[]{:S(2)}, u32[]{:S(2)}) async-start(bf16[16,128,128]{2,1,0:T(8,128)(2,1)} %broadcast_in_dim.58), calls=%async_computation | async-start | bytes 1048576 | tf_op jit(solution)/shard_map/all_to_all | solution.py:19
  19.1 6.7 %all-to-all-done = bf16[16,128,128]{2,1,0:T(8,128)(2,1)S(1)} async-done(((bf16[16,128,128]{2,1,0:T(8,128)(2,1)}), bf16[16,128,128]{2,1,0:T(8,128)(2,1)S(1)}, u32[]{:S(2)}, u32[]{:S(2)}) %all-to-all-start) | async-done | bytes 524320 | tf_op jit(solution)/shard_map/all_to_all | solution.py:19
  25.9 7.1 %all_to_all.45 = bf16[2,2048,128]{2,1,0:T(8,128)(2,1)S(1)} all-to-all(bf16[2,2048,128]{2,1,0:T(8,128)(2,1)S(1)} %broadcast_in_dim.60), channel_id=1, replica_groups=mesh['zl'=2,'y'=8,'x'=4,'zh'=4,'co'=2] {'co'}, dimensions={0} | all-to-all | bytes 2097152 | tf_op jit(solution)/shard_map/all_to_all | solution.py:19
  35.0 4.7 %all_to_all.46 = bf16[2,64,4096]{2,1,0:T(8,128)(2,1)S(1)} all-to-all(bf16[2,64,4096]{2,1,0:T(8,128)(2,1)S(1)} %bitcast.61), channel_id=1, replica_groups=mesh['zl'=2,'y'=8,'x'=4,'zh'=4,'co'=2] {'co'}, dimensions={0} | all-to-all | bytes 2097152 | tf_op jit(solution)/shard_map/all_to_all | solution.py:19
  40.9 4.1 %all-to-all-start.3 = ((bf16[4,16,4096]{2,1,0:T(8,128)(2,1)}), bf16[4,16,4096]{2,1,0:T(8,128)(2,1)S(1)}, u32[]{:S(2)}, u32[]{:S(2)}) async-start(bf16[4,16,4096]{2,1,0:T(8,128)(2,1)} %bitcast.64), calls=%async_computation.3 | async-start | bytes 1048576 | tf_op jit(solution)/shard_map/all_to_all | solution.py:19
  45.3 8.6 %all-to-all-done.3 = bf16[4,16,4096]{2,1,0:T(8,128)(2,1)S(1)} async-done(((bf16[4,16,4096]{2,1,0:T(8,128)(2,1)}), bf16[4,16,4096]{2,1,0:T(8,128)(2,1)S(1)}, u32[]{:S(2)}, u32[]{:S(2)}) %all-to-all-start.3) | async-done | bytes 524320 | tf_op jit(solution)/shard_map/all_to_all | solution.py:19
  55.6 9.1 %all-to-all-start.4 = ((bf16[4,16,4224]{2,1,0:T(8,128)(2,1)}), bf16[4,16,4224]{2,1,0:T(8,128)(2,1)S(1)}, u32[]{:S(2)}, u32[]{:S(2)}) async-start(bf16[4,16,4224]{2,1,0:T(8,128)(2,1)} %broadcast_in_dim.69), calls=%async_computation.4 | async-start | bytes 1081344 | tf_op jit(solution)/shard_map/all_to_all | solution.py:19
  67.8 12.0 %all-to-all-done.4.parts_ref = bf16[4,16,4224]{2,1,0:T(8,128)(2,1)S(1)} async-done(((bf16[4,16,4224]{2,1,0:T(8,128)(2,1)}), bf16[4,16,4224]{2,1,0:T(8,128)(2,1)S(1)}, u32[]{:S(2)}, u32[]{:S(2)}) %all-to-all-start.4) | async-done | bytes 540704 | tf_op jit(solution)/shard_map/all_to_all | solution.py:19
  82.2 5.4 %all-to-all-start.5 = ((bf16[8,8,4224]{2,1,0:T(8,128)(2,1)}), bf16[8,8,4224]{2,1,0:T(8,128)(2,1)S(1)}, u32[]{:S(2)}, u32[]{:S(2)}) async-start(bf16[8,8,4224]{2,1,0:T(8,128)(2,1)} %copy-done.8), calls=%async_computation.5 | async-start | bytes 1081344 | tf_op jit(solution)/shard_map/all_to_all | solution.py:19
  87.5 9.7 %all-to-all-done.5 = bf16[8,8,4224]{2,1,0:T(8,128)(2,1)S(1)} async-done(((bf16[8,8,4224]{2,1,0:T(8,128)(2,1)}), bf16[8,8,4224]{2,1,0:T(8,128)(2,1)S(1)}, u32[]{:S(2)}, u32[]{:S(2)}) %all-to-all-start.5) | async-done | bytes 540704 | tf_op jit(solution)/shard_map/all_to_all | solution.py:19
  103.7 9.5 %collective-permute-done.3.refs_1_.refs_9_ = bf16[64,4224]{1,0:T(8,128)(2,1)S(1)} collective-permute-done((bf16[64,4224]{1,0:T(8,128)(2,1)S(1)}, bf16[64,4224]{1,0:T(8,128)(2,1)S(1)}, u32[]{:S(2)}, u32[]{:S(2)}) %collective-permute-start.3) | collective-permute-done | bytes 540704 | tf_op jit(solution)/shard_map/ppermute | solution.py:402
  115.6 3.9 %collective-permute-start.9 = (bf16[1536,256]{1,0:T(8,128)(2,1)}, bf16[1536,256]{1,0:T(8,128)(2,1)S(1)}, u32[]{:S(2)}, u32[]{:S(2)}) collective-permute-start(bf16[1536,256]{1,0:T(8,128)(2,1)} %bitcast.58), channel_id=1, source_target_pairs={{0,256},{256,0},{1,257},{257,1},{2,258},{258,2},{3,259},{259,3},{4... | collective-permute-start | bytes 2359304 | tf_op jit(solution)/shard_map/ppermute | solution.py:409
  119.5 4.6 %collective-permute-start.8 = (bf16[64,4224]{1,0:T(8,128)(2,1)S(1)}, bf16[64,4224]{1,0:T(8,128)(2,1)S(1)}, u32[]{:S(2)}, u32[]{:S(2)}) collective-permute-start(bf16[64,4224]{1,0:T(8,128)(2,1)S(1)} %collective-permute-done.7.refs_2_.refs_10_), channel_id=1, source_target_pairs={{32,0},{64,32},{96,64},{128,96},{160,128},{192,160},{224,192},{0,2... | collective-permute-start | bytes 1622024 | tf_op jit(solution)/shard_map/ppermute | solution.py:405
  124.1 4.2 %collective-permute-done.4.refs_3_.refs_11_ = bf16[64,4224]{1,0:T(8,128)(2,1)S(1)} collective-permute-done((bf16[64,4224]{1,0:T(8,128)(2,1)S(1)}, bf16[64,4224]{1,0:T(8,128)(2,1)S(1)}, u32[]{:S(2)}, u32[]{:S(2)}) %collective-permute-start.4) | collective-permute-done | bytes 540704 | tf_op jit(solution)/shard_map/ppermute | solution.py:402
  130.2 5.5 %collective-permute-done.9.refs_2_ = bf16[1536,256]{1,0:T(8,128)(2,1)S(1)} collective-permute-done((bf16[1536,256]{1,0:T(8,128)(2,1)}, bf16[1536,256]{1,0:T(8,128)(2,1)S(1)}, u32[]{:S(2)}, u32[]{:S(2)}) %collective-permute-start.9) | collective-permute-done | bytes 786464 | tf_op jit(solution)/shard_map/ppermute | solution.py:409
  136.6 4.6 %collective-permute-start.10 = (bf16[64,4224]{1,0:T(8,128)(2,1)S(1)}, bf16[64,4224]{1,0:T(8,128)(2,1)S(1)}, u32[]{:S(2)}, u32[]{:S(2)}) collective-permute-start(bf16[64,4224]{1,0:T(8,128)(2,1)S(1)} %collective-permute-done.8.refs_4_.refs_12_), channel_id=1, source_target_pairs={{32,0},{64,32},{96,64},{128,96},{160,128},{192,160},{224,192},{0,2... | collective-permute-start | bytes 1622024 | tf_op jit(solution)/shard_map/ppermute | solution.py:405
  145.6 5.1 %shard_map.132.refs_6_ = bf16[192,320]{1,0:T(8,128)(2,1)S(1)} custom-call(s32[1]{0:T(128)} %bitcast.20.zl_ref, bf16[64,4224]{1,0:T(8,128)(2,1)S(1)} %bitcast.54, bf16[64,4224]{1,0:T(8,128)(2,1)S(1)} %collective-permute-done.3.refs_1_.refs_9_, bf16[64,4224]{1,0:T(8,128)(2,1)S(1)} %collective-permute-done.7.refs_2_.refs_10_, ...), custom_call_target="tpu_custom_call" | custom-call | flops 1006632960 | bytes 5767168 | tf_op jit(solution)/shard_map/pallas_call | solution.py:224
  150.7 3.9 %shard_map.133.refs_7_ = bf16[192,128]{1,0:T(8,128)(2,1)S(1)} custom-call(s32[1]{0:T(128)} %bitcast.20.zl_ref, bf16[64,4224]{1,0:T(8,128)(2,1)S(1)} %collective-permute-done.5.refs_0_.refs_13_, bf16[64,4224]{1,0:T(8,128)(2,1)S(1)} %collective-permute-done.10.refs_1_.refs_14_, bf16[96,4096]{1,0:T(8,128)(2,1)S(1)} %bitcast.46, ...), custom_call_target="tpu_custom_call" | custom-call | flops 402653184 | bytes 4194304 | tf_op jit(solution)/shard_map/pallas_call | solution.py:224
  155.7 4.9 %shard_map.134 = (bf16[8,192,256]{2,1,0:T(8,128)(2,1)S(1)}, bf16[512,128]{1,0:T(8,128)(2,1)S(1)}) custom-call(s32[2]{0:T(128)S(1)} %pad_add_fusion.1.refs_0_, bf16[64,4224]{1,0:T(8,128)(2,1)S(1)} %collective-permute-done.6.refs_1_.refs_15_, bf16[96,4096]{1,0:T(8,128)(2,1)S(1)} %bitcast.47, bf16[96,4096]{1,0:T(8,128)(2,1)} %collective-permute-done.refs_6_.refs_3_, ...), custom_call_target="tpu_custom_call" | custom-call | flops 201326592 | bytes 3670016 | tf_op jit(solution)/shard_map/pallas_call | solution.py:244
  161.6 6.2 %all-to-all-start.6 = ((bf16[8,192,256]{2,1,0:T(8,128)(2,1)}), bf16[8,192,256]{2,1,0:T(8,128)(2,1)S(1)}, u32[]{:S(2)}, u32[]{:S(2)}) async-start(bf16[8,192,256]{2,1,0:T(8,128)(2,1)} %copy-done.7), calls=%async_computation.6 | async-start | bytes 1572864 | tf_op jit(solution)/shard_map/all_to_all | solution.py:19
  171.5 13.4 %collective-permute-done.11.refs_3_ = bf16[1536,256]{1,0:T(8,128)(2,1)} collective-permute-done((bf16[1536,256]{1,0:T(8,128)(2,1)}, bf16[1536,256]{1,0:T(8,128)(2,1)}, u32[]{:S(2)}, u32[]{:S(2)}) %collective-permute-start.11) | collective-permute-done | bytes 786464 | tf_op jit(solution)/shard_map/ppermute | solution.py:413
  192.9 28.9 %all_to_all.47 = bf16[32,8,1152]{2,1,0:T(8,128)(2,1)S(1)} all-to-all(bf16[32,8,1152]{2,1,0:T(8,128)(2,1)S(1)} %bitcast.56), channel_id=1, replica_groups=mesh['zl'=2,'y'=8,'x'=4,'zh'=4,'co'=2] {'x','zh','co'}, dimensions={0} | all-to-all | bytes 1179648 | tf_op jit(solution)/shard_map/all_to_all | solution.py:19
  222.7 4.7 %all-to-all-start.8 = ((bf16[8,4,1024]{2,1,0:T(4,128)(2,1)}), bf16[8,4,1024]{2,1,0:T(4,128)(2,1)S(1)}, u32[]{:S(2)}, u32[]{:S(2)}) async-start(bf16[8,4,1024]{2,1,0:T(4,128)(2,1)} %reshape.77), calls=%async_computation.8 | async-start | bytes 131072 | tf_op jit(solution)/shard_map/all_to_all | solution.py:19
  227.4 7.2 %all-to-all-done.8 = bf16[8,4,1024]{2,1,0:T(4,128)(2,1)S(1)} async-done(((bf16[8,4,1024]{2,1,0:T(4,128)(2,1)}), bf16[8,4,1024]{2,1,0:T(4,128)(2,1)S(1)}, u32[]{:S(2)}, u32[]{:S(2)}) %all-to-all-start.8) | async-done | bytes 65568 | tf_op jit(solution)/shard_map/all_to_all | solution.py:19
  (87 shorter events, 50.9 us)
Async XLA Ops:
  0.6 33.9 %copy-start = (bf16[256,4096]{1,0:T(8,128)(2,1)S(1)}, bf16[256,4096]{1,0:T(8,128)(2,1)}, u32[]{:S(2)}) copy-start(bf16[256,4096]{1,0:T(8,128)(2,1)} %param.16) | copy-start | bytes 6291460
  2.5 23.3 %all-to-all-start = ((bf16[16,128,128]{2,1,0:T(8,128)(2,1)}), bf16[16,128,128]{2,1,0:T(8,128)(2,1)S(1)}, u32[]{:S(2)}, u32[]{:S(2)}) async-start(bf16[16,128,128]{2,1,0:T(8,128)(2,1)} %broadcast_in_dim.58), calls=%async_computation | async-start | bytes 1048576 | tf_op jit(solution)/shard_map/all_to_all | solution.py:19
  12.1 41.9 %collective-permute-start = (bf16[96,4096]{1,0:T(8,128)(2,1)}, bf16[96,4096]{1,0:T(8,128)(2,1)}, u32[]{:S(2)}, u32[]{:S(2)}) collective-permute-start(bf16[96,4096]{1,0:T(8,128)(2,1)} %bitcast.44), channel_id=1, source_target_pairs={{0,256},{256,0},{1,257},{257,1},{2,258},{258,2},{3,259},{259,3},{4... | collective-permute-start | bytes 2359304 | tf_op jit(solution)/shard_map/ppermute | solution.py:351
  15.3 39.3 %collective-permute-start.1 = (bf16[96,4096]{1,0:T(8,128)(2,1)}, bf16[96,4096]{1,0:T(8,128)(2,1)}, u32[]{:S(2)}, u32[]{:S(2)}) collective-permute-start(bf16[96,4096]{1,0:T(8,128)(2,1)} %bitcast.48), channel_id=1, source_target_pairs={{0,256},{256,0},{1,257},{257,1},{2,258},{258,2},{3,259},{259,3},{4... | collective-permute-start | bytes 2359304 | tf_op jit(solution)/shard_map/ppermute | solution.py:351
  35.0 10.0 %copy-start.12 = (f32[4,8]{1,0:T(4,128)S(1)}, f32[4,8]{1,0:T(4,128)}, u32[]{:S(2)}) copy-start(f32[4,8]{1,0:T(4,128)} %param.19) | copy-start | bytes 388
  35.0 10.0 %copy-start.11 = (s32[4,8]{1,0:T(4,128)S(1)}, s32[4,8]{1,0:T(4,128)}, u32[]{:S(2)}) copy-start(s32[4,8]{1,0:T(4,128)} %param.18) | copy-start | bytes 388
  35.0 10.1 %copy-start.10 = (bf16[4,4096]{1,0:T(4,128)(2,1)S(1)}, bf16[4,4096]{1,0:T(4,128)(2,1)}, u32[]{:S(2)}) copy-start(bf16[4,4096]{1,0:T(4,128)(2,1)} %param.15) | copy-start | bytes 98308
  40.9 39.0 %copy-start.9 = (f32[4096]{0:T(1024)S(1)}, f32[4096]{0:T(1024)}, u32[]{:S(2)}) copy-start(f32[4096]{0:T(1024)} %param.17) | copy-start | bytes 49156
  40.9 13.1 %all-to-all-start.3 = ((bf16[4,16,4096]{2,1,0:T(8,128)(2,1)}), bf16[4,16,4096]{2,1,0:T(8,128)(2,1)S(1)}, u32[]{:S(2)}, u32[]{:S(2)}) async-start(bf16[4,16,4096]{2,1,0:T(8,128)(2,1)} %bitcast.64), calls=%async_computation.3 | async-start | bytes 1048576 | tf_op jit(solution)/shard_map/all_to_all | solution.py:19
  54.0 90.5 %copy-start.1 = (bf16[1,4096,96]{1,2,0:T(8,128)(2,1)S(1)}, bf16[1,4096,96]{1,2,0:T(8,128)(2,1)}, u32[]{:S(2)}) copy-start(bf16[1,4096,96]{1,2,0:T(8,128)(2,1)} %param.20) | copy-start | bytes 2359300
  55.6 24.3 %all-to-all-start.4 = ((bf16[4,16,4224]{2,1,0:T(8,128)(2,1)}), bf16[4,16,4224]{2,1,0:T(8,128)(2,1)S(1)}, u32[]{:S(2)}, u32[]{:S(2)}) async-start(bf16[4,16,4224]{2,1,0:T(8,128)(2,1)} %broadcast_in_dim.69), calls=%async_computation.4 | async-start | bytes 1081344 | tf_op jit(solution)/shard_map/all_to_all | solution.py:19
  64.7 22.8 %collective-permute-start.2 = (bf16[1536,256]{1,0:T(8,128)(2,1)}, bf16[1536,256]{1,0:T(8,128)(2,1)}, u32[]{:S(2)}, u32[]{:S(2)}) collective-permute-start(bf16[1536,256]{1,0:T(8,128)(2,1)} %bitcast.57), channel_id=1, source_target_pairs={{0,32},{32,0},{64,96},{96,64},{128,160},{160,128},{192,224},{224,1... | collective-permute-start | bytes 2359304 | tf_op jit(solution)/shard_map/ppermute | solution.py:380
  82.2 15.0 %all-to-all-start.5 = ((bf16[8,8,4224]{2,1,0:T(8,128)(2,1)}), bf16[8,8,4224]{2,1,0:T(8,128)(2,1)S(1)}, u32[]{:S(2)}, u32[]{:S(2)}) async-start(bf16[8,8,4224]{2,1,0:T(8,128)(2,1)} %copy-done.8), calls=%async_computation.5 | async-start | bytes 1081344 | tf_op jit(solution)/shard_map/all_to_all | solution.py:19
  97.2 16.0 %collective-permute-start.3 = (bf16[64,4224]{1,0:T(8,128)(2,1)S(1)}, bf16[64,4224]{1,0:T(8,128)(2,1)S(1)}, u32[]{:S(2)}, u32[]{:S(2)}) collective-permute-start(bf16[64,4224]{1,0:T(8,128)(2,1)S(1)} %bitcast.52), channel_id=1, source_target_pairs={{0,32},{32,64},{64,96},{96,128},{128,160},{160,192},{192,224},{224... | collective-permute-start | bytes 1622024 | tf_op jit(solution)/shard_map/ppermute | solution.py:402
  100.8 18.7 %collective-permute-start.7 = (bf16[64,4224]{1,0:T(8,128)(2,1)S(1)}, bf16[64,4224]{1,0:T(8,128)(2,1)S(1)}, u32[]{:S(2)}, u32[]{:S(2)}) collective-permute-start(bf16[64,4224]{1,0:T(8,128)(2,1)S(1)} %bitcast.53), channel_id=1, source_target_pairs={{32,0},{64,32},{96,64},{128,96},{160,128},{192,160},{224,192},{0,2... | collective-permute-start | bytes 1622024 | tf_op jit(solution)/shard_map/ppermute | solution.py:405
  113.2 15.1 %collective-permute-start.4 = (bf16[64,4224]{1,0:T(8,128)(2,1)S(1)}, bf16[64,4224]{1,0:T(8,128)(2,1)S(1)}, u32[]{:S(2)}, u32[]{:S(2)}) collective-permute-start(bf16[64,4224]{1,0:T(8,128)(2,1)S(1)} %collective-permute-done.3.refs_1_.refs_9_), channel_id=1, source_target_pairs={{0,32},{32,64},{64,96},{96,128},{128,160},{160,192},{192,224},{224... | collective-permute-start | bytes 1622024 | tf_op jit(solution)/shard_map/ppermute | solution.py:402
  115.6 20.1 %collective-permute-start.9 = (bf16[1536,256]{1,0:T(8,128)(2,1)}, bf16[1536,256]{1,0:T(8,128)(2,1)S(1)}, u32[]{:S(2)}, u32[]{:S(2)}) collective-permute-start(bf16[1536,256]{1,0:T(8,128)(2,1)} %bitcast.58), channel_id=1, source_target_pairs={{0,256},{256,0},{1,257},{257,1},{2,258},{258,2},{3,259},{259,3},{4... | collective-permute-start | bytes 2359304 | tf_op jit(solution)/shard_map/ppermute | solution.py:409
  119.5 17.1 %collective-permute-start.8 = (bf16[64,4224]{1,0:T(8,128)(2,1)S(1)}, bf16[64,4224]{1,0:T(8,128)(2,1)S(1)}, u32[]{:S(2)}, u32[]{:S(2)}) collective-permute-start(bf16[64,4224]{1,0:T(8,128)(2,1)S(1)} %collective-permute-done.7.refs_2_.refs_10_), channel_id=1, source_target_pairs={{32,0},{64,32},{96,64},{128,96},{160,128},{192,160},{224,192},{0,2... | collective-permute-start | bytes 1622024 | tf_op jit(solution)/shard_map/ppermute | solution.py:405
  128.3 14.2 %collective-permute-start.5 = (bf16[64,4224]{1,0:T(8,128)(2,1)S(1)}, bf16[64,4224]{1,0:T(8,128)(2,1)S(1)}, u32[]{:S(2)}, u32[]{:S(2)}) collective-permute-start(bf16[64,4224]{1,0:T(8,128)(2,1)S(1)} %collective-permute-done.4.refs_3_.refs_11_), channel_id=1, source_target_pairs={{0,32},{32,64},{64,96},{96,128},{128,160},{160,192},{192,224},{224... | collective-permute-start | bytes 1622024 | tf_op jit(solution)/shard_map/ppermute | solution.py:402
  136.6 14.1 %collective-permute-start.10 = (bf16[64,4224]{1,0:T(8,128)(2,1)S(1)}, bf16[64,4224]{1,0:T(8,128)(2,1)S(1)}, u32[]{:S(2)}, u32[]{:S(2)}) collective-permute-start(bf16[64,4224]{1,0:T(8,128)(2,1)S(1)} %collective-permute-done.8.refs_4_.refs_12_), channel_id=1, source_target_pairs={{32,0},{64,32},{96,64},{128,96},{160,128},{192,160},{224,192},{0,2... | collective-permute-start | bytes 1622024 | tf_op jit(solution)/shard_map/ppermute | solution.py:405
  142.5 13.2 %collective-permute-start.6 = (bf16[64,4224]{1,0:T(8,128)(2,1)S(1)}, bf16[64,4224]{1,0:T(8,128)(2,1)S(1)}, u32[]{:S(2)}, u32[]{:S(2)}) collective-permute-start(bf16[64,4224]{1,0:T(8,128)(2,1)S(1)} %collective-permute-done.5.refs_0_.refs_13_), channel_id=1, source_target_pairs={{0,32},{32,64},{64,96},{96,128},{128,160},{160,192},{192,224},{224... | collective-permute-start | bytes 1622024 | tf_op jit(solution)/shard_map/ppermute | solution.py:402
  161.6 26.1 %all-to-all-start.6 = ((bf16[8,192,256]{2,1,0:T(8,128)(2,1)}), bf16[8,192,256]{2,1,0:T(8,128)(2,1)S(1)}, u32[]{:S(2)}, u32[]{:S(2)}) async-start(bf16[8,192,256]{2,1,0:T(8,128)(2,1)} %copy-done.7), calls=%async_computation.6 | async-start | bytes 1572864 | tf_op jit(solution)/shard_map/all_to_all | solution.py:19
  167.7 17.2 %collective-permute-start.11 = (bf16[1536,256]{1,0:T(8,128)(2,1)}, bf16[1536,256]{1,0:T(8,128)(2,1)}, u32[]{:S(2)}, u32[]{:S(2)}) collective-permute-start(bf16[1536,256]{1,0:T(8,128)(2,1)} %collective-permute-done.2.refs_1_), channel_id=1, source_target_pairs={{0,256},{256,0},{1,257},{257,1},{2,258},{258,2},{3,259},{259,3},{4... | collective-permute-start | bytes 2359304 | tf_op jit(solution)/shard_map/ppermute | solution.py:413
  222.7 11.9 %all-to-all-start.8 = ((bf16[8,4,1024]{2,1,0:T(4,128)(2,1)}), bf16[8,4,1024]{2,1,0:T(4,128)(2,1)S(1)}, u32[]{:S(2)}, u32[]{:S(2)}) async-start(bf16[8,4,1024]{2,1,0:T(4,128)(2,1)} %reshape.77), calls=%async_computation.8 | async-start | bytes 131072 | tf_op jit(solution)/shard_map/all_to_all | solution.py:19
  (7 other events, 11.2 us)
